TPU v7x, 32 devices: a whole 2x2x4 slice. The times are simulated.
32 devices in a mesh: wide: 8 (over z, y), narrow: 4 (over x, core).
Axes of the slice: x: 2, y: 2, z: 4, core: 2. Of those that a mesh axis runs over, the one named last changes fastest.
Arguments:
- patches: bfloat16 [8192, 1280], P('wide', 'narrow'), may hold values from -6 to 6
- norm_gain: float32 [1280], replicated, may hold values from 0.1 to 1.9
- norm_bias: float32 [1280], replicated, may hold values from -3 to 3
- w_in: bfloat16 [1280, 5120], P('wide', 'narrow'), may hold values from -0.15625 to 0.15625
- b_in: float32 [5120], P('narrow'), may hold values from -3 to 3
- w_out: bfloat16 [5120, 1280], P('narrow', 'wide'), may hold values from -0.078125 to 0.078125
- b_out: float32 [1280], P('narrow'), may hold values from -3 to 3
- w_proj: bfloat16 [4, 1280, 1280], P(None, 'narrow', 'wide'), may hold values from -0.078125 to 0.078125
- b_proj: float32 [1280], P('narrow'), may hold values from -3 to 3
- text: bfloat16 [4096, 1280], P('wide', 'narrow'), may hold values from -6 to 6
- place: int32 [2048], replicated, may hold values from -1 to 4095, as said below
Outputs:
- prompt_embeds: bfloat16 [4096, 1280], P('wide', 'narrow')
Inputs may be any that keep to these rules, and one draw needn't show every extreme that they name: `place`: of the 256 entries of one wide index (entries i * 256 to (i + 1) * 256 - 1), the valid ones (>= 0) come first and -1 fills the rest; three quarters or more are valid, and all are valid for some wide index. Valid values are distinct. For one wide index, at most 64 valid entries v have the same v // 512, and every wide index reaches 64 for some value.
All inputs are finite; a program needn't handle non-finite values.
Results may differ from a plain program's by a relative error of at most 0.012.
Values may be sent and summed in bfloat16 or wider, within the bound.
No kernel may reach another device: no remote copies, remote signals or barrier semaphores. Data moves between devices by JAX's collectives and lax.ppermute only.
A program may use at most 64 MiB of HBM per device.

v0:
```python
import jax
import jax.numpy as jnp
from jax import lax
from jax.sharding import PartitionSpec as P


def per_device(
    patches, norm_gain, norm_bias, w_in, b_in, w_out, b_out, w_proj, b_proj, text, place
):
    whole = lax.all_gather(patches, "narrow", axis=1, tiled=True)
    values = whole.astype(jnp.float32)
    center = jnp.mean(values, axis=-1, keepdims=True)
    spread = jnp.mean(jnp.square(values - center), axis=-1, keepdims=True)
    normed = ((values - center) * lax.rsqrt(spread + 1e-06) * norm_gain + norm_bias).astype(
        jnp.bfloat16
    )
    rows_in, cols_out, proj_cols = (
        lax.all_gather(w_in, "wide", axis=0, tiled=True),
        lax.all_gather(w_out, "wide", axis=1, tiled=True),
        lax.all_gather(w_proj, "wide", axis=2, tiled=True),
    )
    product = jnp.dot(normed, rows_in, preferred_element_type=jnp.float32)
    hidden = jax.nn.gelu(product + b_in, approximate=False).astype(jnp.bfloat16)
    partial_out = jnp.dot(hidden, cols_out, preferred_element_type=jnp.float32)
    mlp_out = lax.psum_scatter(
        partial_out.astype(jnp.bfloat16), "narrow", scatter_dimension=1, tiled=True
    ).astype(jnp.float32)
    stream = (patches.astype(jnp.float32) + (mlp_out + b_out)).astype(jnp.bfloat16)
    merge_count = stream.shape[0] // 4
    merged = stream.reshape(merge_count, 4 * stream.shape[1])
    groups = lax.axis_size("wide")
    own_index = lax.axis_index("wide")
    seq_rows = text.shape[0]
    bucket = seq_rows // groups
    place_table = place.reshape(groups, merge_count)
    owners = jnp.where(place_table >= 0, place_table // seq_rows, groups)
    own_owners = lax.dynamic_index_in_dim(owners, own_index, 0, keepdims=False)
    owner_hits = (own_owners[:, None] == jnp.arange(groups, dtype=jnp.int32)[None, :]).astype(
        jnp.int32
    )
    slot_out = jnp.sum(jnp.cumsum(owner_hits, axis=0) * owner_hits, axis=1) - 1
    slot_out = jnp.where(own_owners < groups, slot_out, bucket)
    arriving = owners == own_index
    slot_in = jnp.cumsum(arriving.astype(jnp.int32), axis=1) - 1
    slot_in = jnp.where(arriving, slot_in, bucket)
    local_row = jnp.where(arriving, place_table % seq_rows, seq_rows)
    source_ids = jnp.arange(groups, dtype=jnp.int32)[:, None]
    targets = (
        jnp.full((groups, bucket), seq_rows, jnp.int32)
        .at[source_ids, slot_in]
        .set(local_row, mode="drop")
    )
    buffer = jnp.zeros((groups, bucket, merged.shape[1]), merged.dtype)
    received = lax.all_to_all(
        buffer.at[own_owners, slot_out].set(merged, mode="drop"),
        "wide",
        split_axis=0,
        concat_axis=0,
        tiled=True,
    )
    slot_rows = received.reshape(-1, received.shape[2])
    late_terms = jnp.dot(
        slot_rows, proj_cols.reshape(-1, proj_cols.shape[2]), preferred_element_type=jnp.float32
    )
    vision = (
        lax.psum_scatter(
            late_terms.astype(jnp.bfloat16), "narrow", scatter_dimension=1, tiled=True
        ).astype(jnp.float32)
        + b_proj
    ).astype(jnp.bfloat16)
    received = vision.reshape(groups, bucket, vision.shape[1])
    return text.at[targets.reshape(-1)].set(received.reshape(-1, received.shape[2]), mode="drop")


def solution(mesh):
    placed = (
        P("wide", "narrow"),
        P(),
        P(),
        P("wide", "narrow"),
        P("narrow"),
        P("narrow", "wide"),
        P("narrow"),
        P(None, "narrow", "wide"),
        P("narrow"),
        P("wide", "narrow"),
        P(),
    )
    return jax.shard_map(
        per_device, mesh=mesh, in_specs=placed, out_specs=P("wide", "narrow"), check_vma=False
    )
```

profile of v0, /device:TPU:0, one launch (start us, length us, event | category | flops | bytes accessed | tf_op | source)
XLA Modules:
  0.0 362.5 jit_solution(7554508558939585281)
XLA Ops:
  6.5 0.7 all-gather.5.cloned.1.call-update
  7.3 0.7 all-gather.7.cloned.1.call-update
  8.1 0.7 all-gather.9.cloned.1.call-update
  8.8 28.4 %all-gather.5.cloned.1.call-done = bf16[1024,1280]{0,1:T(8,128)(2,1)} async-done(((bf16[1024,320]{0,1:T(8,128)(2,1)}), bf16[1024,1280]{0,1:T(8,128)(2,1)}) %all-gather.5.cloned.1.call-update) | async-done | bytes 2621456 | tf_op jit(solution)/shard_map/all_gather | solution.py:10
  37.2 2.3 convert_reduce_fusion
  39.7 0.7 fusion.2
  40.5 60.9 %all-gather.7.cloned.1.call-done = bf16[1280,1280]{1,0:T(8,128)(2,1)} async-done(((bf16[160,1280]{1,0:T(8,128)(2,1)}), bf16[1280,1280]{1,0:T(8,128)(2,1)}) %all-gather.7.cloned.1.call-update) | async-done | bytes 3276816 | tf_op jit(solution)/shard_map/all_gather | solution.py:18
  101.4 62.8 %all-gather.9.cloned.1.call-done = bf16[1280,1280]{0,1:T(8,128)(2,1)} async-done(((bf16[1280,160]{0,1:T(8,128)(2,1)}), bf16[1280,1280]{0,1:T(8,128)(2,1)}) %all-gather.9.cloned.1.call-update) | async-done | bytes 3276816 | tf_op jit(solution)/shard_map/all_gather | solution.py:19
  164.2 21.4 %convolution_convert_fusion = bf16[1024,1280]{0,1:T(8,128)(2,1)} fusion(bf16[1280,1280]{0,1:T(8,128)(2,1)} %all-gather.9.cloned.1.call-done, bf16[1280,1280]{1,0:T(8,128)(2,1)} %all-gather.7.cloned.1.call-done, bf16[1024,1280]{0,1:T(8,128)(2,1)S(1)} %copy-done, f32[1280]{0:T(1024)S(1)} %copy-done.8, f32[1280]{0:T(1024)S(1)} %copy-done.9, ...), kind=kOutput, calls=%fused_computation.30 | convolution fusion | flops 6806568960 | bytes 11820032 | tf_op jit(solution)/shard_map/dot_general | solution.py:24
  185.7 1.1 copy.28
  186.9 0.6 reduce-window.16
  187.5 0.2 slice_reduce_fusion
  187.8 31.2 %reduce-scatter.3.cloned.1.call-done = bf16[1024,320]{0,1:T(8,128)(2,1)} async-done(((bf16[1024,1280]{0,1:T(8,128)(2,1)}), bf16[1024,320]{0,1:T(8,128)(2,1)}) %reduce-scatter.3.cloned.1.call-update) | async-done | bytes 655376 | tf_op jit(solution)/shard_map/reduce_scatter | solution.py:25
  219.0 1.3 add_convert_fusion
  220.4 0.4 copy.27
  220.8 0.7 reshape.297
  221.5 1.2 broadcast_in_dim.47
  222.7 38.8 %scatter_fusion = bf16[8,64,1280]{2,1,0:T(8,128)(2,1)} fusion(bf16[8,64,1280]{2,1,0:T(8,128)(2,1)} %broadcast_in_dim.47, s32[256]{0:T(256)S(1)} %bitcast.34, bf16[256,1280]{1,0:T(8,128)(2,1)S(1)} %reshape.297), kind=kCustom, calls=%fused_computation | custom fusion | bytes 1968128 | tf_op jit(solution)/shard_map/scatter | solution.py:55
  261.5 5.6 %all-to-all-start = ((bf16[8,64,1280]{2,1,0:T(8,128)(2,1)}), bf16[8,64,1280]{2,1,0:T(8,128)(2,1)}, u32[]{:S(2)}, u32[]{:S(2)}) async-start(bf16[8,64,1280]{2,1,0:T(8,128)(2,1)} %scatter_fusion), calls=%async_computation.1 | async-start | bytes 2621440 | tf_op jit(solution)/shard_map/all_to_all | solution.py:54
  267.1 0.3 reduce-scatter.5.cloned.1.call-start
  267.3 47.3 %all-gather.11.cloned.1.call-done = bf16[4,320,1280]{1,0,2:T(4,128)(2,1)} async-done(((bf16[4,320,160]{1,0,2:T(4,128)(2,1)}), bf16[4,320,1280]{1,0,2:T(4,128)(2,1)}) %all-gather.11.cloned.1.call-update) | async-done | bytes 3276816 | tf_op jit(solution)/shard_map/all_gather | solution.py:20
  314.7 7.3 %copy.29 = bf16[4,320,1280]{2,1,0:T(8,128)(2,1)S(1)} copy(bf16[4,320,1280]{1,0,2:T(4,128)(2,1)} %all-gather.11.cloned.1.call-done) | data formatting | bytes 6553600 | tf_op jit(solution)/shard_map/all_gather | solution.py:20
  322.1 4.3 %convolution_convert_fusion.1 = bf16[512,1280]{0,1:T(8,128)(2,1)} fusion(bf16[512,1280]{1,0:T(8,128)(2,1)} %bitcast.11, bf16[1280,1280]{1,0:T(8,128)(2,1)S(1)} %bitcast.35), kind=kOutput, calls=%fused_computation.31 | convolution fusion | flops 1678376960 | bytes 5898240 | tf_op jit(solution)/shard_map/dot_general | solution.py:62
  326.4 0.6 reduce-window.14
  327.0 0.2 slice_reduce_fusion.1
  327.6 1.2 copy.30
  328.7 8.0 %scatter_custom_fusion.2 = s32[512]{0:T(512)S(1)} fusion(s32[2048]{0:T(1024)S(1)} %bitcast.41, s32[2048]{0:T(1024)S(1)} %bitcast.42, s32[]{:T(128)} %constant.43.clone.1), kind=kCustom, calls=%fused_computation.91 | custom fusion | bytes 2052
  336.8 14.0 %reduce-scatter.5.cloned.1.call-done = bf16[512,320]{0,1:T(8,128)(2,1)} async-done(((bf16[512,1280]{0,1:T(8,128)(2,1)}), bf16[512,320]{0,1:T(8,128)(2,1)}) %reduce-scatter.5.cloned.1.call-update) | async-done | bytes 327696 | tf_op jit(solution)/shard_map/reduce_scatter | solution.py:66
  350.8 1.1 add_convert_fusion.1
  351.9 0.2 copy.31
  352.2 2.6 scatter_fusion.1
  354.7 0.9 copy.32
  (54 shorter events, 1.0 us)
Async XLA Ops:
  6.5 157.7 %copy-start.8 = (f32[1280]{0:T(1024)S(1)}, f32[1280]{0:T(1024)}, u32[]{:S(2)}) copy-start(f32[1280]{0:T(1024)} %param.15) | copy-start | bytes 15364
  6.5 157.7 %copy-start.9 = (f32[1280]{0:T(1024)S(1)}, f32[1280]{0:T(1024)}, u32[]{:S(2)}) copy-start(f32[1280]{0:T(1024)} %param.13) | copy-start | bytes 15364
  6.5 157.7 %copy-start.10 = (f32[1280]{0:T(1024)S(1)}, f32[1280]{0:T(1024)}, u32[]{:S(2)}) copy-start(f32[1280]{0:T(1024)} %param.12) | copy-start | bytes 15364
  6.5 30.7 %all-gather.5.cloned.1.call-start = ((), (), s32[]{:S(2)}) async-start(), calls=%async_computation.3 | async-start | bytes 3276800 | tf_op jit(solution)/shard_map/all_gather | solution.py:10
  7.3 94.1 %all-gather.7.cloned.1.call-start = ((), (), s32[]{:S(2)}) async-start(), calls=%async_computation.4 | async-start | bytes 3686400 | tf_op jit(solution)/shard_map/all_gather | solution.py:18
  8.0 156.2 %all-gather.9.cloned.1.call-start = ((), (), s32[]{:S(2)}) async-start(), calls=%async_computation.5 | async-start | bytes 3686400 | tf_op jit(solution)/shard_map/all_gather | solution.py:19
  8.7 210.3 %reduce-scatter.3.cloned.1.call-start = ((), (), s32[]{:S(2)}) async-start(), calls=%async_computation.6 | async-start | bytes 3276800 | tf_op jit(solution)/shard_map/reduce_scatter | solution.py:25
  37.2 2.5 copy-start
  40.5 145.2 %copy-start.2 = (bf16[4,320,160]{1,2,0:T(8,128)(2,1)S(1)}, bf16[4,320,160]{1,2,0:T(8,128)(2,1)}, u32[]{:S(2)}) copy-start(bf16[4,320,160]{1,2,0:T(8,128)(2,1)} %param.18) | copy-start | bytes 1228804
  185.6 1.2 copy-start.3
  185.6 33.4 %copy-start.1 = (bf16[1024,320]{0,1:T(8,128)(2,1)S(1)}, bf16[1024,320]{0,1:T(8,128)(2,1)}, u32[]{:S(2)}) copy-start(bf16[1024,320]{0,1:T(8,128)(2,1)} %param.11) | copy-start | bytes 1966084
  185.6 33.4 %copy-start.4 = (f32[320]{0:T(512)S(1)}, f32[320]{0:T(512)}, u32[]{:S(2)}) copy-start(f32[320]{0:T(512)} %param.17) | copy-start | bytes 3844
  185.6 129.1 %all-gather.11.cloned.1.call-start = ((), (), s32[]{:S(2)}) async-start(), calls=%async_computation.7 | async-start | bytes 4423680 | tf_op jit(solution)/shard_map/all_gather | solution.py:20
  261.5 60.6 %all-to-all-start = ((bf16[8,64,1280]{2,1,0:T(8,128)(2,1)}), bf16[8,64,1280]{2,1,0:T(8,128)(2,1)}, u32[]{:S(2)}, u32[]{:S(2)}) async-start(bf16[8,64,1280]{2,1,0:T(8,128)(2,1)} %scatter_fusion), calls=%async_computation.1 | async-start | bytes 2621440 | tf_op jit(solution)/shard_map/all_to_all | solution.py:54
  267.1 83.7 %reduce-scatter.5.cloned.1.call-start = ((), (), s32[]{:S(2)}) async-start(), calls=%async_computation.8 | async-start | bytes 1638400 | tf_op jit(solution)/shard_map/reduce_scatter | solution.py:66
  322.0 5.3 %copy-start.7 = (s32[2]{0:T(128)S(1)}, s32[2]{0:T(128)}, u32[]{:S(2)}) copy-start(s32[2]{0:T(128)} %constant.134) | copy-start | bytes 28
  322.0 5.4 %copy-start.6 = (s32[2]{0:T(128)S(1)}, s32[2]{0:T(128)}, u32[]{:S(2)}) copy-start(s32[2]{0:T(128)} %constant.137) | copy-start | bytes 28
  322.1 28.8 %copy-start.5 = (f32[320]{0:T(512)S(1)}, f32[320]{0:T(512)}, u32[]{:S(2)}) copy-start(f32[320]{0:T(512)} %param.19) | copy-start | bytes 3844
Sparse Core Ops, SparseCore 0:
  8.9 28.2 all-gather.4
  39.4 61.9 all-gather.6
  103.6 60.5 all-gather.8
  185.8 33.2 reduce-scatter.2
  221.3 93.3 all-gather.10
  326.5 24.2 reduce-scatter.4
where the time goes:
time: 364 us; the launch traced here: 362 us
  waiting for transfers between devices  247 us (68%)
  local copies, waits for them, and re-layouts  63 us (17%)
  matrix products  25.7 us (7%)
  between operations  13.7 us (4%)
  other arithmetic  7.17 us (2%)
  starting transfers between devices  6.02 us (2%)
    all_gather x1, waiting for transfers between devices, per_device(): lax.all_gather(w_out, 'wide', axis=1, tiled=True)  62.8 us
    all_gather x1, waiting for transfers between devices, per_device(): lax.all_gather(w_in, 'wide', axis=0, tiled=True)  60.9 us
    all_gather x1, waiting for transfers between devices, per_device(): lax.all_gather(w_proj, 'wide', axis=2, tiled=True)  47.3 us
    scatter x1, local copies, waits for them, and re-layouts, per_device(): buffer.at[own_owners, slot_out].set(merged, mode='drop')  38.8 us
    reduce_scatter x1, waiting for transfers between devices, per_device(): lax.psum_scatter(partial_out.astype(jnp.bfloat16), 'narrow', scatter_dime...  31.2 us
    all_gather x1, waiting for transfers between devices, per_device(): whole = lax.all_gather(patches, 'narrow', axis=1, tiled=True)  28.4 us
    dot_general x1, matrix products, per_device(): partial_out = jnp.dot(hidden, cols_out, preferred_element_type=jnp.float32)  21.4 us
    reduce_scatter x1, waiting for transfers between devices, per_device(): lax.psum_scatter(late_terms.astype(jnp.bfloat16), 'narrow', scatter_dimen...  14 us
  transfers between devices with their start and end apart: 7, of which 6 were waited for; matrix products, arithmetic and copies ran while one was open for 18% of the time, Pallas kernels for 0%

commit v1 on v0

v1 whole, which is shorter than its diff:
```python
import functools

import jax
import jax.numpy as jnp
from jax import lax
from jax.experimental import pallas as pl
from jax.experimental.pallas import tpu as pltpu
from jax.sharding import PartitionSpec as P

F32 = jnp.float32
BF16 = jnp.bfloat16
WINDOW = 4
ANY = pl.BlockSpec(memory_space=pl.ANY)
SMEM = pl.BlockSpec(memory_space=pltpu.SMEM)
VMEM = pl.BlockSpec(memory_space=pltpu.VMEM)


def call(kernel, operands, specs, outs, scratch=(), flops=0, moved=0, special=0, name=None):
    single = not isinstance(outs, (list, tuple))
    return pl.pallas_call(
        kernel,
        out_shape=outs,
        in_specs=specs,
        out_specs=VMEM if single else [VMEM] * len(outs),
        scratch_shapes=list(scratch),
        compiler_params=pltpu.CompilerParams(vmem_limit_bytes=48 * 1024 * 1024),
        cost_estimate=pl.CostEstimate(
            flops=flops, bytes_accessed=moved, transcendentals=special
        ),
        name=name,
    )(*operands)


def shape(*dims, dtype=BF16):
    return jax.ShapeDtypeStruct(dims, dtype)


def load_rows(offsets, sources, layout, target, sem):
    copies = []
    for i, (array_at, start, rows) in enumerate(layout):
        at = pl.multiple_of(offsets[i], 16)
        copies.append(
            pltpu.make_async_copy(
                sources[array_at].at[pl.ds(start, rows)], target.at[pl.ds(at, rows)], sem.at[i]
            )
        )
    for copy in copies:
        copy.start()
    return copies


def order_kernel(x_ref, o_ref):
    tokens = x_ref.shape[1]
    windows = tokens // WINDOW
    source = lax.broadcasted_iota(jnp.int32, (tokens, windows), 0)
    window = lax.broadcasted_iota(jnp.int32, (tokens, windows), 1)
    for p in range(WINDOW):
        pick = jnp.where(source == WINDOW * window + p, 1.0, 0.0).astype(BF16)
        o_ref[:, p * windows : (p + 1) * windows] = jnp.dot(
            x_ref[...], pick, preferred_element_type=F32
        ).astype(BF16)


def norm_kernel(layout, count, offsets, gain, bias, *refs):
    sources, o_ref, whole, sem = refs[:count], refs[count], refs[count + 1], refs[count + 2]
    for copy in load_rows(offsets, sources, layout, whole, sem):
        copy.wait()
    width, tokens = whole.shape
    step = 128
    for t in range(0, tokens, step):
        values = whole[:, t : t + step].astype(F32)
        center = jnp.sum(values, axis=0, keepdims=True) * (1.0 / width)
        values = values - center
        spread = jnp.sum(values * values, axis=0, keepdims=True) * (1.0 / width)
        values = (values * lax.rsqrt(spread + 1e-06)).T
        o_ref[t : t + step, :] = (values * gain[...] + bias[...]).astype(BF16)


def hidden_kernel(layout, count, offsets, normed, bias, *refs):
    sources, o_ref, whole, sem = refs[:count], refs[count], refs[count + 1], refs[count + 2]
    for copy in load_rows(offsets, sources, layout, whole, sem):
        copy.wait()
    step = 256
    for f in range(0, whole.shape[1], step):
        v = jnp.dot(normed[...], whole[:, f : f + step], preferred_element_type=F32)
        v = v + bias[:, f : f + step]
        o_ref[:, f : f + step] = (0.5 * v * (1.0 + lax.erf(v * (2.0**-0.5)))).astype(BF16)


def out_kernel(layout, count, offsets, hidden, *refs):
    sources, keep, give, whole, sem = refs[:count], *refs[count:]
    for copy in load_rows(offsets, sources, layout, whole, sem):
        copy.wait()
    tokens = hidden.shape[0]
    half, rows = whole.shape[0] // 2, keep.shape[1]
    step = 256
    for target, base in ((give, half), (keep, 0)):
        for t in range(0, tokens, step):
            v = lax.dot_general(
                whole[base : base + half, :],
                hidden[t : t + step, :],
                (((1,), (1,)), ((), ())),
                preferred_element_type=F32,
            ).astype(BF16)
            for j in range(2):
                target[j, :, t : t + step] = v[j * rows : (j + 1) * rows]


def proj_kernel(layout, count, offsets, merged, *refs):
    sources, keep, give, whole, sem = refs[:count], *refs[count:]
    for copy in load_rows(offsets, sources, layout, whole, sem):
        copy.wait()
    half, rows = whole.shape[0] // 2, keep.shape[1]
    for target, base in ((give, half), (keep, 0)):
        v = jnp.dot(
            whole[base : base + half, :], merged[...], preferred_element_type=F32
        ).astype(BF16)
        for j in range(2):
            target[j] = v[j * rows : (j + 1) * rows]


def stream_kernel(own, keep, near, far, bias, o_ref):
    total = keep[0].astype(F32) + near[0].astype(F32) + far[...].astype(F32)
    stream = (own[...].astype(F32) + (total + bias[...])).astype(BF16)
    rows, windows = own.shape[0], own.shape[1] // WINDOW
    for p in range(WINDOW):
        o_ref[p * rows : (p + 1) * rows, :] = stream[:, p * windows : (p + 1) * windows]


def pack_kernel(slots_of, keep, near, far, bias, o_ref):
    total = keep[0].astype(F32) + near[0].astype(F32) + far[...].astype(F32)
    vision = (total + bias[...]).astype(BF16)
    slots = o_ref.shape[0]
    windows = vision.shape[1]
    slot = lax.broadcasted_iota(jnp.int32, (slots, windows), 0)
    pick = jnp.where(slot == slots_of[...], 1.0, 0.0).astype(BF16)
    o_ref[...] = lax.dot_general(
        pick, vision, (((1,), (1,)), ((), ())), preferred_element_type=F32
    ).astype(BF16)


def place_kernel(targets, arrived, text, o_ref):
    slots, rows = arrived.shape[0], text.shape[1]
    row = lax.broadcasted_iota(jnp.int32, (slots, rows), 1)
    pick = jnp.where(row == targets[...], 1.0, 0.0)
    hit = jnp.sum(pick, axis=0, keepdims=True) > 0.5
    moved = lax.dot_general(
        arrived[...], pick.astype(BF16), (((0,), (0,)), ((), ())), preferred_element_type=F32
    ).astype(BF16)
    o_ref[...] = jnp.where(hit, moved, text[...])


def ring_order(count):
    return list(range(0, count, 2)) + list(range(count - 1, 0, -2))


class Rings:
    def __init__(self, axis, count, depth):
        self.axis, self.count, self.depth = axis, count, depth
        order = ring_order(count)
        self.right = [(order[i], order[(i + 1) % count]) for i in range(count)]
        self.left = [(b, a) for a, b in self.right]
        self.table = jnp.asarray(order, jnp.int32)
        place_of = [order.index(i) for i in range(count)]
        self.place = jnp.asarray(place_of, jnp.int32)[lax.axis_index(axis)]
        self.sent = {0: [], 1: []}

    def hop(self, block, way, tied):
        past = self.sent[way]
        if tied and len(past) >= self.depth:
            block, _ = lax.optimization_barrier((block, past[-self.depth]))
        block = lax.ppermute(block, self.axis, self.right if way == 0 else self.left)
        past.append(block)
        return block

    def gather(self, shard):
        rows = shard.shape[0] // 2
        me = lax.axis_index(self.axis)
        halves = [shard[:rows], shard[rows:]]
        pieces = [(halves[0], me, 0), (halves[1], me, 1)]
        last = self.count // 2
        held = {(way, h): halves[h] for way in (0, 1) for h in (0, 1)}
        for step in range(1, last + 1):
            for h in (0, 1):
                for way in (0, 1):
                    half = h if way == 0 else 1 - h
                    if step == last and h == 1:
                        continue
                    block = self.hop(held[way, half], way, step == 1)
                    held[way, half] = block
                    shift = -step if way == 0 else step
                    owner = self.table[(self.place + shift) % self.count]
                    pieces.append((block, owner, half))
        return pieces


def per_device(
    patches, norm_gain, norm_bias, w_in, b_in, w_out, b_out, w_proj, b_proj, text, place
):
    groups, parts = lax.axis_size("wide"), lax.axis_size("narrow")
    me, part = lax.axis_index("wide"), lax.axis_index("narrow")
    tokens, width = patches.shape[0], patches.shape[1]
    full = width * parts
    windows = tokens // WINDOW
    seq_rows = text.shape[0]
    bucket = seq_rows // groups
    slots = groups * bucket

    near_pairs = [(i, i ^ 1) for i in range(parts)]
    far_pairs = [(i, i ^ 2) for i in range(parts)]

    def near(x):
        return lax.ppermute(x, "narrow", near_pairs)

    def far(x):
        return lax.ppermute(x, "narrow", far_pairs)

    shards = [
        w_in,
        w_out.T,
        jnp.transpose(w_proj, (2, 0, 1)).reshape(w_proj.shape[2], -1),
    ]
    rows = [s.shape[0] for s in shards]
    block = full // parts
    swap = part ^ jnp.arange(parts, dtype=jnp.int32)
    place_of_block = (swap % 2) * 2 + swap // 2

    if groups <= 8 and all(r % 32 == 0 for r in rows):
        rings = Rings("wide", groups, 2)
        gathered = []
        for i, shard in enumerate(shards):
            pieces = rings.gather(shard)
            r = rows[i]
            per_block = block // r
            offsets = []
            for _, owner, half in pieces:
                if i == 0:
                    at = owner * r
                else:
                    at = place_of_block[owner // per_block] * block + (owner % per_block) * r
                offsets.append(at + half * (r // 2))
            layout = [(k, 0, r // 2) for k in range(len(pieces))]
            gathered.append((layout, [p[0] for p in pieces], jnp.stack(offsets).astype(jnp.int32)))
    else:
        gathered = []
        for i, shard in enumerate(shards):
            whole = lax.all_gather(shard, "wide", axis=0, tiled=True)
            layout = [(0, k * block, block) for k in range(parts)]
            at = jnp.arange(parts, dtype=jnp.int32) if i == 0 else place_of_block
            gathered.append((layout, [whole], (at * block).astype(jnp.int32)))

    own = call(
        order_kernel, (patches.T,), [VMEM], shape(width, tokens),
        flops=2 * width * tokens * tokens, moved=4 * width * tokens, name="order_tokens",
    )
    over_x = far(own)
    over_core = near(own)
    over_both = near(over_x)
    feature_blocks = [own, over_x, over_core, over_both]
    feature_at = (part ^ jnp.asarray([0, 2, 1, 3], jnp.int32)) * width
    layout = [(k, 0, width) for k in range(parts)]
    normed = call(
        functools.partial(norm_kernel, layout, parts),
        (feature_at.astype(jnp.int32), norm_gain[None], norm_bias[None], *feature_blocks),
        [SMEM, VMEM, VMEM] + [ANY] * parts,
        shape(tokens, full),
        scratch=[pltpu.VMEM((full, tokens), BF16), pltpu.SemaphoreType.DMA((parts,))],
        flops=10 * full * tokens, moved=4 * full * tokens, name="norm",
    )

    def weighted(kernel, which, operands, outs, flops, moved, special, name):
        layout, sources, offsets = gathered[which]
        columns = sources[0].shape[1]
        return call(
            functools.partial(kernel, layout, len(sources)),
            (offsets, *operands, *sources),
            [SMEM] + [VMEM] * len(operands) + [ANY] * len(sources),
            outs,
            scratch=[
                pltpu.VMEM((full, columns), BF16),
                pltpu.SemaphoreType.DMA((len(layout),)),
            ],
            flops=flops, moved=moved, special=special, name=name,
        )

    ff = w_in.shape[1]
    hidden = weighted(
        hidden_kernel, 0, (normed, b_in[None]), shape(tokens, ff),
        2 * tokens * full * ff, 2 * (tokens * full + full * ff + tokens * ff), tokens * ff,
        "hidden",
    )
    keep, give = weighted(
        out_kernel, 1, (hidden,),
        [shape(2, width, tokens), shape(2, width, tokens)],
        2 * tokens * full * ff, 2 * (tokens * ff + full * ff + tokens * full), 0, "mlp_out",
    )
    core_sums = near(give)
    x_give = (keep[1].astype(F32) + core_sums[1].astype(F32)).astype(BF16)
    x_sums = far(x_give)
    merged = call(
        stream_kernel, (own, keep, core_sums, x_sums, b_out[:, None]),
        [VMEM] * 5, shape(WINDOW * width, windows),
        flops=4 * width * tokens, moved=10 * width * tokens, name="stream",
    )

    place_table = place.reshape(groups, windows)
    owners = jnp.where(place_table >= 0, place_table // seq_rows, groups)
    own_owners = lax.dynamic_index_in_dim(owners, me, 0, keepdims=False)
    earlier = (jnp.arange(windows)[:, None] <= jnp.arange(windows)[None, :]).astype(BF16)
    owner_hits = own_owners[None, :] == jnp.arange(groups, dtype=jnp.int32)[:, None]
    rank_out = jnp.dot(owner_hits.astype(BF16), earlier, preferred_element_type=F32)
    rank_out = jnp.sum(jnp.where(owner_hits, rank_out, 0.0), axis=0).astype(jnp.int32) - 1
    slots_of = jnp.where(own_owners < groups, own_owners * bucket + rank_out, slots)
    arriving = owners == me
    rank_in = jnp.dot(arriving.astype(BF16), earlier, preferred_element_type=F32).astype(jnp.int32)
    match = (
        rank_in[:, None, :] == jnp.arange(1, bucket + 1, dtype=jnp.int32)[None, :, None]
    ) & arriving[:, None, :]
    local_row = (place_table % seq_rows + 1)[:, None, :]
    targets = jnp.sum(jnp.where(match, local_row, 0), axis=2) - 1
    targets = targets.reshape(slots, 1)

    keep, give = weighted(
        proj_kernel, 2, (merged,),
        [shape(2, width, windows), shape(2, width, windows)],
        2 * windows * full * WINDOW * width,
        2 * (full * WINDOW * width + windows * WINDOW * width + windows * full), 0, "proj",
    )
    core_sums = near(give)
    x_give = (keep[1].astype(F32) + core_sums[1].astype(F32)).astype(BF16)
    x_sums = far(x_give)
    buffer = call(
        pack_kernel, (slots_of[None], keep, core_sums, x_sums, b_proj[:, None]),
        [VMEM] * 5, shape(slots, width),
        flops=2 * slots * windows * width, moved=8 * width * windows + 2 * slots * width,
        name="pack",
    )
    arrived = lax.all_to_all(
        buffer.reshape(groups, bucket, width), "wide", split_axis=0, concat_axis=0, tiled=True
    )
    out = call(
        place_kernel, (targets, arrived.reshape(slots, width), text.T),
        [VMEM] * 3, shape(width, seq_rows),
        flops=2 * slots * seq_rows * width, moved=6 * width * seq_rows, name="place",
    )
    return out.T


def solution(mesh):
    placed = (
        P("wide", "narrow"),
        P(),
        P(),
        P("wide", "narrow"),
        P("narrow"),
        P("narrow", "wide"),
        P("narrow"),
        P(None, "narrow", "wide"),
        P("narrow"),
        P("wide", "narrow"),
        P(),
    )
    return jax.shard_map(
        per_device, mesh=mesh, in_specs=placed, out_specs=P("wide", "narrow"), check_vma=False
    )
```

time: 364 us -> 202 us (0.55)
  waiting for transfers between devices: 247 us -> 55.4 us
  starting transfers between devices: 6.02 us -> 53 us
  local copies, waits for them, and re-layouts: 63 us -> 21.8 us
  Pallas kernels: 0 us -> 32.5 us
  matrix products: 25.7 us -> 0.31 us
  between operations: 13.7 us -> 36.3 us
  other arithmetic: 7.17 us -> 1.5 us
    all_gather x4 -> x0, waiting for transfers between devices: 199 us -> none  [the longest x1 62.8 us: per_device(): lax.all_gather(w_out, 'wide', axis=1, tiled=True)]
    ppermute x0 -> x49, starting transfers between devices: none -> 47.4 us  [the longest x42 43.3 us: hop(): lax.ppermute(block, self.axis, self.right if way == 0 else self.left)]
    reduce_scatter x2 -> x0, waiting for transfers between devices: 45.2 us -> none  [the longest x1 31.2 us: per_device(): lax.psum_scatter(partial_out.astype(jnp.bfloat16), 'narrow', scatter_dime...]
    ppermute x0 -> x49, waiting for transfers between devices: none -> 44.9 us  [the longest x42 37.7 us: hop(): lax.ppermute(block, self.axis, self.right if way == 0 else self.left)]
    scatter x3 -> x0, local copies, waits for them, and re-layouts: 42.3 us -> none  [the longest x1 38.8 us: per_device(): buffer.at[own_owners, slot_out].set(merged, mode='drop')]
    pallas_call x0 -> x8, Pallas kernels: none -> 32.5 us  [call(): pl.pallas_call(kernel, out_shape=outs, in_specs=specs, out_specs=VMEM if...]
    dot_general x2, matrix products: 25.7 us -> 0.31 us  [the longest x1 0.16 us: per_device(): jnp.dot(owner_hits.astype(BF16), earlier, preferred_element_type=F32)]
    all_to_all x1, waiting for transfers between devices: 0.01 us -> 10.5 us  [per_device(): lax.all_to_all(buffer.reshape(groups, bucket, width), 'wide', split_axis=...]
  transfers between devices with their start and end apart: 7 -> 50, of which waited for: 6 -> 24; matrix products, arithmetic and copies ran while one was open for 18% -> 6% of each run, Pallas kernels for 0% -> 8%
where the time goes in v1:
time: 202 us; the launch traced here: 201 us
  waiting for transfers between devices  55.4 us (27%)
  starting transfers between devices  53 us (26%)
  between operations  36.3 us (18%)
  Pallas kernels  32.5 us (16%)
  local copies, waits for them, and re-layouts  21.8 us (11%)
    ppermute x42, starting transfers between devices, hop(): lax.ppermute(block, self.axis, self.right if way == 0 else self.left)  43.3 us
    ppermute x42, waiting for transfers between devices, hop(): lax.ppermute(block, self.axis, self.right if way == 0 else self.left)  37.7 us
    pallas_call x8, Pallas kernels, call(): pl.pallas_call(kernel, out_shape=outs, in_specs=specs, out_specs=VMEM if...  32.5 us
    unnamed x92, local copies, waits for them, and re-layouts  12.1 us
    all_to_all x1, waiting for transfers between devices, per_device(): lax.all_to_all(buffer.reshape(groups, bucket, width), 'wide', split_axis=...  10.5 us
    slice x7, local copies, waits for them, and re-layouts, gather(): halves = [shard[:rows], shard[rows:]]  6.42 us
    ppermute x3, waiting for transfers between devices, far(): return lax.ppermute(x, 'narrow', far_pairs)  5.59 us
    all_to_all x1, starting transfers between devices, per_device(): lax.all_to_all(buffer.reshape(groups, bucket, width), 'wide', split_axis=...  5.55 us
  transfers between devices with their start and end apart: 50, of which 24 were waited for; matrix products, arithmetic and copies ran while one was open for 6% of the time, Pallas kernels for 8%

profile of v1, /device:TPU:0, one launch (start us, length us, event | category | flops | bytes accessed | tf_op | source)
XLA Modules:
  0.0 200.7 jit_solution(8217833863234871143)
XLA Ops:
  2.0 3.0 %collective-permute-start = (bf16[320,1024]{1,0:T(8,128)(2,1)S(1)}, bf16[320,1024]{1,0:T(8,128)(2,1)S(1)}, u32[]{:S(2)}, u32[]{:S(2)}) collective-permute-start(bf16[320,1024]{1,0:T(8,128)(2,1)S(1)} %order_tokens.1.refs_0_.own), channel_id=1, source_target_pairs={{0,2},{1,3},{2,0},{3,1},{4,6},{5,7},{6,4},{7,5},{8,10},{9,11},{10,... | collective-permute-start | bytes 1966088 | tf_op jit(solution)/shard_map/ppermute | solution.py:216
  5.1 1.6 collective-permute-start.3
  7.1 1.6 collective-permute-start.5
  9.2 3.9 %collective-permute-done.3.refs_2_ = bf16[80,1280]{1,0:T(8,128)(2,1)S(1)} collective-permute-done((bf16[80,1280]{1,0:T(8,128)(2,1)S(1)}, bf16[80,1280]{1,0:T(8,128)(2,1)S(1)}, u32[]{:S(2)}, u32[]{:S(2)}) %collective-permute-start.3) | collective-permute-done | bytes 204832 | tf_op jit(solution)/shard_map/ppermute | solution.py:172
  13.1 1.6 collective-permute-start.7
  26.3 1.6 collective-permute-done.10.refs_9_
  27.9 1.6 collective-permute-start.13
  32.1 3.7 %collective-permute-done.13.refs_12_ = bf16[80,1280]{1,0:T(8,128)(2,1)S(1)} collective-permute-done((bf16[80,1280]{1,0:T(8,128)(2,1)S(1)}, bf16[80,1280]{1,0:T(8,128)(2,1)S(1)}, u32[]{:S(2)}, u32[]{:S(2)}) %collective-permute-start.13) | collective-permute-done | bytes 204832 | tf_op jit(solution)/shard_map/ppermute | solution.py:172
  37.7 1.6 collective-permute-start.17
  40.4 4.1 %collective-permute-done.16.refs_15_ = bf16[80,1280]{1,0:T(8,128)(2,1)S(1)} collective-permute-done((bf16[80,1280]{1,0:T(8,128)(2,1)S(1)}, bf16[80,1280]{1,0:T(8,128)(2,1)S(1)}, u32[]{:S(2)}, u32[]{:S(2)}) %collective-permute-start.16) | collective-permute-done | bytes 204832 | tf_op jit(solution)/shard_map/ppermute | solution.py:172
  45.2 1.6 collective-permute-start.19
  47.2 1.6 collective-permute-start.21
  87.2 1.8 collective-permute-start.23
  89.3 1.8 collective-permute-start.25
  91.5 3.8 %collective-permute-done.23.refs_8_ = bf16[80,1280]{1,0:T(8,128)(2,1)S(1)} collective-permute-done((bf16[80,1280]{1,0:T(8,128)(2,1)}, bf16[80,1280]{1,0:T(8,128)(2,1)S(1)}, u32[]{:S(2)}, u32[]{:S(2)}) %collective-permute-start.23) | collective-permute-done | bytes 204832 | tf_op jit(solution)/shard_map/ppermute | solution.py:172
  95.3 1.9 collective-permute-start.27
  97.5 2.2 %collective-permute-done.25.refs_10_ = bf16[80,1280]{1,0:T(8,128)(2,1)S(1)} collective-permute-done((bf16[80,1280]{1,0:T(8,128)(2,1)}, bf16[80,1280]{1,0:T(8,128)(2,1)S(1)}, u32[]{:S(2)}, u32[]{:S(2)}) %collective-permute-start.25) | collective-permute-done | bytes 204832 | tf_op jit(solution)/shard_map/ppermute | solution.py:172
  101.7 3.7 %norm.1.normed = bf16[1024,1280]{1,0:T(8,128)(2,1)S(1)} custom-call(s32[4]{0:T(128)S(1)} %xor_multiply_fusion.offsets, f32[1,1280]{1,0:T(1,128)S(1)} %broadcast_in_dim.53.gain, f32[1,1280]{1,0:T(1,128)S(1)} %broadcast_in_dim.54.bias, bf16[320,1024]{1,0:T(8,128)(2,1)S(1)} %order_tokens.1.refs_0_.own, bf16[320,1024]{1,0:T(8,128)(2,1)S(1)} %collective-permute-done.refs_1_, ...), custom_call_target="tpu_custom_call" | custom-call | flops 13107200 | bytes 5242880 | tf_op jit(solution)/shard_map/norm/pallas_call | solution.py:20
  107.0 10.5 %hidden.1 = bf16[1024,1280]{1,0:T(8,128)(2,1)S(1)} custom-call(s32[16]{0:T(128)S(1)} %stack.152.offsets, bf16[1024,1280]{1,0:T(8,128)(2,1)} %copy-done, f32[1,1280]{1,0:T(1,128)S(1)} %broadcast_in_dim.55.bias, bf16[80,1280]{1,0:T(8,128)(2,1)S(1)} %get-tuple-element.36.refs_0_, bf16[80,1280]{1,0:T(8,128)(2,1)S(1)} %get-tuple-element.35.refs_1_, ...), custom_call_target="tpu_custom_call" | custom-call | flops 3355443200 | bytes 8519680 | tf_op jit(solution)/shard_map/hidden/pallas_call | solution.py:20
  119.1 8.8 %mlp_out.1 = (bf16[2,320,1024]{2,1,0:T(8,128)(2,1)S(1)}, bf16[2,320,1024]{2,1,0:T(8,128)(2,1)}) custom-call(s32[16]{0:T(128)S(1)} %stack.135.offsets, bf16[1024,1280]{1,0:T(8,128)(2,1)} %copy-done.33, bf16[80,1280]{1,0:T(8,128)(2,1)S(1)} %get-tuple-element.20.refs_0_, bf16[80,1280]{1,0:T(8,128)(2,1)S(1)} %get-tuple-element.19.refs_1_, ...), custom_call_target="tpu_custom_call" | custom-call | flops 3355443200 | bytes 8519680 | tf_op jit(solution)/shard_map/mlp_out/pallas_call | solution.py:20
  130.7 1.7 copy.24
  132.4 1.9 slice.45.refs_1_
  138.4 3.9 %collective-permute-done.33.refs_2_ = bf16[80,1280]{1,0:T(8,128)(2,1)} collective-permute-done((bf16[80,1280]{1,0:T(8,128)(2,1)S(1)}, bf16[80,1280]{1,0:T(8,128)(2,1)}, u32[]{:S(2)}, u32[]{:S(2)}) %collective-permute-start.33) | collective-permute-done | bytes 204832 | tf_op jit(solution)/shard_map/ppermute | solution.py:172
  149.0 2.1 %collective-permute-done.37.refs_6_ = bf16[80,1280]{1,0:T(8,128)(2,1)} collective-permute-done((bf16[80,1280]{1,0:T(8,128)(2,1)}, bf16[80,1280]{1,0:T(8,128)(2,1)}, u32[]{:S(2)}, u32[]{:S(2)}) %collective-permute-start.37) | collective-permute-done | bytes 204832 | tf_op jit(solution)/shard_map/ppermute | solution.py:172
  153.4 2.0 collective-permute-done.39.refs_8_
  157.7 2.1 %collective-permute-done.41.refs_10_ = bf16[80,1280]{1,0:T(8,128)(2,1)S(1)} collective-permute-done((bf16[80,1280]{1,0:T(8,128)(2,1)}, bf16[80,1280]{1,0:T(8,128)(2,1)S(1)}, u32[]{:S(2)}, u32[]{:S(2)}) %collective-permute-start.41) | collective-permute-done | bytes 204832 | tf_op jit(solution)/shard_map/ppermute | solution.py:172
  165.0 3.2 %collective-permute-done.45.refs_14_ = bf16[80,1280]{1,0:T(8,128)(2,1)S(1)} collective-permute-done((bf16[80,1280]{1,0:T(8,128)(2,1)S(1)}, bf16[80,1280]{1,0:T(8,128)(2,1)S(1)}, u32[]{:S(2)}, u32[]{:S(2)}) %collective-permute-start.45) | collective-permute-done | bytes 204832 | tf_op jit(solution)/shard_map/ppermute | solution.py:172
  168.7 4.9 %proj.1 = (bf16[2,320,256]{2,1,0:T(8,128)(2,1)S(1)}, bf16[2,320,256]{2,1,0:T(8,128)(2,1)S(1)}) custom-call(s32[16]{0:T(128)S(1)} %stack.135.offsets, bf16[1280,256]{1,0:T(8,128)(2,1)S(1)} %stream.1.merged, bf16[80,1280]{1,0:T(8,128)(2,1)S(1)} %slice.43.refs_0_, bf16[80,1280]{1,0:T(8,128)(2,1)S(1)} %copy-done.1, ...), custom_call_target="tpu_custom_call" | custom-call | flops 838860800 | bytes 4587520 | tf_op jit(solution)/shard_map/proj/pallas_call | solution.py:20
  173.7 1.6 collective-permute-done.47.near
  176.1 5.6 %collective-permute-done.48.far = bf16[320,256]{1,0:T(8,128)(2,1)S(1)} collective-permute-done((bf16[320,256]{1,0:T(8,128)(2,1)S(1)}, bf16[320,256]{1,0:T(8,128)(2,1)S(1)}, u32[]{:S(2)}, u32[]{:S(2)}) %collective-permute-start.48) | collective-permute-done | bytes 163872 | tf_op jit(solution)/shard_map/ppermute | solution.py:216
  182.8 5.6 %all-to-all-start = ((bf16[8,64,320]{2,1,0:T(8,128)(2,1)}), bf16[8,64,320]{2,1,0:T(8,128)(2,1)S(1)}, u32[]{:S(2)}, u32[]{:S(2)}) async-start(bf16[8,64,320]{2,1,0:T(8,128)(2,1)} %bitcast.64), calls=%async_computation | async-start | bytes 786432 | tf_op jit(solution)/shard_map/all_to_all | solution.py:338
  189.0 10.5 %all-to-all-done = bf16[8,64,320]{2,1,0:T(8,128)(2,1)S(1)} async-done(((bf16[8,64,320]{2,1,0:T(8,128)(2,1)}), bf16[8,64,320]{2,1,0:T(8,128)(2,1)S(1)}, u32[]{:S(2)}, u32[]{:S(2)}) %all-to-all-start) | async-done | bytes 327712 | tf_op jit(solution)/shard_map/all_to_all | solution.py:338
  (201 shorter events, 57.2 us)
Async XLA Ops:
  2.0 30.1 %collective-permute-start = (bf16[320,1024]{1,0:T(8,128)(2,1)S(1)}, bf16[320,1024]{1,0:T(8,128)(2,1)S(1)}, u32[]{:S(2)}, u32[]{:S(2)}) collective-permute-start(bf16[320,1024]{1,0:T(8,128)(2,1)S(1)} %order_tokens.1.refs_0_.own), channel_id=1, source_target_pairs={{0,2},{1,3},{2,0},{3,1},{4,6},{5,7},{6,4},{7,5},{8,10},{9,11},{10,... | collective-permute-start | bytes 1966088 | tf_op jit(solution)/shard_map/ppermute | solution.py:216
  6.7 8.7 %collective-permute-start.4 = (bf16[80,1280]{1,0:T(8,128)(2,1)S(1)}, bf16[80,1280]{1,0:T(8,128)(2,1)S(1)}, u32[]{:S(2)}, u32[]{:S(2)}) collective-permute-start(bf16[80,1280]{1,0:T(8,128)(2,1)S(1)} %get-tuple-element.35.refs_1_), channel_id=1, source_target_pairs={{8,0},{16,8},{24,16},{28,24},{20,28},{12,20},{4,12},{0,4},{9,1},{1... | collective-permute-start | bytes 614408 | tf_op jit(solution)/shard_map/ppermute | solution.py:172
  7.1 10.4 %collective-permute-start.5 = (bf16[80,1280]{1,0:T(8,128)(2,1)S(1)}, bf16[80,1280]{1,0:T(8,128)(2,1)S(1)}, u32[]{:S(2)}, u32[]{:S(2)}) collective-permute-start(bf16[80,1280]{1,0:T(8,128)(2,1)S(1)} %get-tuple-element.35.refs_1_), channel_id=1, source_target_pairs={{0,8},{8,16},{16,24},{24,28},{28,20},{20,12},{12,4},{4,0},{1,9},{9... | collective-permute-start | bytes 614408 | tf_op jit(solution)/shard_map/ppermute | solution.py:172
  8.7 11.1 %collective-permute-start.6 = (bf16[80,1280]{1,0:T(8,128)(2,1)S(1)}, bf16[80,1280]{1,0:T(8,128)(2,1)S(1)}, u32[]{:S(2)}, u32[]{:S(2)}) collective-permute-start(bf16[80,1280]{1,0:T(8,128)(2,1)S(1)} %get-tuple-element.36.refs_0_), channel_id=1, source_target_pairs={{8,0},{16,8},{24,16},{28,24},{20,28},{12,20},{4,12},{0,4},{9,1},{1... | collective-permute-start | bytes 614408 | tf_op jit(solution)/shard_map/ppermute | solution.py:172
  13.1 8.8 %collective-permute-start.7 = (bf16[80,1280]{1,0:T(8,128)(2,1)S(1)}, bf16[80,1280]{1,0:T(8,128)(2,1)S(1)}, u32[]{:S(2)}, u32[]{:S(2)}) collective-permute-start(bf16[80,1280]{1,0:T(8,128)(2,1)S(1)} %collective-permute-done.3.refs_2_), channel_id=1, source_target_pairs={{0,8},{8,16},{16,24},{24,28},{28,20},{20,12},{12,4},{4,0},{1,9},{9... | collective-permute-start | bytes 614408 | tf_op jit(solution)/shard_map/ppermute | solution.py:172
  15.4 8.8 %collective-permute-start.8 = (bf16[80,1280]{1,0:T(8,128)(2,1)S(1)}, bf16[80,1280]{1,0:T(8,128)(2,1)S(1)}, u32[]{:S(2)}, u32[]{:S(2)}) collective-permute-start(bf16[80,1280]{1,0:T(8,128)(2,1)S(1)} %collective-permute-done.4.refs_3_), channel_id=1, source_target_pairs={{8,0},{16,8},{24,16},{28,24},{20,28},{12,20},{4,12},{0,4},{9,1},{1... | collective-permute-start | bytes 614408 | tf_op jit(solution)/shard_map/ppermute | solution.py:172
  17.5 8.8 %collective-permute-start.9 = (bf16[80,1280]{1,0:T(8,128)(2,1)S(1)}, bf16[80,1280]{1,0:T(8,128)(2,1)S(1)}, u32[]{:S(2)}, u32[]{:S(2)}) collective-permute-start(bf16[80,1280]{1,0:T(8,128)(2,1)S(1)} %collective-permute-done.5.refs_4_), channel_id=1, source_target_pairs={{0,8},{8,16},{16,24},{24,28},{28,20},{20,12},{12,4},{4,0},{1,9},{9... | collective-permute-start | bytes 614408 | tf_op jit(solution)/shard_map/ppermute | solution.py:172
  26.3 20.5 %collective-permute-start.1 = (bf16[320,1024]{1,0:T(8,128)(2,1)S(1)}, bf16[320,1024]{1,0:T(8,128)(2,1)S(1)}, u32[]{:S(2)}, u32[]{:S(2)}) collective-permute-start(bf16[320,1024]{1,0:T(8,128)(2,1)S(1)} %order_tokens.1.refs_0_.own), channel_id=1, source_target_pairs={{0,1},{1,0},{2,3},{3,2},{4,5},{5,4},{6,7},{7,6},{8,9},{9,8},{10,11... | collective-permute-start | bytes 1966088 | tf_op jit(solution)/shard_map/ppermute | solution.py:213
  32.1 69.6 %collective-permute-start.2 = (bf16[320,1024]{1,0:T(8,128)(2,1)S(1)}, bf16[320,1024]{1,0:T(8,128)(2,1)S(1)}, u32[]{:S(2)}, u32[]{:S(2)}) collective-permute-start(bf16[320,1024]{1,0:T(8,128)(2,1)S(1)} %collective-permute-done.refs_1_), channel_id=1, source_target_pairs={{0,1},{1,0},{2,3},{3,2},{4,5},{5,4},{6,7},{7,6},{8,9},{9,8},{10,11... | collective-permute-start | bytes 1966088 | tf_op jit(solution)/shard_map/ppermute | solution.py:213
  37.7 9.6 %collective-permute-start.17 = (bf16[80,1280]{1,0:T(8,128)(2,1)S(1)}, bf16[80,1280]{1,0:T(8,128)(2,1)}, u32[]{:S(2)}, u32[]{:S(2)}) collective-permute-start(bf16[80,1280]{1,0:T(8,128)(2,1)S(1)} %get-tuple-element.20.refs_0_), channel_id=1, source_target_pairs={{0,8},{8,16},{16,24},{24,28},{28,20},{20,12},{12,4},{4,0},{1,9},{9... | collective-permute-start | bytes 614408 | tf_op jit(solution)/shard_map/ppermute | solution.py:172
  40.0 9.0 %collective-permute-start.18 = (bf16[80,1280]{1,0:T(8,128)(2,1)S(1)}, bf16[80,1280]{1,0:T(8,128)(2,1)}, u32[]{:S(2)}, u32[]{:S(2)}) collective-permute-start(bf16[80,1280]{1,0:T(8,128)(2,1)S(1)} %get-tuple-element.19.refs_1_), channel_id=1, source_target_pairs={{8,0},{16,8},{24,16},{28,24},{20,28},{12,20},{4,12},{0,4},{9,1},{1... | collective-permute-start | bytes 614408 | tf_op jit(solution)/shard_map/ppermute | solution.py:172
  45.2 42.0 %collective-permute-start.19 = (bf16[80,1280]{1,0:T(8,128)(2,1)S(1)}, bf16[80,1280]{1,0:T(8,128)(2,1)}, u32[]{:S(2)}, u32[]{:S(2)}) collective-permute-start(bf16[80,1280]{1,0:T(8,128)(2,1)S(1)} %get-tuple-element.19.refs_1_), channel_id=1, source_target_pairs={{0,8},{8,16},{16,24},{24,28},{28,20},{20,12},{12,4},{4,0},{1,9},{9... | collective-permute-start | bytes 614408 | tf_op jit(solution)/shard_map/ppermute | solution.py:172
  46.8 42.3 %collective-permute-start.20 = (bf16[80,1280]{1,0:T(8,128)(2,1)S(1)}, bf16[80,1280]{1,0:T(8,128)(2,1)}, u32[]{:S(2)}, u32[]{:S(2)}) collective-permute-start(bf16[80,1280]{1,0:T(8,128)(2,1)S(1)} %get-tuple-element.20.refs_0_), channel_id=1, source_target_pairs={{8,0},{16,8},{24,16},{28,24},{20,28},{12,20},{4,12},{0,4},{9,1},{1... | collective-permute-start | bytes 614408 | tf_op jit(solution)/shard_map/ppermute | solution.py:172
  47.2 42.1 %collective-permute-start.21 = (bf16[80,1280]{1,0:T(8,128)(2,1)}, bf16[80,1280]{1,0:T(8,128)(2,1)}, u32[]{:S(2)}, u32[]{:S(2)}) collective-permute-start(bf16[80,1280]{1,0:T(8,128)(2,1)} %collective-permute-done.17.refs_2_), channel_id=1, source_target_pairs={{0,8},{8,16},{16,24},{24,28},{28,20},{20,12},{12,4},{4,0},{1,9},{9... | collective-permute-start | bytes 614408 | tf_op jit(solution)/shard_map/ppermute | solution.py:172
  49.0 42.1 %collective-permute-start.22 = (bf16[80,1280]{1,0:T(8,128)(2,1)}, bf16[80,1280]{1,0:T(8,128)(2,1)}, u32[]{:S(2)}, u32[]{:S(2)}) collective-permute-start(bf16[80,1280]{1,0:T(8,128)(2,1)} %collective-permute-done.18.refs_3_), channel_id=1, source_target_pairs={{8,0},{16,8},{24,16},{28,24},{20,28},{12,20},{4,12},{0,4},{9,1},{1... | collective-permute-start | bytes 614408 | tf_op jit(solution)/shard_map/ppermute | solution.py:172
  89.3 10.4 %collective-permute-start.25 = (bf16[80,1280]{1,0:T(8,128)(2,1)}, bf16[80,1280]{1,0:T(8,128)(2,1)S(1)}, u32[]{:S(2)}, u32[]{:S(2)}) collective-permute-start(bf16[80,1280]{1,0:T(8,128)(2,1)} %collective-permute-done.21.refs_6_), channel_id=1, source_target_pairs={{0,8},{8,16},{16,24},{24,28},{28,20},{20,12},{12,4},{4,0},{1,9},{9... | collective-permute-start | bytes 614408 | tf_op jit(solution)/shard_map/ppermute | solution.py:172
  91.1 9.2 %collective-permute-start.26 = (bf16[80,1280]{1,0:T(8,128)(2,1)}, bf16[80,1280]{1,0:T(8,128)(2,1)S(1)}, u32[]{:S(2)}, u32[]{:S(2)}) collective-permute-start(bf16[80,1280]{1,0:T(8,128)(2,1)} %collective-permute-done.22.refs_7_), channel_id=1, source_target_pairs={{8,0},{16,8},{24,16},{28,24},{20,28},{12,20},{4,12},{0,4},{9,1},{1... | collective-permute-start | bytes 614408 | tf_op jit(solution)/shard_map/ppermute | solution.py:172
  95.3 23.8 %collective-permute-start.27 = (bf16[80,1280]{1,0:T(8,128)(2,1)S(1)}, bf16[80,1280]{1,0:T(8,128)(2,1)S(1)}, u32[]{:S(2)}, u32[]{:S(2)}) collective-permute-start(bf16[80,1280]{1,0:T(8,128)(2,1)S(1)} %collective-permute-done.23.refs_8_), channel_id=1, source_target_pairs={{0,8},{8,16},{16,24},{24,28},{28,20},{20,12},{12,4},{4,0},{1,9},{9... | collective-permute-start | bytes 614408 | tf_op jit(solution)/shard_map/ppermute | solution.py:172
  97.3 21.8 %collective-permute-start.28 = (bf16[80,1280]{1,0:T(8,128)(2,1)S(1)}, bf16[80,1280]{1,0:T(8,128)(2,1)S(1)}, u32[]{:S(2)}, u32[]{:S(2)}) collective-permute-start(bf16[80,1280]{1,0:T(8,128)(2,1)S(1)} %collective-permute-done.24.refs_9_), channel_id=1, source_target_pairs={{8,0},{16,8},{24,16},{28,24},{20,28},{12,20},{4,12},{0,4},{9,1},{1... | collective-permute-start | bytes 614408 | tf_op jit(solution)/shard_map/ppermute | solution.py:172
  99.7 19.4 %collective-permute-start.29 = (bf16[80,1280]{1,0:T(8,128)(2,1)S(1)}, bf16[80,1280]{1,0:T(8,128)(2,1)S(1)}, u32[]{:S(2)}, u32[]{:S(2)}) collective-permute-start(bf16[80,1280]{1,0:T(8,128)(2,1)S(1)} %collective-permute-done.25.refs_10_), channel_id=1, source_target_pairs={{0,8},{8,16},{16,24},{24,28},{28,20},{20,12},{12,4},{4,0},{1,9},{9... | collective-permute-start | bytes 614408 | tf_op jit(solution)/shard_map/ppermute | solution.py:172
  100.3 18.8 %collective-permute-start.30 = (bf16[80,1280]{1,0:T(8,128)(2,1)S(1)}, bf16[80,1280]{1,0:T(8,128)(2,1)S(1)}, u32[]{:S(2)}, u32[]{:S(2)}) collective-permute-start(bf16[80,1280]{1,0:T(8,128)(2,1)S(1)} %collective-permute-done.26.refs_11_), channel_id=1, source_target_pairs={{8,0},{16,8},{24,16},{28,24},{20,28},{12,20},{4,12},{0,4},{9,1},{1... | collective-permute-start | bytes 614408 | tf_op jit(solution)/shard_map/ppermute | solution.py:172
  127.9 16.7 %collective-permute-start.31 = (bf16[2,320,1024]{2,1,0:T(8,128)(2,1)}, bf16[2,320,1024]{2,1,0:T(8,128)(2,1)S(1)}, u32[]{:S(2)}, u32[]{:S(2)}) collective-permute-start(bf16[2,320,1024]{2,1,0:T(8,128)(2,1)} %get-tuple-element.22), channel_id=1, source_target_pairs={{0,1},{1,0},{2,3},{3,2},{4,5},{5,4},{6,7},{7,6},{8,9},{9,8},{10,11... | collective-permute-start | bytes 3932168 | tf_op jit(solution)/shard_map/ppermute | solution.py:213
  136.4 10.5 %collective-permute-start.35 = (bf16[80,1280]{1,0:T(8,128)(2,1)}, bf16[80,1280]{1,0:T(8,128)(2,1)}, u32[]{:S(2)}, u32[]{:S(2)}) collective-permute-start(bf16[80,1280]{1,0:T(8,128)(2,1)} %slice.45.refs_1_), channel_id=1, source_target_pairs={{0,8},{8,16},{16,24},{24,28},{28,20},{20,12},{12,4},{4,0},{1,9},{9... | collective-permute-start | bytes 614408 | tf_op jit(solution)/shard_map/ppermute | solution.py:172
  137.0 10.6 %collective-permute-start.36 = (bf16[80,1280]{1,0:T(8,128)(2,1)S(1)}, bf16[80,1280]{1,0:T(8,128)(2,1)}, u32[]{:S(2)}, u32[]{:S(2)}) collective-permute-start(bf16[80,1280]{1,0:T(8,128)(2,1)S(1)} %slice.43.refs_0_), channel_id=1, source_target_pairs={{8,0},{16,8},{24,16},{28,24},{20,28},{12,20},{4,12},{0,4},{9,1},{1... | collective-permute-start | bytes 614408 | tf_op jit(solution)/shard_map/ppermute | solution.py:172
  142.3 8.8 %collective-permute-start.37 = (bf16[80,1280]{1,0:T(8,128)(2,1)}, bf16[80,1280]{1,0:T(8,128)(2,1)}, u32[]{:S(2)}, u32[]{:S(2)}) collective-permute-start(bf16[80,1280]{1,0:T(8,128)(2,1)} %collective-permute-done.33.refs_2_), channel_id=1, source_target_pairs={{0,8},{8,16},{16,24},{24,28},{28,20},{20,12},{12,4},{4,0},{1,9},{9... | collective-permute-start | bytes 614408 | tf_op jit(solution)/shard_map/ppermute | solution.py:172
  143.2 8.8 %collective-permute-start.38 = (bf16[80,1280]{1,0:T(8,128)(2,1)}, bf16[80,1280]{1,0:T(8,128)(2,1)}, u32[]{:S(2)}, u32[]{:S(2)}) collective-permute-start(bf16[80,1280]{1,0:T(8,128)(2,1)} %collective-permute-done.34.refs_3_), channel_id=1, source_target_pairs={{8,0},{16,8},{24,16},{28,24},{20,28},{12,20},{4,12},{0,4},{9,1},{1... | collective-permute-start | bytes 614408 | tf_op jit(solution)/shard_map/ppermute | solution.py:172
  145.7 16.5 %collective-permute-start.32 = (bf16[320,1024]{1,0:T(8,128)(2,1)}, bf16[320,1024]{1,0:T(8,128)(2,1)}, u32[]{:S(2)}, u32[]{:S(2)}) collective-permute-start(bf16[320,1024]{1,0:T(8,128)(2,1)} %fusion.1), channel_id=1, source_target_pairs={{0,2},{1,3},{2,0},{3,1},{4,6},{5,7},{6,4},{7,5},{8,10},{9,11},{10,... | collective-permute-start | bytes 1966088 | tf_op jit(solution)/shard_map/ppermute | solution.py:216
  151.1 8.7 %collective-permute-start.41 = (bf16[80,1280]{1,0:T(8,128)(2,1)}, bf16[80,1280]{1,0:T(8,128)(2,1)S(1)}, u32[]{:S(2)}, u32[]{:S(2)}) collective-permute-start(bf16[80,1280]{1,0:T(8,128)(2,1)} %collective-permute-done.37.refs_6_), channel_id=1, source_target_pairs={{0,8},{8,16},{16,24},{24,28},{28,20},{20,12},{12,4},{4,0},{1,9},{9... | collective-permute-start | bytes 614408 | tf_op jit(solution)/shard_map/ppermute | solution.py:172
  151.9 8.7 %collective-permute-start.42 = (bf16[80,1280]{1,0:T(8,128)(2,1)}, bf16[80,1280]{1,0:T(8,128)(2,1)S(1)}, u32[]{:S(2)}, u32[]{:S(2)}) collective-permute-start(bf16[80,1280]{1,0:T(8,128)(2,1)} %collective-permute-done.38.refs_7_), channel_id=1, source_target_pairs={{8,0},{16,8},{24,16},{28,24},{20,28},{12,20},{4,12},{0,4},{9,1},{1... | collective-permute-start | bytes 614408 | tf_op jit(solution)/shard_map/ppermute | solution.py:172
  155.4 9.3 %collective-permute-start.43 = (bf16[80,1280]{1,0:T(8,128)(2,1)S(1)}, bf16[80,1280]{1,0:T(8,128)(2,1)S(1)}, u32[]{:S(2)}, u32[]{:S(2)}) collective-permute-start(bf16[80,1280]{1,0:T(8,128)(2,1)S(1)} %collective-permute-done.39.refs_8_), channel_id=1, source_target_pairs={{0,8},{8,16},{16,24},{24,28},{28,20},{20,12},{12,4},{4,0},{1,9},{9... | collective-permute-start | bytes 614408 | tf_op jit(solution)/shard_map/ppermute | solution.py:172
  156.2 8.8 %collective-permute-start.44 = (bf16[80,1280]{1,0:T(8,128)(2,1)S(1)}, bf16[80,1280]{1,0:T(8,128)(2,1)S(1)}, u32[]{:S(2)}, u32[]{:S(2)}) collective-permute-start(bf16[80,1280]{1,0:T(8,128)(2,1)S(1)} %collective-permute-done.40.refs_9_), channel_id=1, source_target_pairs={{8,0},{16,8},{24,16},{28,24},{20,28},{12,20},{4,12},{0,4},{9,1},{1... | collective-permute-start | bytes 614408 | tf_op jit(solution)/shard_map/ppermute | solution.py:172
  182.8 16.8 %all-to-all-start = ((bf16[8,64,320]{2,1,0:T(8,128)(2,1)}), bf16[8,64,320]{2,1,0:T(8,128)(2,1)S(1)}, u32[]{:S(2)}, u32[]{:S(2)}) async-start(bf16[8,64,320]{2,1,0:T(8,128)(2,1)} %bitcast.64), calls=%async_computation | async-start | bytes 786432 | tf_op jit(solution)/shard_map/all_to_all | solution.py:338
  (64 other events, 986.3 us)

commit v2 on v0

v2 whole, which is shorter than its diff:
```python
import functools

import jax
import jax.numpy as jnp
from jax import lax
from jax.experimental import pallas as pl
from jax.experimental.pallas import tpu as pltpu
from jax.sharding import PartitionSpec as P

F32 = jnp.float32
BF16 = jnp.bfloat16
WINDOW = 4
VMEM = pl.BlockSpec(memory_space=pltpu.VMEM)


def call(kernel, operands, outs, scratch=(), flops=0, moved=0, special=0, name=None):
    single = not isinstance(outs, (list, tuple))
    return pl.pallas_call(
        kernel,
        out_shape=outs,
        in_specs=[VMEM] * len(operands),
        out_specs=VMEM if single else [VMEM] * len(outs),
        scratch_shapes=list(scratch),
        compiler_params=pltpu.CompilerParams(vmem_limit_bytes=28 * 1024 * 1024),
        cost_estimate=pl.CostEstimate(
            flops=flops, bytes_accessed=moved, transcendentals=special
        ),
        name=name,
    )(*operands)


def shape(*dims, dtype=BF16):
    return jax.ShapeDtypeStruct(dims, dtype)


def after(x, *others):
    return lax.optimization_barrier((x, *others))[0]


def ring_order(count):
    return list(range(0, count, 2)) + list(range(count - 1, 0, -2))


def ring_owner(me, shift, count):
    half = me // 2
    at = jnp.where(me % 2 == 0, half, count - 1 - half) + (shift + count)
    at = at % count
    return jnp.where(at < count // 2, 2 * at, 2 * (count - 1 - at) + 1)


class Piece:
    def __init__(self, array, start, rows, shift, base, index=0):
        self.array, self.start, self.rows = array, start, rows
        self.shift, self.base, self.index = shift, base, index

    def row(self, count, shard_rows):
        if self.shift is None:
            return self.index * self.rows
        return ring_owner(lax.axis_index("wide"), self.shift, count) * shard_rows + self.base

    def block_row(self, count, shard_rows, block):
        if self.shift is None:
            of, inside = self.index, 0
        else:
            owner = ring_owner(lax.axis_index("wide"), self.shift, count)
            per_block = block // shard_rows
            of, inside = owner // per_block, (owner % per_block) * shard_rows + self.base
        mine = lax.axis_index("narrow")
        over_x = jnp.where(of // 2 == mine // 2, 0, 1)
        over_core = jnp.where(of % 2 == mine % 2, 0, 1)
        return over_x, over_core, inside


def rows_at(start, rows):
    return pl.ds(pl.multiple_of(start, 16), rows)


def order_kernel(x_ref, o_ref):
    tokens = x_ref.shape[1]
    windows = tokens // WINDOW
    source = lax.broadcasted_iota(jnp.int32, (tokens, windows), 0)
    window = lax.broadcasted_iota(jnp.int32, (tokens, windows), 1)
    for p in range(WINDOW):
        pick = jnp.where(source == WINDOW * window + p, 1.0, 0.0).astype(BF16)
        o_ref[:, p * windows : (p + 1) * windows] = jnp.dot(
            x_ref[...], pick, preferred_element_type=F32
        ).astype(BF16)


def shards_kernel(w_out, w_proj, *outs):
    rows, width = w_proj.shape[1], w_proj.shape[2]
    half = rows // (len(outs) // 2)
    flat = jnp.concatenate([w_proj[p] for p in range(WINDOW)], axis=1)
    for i in range(len(outs) // 2):
        outs[i][...] = w_out[i * half : (i + 1) * half, :]
        outs[len(outs) // 2 + i][...] = flat[i * half : (i + 1) * half, :]


def route_kernel(relative, seq_rows, bucket, place, slots_of, targets):
    groups, windows = place.shape
    me = lax.axis_index("wide")
    table = place[...]
    owner = jnp.where(table >= 0, 0, -1)
    for d in range(1, groups):
        owner = owner + jnp.where(table >= d * seq_rows, 1, 0)
    earlier = jnp.where(
        lax.broadcasted_iota(jnp.int32, (windows, windows), 0)
        <= lax.broadcasted_iota(jnp.int32, (windows, windows), 1),
        1.0,
        0.0,
    ).astype(BF16)
    here = jnp.where(owner == me, 1.0, 0.0)
    rank = jnp.dot(here.astype(BF16), earlier, preferred_element_type=F32)
    rank = jnp.where(owner == me, rank, 0.0).astype(jnp.int32)
    local = table - me * seq_rows
    slot = lax.broadcasted_iota(jnp.int32, (bucket, windows), 0) + 1
    source_at = lax.broadcasted_iota(jnp.int32, (groups, windows), 0)
    for k in range(groups):
        wanted = source_at == ((me ^ k) if relative else k)
        of_rank = jnp.sum(jnp.where(wanted, rank, 0), axis=0, keepdims=True)
        of_local = jnp.sum(jnp.where(wanted, local, 0), axis=0, keepdims=True)
        found = jnp.where(of_rank == slot, of_local + 1, 0)
        targets[k * bucket : (k + 1) * bucket, :] = jnp.sum(found, axis=1, keepdims=True) - 1
    mine = jnp.sum(jnp.where(source_at == me, owner, 0), axis=0, keepdims=True)
    hits = source_at == mine
    rank = jnp.dot(
        jnp.where(hits, 1.0, 0.0).astype(BF16), earlier, preferred_element_type=F32
    )
    rank = jnp.sum(jnp.where(hits, rank, 0.0), axis=0, keepdims=True).astype(jnp.int32)
    towards = (mine ^ me) if relative else mine
    slots_of[...] = jnp.where(mine >= 0, towards * bucket + rank - 1, groups * bucket)


def norm_kernel(first, tokens, own, over_x, over_core, over_both, gain, bias, o_ref, whole):
    parts = (own, over_x, over_core, over_both)
    rows = own.shape[0]
    mine = lax.axis_index("narrow")
    for part, flip in zip(parts, (0, 2, 1, 3)):
        at = (mine ^ flip) * rows
        whole[rows_at(at, rows), :] = part[:, first : first + tokens]
    width = whole.shape[0]
    step = 128
    for t in range(0, tokens, step):
        values = whole[:, t : t + step].astype(F32)
        center = jnp.sum(values, axis=0, keepdims=True) * (1.0 / width)
        values = values - center
        spread = jnp.sum(values * values, axis=0, keepdims=True) * (1.0 / width)
        values = (values * lax.rsqrt(spread + 1e-06)).T
        o_ref[t : t + step, :] = (values * gain[...] + bias[...]).astype(BF16)


def hidden_kernel(pieces, count, shard_rows, first, columns, bias, *refs):
    arrays = 1 + max(p.array for p in pieces)
    sources, normed, (o_ref, part) = refs[:arrays], refs[arrays:-2], refs[-2:]
    for p in pieces:
        part[rows_at(p.row(count, shard_rows), p.rows), :] = sources[p.array][
            p.start : p.start + p.rows, first : first + columns
        ]
    at = 0
    for rows in normed:
        v = jnp.dot(rows[...], part[...], preferred_element_type=F32)
        v = v + bias[:, first : first + columns]
        o_ref[at : at + rows.shape[0], :] = (
            0.5 * v * (1.0 + lax.erf(v * (2.0**-0.5)))
        ).astype(BF16)
        at += rows.shape[0]


def out_kernel(pieces, count, shard_rows, over_x, hidden_count, *refs):
    hidden, refs = refs[:hidden_count], refs[hidden_count:]
    sources, (keep, give, part) = refs[:-3], refs[-3:]
    block, tokens = keep.shape
    for p in pieces:
        x, core, inside = p.block_row(count, shard_rows, block)

        @pl.when(x == over_x)
        def _():
            part[rows_at(core * block + inside, p.rows), :] = sources[p.array][
                p.start : p.start + p.rows, :
            ]

    columns = hidden[0].shape[1]
    step = 256
    for t in range(0, tokens, step):
        total = None
        for i, h in enumerate(hidden):
            v = lax.dot_general(
                part[:, i * columns : (i + 1) * columns],
                h[t : t + step, :],
                (((1,), (1,)), ((), ())),
                preferred_element_type=F32,
            )
            total = v if total is None else total + v
        total = total.astype(BF16)
        keep[:, t : t + step] = total[:block]
        give[:, t : t + step] = total[block:]


def proj_kernel(pieces, missing, count, shard_rows, merged, *refs):
    sources, (keep, give, part) = refs[:-3], refs[-3:]
    block = keep.shape[1]
    for p in pieces:
        x, core, inside = p.block_row(count, shard_rows, block)
        at = rows_at(core * 2 * block + x * block + inside, p.rows)
        part[at, :] = sources[p.array][p.start : p.start + p.rows, :]
    if missing is not None:
        x, core, inside = missing.block_row(count, shard_rows, block)
        at = rows_at(core * 2 * block + x * block + inside, missing.rows)
        part[at, :] = jnp.zeros((missing.rows, part.shape[1]), BF16)
    for core, target in ((1, give), (0, keep)):
        v = jnp.dot(
            part[core * 2 * block : (core + 1) * 2 * block, :],
            merged[...],
            preferred_element_type=F32,
        ).astype(BF16)
        target[0] = v[:block]
        target[1] = v[block:]


def last_kernel(first, second, merged, o_ref):
    rows = first.shape[0]
    whole = jnp.concatenate([first[...], second[...]], axis=0)
    o_ref[...] = jnp.dot(whole, merged[...], preferred_element_type=F32).astype(BF16)


def stream_kernel(own, keep, near, far, bias, o_ref):
    total = keep[...].astype(F32) + near[...].astype(F32) + far[...].astype(F32)
    stream = (own[...].astype(F32) + (total + bias[...])).astype(BF16)
    rows, windows = own.shape[0], own.shape[1] // WINDOW
    for p in range(WINDOW):
        o_ref[p * rows : (p + 1) * rows, :] = stream[:, p * windows : (p + 1) * windows]


def pack_kernel(missing, count, shard_rows, extra, slots_of, keep, near, far, bias, *refs):
    late, outs, total = refs[:extra], refs[extra:-1], refs[-1]
    total[...] = keep[0].astype(F32) + near[0].astype(F32) + far[...].astype(F32)
    if extra:
        x, core, inside = missing.block_row(count, shard_rows, total.shape[0])

        @pl.when(x + core == 0)
        def _():
            at = pl.ds(pl.multiple_of(inside, 16), missing.rows)
            added = late[0][...].astype(F32)
            for r in late[1:]:
                added = added + r[...].astype(F32)
            total[at, :] = total[at, :] + added

    vision = (total[...] + bias[...]).astype(BF16)
    slots = outs[0].shape[0]
    slot = lax.broadcasted_iota(jnp.int32, (slots * len(outs), vision.shape[1]), 0)
    pick = jnp.where(slot == slots_of[...], 1.0, 0.0).astype(BF16)
    moved = lax.dot_general(
        pick, vision, (((1,), (1,)), ((), ())), preferred_element_type=F32
    ).astype(BF16)
    for k, o_ref in enumerate(outs):
        o_ref[...] = moved[k * slots : (k + 1) * slots]


def place_kernel(targets, text, *refs):
    arrived, o_ref = refs[:-1], refs[-1]
    slots, rows = arrived[0].shape[0] * len(arrived), text.shape[1]
    row = lax.broadcasted_iota(jnp.int32, (slots, rows), 1)
    pick = jnp.where(row == targets[...], 1.0, 0.0)
    hit = jnp.sum(pick, axis=0, keepdims=True) > 0.5
    whole = jnp.concatenate([r[...] for r in arrived], axis=0)
    moved = lax.dot_general(
        whole, pick.astype(BF16), (((0,), (0,)), ((), ())), preferred_element_type=F32
    ).astype(BF16)
    o_ref[...] = jnp.where(hit, moved, text[...])


def add_kernel(keep, near, o_ref):
    o_ref[...] = (keep[...].astype(F32) + near[...].astype(F32)).astype(BF16)


class Ring:
    def __init__(self, count):
        self.count = count
        order = ring_order(count)
        self.right = [(order[i], order[(i + 1) % count]) for i in range(count)]
        self.left = [(b, a) for a, b in self.right]
        self.done = []
        self.work = []

    def step(self, to_right, to_left):
        waits = list(self.work)
        if len(self.done) >= 2:
            waits += self.done[-2]
        self.work = []
        if waits:
            to_right, to_left = lax.optimization_barrier((to_right, to_left, *waits))[:2]
        pair = (
            lax.ppermute(to_right, "wide", self.right),
            lax.ppermute(to_left, "wide", self.left),
        )
        self.done.append(pair)
        return pair

    def between(self, x):
        if len(self.done) >= 3:
            return after(x, *self.done[-3])
        return x


def per_device(
    patches, norm_gain, norm_bias, w_in, b_in, w_out, b_out, w_proj, b_proj, text, place
):
    groups, parts = lax.axis_size("wide"), lax.axis_size("narrow")
    width, tokens = patches.shape[1], patches.shape[0]
    full = width * parts
    ff = w_in.shape[1]
    windows = tokens // WINDOW
    seq_rows = text.shape[0]
    bucket = seq_rows // groups
    slots = groups * bucket
    shard_rows = [w_in.shape[0], w_out.shape[1], w_proj.shape[2]]
    small = groups == 8 and all(r % 32 == 0 for r in shard_rows)

    near_pairs = [(i, i ^ 1) for i in range(parts)]
    far_pairs = [(i, i ^ 2) for i in range(parts)]

    def near(x):
        return lax.ppermute(x, "narrow", near_pairs)

    def far(x):
        return lax.ppermute(x, "narrow", far_pairs)


    def order(x):
        return call(
            order_kernel, (x,), shape(width, tokens),
            flops=2 * width * tokens * tokens, moved=4 * width * tokens, name="order_tokens",
        )

    def shards(count):
        rows = shard_rows[1] // count
        return call(
            shards_kernel, (w_out.T, jnp.transpose(w_proj, (0, 2, 1))),
            [shape(rows, full)] * (2 * count), moved=8 * shard_rows[1] * full, name="shards",
        )

    def route():
        return call(
            functools.partial(route_kernel, small, seq_rows, bucket),
            (place.reshape(groups, windows),),
            [shape(1, windows, dtype=jnp.int32), shape(slots, 1, dtype=jnp.int32)],
            flops=4 * groups * windows * windows, moved=4 * groups * windows, name="route",
        )

    def norm(blocks, first, count):
        return call(
            functools.partial(norm_kernel, first, count),
            (*blocks, norm_gain[None], norm_bias[None]), shape(count, full),
            scratch=[pltpu.VMEM((full, count), BF16)],
            flops=10 * full * count, moved=4 * full * count, name="norm",
        )

    def hidden(pieces, arrays, normed, first, columns):
        return call(
            functools.partial(hidden_kernel, pieces, groups, shard_rows[0], first, columns),
            (b_in[None], *arrays, *normed), shape(tokens, columns),
            scratch=[pltpu.VMEM((full, columns), BF16)],
            flops=2 * tokens * full * columns,
            moved=2 * (tokens * full + full * columns + tokens * columns),
            special=tokens * columns, name="hidden",
        )

    def mlp_out(pieces, arrays, hiddens, over_x):
        return call(
            functools.partial(
                out_kernel, pieces, groups, shard_rows[1], over_x, len(hiddens)
            ),
            (*hiddens, *arrays), [shape(width, tokens)] * 2,
            scratch=[pltpu.VMEM((2 * width, ff), BF16)],
            flops=4 * tokens * width * ff, moved=2 * (tokens * ff + full * ff), name="mlp_out",
        )

    def add(keep, other):
        return call(
            add_kernel, (keep, other), shape(*keep.shape), flops=keep.size,
            moved=6 * keep.size, name="add",
        )

    def stream(own, keep, core_sums, x_sums):
        return call(
            stream_kernel, (own, keep, core_sums, x_sums, b_out[:, None]),
            shape(WINDOW * width, windows),
            flops=4 * width * tokens, moved=10 * width * tokens, name="stream",
        )

    def proj(pieces, missing, arrays, merged):
        return call(
            functools.partial(proj_kernel, pieces, missing, groups, shard_rows[2]),
            (merged, *arrays), [shape(2, width, windows)] * 2,
            scratch=[pltpu.VMEM((full, WINDOW * width), BF16)],
            flops=2 * windows * full * WINDOW * width,
            moved=2 * (full * WINDOW * width + windows * (WINDOW * width + full)), name="proj",
        )

    def pack(slots_of, missing, keep, core_sums, x_sums, late, count):
        return call(
            functools.partial(pack_kernel, missing, groups, shard_rows[2], len(late)),
            (slots_of, keep, core_sums, x_sums, b_proj[:, None], *late),
            [shape(slots // count, width)] * count,
            scratch=[pltpu.VMEM((width, windows), F32)],
            flops=2 * slots * windows * width, moved=8 * width * windows + 2 * slots * width,
            name="pack",
        )

    def placed(targets, arrived):
        return call(
            place_kernel, (targets, text.T, *arrived), shape(width, seq_rows),
            flops=2 * slots * seq_rows * width, moved=6 * width * seq_rows, name="place",
        ).T


    if not small:
        shard = [w_in, *shards(1)]
        wholes = [lax.all_gather(s, "wide", axis=0, tiled=True) for s in shard]
        rows = full // parts
        pieces = [Piece(0, k * rows, rows, None, 0, k) for k in range(parts)]
        own = order(patches.T)
        over_x = far(own)
        blocks = (own, over_x, near(own), near(over_x))
        normed = norm(blocks, 0, tokens)
        act = hidden(pieces, wholes[:1], [normed], 0, ff)
        keep_x, give_x = mlp_out(pieces, wholes[1:2], [act], 1)
        keep, give = mlp_out(pieces, wholes[1:2], [act], 0)
        x_sums = far(add(keep_x, near(give_x)))
        merged = stream(own, keep, near(give), x_sums)
        slots_of, targets = route()
        keep, give = proj(pieces, None, wholes[2:], merged)
        core_sums = near(give)
        x_sums = far(add(keep[1], core_sums[1]))
        (buffer,) = pack(slots_of, None, keep, core_sums, x_sums, (), 1)
        arrived = lax.all_to_all(
            buffer.reshape(groups, bucket, width), "wide", split_axis=0, concat_axis=0, tiled=True
        )
        return placed(targets, [arrived.reshape(slots, width)])


    ring = Ring(groups)
    half_rows = shard_rows[0] // 2
    last = groups // 2

    def gather(halves, work):
        arrays = list(halves)
        pieces = [Piece(h, 0, half_rows, 0, h * half_rows) for h in (0, 1)]
        held = {(way, h): halves[h] for way in (0, 1) for h in (0, 1)}
        t = 0
        for step in range(1, last + 1):
            for first in (0, 1):
                if step == last and first == 1:
                    continue
                pair = ring.step(held[0, first], held[1, 1 - first])
                for way, h in ((0, first), (1, 1 - first)):
                    held[way, h] = pair[way]
                    shift = -step if way == 0 else step
                    pieces.append(Piece(len(arrays), 0, half_rows, shift, h * half_rows))
                    arrays.append(pair[way])
                if t in work:
                    ring.work += work[t]()
                t += 1
        return pieces, arrays

    state = {}

    def start_tokens():
        state["own"] = order(patches.T)
        state["over_x"] = far(state["own"])
        return [state["own"]]

    def start_shards():
        state["shards"] = shards(2)
        state["over_core"] = near(state["own"])
        return [state["shards"][0]]

    def start_route():
        state["slots_of"], state["targets"] = route()
        return [state["slots_of"]]

    def send_both():
        state["over_both"] = near(state["over_x"])
        return []

    def start_norm(i):
        def run():
            blocks = [state[k] for k in ("own", "over_x", "over_core", "over_both")]
            blocks[0] = ring.between(blocks[0])
            count = tokens // 2
            state["normed", i] = norm(blocks, i * count, count)
            return [state["normed", i]]
        return run

    pieces_in, arrays_in = gather(
        [w_in[:half_rows], w_in[half_rows:]],
        {0: start_tokens, 1: start_shards, 2: start_route, 4: send_both, 5: start_norm(0),
         6: start_norm(1)},
    )

    columns = 256
    hiddens = []

    def start_hidden(i):
        def run():
            normed = [state["normed", 0], state["normed", 1]]
            normed[0] = ring.between(normed[0])
            hiddens.append(hidden(pieces_in, arrays_in, normed, i * columns, columns))
            return [hiddens[-1]]
        return run

    pieces_out, arrays_out = gather(
        state["shards"][:2], {i + 1: start_hidden(i) for i in range(ff // columns)}
    )

    def start_out(over_x):
        def run():
            acts = [ring.between(hiddens[0]), *hiddens[1:]]
            keep, give = mlp_out(pieces_out, arrays_out, acts, over_x)
            state["keep", over_x] = keep
            state["core", over_x] = near(give)
            return [keep]
        return run

    def start_sums():
        state["x_give"] = add(state["keep", 1], state["core", 1])
        state["x_sums"] = far(state["x_give"])
        return [state["x_give"]]

    pieces_proj, arrays_proj = gather(
        state["shards"][2:], {1: start_out(1), 2: start_out(0), 3: start_sums}
    )

    merged = stream(state["own"], state["keep", 0], state["core", 0], state["x_sums"])
    missing = Piece(0, 0, shard_rows[2], last, 0)
    keep, give = proj(pieces_proj[:-2], missing, arrays_proj[:-2], merged)
    core_sums = near(give)
    x_sums = far(add(keep[1], core_sums[1]))

    halves = sorted(pieces_proj[-2:], key=lambda p: p.base)
    late = call(
        last_kernel, (*[arrays_proj[p.array] for p in halves], merged),
        shape(shard_rows[2], windows), flops=2 * windows * shard_rows[2] * WINDOW * width,
        moved=2 * WINDOW * width * (shard_rows[2] + windows), name="proj_last",
    )
    order_of = ring_order(groups)
    keeper = [
        order_of[(order_of.index(w) + last) % groups] * shard_rows[2] // width
        for w in range(groups)
    ]
    lates = [late]
    for flip in range(1, parts):
        pairs = [(w * parts + (keeper[w] ^ flip), w * parts + keeper[w]) for w in range(groups)]
        lates.append(lax.ppermute(late, ("wide", "narrow"), pairs))

    out_blocks = pack(state["slots_of"], missing, keep, core_sums, x_sums, lates, groups)
    arrived = [out_blocks[0]]
    for k in range(1, groups):
        arrived.append(lax.ppermute(out_blocks[k], "wide", [(w, w ^ k) for w in range(groups)]))
    return placed(state["targets"], arrived)


def solution(mesh):
    placed = (
        P("wide", "narrow"),
        P(),
        P(),
        P("wide", "narrow"),
        P("narrow"),
        P("narrow", "wide"),
        P("narrow"),
        P(None, "narrow", "wide"),
        P("narrow"),
        P("wide", "narrow"),
        P(),
    )
    return jax.shard_map(
        per_device, mesh=mesh, in_specs=placed, out_specs=P("wide", "narrow"), check_vma=False
    )
```

time: 364 us -> 164 us (0.45)
  waiting for transfers between devices: 247 us -> 70.5 us
  starting transfers between devices: 6.02 us -> 68.7 us
  local copies, waits for them, and re-layouts: 63 us -> 4.13 us
  matrix products: 25.7 us -> 0 us
  Pallas kernels: 0 us -> 19.6 us
  between operations: 13.7 us -> 0.48 us
  other arithmetic: 7.17 us -> 0 us
    all_gather x4 -> x0, waiting for transfers between devices: 199 us -> none  [the longest x1 62.8 us: per_device(): lax.all_gather(w_out, 'wide', axis=1, tiled=True)]
    ppermute x0 -> x60, waiting for transfers between devices: none -> 70.5 us  [the longest x21 30.2 us: step(): lax.ppermute(to_right, 'wide', self.right)]
    ppermute x0 -> x60, starting transfers between devices: none -> 68.7 us  [the longest x21 31 us: step(): lax.ppermute(to_right, 'wide', self.right)]
    reduce_scatter x2 -> x0, waiting for transfers between devices: 45.2 us -> none  [the longest x1 31.2 us: per_device(): lax.psum_scatter(partial_out.astype(jnp.bfloat16), 'narrow', scatter_dime...]
    scatter x3 -> x0, local copies, waits for them, and re-layouts: 42.3 us -> none  [the longest x1 38.8 us: per_device(): buffer.at[own_owners, slot_out].set(merged, mode='drop')]
    dot_general x2 -> x0, matrix products: 25.7 us -> none  [the longest x1 21.4 us: per_device(): partial_out = jnp.dot(hidden, cols_out, preferred_element_type=jnp.float32)]
    pallas_call x0 -> x19, Pallas kernels: none -> 19.6 us  [call(): pl.pallas_call(kernel, out_shape=outs, in_specs=[VMEM] * len(operands), o...]
    all_gather x1 -> x0, local copies, waits for them, and re-layouts: 7.33 us -> none  [per_device(): lax.all_gather(w_proj, 'wide', axis=2, tiled=True)]
  transfers between devices with their start and end apart: 7 -> 60, of which waited for: 6 -> 34; matrix products, arithmetic and copies ran while one was open for 18% -> 0% of each run, Pallas kernels for 0% -> 8%
where the time goes in v2:
time: 164 us; the launch traced here: 163 us
  waiting for transfers between devices  70.5 us (43%)
  starting transfers between devices  68.7 us (42%)
  Pallas kernels  19.6 us (12%)
  local copies, waits for them, and re-layouts  4.13 us (3%)
    ppermute x21, starting transfers between devices, step(): lax.ppermute(to_right, 'wide', self.right)  31 us
    ppermute x21, waiting for transfers between devices, step(): lax.ppermute(to_right, 'wide', self.right)  30.2 us
    ppermute x21, waiting for transfers between devices, step(): lax.ppermute(to_left, 'wide', self.left)  21.4 us
    pallas_call x19, Pallas kernels, call(): pl.pallas_call(kernel, out_shape=outs, in_specs=[VMEM] * len(operands), o...  19.6 us
    ppermute x21, starting transfers between devices, step(): lax.ppermute(to_left, 'wide', self.left)  16.1 us
    ppermute x3, waiting for transfers between devices, far(): return lax.ppermute(x, 'narrow', far_pairs)  12.6 us
    ppermute x7, starting transfers between devices, per_device(): lax.ppermute(out_blocks[k], 'wide', [(w, w ^ k) for w in range(groups)])  11.8 us
    ppermute x3, starting transfers between devices, far(): return lax.ppermute(x, 'narrow', far_pairs)  5.92 us
  transfers between devices with their start and end apart: 60, of which 34 were waited for; matrix products, arithmetic and copies ran while one was open for 0% of the time, Pallas kernels for 8%

profile of v2, /device:TPU:0, one launch (start us, length us, event | category | flops | bytes accessed | tf_op | source)
XLA Modules:
  0.0 163.4 jit_solution(11227346681415236893)
XLA Ops:
  2.0 3.0 %collective-permute-start.12 = (bf16[320,1024]{1,0:T(8,128)(2,1)S(1)}, bf16[320,1024]{1,0:T(8,128)(2,1)S(1)}, u32[]{:S(2)}, u32[]{:S(2)}) collective-permute-start(bf16[320,1024]{1,0:T(8,128)(2,1)S(1)} %order_tokens.1.own), channel_id=1, source_target_pairs={{0,2},{1,3},{2,0},{3,1},{4,6},{5,7},{6,4},{7,5},{8,10},{9,11},{10,... | collective-permute-start | bytes 1966088 | tf_op jit(solution)/shard_map/ppermute | solution.py:326
  7.1 12.6 %collective-permute-done.12.over_x = bf16[320,1024]{1,0:T(8,128)(2,1)S(1)} collective-permute-done((bf16[320,1024]{1,0:T(8,128)(2,1)S(1)}, bf16[320,1024]{1,0:T(8,128)(2,1)S(1)}, u32[]{:S(2)}, u32[]{:S(2)}) %collective-permute-start.12) | collective-permute-done | bytes 655392 | tf_op jit(solution)/shard_map/ppermute | solution.py:326
  19.7 1.8 %collective-permute-start.2 = (bf16[80,1280]{1,0:T(8,128)(2,1)S(1)}, bf16[80,1280]{1,0:T(8,128)(2,1)S(1)}, u32[]{:S(2)}, u32[]{:S(2)}) collective-permute-start(bf16[80,1280]{1,0:T(8,128)(2,1)S(1)} %get-tuple-element.76.refs_1_), channel_id=1, source_target_pairs={{0,8},{8,16},{16,24},{24,28},{28,20},{20,12},{12,4},{4,0},{1,9},{9... | collective-permute-start | bytes 614408 | tf_op jit(solution)/shard_map/ppermute | solution.py:293
  24.6 1.8 %collective-permute-start.4 = (bf16[80,1280]{1,0:T(8,128)(2,1)S(1)}, bf16[80,1280]{1,0:T(8,128)(2,1)S(1)}, u32[]{:S(2)}, u32[]{:S(2)}) collective-permute-start(bf16[80,1280]{1,0:T(8,128)(2,1)S(1)} %collective-permute-done.refs_2_), channel_id=1, source_target_pairs={{0,8},{8,16},{16,24},{24,28},{28,20},{20,12},{12,4},{4,0},{1,9},{9... | collective-permute-start | bytes 614408 | tf_op jit(solution)/shard_map/ppermute | solution.py:293
  30.3 1.8 %collective-permute-done.4.refs_6_ = bf16[80,1280]{1,0:T(8,128)(2,1)S(1)} collective-permute-done((bf16[80,1280]{1,0:T(8,128)(2,1)S(1)}, bf16[80,1280]{1,0:T(8,128)(2,1)S(1)}, u32[]{:S(2)}, u32[]{:S(2)}) %collective-permute-start.4) | collective-permute-done | bytes 204832 | tf_op jit(solution)/shard_map/ppermute | solution.py:293
  32.2 1.9 %collective-permute-start.7 = (bf16[80,1280]{1,0:T(8,128)(2,1)S(1)}, bf16[80,1280]{1,0:T(8,128)(2,1)S(1)}, u32[]{:S(2)}, u32[]{:S(2)}) collective-permute-start(bf16[80,1280]{1,0:T(8,128)(2,1)S(1)} %collective-permute-done.3.refs_5_), channel_id=1, source_target_pairs={{8,0},{16,8},{24,16},{28,24},{20,28},{12,20},{4,12},{0,4},{9,1},{1... | collective-permute-start | bytes 614408 | tf_op jit(solution)/shard_map/ppermute | solution.py:294
  36.5 1.8 %collective-permute-start.9 = (bf16[80,1280]{1,0:T(8,128)(2,1)S(1)}, bf16[80,1280]{1,0:T(8,128)(2,1)S(1)}, u32[]{:S(2)}, u32[]{:S(2)}) collective-permute-start(bf16[80,1280]{1,0:T(8,128)(2,1)S(1)} %collective-permute-done.5.refs_7_), channel_id=1, source_target_pairs={{8,0},{16,8},{24,16},{28,24},{20,28},{12,20},{4,12},{0,4},{9,1},{1... | collective-permute-start | bytes 614408 | tf_op jit(solution)/shard_map/ppermute | solution.py:294
  38.9 1.8 %collective-permute-start.10 = (bf16[80,1280]{1,0:T(8,128)(2,1)S(1)}, bf16[80,1280]{1,0:T(8,128)(2,1)S(1)}, u32[]{:S(2)}, u32[]{:S(2)}) collective-permute-start(bf16[80,1280]{1,0:T(8,128)(2,1)S(1)} %collective-permute-done.6.refs_8_), channel_id=1, source_target_pairs={{0,8},{8,16},{16,24},{24,28},{28,20},{20,12},{12,4},{4,0},{1,9},{9... | collective-permute-start | bytes 614408 | tf_op jit(solution)/shard_map/ppermute | solution.py:293
  41.0 2.5 %norm.2.refs_16_ = bf16[512,1280]{1,0:T(8,128)(2,1)S(1)} custom-call(bf16[320,1024]{1,0:T(8,128)(2,1)S(1)} %order_tokens.1.own, bf16[320,1024]{1,0:T(8,128)(2,1)S(1)} %collective-permute-done.12.over_x, bf16[320,1024]{1,0:T(8,128)(2,1)S(1)} %collective-permute-done.13.over_core, bf16[320,1024]{1,0:T(8,128)(2,1)} %collective-permute-done.14.over_both, ...), custom_call_target="tpu_custom_call" | custom-call | flops 6553600 | bytes 2621440 | tf_op jit(solution)/shard_map/norm/pallas_call | solution.py:18
  44.5 1.9 %collective-permute-start.15 = (bf16[80,1280]{1,0:T(8,128)(2,1)S(1)}, bf16[80,1280]{1,0:T(8,128)(2,1)S(1)}, u32[]{:S(2)}, u32[]{:S(2)}) collective-permute-start(bf16[80,1280]{1,0:T(8,128)(2,1)S(1)} %collective-permute-done.8.refs_10_), channel_id=1, source_target_pairs={{0,8},{8,16},{16,24},{24,28},{28,20},{20,12},{12,4},{4,0},{1,9},{9... | collective-permute-start | bytes 614408 | tf_op jit(solution)/shard_map/ppermute | solution.py:293
  46.5 2.5 %norm.3.refs_17_ = bf16[512,1280]{1,0:T(8,128)(2,1)S(1)} custom-call(bf16[320,1024]{1,0:T(8,128)(2,1)S(1)} %order_tokens.1.own, bf16[320,1024]{1,0:T(8,128)(2,1)S(1)} %collective-permute-done.12.over_x, bf16[320,1024]{1,0:T(8,128)(2,1)S(1)} %collective-permute-done.13.over_core, bf16[320,1024]{1,0:T(8,128)(2,1)} %collective-permute-done.14.over_both, ...), custom_call_target="tpu_custom_call" | custom-call | flops 6553600 | bytes 2621440 | tf_op jit(solution)/shard_map/norm/pallas_call | solution.py:18
  49.0 2.0 %collective-permute-start.19 = (bf16[80,1280]{1,0:T(8,128)(2,1)S(1)}, bf16[80,1280]{1,0:T(8,128)(2,1)S(1)}, u32[]{:S(2)}, u32[]{:S(2)}) collective-permute-start(bf16[80,1280]{1,0:T(8,128)(2,1)S(1)} %copy-done.9), channel_id=1, source_target_pairs={{0,8},{8,16},{16,24},{24,28},{28,20},{20,12},{12,4},{4,0},{1,9},{9... | collective-permute-start | bytes 614408 | tf_op jit(solution)/shard_map/ppermute | solution.py:293
  52.3 1.8 %collective-permute-done.16.refs_15_ = bf16[80,1280]{1,0:T(8,128)(2,1)S(1)} collective-permute-done((bf16[80,1280]{1,0:T(8,128)(2,1)S(1)}, bf16[80,1280]{1,0:T(8,128)(2,1)S(1)}, u32[]{:S(2)}, u32[]{:S(2)}) %collective-permute-start.16) | collective-permute-done | bytes 204832 | tf_op jit(solution)/shard_map/ppermute | solution.py:294
  57.2 1.8 %collective-permute-done.20.refs_8_ = bf16[80,1280]{1,0:T(8,128)(2,1)S(1)} collective-permute-done((bf16[80,1280]{1,0:T(8,128)(2,1)S(1)}, bf16[80,1280]{1,0:T(8,128)(2,1)S(1)}, u32[]{:S(2)}, u32[]{:S(2)}) %collective-permute-start.20) | collective-permute-done | bytes 204832 | tf_op jit(solution)/shard_map/ppermute | solution.py:294
  72.5 2.2 %collective-permute-done.29.refs_15_ = bf16[80,1280]{1,0:T(8,128)(2,1)S(1)} collective-permute-done((bf16[80,1280]{1,0:T(8,128)(2,1)S(1)}, bf16[80,1280]{1,0:T(8,128)(2,1)S(1)}, u32[]{:S(2)}, u32[]{:S(2)}) %collective-permute-start.29) | collective-permute-done | bytes 204832 | tf_op jit(solution)/shard_map/ppermute | solution.py:293
  82.0 1.8 %collective-permute-done.25.refs_17_ = bf16[80,1280]{1,0:T(8,128)(2,1)S(1)} collective-permute-done((bf16[80,1280]{1,0:T(8,128)(2,1)S(1)}, bf16[80,1280]{1,0:T(8,128)(2,1)S(1)}, u32[]{:S(2)}, u32[]{:S(2)}) %collective-permute-start.25) | collective-permute-done | bytes 204832 | tf_op jit(solution)/shard_map/ppermute | solution.py:293
  84.2 2.3 %mlp_out.3 = (bf16[320,1024]{1,0:T(8,128)(2,1)S(1)}, bf16[320,1024]{1,0:T(8,128)(2,1)S(1)}) custom-call(bf16[1024,256]{1,0:T(8,128)(2,1)S(1)} %hidden.5.refs_0_, bf16[1024,256]{1,0:T(8,128)(2,1)S(1)} %hidden.6.refs_1_, bf16[1024,256]{1,0:T(8,128)(2,1)S(1)} %hidden.8.refs_2_, bf16[1024,256]{1,0:T(8,128)(2,1)S(1)} %hidden.7.refs_3_, ...), custom_call_target="tpu_custom_call" | custom-call | flops 1677721600 | bytes 5898240 | tf_op jit(solution)/shard_map/mlp_out/pallas_call | solution.py:18
  88.7 5.4 %collective-permute-done.27.refs_2_ = bf16[80,1280]{1,0:T(8,128)(2,1)S(1)} collective-permute-done((bf16[80,1280]{1,0:T(8,128)(2,1)S(1)}, bf16[80,1280]{1,0:T(8,128)(2,1)S(1)}, u32[]{:S(2)}, u32[]{:S(2)}) %collective-permute-start.27) | collective-permute-done | bytes 204832 | tf_op jit(solution)/shard_map/ppermute | solution.py:293
  95.5 2.2 %mlp_out.2 = (bf16[320,1024]{1,0:T(8,128)(2,1)S(1)}, bf16[320,1024]{1,0:T(8,128)(2,1)S(1)}) custom-call(bf16[1024,256]{1,0:T(8,128)(2,1)S(1)} %hidden.5.refs_0_, bf16[1024,256]{1,0:T(8,128)(2,1)S(1)} %hidden.6.refs_1_, bf16[1024,256]{1,0:T(8,128)(2,1)S(1)} %hidden.8.refs_2_, bf16[1024,256]{1,0:T(8,128)(2,1)S(1)} %hidden.7.refs_3_, ...), custom_call_target="tpu_custom_call" | custom-call | flops 1677721600 | bytes 5898240 | tf_op jit(solution)/shard_map/mlp_out/pallas_call | solution.py:18
  97.8 1.8 %collective-permute-start.36 = (bf16[80,1280]{1,0:T(8,128)(2,1)S(1)}, bf16[80,1280]{1,0:T(8,128)(2,1)S(1)}, u32[]{:S(2)}, u32[]{:S(2)}) collective-permute-start(bf16[80,1280]{1,0:T(8,128)(2,1)S(1)} %copy-done.6), channel_id=1, source_target_pairs={{0,8},{8,16},{16,24},{24,28},{28,20},{20,12},{12,4},{4,0},{1,9},{9... | collective-permute-start | bytes 614408 | tf_op jit(solution)/shard_map/ppermute | solution.py:293
  101.5 3.8 %collective-permute-done.36.refs_4_ = bf16[80,1280]{1,0:T(8,128)(2,1)S(1)} collective-permute-done((bf16[80,1280]{1,0:T(8,128)(2,1)S(1)}, bf16[80,1280]{1,0:T(8,128)(2,1)S(1)}, u32[]{:S(2)}, u32[]{:S(2)}) %collective-permute-start.36) | collective-permute-done | bytes 204832 | tf_op jit(solution)/shard_map/ppermute | solution.py:293
  110.5 4.3 %collective-permute-done.40.refs_8_ = bf16[80,1280]{1,0:T(8,128)(2,1)S(1)} collective-permute-done((bf16[80,1280]{1,0:T(8,128)(2,1)S(1)}, bf16[80,1280]{1,0:T(8,128)(2,1)S(1)}, u32[]{:S(2)}, u32[]{:S(2)}) %collective-permute-start.40) | collective-permute-done | bytes 204832 | tf_op jit(solution)/shard_map/ppermute | solution.py:293
  116.8 2.4 %collective-permute-done.38.refs_6_ = bf16[80,1280]{1,0:T(8,128)(2,1)S(1)} collective-permute-done((bf16[80,1280]{1,0:T(8,128)(2,1)S(1)}, bf16[80,1280]{1,0:T(8,128)(2,1)S(1)}, u32[]{:S(2)}, u32[]{:S(2)}) %collective-permute-start.38) | collective-permute-done | bytes 204832 | tf_op jit(solution)/shard_map/ppermute | solution.py:293
  119.4 3.1 %collective-permute-done.39.refs_7_ = bf16[80,1280]{1,0:T(8,128)(2,1)S(1)} collective-permute-done((bf16[80,1280]{1,0:T(8,128)(2,1)S(1)}, bf16[80,1280]{1,0:T(8,128)(2,1)S(1)}, u32[]{:S(2)}, u32[]{:S(2)}) %collective-permute-start.39) | collective-permute-done | bytes 204832 | tf_op jit(solution)/shard_map/ppermute | solution.py:294
  125.1 2.0 %collective-permute-done.45.refs_13_ = bf16[80,1280]{1,0:T(8,128)(2,1)S(1)} collective-permute-done((bf16[80,1280]{1,0:T(8,128)(2,1)S(1)}, bf16[80,1280]{1,0:T(8,128)(2,1)S(1)}, u32[]{:S(2)}, u32[]{:S(2)}) %collective-permute-start.45) | collective-permute-done | bytes 204832 | tf_op jit(solution)/shard_map/ppermute | solution.py:294
  135.1 3.8 %collective-permute-done.48.first = bf16[80,1280]{1,0:T(8,128)(2,1)S(1)} collective-permute-done((bf16[80,1280]{1,0:T(8,128)(2,1)S(1)}, bf16[80,1280]{1,0:T(8,128)(2,1)S(1)}, u32[]{:S(2)}, u32[]{:S(2)}) %collective-permute-start.48) | collective-permute-done | bytes 204832 | tf_op jit(solution)/shard_map/ppermute | solution.py:293
  139.9 2.3 %collective-permute-start.52 = (bf16[160,256]{1,0:T(8,128)(2,1)S(1)}, bf16[160,256]{1,0:T(8,128)(2,1)S(1)}, u32[]{:S(2)}, u32[]{:S(2)}) collective-permute-start(bf16[160,256]{1,0:T(8,128)(2,1)S(1)} %proj_last.1.refs_0_), channel_id=1, source_target_pairs={{0,3},{4,7},{9,10},{13,14},{18,17},{22,21},{27,24},{31,28}} | collective-permute-start | bytes 245768 | tf_op jit(solution)/shard_map/ppermute | solution.py:554
  145.9 2.6 %collective-permute-start.54 = (bf16[64,320]{1,0:T(8,128)(2,1)S(1)}, bf16[64,320]{1,0:T(8,128)(2,1)S(1)}, u32[]{:S(2)}, u32[]{:S(2)}) collective-permute-start(bf16[64,320]{1,0:T(8,128)(2,1)S(1)} %get-tuple-element.137), channel_id=1, source_target_pairs={{0,8},{4,12},{8,0},{12,4},{16,24},{20,28},{24,16},{28,20},{1,9},{5... | collective-permute-start | bytes 122888 | tf_op jit(solution)/shard_map/ppermute | solution.py:559
  149.0 1.8 %collective-permute-start.56 = (bf16[64,320]{1,0:T(8,128)(2,1)S(1)}, bf16[64,320]{1,0:T(8,128)(2,1)S(1)}, u32[]{:S(2)}, u32[]{:S(2)}) collective-permute-start(bf16[64,320]{1,0:T(8,128)(2,1)S(1)} %get-tuple-element.139), channel_id=1, source_target_pairs={{0,16},{4,20},{8,24},{12,28},{16,0},{20,4},{24,8},{28,12},{1,17},{... | collective-permute-start | bytes 122888 | tf_op jit(solution)/shard_map/ppermute | solution.py:559
  152.3 3.1 %collective-permute-start.58 = (bf16[64,320]{1,0:T(8,128)(2,1)S(1)}, bf16[64,320]{1,0:T(8,128)(2,1)S(1)}, u32[]{:S(2)}, u32[]{:S(2)}) collective-permute-start(bf16[64,320]{1,0:T(8,128)(2,1)S(1)} %get-tuple-element.141), channel_id=1, source_target_pairs={{0,24},{4,28},{8,16},{12,20},{16,8},{20,12},{24,0},{28,4},{1,25},{... | collective-permute-start | bytes 122888 | tf_op jit(solution)/shard_map/ppermute | solution.py:559
  156.7 2.5 %collective-permute-done.57.refs_5_ = bf16[64,320]{1,0:T(8,128)(2,1)S(1)} collective-permute-done((bf16[64,320]{1,0:T(8,128)(2,1)S(1)}, bf16[64,320]{1,0:T(8,128)(2,1)S(1)}, u32[]{:S(2)}, u32[]{:S(2)}) %collective-permute-start.57) | collective-permute-done | bytes 40992 | tf_op jit(solution)/shard_map/ppermute | solution.py:559
  159.2 3.0 %collective-permute-done.59.refs_7_ = bf16[64,320]{1,0:T(8,128)(2,1)S(1)} collective-permute-done((bf16[64,320]{1,0:T(8,128)(2,1)S(1)}, bf16[64,320]{1,0:T(8,128)(2,1)S(1)}, u32[]{:S(2)}, u32[]{:S(2)}) %collective-permute-start.59) | collective-permute-done | bytes 40992 | tf_op jit(solution)/shard_map/ppermute | solution.py:559
  (154 shorter events, 73.5 us)
Async XLA Ops:
  2.0 17.7 %collective-permute-start.12 = (bf16[320,1024]{1,0:T(8,128)(2,1)S(1)}, bf16[320,1024]{1,0:T(8,128)(2,1)S(1)}, u32[]{:S(2)}, u32[]{:S(2)}) collective-permute-start(bf16[320,1024]{1,0:T(8,128)(2,1)S(1)} %order_tokens.1.own), channel_id=1, source_target_pairs={{0,2},{1,3},{2,0},{3,1},{4,6},{5,7},{6,4},{7,5},{8,10},{9,11},{10,... | collective-permute-start | bytes 1966088 | tf_op jit(solution)/shard_map/ppermute | solution.py:326
  5.0 16.5 %collective-permute-start.1 = (bf16[80,1280]{1,0:T(8,128)(2,1)S(1)}, bf16[80,1280]{1,0:T(8,128)(2,1)S(1)}, u32[]{:S(2)}, u32[]{:S(2)}) collective-permute-start(bf16[80,1280]{1,0:T(8,128)(2,1)S(1)} %get-tuple-element.76.refs_1_), channel_id=1, source_target_pairs={{8,0},{16,8},{24,16},{28,24},{20,28},{12,20},{4,12},{0,4},{9,1},{1... | collective-permute-start | bytes 614408 | tf_op jit(solution)/shard_map/ppermute | solution.py:294
  6.6 34.1 %collective-permute-start.13 = (bf16[320,1024]{1,0:T(8,128)(2,1)S(1)}, bf16[320,1024]{1,0:T(8,128)(2,1)S(1)}, u32[]{:S(2)}, u32[]{:S(2)}) collective-permute-start(bf16[320,1024]{1,0:T(8,128)(2,1)S(1)} %order_tokens.1.own), channel_id=1, source_target_pairs={{0,1},{1,0},{2,3},{3,2},{4,5},{5,4},{6,7},{7,6},{8,9},{9,8},{10,11... | collective-permute-start | bytes 1966088 | tf_op jit(solution)/shard_map/ppermute | solution.py:323
  6.6 18.0 %collective-permute-start = (bf16[80,1280]{1,0:T(8,128)(2,1)S(1)}, bf16[80,1280]{1,0:T(8,128)(2,1)S(1)}, u32[]{:S(2)}, u32[]{:S(2)}) collective-permute-start(bf16[80,1280]{1,0:T(8,128)(2,1)S(1)} %get-tuple-element.77.refs_0_), channel_id=1, source_target_pairs={{0,8},{8,16},{16,24},{24,28},{28,20},{20,12},{12,4},{4,0},{1,9},{9... | collective-permute-start | bytes 614408 | tf_op jit(solution)/shard_map/ppermute | solution.py:293
  19.7 21.2 %collective-permute-start.14 = (bf16[320,1024]{1,0:T(8,128)(2,1)S(1)}, bf16[320,1024]{1,0:T(8,128)(2,1)}, u32[]{:S(2)}, u32[]{:S(2)}) collective-permute-start(bf16[320,1024]{1,0:T(8,128)(2,1)S(1)} %collective-permute-done.12.over_x), channel_id=1, source_target_pairs={{0,1},{1,0},{2,3},{3,2},{4,5},{5,4},{6,7},{7,6},{8,9},{9,8},{10,11... | collective-permute-start | bytes 1966088 | tf_op jit(solution)/shard_map/ppermute | solution.py:323
  24.6 7.6 %collective-permute-start.4 = (bf16[80,1280]{1,0:T(8,128)(2,1)S(1)}, bf16[80,1280]{1,0:T(8,128)(2,1)S(1)}, u32[]{:S(2)}, u32[]{:S(2)}) collective-permute-start(bf16[80,1280]{1,0:T(8,128)(2,1)S(1)} %collective-permute-done.refs_2_), channel_id=1, source_target_pairs={{0,8},{8,16},{16,24},{24,28},{28,20},{20,12},{12,4},{4,0},{1,9},{9... | collective-permute-start | bytes 614408 | tf_op jit(solution)/shard_map/ppermute | solution.py:293
  34.5 9.0 %collective-permute-start.8 = (bf16[80,1280]{1,0:T(8,128)(2,1)S(1)}, bf16[80,1280]{1,0:T(8,128)(2,1)S(1)}, u32[]{:S(2)}, u32[]{:S(2)}) collective-permute-start(bf16[80,1280]{1,0:T(8,128)(2,1)S(1)} %collective-permute-done.4.refs_6_), channel_id=1, source_target_pairs={{0,8},{8,16},{16,24},{24,28},{28,20},{20,12},{12,4},{4,0},{1,9},{9... | collective-permute-start | bytes 614408 | tf_op jit(solution)/shard_map/ppermute | solution.py:293
  36.5 8.0 %collective-permute-start.9 = (bf16[80,1280]{1,0:T(8,128)(2,1)S(1)}, bf16[80,1280]{1,0:T(8,128)(2,1)S(1)}, u32[]{:S(2)}, u32[]{:S(2)}) collective-permute-start(bf16[80,1280]{1,0:T(8,128)(2,1)S(1)} %collective-permute-done.5.refs_7_), channel_id=1, source_target_pairs={{8,0},{16,8},{24,16},{28,24},{20,28},{12,20},{4,12},{0,4},{9,1},{1... | collective-permute-start | bytes 614408 | tf_op jit(solution)/shard_map/ppermute | solution.py:294
  38.9 10.1 %collective-permute-start.10 = (bf16[80,1280]{1,0:T(8,128)(2,1)S(1)}, bf16[80,1280]{1,0:T(8,128)(2,1)S(1)}, u32[]{:S(2)}, u32[]{:S(2)}) collective-permute-start(bf16[80,1280]{1,0:T(8,128)(2,1)S(1)} %collective-permute-done.6.refs_8_), channel_id=1, source_target_pairs={{0,8},{8,16},{16,24},{24,28},{28,20},{20,12},{12,4},{4,0},{1,9},{9... | collective-permute-start | bytes 614408 | tf_op jit(solution)/shard_map/ppermute | solution.py:293
  40.7 8.4 %collective-permute-start.11 = (bf16[80,1280]{1,0:T(8,128)(2,1)S(1)}, bf16[80,1280]{1,0:T(8,128)(2,1)S(1)}, u32[]{:S(2)}, u32[]{:S(2)}) collective-permute-start(bf16[80,1280]{1,0:T(8,128)(2,1)S(1)} %collective-permute-done.7.refs_9_), channel_id=1, source_target_pairs={{8,0},{16,8},{24,16},{28,24},{20,28},{12,20},{4,12},{0,4},{9,1},{1... | collective-permute-start | bytes 614408 | tf_op jit(solution)/shard_map/ppermute | solution.py:294
  44.5 7.8 %collective-permute-start.15 = (bf16[80,1280]{1,0:T(8,128)(2,1)S(1)}, bf16[80,1280]{1,0:T(8,128)(2,1)S(1)}, u32[]{:S(2)}, u32[]{:S(2)}) collective-permute-start(bf16[80,1280]{1,0:T(8,128)(2,1)S(1)} %collective-permute-done.8.refs_10_), channel_id=1, source_target_pairs={{0,8},{8,16},{16,24},{24,28},{28,20},{20,12},{12,4},{4,0},{1,9},{9... | collective-permute-start | bytes 614408 | tf_op jit(solution)/shard_map/ppermute | solution.py:293
  46.4 7.7 %collective-permute-start.16 = (bf16[80,1280]{1,0:T(8,128)(2,1)S(1)}, bf16[80,1280]{1,0:T(8,128)(2,1)S(1)}, u32[]{:S(2)}, u32[]{:S(2)}) collective-permute-start(bf16[80,1280]{1,0:T(8,128)(2,1)S(1)} %collective-permute-done.9.refs_11_), channel_id=1, source_target_pairs={{8,0},{16,8},{24,16},{28,24},{20,28},{12,20},{4,12},{0,4},{9,1},{1... | collective-permute-start | bytes 614408 | tf_op jit(solution)/shard_map/ppermute | solution.py:294
  49.0 8.1 %collective-permute-start.19 = (bf16[80,1280]{1,0:T(8,128)(2,1)S(1)}, bf16[80,1280]{1,0:T(8,128)(2,1)S(1)}, u32[]{:S(2)}, u32[]{:S(2)}) collective-permute-start(bf16[80,1280]{1,0:T(8,128)(2,1)S(1)} %copy-done.9), channel_id=1, source_target_pairs={{0,8},{8,16},{16,24},{24,28},{28,20},{20,12},{12,4},{4,0},{1,9},{9... | collective-permute-start | bytes 614408 | tf_op jit(solution)/shard_map/ppermute | solution.py:293
  51.0 8.0 %collective-permute-start.20 = (bf16[80,1280]{1,0:T(8,128)(2,1)S(1)}, bf16[80,1280]{1,0:T(8,128)(2,1)S(1)}, u32[]{:S(2)}, u32[]{:S(2)}) collective-permute-start(bf16[80,1280]{1,0:T(8,128)(2,1)S(1)} %copy-done.11), channel_id=1, source_target_pairs={{8,0},{16,8},{24,16},{28,24},{20,28},{12,20},{4,12},{0,4},{9,1},{1... | collective-permute-start | bytes 614408 | tf_op jit(solution)/shard_map/ppermute | solution.py:294
  54.1 7.9 %collective-permute-start.17 = (bf16[80,1280]{1,0:T(8,128)(2,1)S(1)}, bf16[80,1280]{1,0:T(8,128)(2,1)S(1)}, u32[]{:S(2)}, u32[]{:S(2)}) collective-permute-start(bf16[80,1280]{1,0:T(8,128)(2,1)S(1)} %copy-done.11), channel_id=1, source_target_pairs={{0,8},{8,16},{16,24},{24,28},{28,20},{20,12},{12,4},{4,0},{1,9},{9... | collective-permute-start | bytes 614408 | tf_op jit(solution)/shard_map/ppermute | solution.py:293
  55.8 7.7 %collective-permute-start.18 = (bf16[80,1280]{1,0:T(8,128)(2,1)S(1)}, bf16[80,1280]{1,0:T(8,128)(2,1)S(1)}, u32[]{:S(2)}, u32[]{:S(2)}) collective-permute-start(bf16[80,1280]{1,0:T(8,128)(2,1)S(1)} %copy-done.9), channel_id=1, source_target_pairs={{8,0},{16,8},{24,16},{28,24},{20,28},{12,20},{4,12},{0,4},{9,1},{1... | collective-permute-start | bytes 614408 | tf_op jit(solution)/shard_map/ppermute | solution.py:294
  59.0 7.6 %collective-permute-start.23 = (bf16[80,1280]{1,0:T(8,128)(2,1)S(1)}, bf16[80,1280]{1,0:T(8,128)(2,1)S(1)}, u32[]{:S(2)}, u32[]{:S(2)}) collective-permute-start(bf16[80,1280]{1,0:T(8,128)(2,1)S(1)} %collective-permute-done.19.refs_7_), channel_id=1, source_target_pairs={{0,8},{8,16},{16,24},{24,28},{28,20},{20,12},{12,4},{4,0},{1,9},{9... | collective-permute-start | bytes 614408 | tf_op jit(solution)/shard_map/ppermute | solution.py:293
  60.5 7.7 %collective-permute-start.24 = (bf16[80,1280]{1,0:T(8,128)(2,1)S(1)}, bf16[80,1280]{1,0:T(8,128)(2,1)S(1)}, u32[]{:S(2)}, u32[]{:S(2)}) collective-permute-start(bf16[80,1280]{1,0:T(8,128)(2,1)S(1)} %collective-permute-done.20.refs_8_), channel_id=1, source_target_pairs={{8,0},{16,8},{24,16},{28,24},{20,28},{12,20},{4,12},{0,4},{9,1},{1... | collective-permute-start | bytes 614408 | tf_op jit(solution)/shard_map/ppermute | solution.py:294
  63.6 7.8 %collective-permute-start.21 = (bf16[80,1280]{1,0:T(8,128)(2,1)S(1)}, bf16[80,1280]{1,0:T(8,128)(2,1)S(1)}, u32[]{:S(2)}, u32[]{:S(2)}) collective-permute-start(bf16[80,1280]{1,0:T(8,128)(2,1)S(1)} %collective-permute-done.17.refs_9_), channel_id=1, source_target_pairs={{0,8},{8,16},{16,24},{24,28},{28,20},{20,12},{12,4},{4,0},{1,9},{9... | collective-permute-start | bytes 614408 | tf_op jit(solution)/shard_map/ppermute | solution.py:293
  86.5 13.4 %collective-permute-start.34 = (bf16[320,1024]{1,0:T(8,128)(2,1)S(1)}, bf16[320,1024]{1,0:T(8,128)(2,1)S(1)}, u32[]{:S(2)}, u32[]{:S(2)}) collective-permute-start(bf16[320,1024]{1,0:T(8,128)(2,1)S(1)} %get-tuple-element.120), channel_id=1, source_target_pairs={{0,1},{1,0},{2,3},{3,2},{4,5},{5,4},{6,7},{7,6},{8,9},{9,8},{10,11... | collective-permute-start | bytes 1966088 | tf_op jit(solution)/shard_map/ppermute | solution.py:323
  97.7 26.6 %collective-permute-start.33 = (bf16[320,1024]{1,0:T(8,128)(2,1)S(1)}, bf16[320,1024]{1,0:T(8,128)(2,1)S(1)}, u32[]{:S(2)}, u32[]{:S(2)}) collective-permute-start(bf16[320,1024]{1,0:T(8,128)(2,1)S(1)} %get-tuple-element.117), channel_id=1, source_target_pairs={{0,1},{1,0},{2,3},{3,2},{4,5},{5,4},{6,7},{7,6},{8,9},{9,8},{10,11... | collective-permute-start | bytes 1966088 | tf_op jit(solution)/shard_map/ppermute | solution.py:323
  100.0 24.7 %collective-permute-start.35 = (bf16[320,1024]{1,0:T(8,128)(2,1)S(1)}, bf16[320,1024]{1,0:T(8,128)(2,1)S(1)}, u32[]{:S(2)}, u32[]{:S(2)}) collective-permute-start(bf16[320,1024]{1,0:T(8,128)(2,1)S(1)} %add.2), channel_id=1, source_target_pairs={{0,2},{1,3},{2,0},{3,1},{4,6},{5,7},{6,4},{7,5},{8,10},{9,11},{10,... | collective-permute-start | bytes 1966088 | tf_op jit(solution)/shard_map/ppermute | solution.py:326
  106.7 8.0 %collective-permute-start.40 = (bf16[80,1280]{1,0:T(8,128)(2,1)S(1)}, bf16[80,1280]{1,0:T(8,128)(2,1)S(1)}, u32[]{:S(2)}, u32[]{:S(2)}) collective-permute-start(bf16[80,1280]{1,0:T(8,128)(2,1)S(1)} %collective-permute-done.36.refs_4_), channel_id=1, source_target_pairs={{0,8},{8,16},{16,24},{24,28},{28,20},{20,12},{12,4},{4,0},{1,9},{9... | collective-permute-start | bytes 614408 | tf_op jit(solution)/shard_map/ppermute | solution.py:293
  108.8 10.4 %collective-permute-start.38 = (bf16[80,1280]{1,0:T(8,128)(2,1)S(1)}, bf16[80,1280]{1,0:T(8,128)(2,1)S(1)}, u32[]{:S(2)}, u32[]{:S(2)}) collective-permute-start(bf16[80,1280]{1,0:T(8,128)(2,1)S(1)} %collective-permute-done.27.refs_2_), channel_id=1, source_target_pairs={{0,8},{8,16},{16,24},{24,28},{28,20},{20,12},{12,4},{4,0},{1,9},{9... | collective-permute-start | bytes 614408 | tf_op jit(solution)/shard_map/ppermute | solution.py:293
  114.8 7.8 %collective-permute-start.39 = (bf16[80,1280]{1,0:T(8,128)(2,1)S(1)}, bf16[80,1280]{1,0:T(8,128)(2,1)S(1)}, u32[]{:S(2)}, u32[]{:S(2)}) collective-permute-start(bf16[80,1280]{1,0:T(8,128)(2,1)S(1)} %collective-permute-done.28.refs_3_), channel_id=1, source_target_pairs={{8,0},{16,8},{24,16},{28,24},{20,28},{12,20},{4,12},{0,4},{9,1},{1... | collective-permute-start | bytes 614408 | tf_op jit(solution)/shard_map/ppermute | solution.py:294
  115.0 10.1 %collective-permute-start.44 = (bf16[80,1280]{1,0:T(8,128)(2,1)S(1)}, bf16[80,1280]{1,0:T(8,128)(2,1)S(1)}, u32[]{:S(2)}, u32[]{:S(2)}) collective-permute-start(bf16[80,1280]{1,0:T(8,128)(2,1)S(1)} %collective-permute-done.40.refs_8_), channel_id=1, source_target_pairs={{0,8},{8,16},{16,24},{24,28},{28,20},{20,12},{12,4},{4,0},{1,9},{9... | collective-permute-start | bytes 614408 | tf_op jit(solution)/shard_map/ppermute | solution.py:293
  119.1 8.0 %collective-permute-start.45 = (bf16[80,1280]{1,0:T(8,128)(2,1)S(1)}, bf16[80,1280]{1,0:T(8,128)(2,1)S(1)}, u32[]{:S(2)}, u32[]{:S(2)}) collective-permute-start(bf16[80,1280]{1,0:T(8,128)(2,1)S(1)} %collective-permute-done.41.refs_9_), channel_id=1, source_target_pairs={{8,0},{16,8},{24,16},{28,24},{20,28},{12,20},{4,12},{0,4},{9,1},{1... | collective-permute-start | bytes 614408 | tf_op jit(solution)/shard_map/ppermute | solution.py:294
  133.6 10.7 %collective-permute-start.47 = (bf16[320,256]{1,0:T(8,128)(2,1)S(1)}, bf16[320,256]{1,0:T(8,128)(2,1)S(1)}, u32[]{:S(2)}, u32[]{:S(2)}) collective-permute-start(bf16[320,256]{1,0:T(8,128)(2,1)S(1)} %add.3), channel_id=1, source_target_pairs={{0,2},{1,3},{2,0},{3,1},{4,6},{5,7},{6,4},{7,5},{8,10},{9,11},{10,... | collective-permute-start | bytes 491528 | tf_op jit(solution)/shard_map/ppermute | solution.py:326
  145.9 9.5 %collective-permute-start.54 = (bf16[64,320]{1,0:T(8,128)(2,1)S(1)}, bf16[64,320]{1,0:T(8,128)(2,1)S(1)}, u32[]{:S(2)}, u32[]{:S(2)}) collective-permute-start(bf16[64,320]{1,0:T(8,128)(2,1)S(1)} %get-tuple-element.137), channel_id=1, source_target_pairs={{0,8},{4,12},{8,0},{12,4},{16,24},{20,28},{24,16},{28,20},{1,9},{5... | collective-permute-start | bytes 122888 | tf_op jit(solution)/shard_map/ppermute | solution.py:559
  148.5 8.2 %collective-permute-start.55 = (bf16[64,320]{1,0:T(8,128)(2,1)S(1)}, bf16[64,320]{1,0:T(8,128)(2,1)S(1)}, u32[]{:S(2)}, u32[]{:S(2)}) collective-permute-start(bf16[64,320]{1,0:T(8,128)(2,1)S(1)} %get-tuple-element.138), channel_id=1, source_target_pairs={{0,12},{4,8},{8,4},{12,0},{16,28},{20,24},{24,20},{28,16},{1,13},{... | collective-permute-start | bytes 122888 | tf_op jit(solution)/shard_map/ppermute | solution.py:559
  149.0 7.7 %collective-permute-start.56 = (bf16[64,320]{1,0:T(8,128)(2,1)S(1)}, bf16[64,320]{1,0:T(8,128)(2,1)S(1)}, u32[]{:S(2)}, u32[]{:S(2)}) collective-permute-start(bf16[64,320]{1,0:T(8,128)(2,1)S(1)} %get-tuple-element.139), channel_id=1, source_target_pairs={{0,16},{4,20},{8,24},{12,28},{16,0},{20,4},{24,8},{28,12},{1,17},{... | collective-permute-start | bytes 122888 | tf_op jit(solution)/shard_map/ppermute | solution.py:559
  150.8 8.4 %collective-permute-start.57 = (bf16[64,320]{1,0:T(8,128)(2,1)S(1)}, bf16[64,320]{1,0:T(8,128)(2,1)S(1)}, u32[]{:S(2)}, u32[]{:S(2)}) collective-permute-start(bf16[64,320]{1,0:T(8,128)(2,1)S(1)} %get-tuple-element.140), channel_id=1, source_target_pairs={{0,20},{4,16},{8,28},{12,24},{16,4},{20,0},{24,12},{28,8},{1,21},{... | collective-permute-start | bytes 122888 | tf_op jit(solution)/shard_map/ppermute | solution.py:559
  (47 other events, 442.1 us)

commit v3 on v2

v3 whole, which is shorter than its diff:
```python
import functools

import jax
import jax.numpy as jnp
from jax import lax
from jax.experimental import pallas as pl
from jax.experimental.pallas import tpu as pltpu
from jax.sharding import PartitionSpec as P

F32 = jnp.float32
BF16 = jnp.bfloat16
WINDOW = 4
VMEM = pl.BlockSpec(memory_space=pltpu.VMEM)


def call(kernel, operands, outs, scratch=(), name=None):
    single = not isinstance(outs, (list, tuple))
    return pl.pallas_call(
        kernel,
        out_shape=outs,
        in_specs=[VMEM] * len(operands),
        out_specs=VMEM if single else [VMEM] * len(outs),
        scratch_shapes=list(scratch),
        compiler_params=pltpu.CompilerParams(vmem_limit_bytes=28 * 1024 * 1024),
        cost_estimate=pl.CostEstimate(flops=0, bytes_accessed=0, transcendentals=0),
        name=name,
    )(*operands)


def shape(*dims, dtype=BF16):
    return jax.ShapeDtypeStruct(dims, dtype)


def after(x, *others):
    return lax.optimization_barrier((x, *others))[0]


def ring_order(count):
    return list(range(0, count, 2)) + list(range(count - 1, 0, -2))


def ring_owner(me, shift, count):
    half = me // 2
    at = jnp.where(me % 2 == 0, half, count - 1 - half) + (shift + count)
    at = at % count
    return jnp.where(at < count // 2, 2 * at, 2 * (count - 1 - at) + 1)


class Piece:
    def __init__(self, array, start, rows, shift, base, index=0):
        self.array, self.start, self.rows = array, start, rows
        self.shift, self.base, self.index = shift, base, index

    def row(self, count, shard_rows):
        if self.shift is None:
            return self.index * self.rows
        return ring_owner(lax.axis_index("wide"), self.shift, count) * shard_rows + self.base

    def block_row(self, count, shard_rows, block):
        if self.shift is None:
            of, inside = self.index, 0
        else:
            owner = ring_owner(lax.axis_index("wide"), self.shift, count)
            per_block = block // shard_rows
            of, inside = owner // per_block, (owner % per_block) * shard_rows + self.base
        mine = lax.axis_index("narrow")
        over_x = jnp.where(of // 2 == mine // 2, 0, 1)
        over_core = jnp.where(of % 2 == mine % 2, 0, 1)
        return over_x, over_core, inside


def rows_at(start, rows):
    return pl.ds(pl.multiple_of(start, 16), rows)


def order_kernel(x_ref, *outs):
    tokens = x_ref.shape[1]
    windows = tokens // WINDOW
    source = lax.broadcasted_iota(jnp.int32, (tokens, windows), 0)
    window = lax.broadcasted_iota(jnp.int32, (tokens, windows), 1)
    each = WINDOW // len(outs)
    for p in range(WINDOW):
        pick = jnp.where(source == WINDOW * window + p, 1.0, 0.0).astype(BF16)
        outs[p // each][p % each] = jnp.dot(
            x_ref[...], pick, preferred_element_type=F32
        ).astype(BF16)


def shards_kernel(w_out, w_proj, *outs):
    rows, width = w_proj.shape[1], w_proj.shape[2]
    half = rows // (len(outs) // 2)
    flat = jnp.concatenate([w_proj[p] for p in range(WINDOW)], axis=1)
    for i in range(len(outs) // 2):
        outs[i][...] = w_out[i * half : (i + 1) * half, :]
        outs[len(outs) // 2 + i][...] = flat[i * half : (i + 1) * half, :]


def route_kernel(seq_rows, bucket, place, slots_of, targets):
    groups, windows = place.shape
    me = lax.axis_index("wide")
    table = place[...]
    owner = jnp.where(table >= 0, 0, -1)
    for d in range(1, groups):
        owner = owner + jnp.where(table >= d * seq_rows, 1, 0)
    earlier = jnp.where(
        lax.broadcasted_iota(jnp.int32, (windows, windows), 0)
        <= lax.broadcasted_iota(jnp.int32, (windows, windows), 1),
        1.0,
        0.0,
    ).astype(BF16)
    here = jnp.where(owner == me, 1.0, 0.0)
    rank = jnp.dot(here.astype(BF16), earlier, preferred_element_type=F32)
    rank = jnp.where(owner == me, rank, 0.0).astype(jnp.int32)
    local = table - me * seq_rows
    slot = lax.broadcasted_iota(jnp.int32, (bucket, windows), 0) + 1
    source_at = lax.broadcasted_iota(jnp.int32, (groups, windows), 0)
    for k in range(groups):
        wanted = source_at == k
        of_rank = jnp.sum(jnp.where(wanted, rank, 0), axis=0, keepdims=True)
        of_local = jnp.sum(jnp.where(wanted, local, 0), axis=0, keepdims=True)
        found = jnp.where(of_rank == slot, of_local + 1, 0)
        targets[k * bucket : (k + 1) * bucket, :] = jnp.sum(found, axis=1, keepdims=True) - 1
    mine = jnp.sum(jnp.where(source_at == me, owner, 0), axis=0, keepdims=True)
    hits = source_at == mine
    rank = jnp.dot(
        jnp.where(hits, 1.0, 0.0).astype(BF16), earlier, preferred_element_type=F32
    )
    rank = jnp.sum(jnp.where(hits, rank, 0.0), axis=0, keepdims=True).astype(jnp.int32)
    slots_of[...] = jnp.where(mine >= 0, mine * bucket + rank - 1, groups * bucket)


def norm_kernel(own, over_x, over_core, over_both, gain, bias, o_ref, whole):
    parts = (own, over_x, over_core, over_both)
    each, rows, windows = own.shape
    tokens = each * windows
    mine = lax.axis_index("narrow")
    for part, flip in zip(parts, (0, 2, 1, 3)):
        at = (mine ^ flip) * rows
        for j in range(each):
            whole[rows_at(at, rows), j * windows : (j + 1) * windows] = part[j]
    width = whole.shape[0]
    step = 128
    for t in range(0, tokens, step):
        values = whole[:, t : t + step].astype(F32)
        center = jnp.sum(values, axis=0, keepdims=True) * (1.0 / width)
        values = values - center
        spread = jnp.sum(values * values, axis=0, keepdims=True) * (1.0 / width)
        values = (values * lax.rsqrt(spread + 1e-06)).T
        o_ref[t : t + step, :] = (values * gain[...] + bias[...]).astype(BF16)


def hidden_kernel(pieces, count, shard_rows, first, columns, bias, *refs):
    arrays = 1 + max(p.array for p in pieces)
    sources, normed, (o_ref, part) = refs[:arrays], refs[arrays:-2], refs[-2:]
    for p in pieces:
        part[rows_at(p.row(count, shard_rows), p.rows), :] = sources[p.array][
            p.start : p.start + p.rows, first : first + columns
        ]
    at = 0
    for rows in normed:
        v = jnp.dot(rows[...], part[...], preferred_element_type=F32)
        v = v + bias[:, first : first + columns]
        o_ref[at : at + rows.shape[0], :] = (
            0.5 * v * (1.0 + lax.erf(v * (2.0**-0.5)))
        ).astype(BF16)
        at += rows.shape[0]


def out_kernel(pieces, count, shard_rows, over_x, hidden_count, chunks, *refs):
    hidden, refs = refs[:hidden_count], refs[hidden_count:]
    outs, part = refs[-1 - 2 * chunks : -1], refs[-1]
    keep, give = outs[:chunks], outs[chunks:]
    sources = refs[: -1 - 2 * chunks]
    block, tokens = keep[0].shape
    for p in pieces:
        x, core, inside = p.block_row(count, shard_rows, block)

        @pl.when(x == over_x)
        def _():
            part[rows_at(core * block + inside, p.rows), :] = sources[p.array][
                p.start : p.start + p.rows, :
            ]

    columns = hidden[0].shape[1]
    step = 256
    for t in range(0, tokens * chunks, step):
        total = None
        for i, h in enumerate(hidden):
            v = lax.dot_general(
                part[:, i * columns : (i + 1) * columns],
                h[t : t + step, :],
                (((1,), (1,)), ((), ())),
                preferred_element_type=F32,
            )
            total = v if total is None else total + v
        total = total.astype(BF16)
        c, at = t // tokens, t % tokens
        keep[c][:, at : at + step] = total[:block]
        give[c][:, at : at + step] = total[block:]


def proj_kernel(pieces, missing, count, shard_rows, merged, *refs):
    sources, (keep, give, part) = refs[:-3], refs[-3:]
    block = keep.shape[1]
    for p in pieces:
        x, core, inside = p.block_row(count, shard_rows, block)
        at = rows_at(core * 2 * block + x * block + inside, p.rows)
        part[at, :] = sources[p.array][p.start : p.start + p.rows, :]
    if missing is not None:
        x, core, inside = missing.block_row(count, shard_rows, block)
        at = rows_at(core * 2 * block + x * block + inside, missing.rows)
        part[at, :] = jnp.zeros((missing.rows, part.shape[1]), BF16)
    for core, target in ((1, give), (0, keep)):
        v = jnp.dot(
            part[core * 2 * block : (core + 1) * 2 * block, :],
            merged[...],
            preferred_element_type=F32,
        ).astype(BF16)
        target[0] = v[:block]
        target[1] = v[block:]


def last_kernel(first, second, merged, o_ref):
    rows = first.shape[0]
    whole = jnp.concatenate([first[...], second[...]], axis=0)
    o_ref[...] = jnp.dot(whole, merged[...], preferred_element_type=F32).astype(BF16)


def stream_kernel(chunks, bias, *refs):
    o_ref = refs[-1]
    own, keep, near, far = (refs[i * chunks : (i + 1) * chunks] for i in range(4))
    each, rows, windows = own[0].shape
    for c in range(chunks):
        total = keep[c][...].astype(F32) + near[c][...].astype(F32) + far[c][...].astype(F32)
        total = total + bias[...]
        for j in range(each):
            v = own[c][j].astype(F32) + total[:, j * windows : (j + 1) * windows]
            p = c * each + j
            o_ref[p * rows : (p + 1) * rows, :] = v.astype(BF16)


LANES = 128


def compact(width, bucket):
    rest = width % LANES
    return rest > 0 and LANES % rest == 0 and bucket % (16 * (LANES // rest)) == 0


def pack_kernel(missing, count, shard_rows, groups, extra, slots_of, keep, near, far, bias, *refs):
    late, o_ref, total = refs[:extra], refs[-2], refs[-1]
    total[...] = keep[0].astype(F32) + near[0].astype(F32) + far[...].astype(F32)
    if extra:
        x, core, inside = missing.block_row(count, shard_rows, total.shape[0])

        @pl.when(x + core == 0)
        def _():
            at = pl.ds(pl.multiple_of(inside, 16), missing.rows)
            added = late[0][...].astype(F32)
            for r in late[1:]:
                added = added + r[...].astype(F32)
            total[at, :] = total[at, :] + added

    vision = (total[...] + bias[...]).astype(BF16)
    width = vision.shape[0]
    bucket = o_ref.shape[1] * o_ref.shape[2] // width
    slot = lax.broadcasted_iota(jnp.int32, (groups * bucket, vision.shape[1]), 0)
    pick = jnp.where(slot == slots_of[...], 1.0, 0.0).astype(BF16)
    moved = lax.dot_general(
        pick, vision, (((1,), (1,)), ((), ())), preferred_element_type=F32
    ).astype(BF16)
    for k in range(groups):
        rows = moved[k * bucket : (k + 1) * bucket]
        if o_ref.shape[2] == width:
            o_ref[k] = rows
            continue
        tiles = width // LANES
        for i in range(tiles):
            o_ref[k, i * bucket : (i + 1) * bucket, :] = rows[:, i * LANES : (i + 1) * LANES]
        rest = rows[:, tiles * LANES :]
        fold = LANES // rest.shape[1]
        piece = bucket // fold
        o_ref[k, tiles * bucket :, :] = jnp.concatenate(
            [rest[i * piece : (i + 1) * piece] for i in range(fold)], axis=1
        )


def place_kernel(targets, text, arrived, o_ref):
    width, rows = text.shape
    groups = arrived.shape[0]
    bucket = arrived.shape[1] * arrived.shape[2] // width
    slots = groups * bucket
    row = lax.broadcasted_iota(jnp.int32, (slots, rows), 1)
    pick = jnp.where(row == targets[...], 1.0, 0.0)
    hit = jnp.sum(pick, axis=0, keepdims=True) > 0.5
    pick = pick.astype(BF16)

    def moved(blocks):
        return lax.dot_general(
            blocks, pick, (((0,), (0,)), ((), ())), preferred_element_type=F32
        ).astype(BF16)

    if arrived.shape[2] == width:
        whole = jnp.concatenate([arrived[k] for k in range(groups)], axis=0)
        o_ref[...] = jnp.where(hit, moved(whole), text[...])
        return
    tiles = width // LANES
    for i in range(tiles):
        part = jnp.concatenate(
            [arrived[k, i * bucket : (i + 1) * bucket, :] for k in range(groups)], axis=0
        )
        at = slice(i * LANES, (i + 1) * LANES)
        o_ref[at, :] = jnp.where(hit, moved(part), text[at, :])
    rest = width % LANES
    parts = []
    for k in range(groups):
        folded = arrived[k, tiles * bucket :, :]
        parts += [folded[:, i * rest : (i + 1) * rest] for i in range(LANES // rest)]
    at = slice(tiles * LANES, width)
    o_ref[at, :] = jnp.where(hit, moved(jnp.concatenate(parts, axis=0)), text[at, :])


def add_kernel(keep, near, o_ref):
    o_ref[...] = (keep[...].astype(F32) + near[...].astype(F32)).astype(BF16)


class Ring:
    def __init__(self, count):
        self.count = count
        order = ring_order(count)
        self.right = [(order[i], order[(i + 1) % count]) for i in range(count)]
        self.left = [(b, a) for a, b in self.right]
        self.done = []
        self.work = []

    def step(self, to_right, to_left):
        t = len(self.done)
        waits = [x for at, x in self.work if at == t - 2]
        if t >= 2:
            to_right = after(to_right, self.done[t - 2][0], *waits)
            to_left = after(to_left, self.done[t - 2][1])
        pair = (
            lax.ppermute(to_right, "wide", self.right),
            lax.ppermute(to_left, "wide", self.left),
        )
        self.done.append(pair)
        return pair

    def now(self, x):
        if len(self.done) >= 2:
            return after(x, *self.done[-2])
        return x

    def add_work(self, x):
        self.work.append((len(self.done) - 1, x))


def per_device(
    patches, norm_gain, norm_bias, w_in, b_in, w_out, b_out, w_proj, b_proj, text, place
):
    groups, parts = lax.axis_size("wide"), lax.axis_size("narrow")
    width, tokens = patches.shape[1], patches.shape[0]
    full = width * parts
    ff = w_in.shape[1]
    windows = tokens // WINDOW
    seq_rows = text.shape[0]
    bucket = seq_rows // groups
    slots = groups * bucket
    shard_rows = [w_in.shape[0], w_out.shape[1], w_proj.shape[2]]
    small = groups == 8 and all(r % 32 == 0 for r in shard_rows)
    chunks = 2

    near_pairs = [(i, i ^ 1) for i in range(parts)]
    far_pairs = [(i, i ^ 2) for i in range(parts)]

    def near(x):
        return lax.ppermute(x, "narrow", near_pairs)

    def far(x):
        return lax.ppermute(x, "narrow", far_pairs)


    def order(x):
        return call(
            order_kernel, (x,), [shape(WINDOW // chunks, width, windows)] * chunks,
            name="order_tokens",
        )

    def shards(count):
        rows = shard_rows[1] // count
        return call(
            shards_kernel, (w_out.T, jnp.transpose(w_proj, (0, 2, 1))),
            [shape(rows, full)] * (2 * count), name="shards",
        )

    def route():
        return call(
            functools.partial(route_kernel, seq_rows, bucket), (place.reshape(groups, windows),),
            [shape(1, windows, dtype=jnp.int32), shape(slots, 1, dtype=jnp.int32)], name="route",
        )

    def norm(blocks):
        count = tokens // chunks
        return call(
            norm_kernel, (*blocks, norm_gain[None], norm_bias[None]), shape(count, full),
            scratch=[pltpu.VMEM((full, count), BF16)], name="norm",
        )

    def hidden(pieces, arrays, normed, first, columns):
        return call(
            functools.partial(hidden_kernel, pieces, groups, shard_rows[0], first, columns),
            (b_in[None], *arrays, *normed), shape(tokens, columns),
            scratch=[pltpu.VMEM((full, columns), BF16)], name="hidden",
        )

    def mlp_out(pieces, arrays, hiddens, over_x):
        outs = call(
            functools.partial(
                out_kernel, pieces, groups, shard_rows[1], over_x, len(hiddens), chunks
            ),
            (*hiddens, *arrays), [shape(width, tokens // chunks)] * (2 * chunks),
            scratch=[pltpu.VMEM((2 * width, ff), BF16)], name="mlp_out",
        )
        return outs[:chunks], outs[chunks:]

    def add(keep, other):
        return call(add_kernel, (keep, other), shape(*keep.shape), name="add")

    def stream(own, keep, core_sums, x_sums):
        return call(
            functools.partial(stream_kernel, chunks),
            (b_out[:, None], *own, *keep, *core_sums, *x_sums),
            shape(WINDOW * width, windows), name="stream",
        )

    def proj(pieces, missing, arrays, merged):
        return call(
            functools.partial(proj_kernel, pieces, missing, groups, shard_rows[2]),
            (merged, *arrays), [shape(2, width, windows)] * 2,
            scratch=[pltpu.VMEM((full, WINDOW * width), BF16)], name="proj",
        )

    def pack(slots_of, missing, keep, core_sums, x_sums, late):
        block = (bucket, width)
        if compact(width, bucket):
            block = (bucket * width // LANES, LANES)
        return call(
            functools.partial(pack_kernel, missing, groups, shard_rows[2], groups, len(late)),
            (slots_of, keep, core_sums, x_sums, b_proj[:, None], *late), shape(groups, *block),
            scratch=[pltpu.VMEM((width, windows), F32)], name="pack",
        )

    def exchange_and_place(buffer, targets):
        arrived = lax.all_to_all(buffer, "wide", split_axis=0, concat_axis=0, tiled=True)
        return call(
            place_kernel, (targets, text.T, arrived), shape(width, seq_rows), name="place"
        ).T


    if not small:
        shard = [w_in, *shards(1)]
        wholes = [lax.all_gather(s, "wide", axis=0, tiled=True) for s in shard]
        pieces = [Piece(0, k * width, width, None, 0, k) for k in range(parts)]
        own = order(patches.T)
        over_x = [far(x) for x in own]
        normed = [norm((x, y, near(x), near(y))) for x, y in zip(own, over_x)]
        act = hidden(pieces, wholes[:1], normed, 0, ff)
        keep_x, give_x = mlp_out(pieces, wholes[1:2], [act], 1)
        keep, give = mlp_out(pieces, wholes[1:2], [act], 0)
        x_sums = [far(add(k, near(g))) for k, g in zip(keep_x, give_x)]
        merged = stream(own, keep, [near(g) for g in give], x_sums)
        slots_of, targets = route()
        keep, give = proj(pieces, None, wholes[2:], merged)
        core_sums = near(give)
        x_sums = far(add(keep[1], core_sums[1]))
        return exchange_and_place(pack(slots_of, None, keep, core_sums, x_sums, ()), targets)


    ring = Ring(groups)
    half_rows = shard_rows[0] // 2
    last = groups // 2

    def gather(halves, work):
        arrays = list(halves)
        pieces = [Piece(h, 0, half_rows, 0, h * half_rows) for h in (0, 1)]
        held = {(way, h): halves[h] for way in (0, 1) for h in (0, 1)}
        t = 0
        for step in range(1, last + 1):
            for first in (0, 1):
                if step == last and first == 1:
                    continue
                pair = ring.step(held[0, first], held[1, 1 - first])
                for way, h in ((0, first), (1, 1 - first)):
                    held[way, h] = pair[way]
                    shift = -step if way == 0 else step
                    pieces.append(Piece(len(arrays), 0, half_rows, shift, h * half_rows))
                    arrays.append(pair[way])
                if t in work:
                    work[t]()
                t += 1
        return pieces, arrays

    own, over_x, over_core, over_both, normed = [], [], [], [], []
    got = {}

    def start_tokens():
        own.extend(order(patches.T))
        over_x.append(far(own[0]))
        ring.add_work(own[0])

    def start_shards():
        got["shards"] = shards(2)
        ring.add_work(got["shards"][0])
        over_core.extend(near(x) for x in own)

    def send_second():
        over_x.append(far(ring.now(own[1])))
        got["slots_of"], got["targets"] = route()

    def send_both():
        over_both.append(near(ring.now(over_x[len(over_both)])))

    def start_norm():
        i = len(normed)
        first = ring.now(own[i])
        normed.append(norm((first, over_x[i], over_core[i], over_both[i])))
        ring.add_work(normed[i])

    def both_and_norm():
        send_both()
        start_norm()

    pieces_in, arrays_in = gather(
        [w_in[:half_rows], w_in[half_rows:]],
        {0: start_tokens, 1: start_shards, 2: send_second, 4: send_both, 5: both_and_norm,
         6: start_norm},
    )

    columns = 256
    hiddens = []

    def start_hidden():
        rows = [ring.now(normed[0]), *normed[1:]]
        hiddens.append(hidden(pieces_in, arrays_in, rows, len(hiddens) * columns, columns))
        ring.add_work(hiddens[-1])

    pieces_out, arrays_out = gather(
        got["shards"][:2], {t: start_hidden for t in range(ff // columns)}
    )

    def start_out(over_x):
        acts = [ring.now(hiddens[0]), *hiddens[1:]]
        keep, give = mlp_out(pieces_out, arrays_out, acts, over_x)
        got["keep", over_x] = keep
        got["core", over_x] = [near(g) for g in give]
        ring.add_work(keep[0])

    def start_sums():
        core = [ring.now(got["core", 1][0]), *got["core", 1][1:]]
        sums = [add(k, c) for k, c in zip(got["keep", 1], core)]
        got["x_sums"] = [far(x) for x in sums]
        ring.add_work(sums[0])
        start_out(0)

    pieces_proj, arrays_proj = gather(
        got["shards"][2:], {0: lambda: start_out(1), 1: start_sums}
    )

    merged = stream(own, got["keep", 0], got["core", 0], got["x_sums"])
    missing = Piece(0, 0, shard_rows[2], last, 0)
    keep, give = proj(pieces_proj[:-2], missing, arrays_proj[:-2], merged)
    core_sums = near(give)
    x_sums = far(add(keep[1], core_sums[1]))

    halves = sorted(pieces_proj[-2:], key=lambda p: p.base)
    late = call(
        last_kernel, (*[arrays_proj[p.array] for p in halves], merged),
        shape(shard_rows[2], windows), name="proj_last",
    )
    order_of = ring_order(groups)
    keeper = [
        order_of[(order_of.index(w) + last) % groups] * shard_rows[2] // width
        for w in range(groups)
    ]
    lates = [late]
    for flip in range(1, parts):
        pairs = [(w * parts + (keeper[w] ^ flip), w * parts + keeper[w]) for w in range(groups)]
        lates.append(lax.ppermute(late, ("wide", "narrow"), pairs))

    buffer = pack(got["slots_of"], missing, keep, core_sums, x_sums, lates)
    return exchange_and_place(buffer, got["targets"])


def solution(mesh):
    placed = (
        P("wide", "narrow"),
        P(),
        P(),
        P("wide", "narrow"),
        P("narrow"),
        P("narrow", "wide"),
        P("narrow"),
        P(None, "narrow", "wide"),
        P("narrow"),
        P("wide", "narrow"),
        P(),
    )
    return jax.shard_map(
        per_device, mesh=mesh, in_specs=placed, out_specs=P("wide", "narrow"), check_vma=False
    )
```

time: 164 us -> 146 us (0.89)
  starting transfers between devices: 68.7 us -> 53.4 us
  blocking collectives: 0 us -> 15.3 us
  waiting for transfers between devices: 70.5 us -> 55.8 us
  Pallas kernels: 19.6 us -> 17.6 us
    ppermute x21, starting transfers between devices: 31 us -> 14.1 us  [step(): lax.ppermute(to_right, 'wide', self.right)]
    all_to_all x0 -> x1, blocking collectives: none -> 15.3 us  [exchange_and_place(): lax.all_to_all(buffer, 'wide', split_axis=0, concat_axis=0, tiled=True)]
    ppermute x21, starting transfers between devices: 16.1 us -> 28.3 us  [step(): lax.ppermute(to_left, 'wide', self.left)]
    ppermute x7 -> x0, starting transfers between devices: 11.8 us -> none  [per_device(): lax.ppermute(out_blocks[k], 'wide', [(w, w ^ k) for w in range(groups)])]
    ppermute x3 -> x5, waiting for transfers between devices: 12.6 us -> 3.43 us  [far(): return lax.ppermute(x, 'narrow', far_pairs)]
    ppermute x21, waiting for transfers between devices: 30.2 us -> 22.4 us  [step(): lax.ppermute(to_right, 'wide', self.right)]
    ppermute x21, waiting for transfers between devices: 21.4 us -> 28.4 us  [step(): lax.ppermute(to_left, 'wide', self.left)]
    ppermute x7 -> x0, waiting for transfers between devices: 5.59 us -> none  [per_device(): lax.ppermute(out_blocks[k], 'wide', [(w, w ^ k) for w in range(groups)])]
  transfers between devices with their start and end apart: 60 -> 59, of which waited for: 34 -> 26; matrix products, arithmetic and copies ran while one was open for 0% -> 0% of each run, Pallas kernels for 8% -> 10%
where the time goes in v3:
time: 146 us
  waiting for transfers between devices  55.8 us (38%)
  starting transfers between devices  53.4 us (37%)
  Pallas kernels  17.6 us (12%)
  blocking collectives  15.3 us (10%)
  local copies, waits for them, and re-layouts  3.48 us (2%)
    ppermute x21, waiting for transfers between devices, step(): lax.ppermute(to_left, 'wide', self.left)  28.4 us
    ppermute x21, starting transfers between devices, step(): lax.ppermute(to_left, 'wide', self.left)  28.3 us
    ppermute x21, waiting for transfers between devices, step(): lax.ppermute(to_right, 'wide', self.right)  22.4 us
    pallas_call x20, Pallas kernels, call(): pl.pallas_call(kernel, out_shape=outs, in_specs=[VMEM] * len(operands), o...  17.6 us
    all_to_all x1, blocking collectives, exchange_and_place(): lax.all_to_all(buffer, 'wide', split_axis=0, concat_axis=0, tiled=True)  15.3 us
    ppermute x21, starting transfers between devices, step(): lax.ppermute(to_right, 'wide', self.right)  14.1 us
    ppermute x3, starting transfers between devices, per_device(): lates.append(lax.ppermute(late, ('wide', 'narrow'), pairs))  4.99 us
    ppermute x5, starting transfers between devices, far(): return lax.ppermute(x, 'narrow', far_pairs)  4.83 us
  transfers between devices with their start and end apart: 59, of which 26 were waited for; matrix products, arithmetic and copies ran while one was open for 0% of the time, Pallas kernels for 10%

profile of v3, /device:TPU:0, one launch (start us, length us, event | category | flops | bytes accessed | tf_op | source)
XLA Modules:
  0.0 146.1 jit_solution(3055056333826629570)
XLA Ops:
  1.1 3.0 %collective-permute-start.1 = (bf16[80,1280]{1,0:T(8,128)(2,1)S(1)}, bf16[80,1280]{1,0:T(8,128)(2,1)S(1)}, u32[]{:S(2)}, u32[]{:S(2)}) collective-permute-start(bf16[80,1280]{1,0:T(8,128)(2,1)S(1)} %get-tuple-element.143.refs_1_), channel_id=1, source_target_pairs={{8,0},{16,8},{24,16},{28,24},{20,28},{12,20},{4,12},{0,4},{9,1},{1... | collective-permute-start | bytes 614408 | tf_op jit(solution)/shard_map/ppermute | solution.py:344
  6.2 1.9 %collective-permute-start.14 = (bf16[2,320,256]{2,1,0:T(8,128)(2,1)S(1)}, bf16[2,320,256]{2,1,0:T(8,128)(2,1)S(1)}, u32[]{:S(2)}, u32[]{:S(2)}) collective-permute-start(bf16[2,320,256]{2,1,0:T(8,128)(2,1)S(1)} %get-tuple-element.89.own.refs_0_), channel_id=1, source_target_pairs={{0,2},{1,3},{2,0},{3,1},{4,6},{5,7},{6,4},{7,5},{8,10},{9,11},{10,... | collective-permute-start | bytes 983048 | tf_op jit(solution)/shard_map/ppermute | solution.py:380
  8.1 1.5 %collective-permute-start.3 = (bf16[80,1280]{1,0:T(8,128)(2,1)S(1)}, bf16[80,1280]{1,0:T(8,128)(2,1)S(1)}, u32[]{:S(2)}, u32[]{:S(2)}) collective-permute-start(bf16[80,1280]{1,0:T(8,128)(2,1)S(1)} %get-tuple-element.144.refs_0_), channel_id=1, source_target_pairs={{8,0},{16,8},{24,16},{28,24},{20,28},{12,20},{4,12},{0,4},{9,1},{1... | collective-permute-start | bytes 614408 | tf_op jit(solution)/shard_map/ppermute | solution.py:344
  10.2 1.5 %collective-permute-start.5 = (bf16[80,1280]{1,0:T(8,128)(2,1)S(1)}, bf16[80,1280]{1,0:T(8,128)(2,1)S(1)}, u32[]{:S(2)}, u32[]{:S(2)}) collective-permute-start(bf16[80,1280]{1,0:T(8,128)(2,1)S(1)} %collective-permute-done.1.refs_3_), channel_id=1, source_target_pairs={{8,0},{16,8},{24,16},{28,24},{20,28},{12,20},{4,12},{0,4},{9,1},{1... | collective-permute-start | bytes 614408 | tf_op jit(solution)/shard_map/ppermute | solution.py:344
  12.2 4.0 %collective-permute-done.3.refs_5_ = bf16[80,1280]{1,0:T(8,128)(2,1)S(1)} collective-permute-done((bf16[80,1280]{1,0:T(8,128)(2,1)S(1)}, bf16[80,1280]{1,0:T(8,128)(2,1)S(1)}, u32[]{:S(2)}, u32[]{:S(2)}) %collective-permute-start.3) | collective-permute-done | bytes 204832 | tf_op jit(solution)/shard_map/ppermute | solution.py:344
  17.6 1.6 %collective-permute-start.7 = (bf16[80,1280]{1,0:T(8,128)(2,1)S(1)}, bf16[80,1280]{1,0:T(8,128)(2,1)S(1)}, u32[]{:S(2)}, u32[]{:S(2)}) collective-permute-start(bf16[80,1280]{1,0:T(8,128)(2,1)S(1)} %collective-permute-done.3.refs_5_), channel_id=1, source_target_pairs={{8,0},{16,8},{24,16},{28,24},{20,28},{12,20},{4,12},{0,4},{9,1},{1... | collective-permute-start | bytes 614408 | tf_op jit(solution)/shard_map/ppermute | solution.py:344
  21.5 1.6 %collective-permute-start.9 = (bf16[80,1280]{1,0:T(8,128)(2,1)S(1)}, bf16[80,1280]{1,0:T(8,128)(2,1)S(1)}, u32[]{:S(2)}, u32[]{:S(2)}) collective-permute-start(bf16[80,1280]{1,0:T(8,128)(2,1)S(1)} %collective-permute-done.5.refs_7_), channel_id=1, source_target_pairs={{8,0},{16,8},{24,16},{28,24},{20,28},{12,20},{4,12},{0,4},{9,1},{1... | collective-permute-start | bytes 614408 | tf_op jit(solution)/shard_map/ppermute | solution.py:344
  23.0 2.2 %collective-permute-done.7.refs_9_ = bf16[80,1280]{1,0:T(8,128)(2,1)S(1)} collective-permute-done((bf16[80,1280]{1,0:T(8,128)(2,1)S(1)}, bf16[80,1280]{1,0:T(8,128)(2,1)S(1)}, u32[]{:S(2)}, u32[]{:S(2)}) %collective-permute-start.7) | collective-permute-done | bytes 204832 | tf_op jit(solution)/shard_map/ppermute | solution.py:344
  26.0 1.8 %collective-permute-done.6.refs_8_ = bf16[80,1280]{1,0:T(8,128)(2,1)S(1)} collective-permute-done((bf16[80,1280]{1,0:T(8,128)(2,1)S(1)}, bf16[80,1280]{1,0:T(8,128)(2,1)S(1)}, u32[]{:S(2)}, u32[]{:S(2)}) %collective-permute-start.6) | collective-permute-done | bytes 204832 | tf_op jit(solution)/shard_map/ppermute | solution.py:343
  27.8 1.7 %collective-permute-start.11 = (bf16[80,1280]{1,0:T(8,128)(2,1)S(1)}, bf16[80,1280]{1,0:T(8,128)(2,1)S(1)}, u32[]{:S(2)}, u32[]{:S(2)}) collective-permute-start(bf16[80,1280]{1,0:T(8,128)(2,1)S(1)} %collective-permute-done.7.refs_9_), channel_id=1, source_target_pairs={{8,0},{16,8},{24,16},{28,24},{20,28},{12,20},{4,12},{0,4},{9,1},{1... | collective-permute-start | bytes 614408 | tf_op jit(solution)/shard_map/ppermute | solution.py:344
  31.6 2.8 %collective-permute-done.11.refs_13_ = bf16[80,1280]{1,0:T(8,128)(2,1)S(1)} collective-permute-done((bf16[80,1280]{1,0:T(8,128)(2,1)S(1)}, bf16[80,1280]{1,0:T(8,128)(2,1)S(1)}, u32[]{:S(2)}, u32[]{:S(2)}) %collective-permute-start.11) | collective-permute-done | bytes 204832 | tf_op jit(solution)/shard_map/ppermute | solution.py:344
  34.4 2.6 %collective-permute-done.10.refs_12_ = bf16[80,1280]{1,0:T(8,128)(2,1)S(1)} collective-permute-done((bf16[80,1280]{1,0:T(8,128)(2,1)S(1)}, bf16[80,1280]{1,0:T(8,128)(2,1)S(1)}, u32[]{:S(2)}, u32[]{:S(2)}) %collective-permute-start.10) | collective-permute-done | bytes 204832 | tf_op jit(solution)/shard_map/ppermute | solution.py:343
  41.0 2.7 %collective-permute-done.22.refs_8_ = bf16[80,1280]{1,0:T(8,128)(2,1)S(1)} collective-permute-done((bf16[80,1280]{1,0:T(8,128)(2,1)S(1)}, bf16[80,1280]{1,0:T(8,128)(2,1)S(1)}, u32[]{:S(2)}, u32[]{:S(2)}) %collective-permute-start.22) | collective-permute-done | bytes 204832 | tf_op jit(solution)/shard_map/ppermute | solution.py:344
  47.0 1.7 %collective-permute-start.20 = (bf16[80,1280]{1,0:T(8,128)(2,1)S(1)}, bf16[80,1280]{1,0:T(8,128)(2,1)S(1)}, u32[]{:S(2)}, u32[]{:S(2)}) collective-permute-start(bf16[80,1280]{1,0:T(8,128)(2,1)S(1)} %get-tuple-element.99.refs_6_), channel_id=1, source_target_pairs={{0,8},{8,16},{16,24},{24,28},{28,20},{20,12},{12,4},{4,0},{1,9},{9... | collective-permute-start | bytes 614408 | tf_op jit(solution)/shard_map/ppermute | solution.py:343
  53.1 2.9 %collective-permute-done.25.refs_12_ = bf16[80,1280]{1,0:T(8,128)(2,1)S(1)} collective-permute-done((bf16[80,1280]{1,0:T(8,128)(2,1)S(1)}, bf16[80,1280]{1,0:T(8,128)(2,1)S(1)}, u32[]{:S(2)}, u32[]{:S(2)}) %collective-permute-start.25) | collective-permute-done | bytes 204832 | tf_op jit(solution)/shard_map/ppermute | solution.py:344
  60.5 1.8 %collective-permute-start.30 = (bf16[80,1280]{1,0:T(8,128)(2,1)S(1)}, bf16[80,1280]{1,0:T(8,128)(2,1)S(1)}, u32[]{:S(2)}, u32[]{:S(2)}) collective-permute-start(bf16[80,1280]{1,0:T(8,128)(2,1)S(1)} %collective-permute-done.29.refs_14_), channel_id=1, source_target_pairs={{8,0},{16,8},{24,16},{28,24},{20,28},{12,20},{4,12},{0,4},{9,1},{1... | collective-permute-start | bytes 614408 | tf_op jit(solution)/shard_map/ppermute | solution.py:344
  62.3 2.6 %collective-permute-done.33.refs_16_ = bf16[80,1280]{1,0:T(8,128)(2,1)S(1)} collective-permute-done((bf16[80,1280]{1,0:T(8,128)(2,1)S(1)}, bf16[80,1280]{1,0:T(8,128)(2,1)S(1)}, u32[]{:S(2)}, u32[]{:S(2)}) %collective-permute-start.33) | collective-permute-done | bytes 204832 | tf_op jit(solution)/shard_map/ppermute | solution.py:344
  69.3 1.8 %collective-permute-start.31 = (bf16[80,1280]{1,0:T(8,128)(2,1)S(1)}, bf16[80,1280]{1,0:T(8,128)(2,1)S(1)}, u32[]{:S(2)}, u32[]{:S(2)}) collective-permute-start(bf16[80,1280]{1,0:T(8,128)(2,1)S(1)} %get-tuple-element.129.refs_1_), channel_id=1, source_target_pairs={{8,0},{16,8},{24,16},{28,24},{20,28},{12,20},{4,12},{0,4},{9,1},{1... | collective-permute-start | bytes 614408 | tf_op jit(solution)/shard_map/ppermute | solution.py:344
  71.0 2.6 %collective-permute-done.35.refs_20_ = bf16[80,1280]{1,0:T(8,128)(2,1)S(1)} collective-permute-done((bf16[80,1280]{1,0:T(8,128)(2,1)S(1)}, bf16[80,1280]{1,0:T(8,128)(2,1)S(1)}, u32[]{:S(2)}, u32[]{:S(2)}) %collective-permute-start.35) | collective-permute-done | bytes 204832 | tf_op jit(solution)/shard_map/ppermute | solution.py:344
  76.4 2.3 %mlp_out.3 = (bf16[320,512]{1,0:T(8,128)(2,1)S(1)}, bf16[320,512]{1,0:T(8,128)(2,1)S(1)}, bf16[320,512]{1,0:T(8,128)(2,1)S(1)}, bf16[320,512]{1,0:T(8,128)(2,1)S(1)}) custom-call(bf16[1024,256]{1,0:T(8,128)(2,1)S(1)} %hidden.5.refs_0_, bf16[1024,256]{1,0:T(8,128)(2,1)S(1)} %hidden.6.refs_1_, bf16[1024,256]{1,0:T(8,128)(2,1)S(1)} %hidden.8.refs_2_, ...), custom_call_target="tpu_custom_call" | custom-call | tf_op jit(solution)/shard_map/mlp_out/pallas_call | solution.py:18
  80.2 1.7 %collective-permute-start.45 = (bf16[80,1280]{1,0:T(8,128)(2,1)S(1)}, bf16[80,1280]{1,0:T(8,128)(2,1)S(1)}, u32[]{:S(2)}, u32[]{:S(2)}) collective-permute-start(bf16[80,1280]{1,0:T(8,128)(2,1)S(1)} %collective-permute-done.31.refs_3_), channel_id=1, source_target_pairs={{8,0},{16,8},{24,16},{28,24},{20,28},{12,20},{4,12},{0,4},{9,1},{1... | collective-permute-start | bytes 614408 | tf_op jit(solution)/shard_map/ppermute | solution.py:344
  81.9 5.3 %collective-permute-done.27.refs_2_ = bf16[80,1280]{1,0:T(8,128)(2,1)S(1)} collective-permute-done((bf16[80,1280]{1,0:T(8,128)(2,1)S(1)}, bf16[80,1280]{1,0:T(8,128)(2,1)S(1)}, u32[]{:S(2)}, u32[]{:S(2)}) %collective-permute-start.27) | collective-permute-done | bytes 204832 | tf_op jit(solution)/shard_map/ppermute | solution.py:343
  87.6 2.2 %mlp_out.2 = (bf16[320,512]{1,0:T(8,128)(2,1)S(1)}, bf16[320,512]{1,0:T(8,128)(2,1)S(1)}, bf16[320,512]{1,0:T(8,128)(2,1)S(1)}, bf16[320,512]{1,0:T(8,128)(2,1)S(1)}) custom-call(bf16[1024,256]{1,0:T(8,128)(2,1)S(1)} %hidden.5.refs_0_, bf16[1024,256]{1,0:T(8,128)(2,1)S(1)} %hidden.6.refs_1_, bf16[1024,256]{1,0:T(8,128)(2,1)S(1)} %hidden.8.refs_2_, ...), custom_call_target="tpu_custom_call" | custom-call | tf_op jit(solution)/shard_map/mlp_out/pallas_call | solution.py:18
  93.7 4.4 %collective-permute-done.44.refs_6_ = bf16[80,1280]{1,0:T(8,128)(2,1)S(1)} collective-permute-done((bf16[80,1280]{1,0:T(8,128)(2,1)S(1)}, bf16[80,1280]{1,0:T(8,128)(2,1)S(1)}, u32[]{:S(2)}, u32[]{:S(2)}) %collective-permute-start.44) | collective-permute-done | bytes 204832 | tf_op jit(solution)/shard_map/ppermute | solution.py:343
  98.9 2.4 %collective-permute-done.46.refs_8_ = bf16[80,1280]{1,0:T(8,128)(2,1)S(1)} collective-permute-done((bf16[80,1280]{1,0:T(8,128)(2,1)S(1)}, bf16[80,1280]{1,0:T(8,128)(2,1)S(1)}, u32[]{:S(2)}, u32[]{:S(2)}) %collective-permute-start.46) | collective-permute-done | bytes 204832 | tf_op jit(solution)/shard_map/ppermute | solution.py:343
  103.7 1.6 %collective-permute-start.50 = (bf16[80,1280]{1,0:T(8,128)(2,1)S(1)}, bf16[80,1280]{1,0:T(8,128)(2,1)S(1)}, u32[]{:S(2)}, u32[]{:S(2)}) collective-permute-start(bf16[80,1280]{1,0:T(8,128)(2,1)S(1)} %collective-permute-done.46.refs_8_), channel_id=1, source_target_pairs={{0,8},{8,16},{16,24},{24,28},{28,20},{20,12},{12,4},{4,0},{1,9},{9... | collective-permute-start | bytes 614408 | tf_op jit(solution)/shard_map/ppermute | solution.py:343
  105.5 3.4 %collective-permute-done.39.refs_6_ = bf16[320,512]{1,0:T(8,128)(2,1)S(1)} collective-permute-done((bf16[320,512]{1,0:T(8,128)(2,1)S(1)}, bf16[320,512]{1,0:T(8,128)(2,1)S(1)}, u32[]{:S(2)}, u32[]{:S(2)}) %collective-permute-start.39) | collective-permute-done | bytes 327712 | tf_op jit(solution)/shard_map/ppermute | solution.py:380
  109.3 2.2 %collective-permute-done.51.refs_13_ = bf16[80,1280]{1,0:T(8,128)(2,1)S(1)} collective-permute-done((bf16[80,1280]{1,0:T(8,128)(2,1)S(1)}, bf16[80,1280]{1,0:T(8,128)(2,1)S(1)}, u32[]{:S(2)}, u32[]{:S(2)}) %collective-permute-start.51) | collective-permute-done | bytes 204832 | tf_op jit(solution)/shard_map/ppermute | solution.py:344
  114.5 1.7 %collective-permute-start.54 = (bf16[80,1280]{1,0:T(8,128)(2,1)S(1)}, bf16[80,1280]{1,0:T(8,128)(2,1)S(1)}, u32[]{:S(2)}, u32[]{:S(2)}) collective-permute-start(bf16[80,1280]{1,0:T(8,128)(2,1)S(1)} %collective-permute-done.48.refs_10_), channel_id=1, source_target_pairs={{0,8},{8,16},{16,24},{24,28},{28,20},{20,12},{12,4},{4,0},{1,9},{9... | collective-permute-start | bytes 614408 | tf_op jit(solution)/shard_map/ppermute | solution.py:343
  116.7 4.8 %collective-permute-done.55.second = bf16[80,1280]{1,0:T(8,128)(2,1)S(1)} collective-permute-done((bf16[80,1280]{1,0:T(8,128)(2,1)S(1)}, bf16[80,1280]{1,0:T(8,128)(2,1)S(1)}, u32[]{:S(2)}, u32[]{:S(2)}) %collective-permute-start.55) | collective-permute-done | bytes 204832 | tf_op jit(solution)/shard_map/ppermute | solution.py:344
  123.4 3.5 %collective-permute-start.58 = (bf16[160,256]{1,0:T(8,128)(2,1)S(1)}, bf16[160,256]{1,0:T(8,128)(2,1)S(1)}, u32[]{:S(2)}, u32[]{:S(2)}) collective-permute-start(bf16[160,256]{1,0:T(8,128)(2,1)S(1)} %proj_last.1.refs_0_), channel_id=1, source_target_pairs={{0,3},{4,7},{9,10},{13,14},{18,17},{22,21},{27,24},{31,28}} | collective-permute-start | bytes 245768 | tf_op jit(solution)/shard_map/ppermute | solution.py:588
  129.4 15.3 %all_to_all.5.arrived = bf16[8,160,128]{2,1,0:T(8,128)(2,1)S(1)} all-to-all(bf16[8,160,128]{2,1,0:T(8,128)(2,1)S(1)} %pack.1), channel_id=1, replica_groups=mesh['wide'=8,'narrow'=4] {'wide'}, dimensions={0} | all-to-all | bytes 655360 | tf_op jit(solution)/shard_map/all_to_all | solution.py:454
  (136 shorter events, 52.3 us)
Async XLA Ops:
  1.1 9.1 %collective-permute-start.1 = (bf16[80,1280]{1,0:T(8,128)(2,1)S(1)}, bf16[80,1280]{1,0:T(8,128)(2,1)S(1)}, u32[]{:S(2)}, u32[]{:S(2)}) collective-permute-start(bf16[80,1280]{1,0:T(8,128)(2,1)S(1)} %get-tuple-element.143.refs_1_), channel_id=1, source_target_pairs={{8,0},{16,8},{24,16},{28,24},{20,28},{12,20},{4,12},{0,4},{9,1},{1... | collective-permute-start | bytes 614408 | tf_op jit(solution)/shard_map/ppermute | solution.py:344
  6.2 14.1 %collective-permute-start.14 = (bf16[2,320,256]{2,1,0:T(8,128)(2,1)S(1)}, bf16[2,320,256]{2,1,0:T(8,128)(2,1)S(1)}, u32[]{:S(2)}, u32[]{:S(2)}) collective-permute-start(bf16[2,320,256]{2,1,0:T(8,128)(2,1)S(1)} %get-tuple-element.89.own.refs_0_), channel_id=1, source_target_pairs={{0,2},{1,3},{2,0},{3,1},{4,6},{5,7},{6,4},{7,5},{8,10},{9,11},{10,... | collective-permute-start | bytes 983048 | tf_op jit(solution)/shard_map/ppermute | solution.py:380
  10.2 10.6 %collective-permute-start.5 = (bf16[80,1280]{1,0:T(8,128)(2,1)S(1)}, bf16[80,1280]{1,0:T(8,128)(2,1)S(1)}, u32[]{:S(2)}, u32[]{:S(2)}) collective-permute-start(bf16[80,1280]{1,0:T(8,128)(2,1)S(1)} %collective-permute-done.1.refs_3_), channel_id=1, source_target_pairs={{8,0},{16,8},{24,16},{28,24},{20,28},{12,20},{4,12},{0,4},{9,1},{1... | collective-permute-start | bytes 614408 | tf_op jit(solution)/shard_map/ppermute | solution.py:344
  11.7 9.8 %collective-permute-start.4 = (bf16[80,1280]{1,0:T(8,128)(2,1)S(1)}, bf16[80,1280]{1,0:T(8,128)(2,1)S(1)}, u32[]{:S(2)}, u32[]{:S(2)}) collective-permute-start(bf16[80,1280]{1,0:T(8,128)(2,1)S(1)} %collective-permute-done.refs_2_), channel_id=1, source_target_pairs={{0,8},{8,16},{16,24},{24,28},{28,20},{20,12},{12,4},{4,0},{1,9},{9... | collective-permute-start | bytes 614408 | tf_op jit(solution)/shard_map/ppermute | solution.py:343
  16.2 13.4 %collective-permute-start.15 = (bf16[2,320,256]{2,1,0:T(8,128)(2,1)S(1)}, bf16[2,320,256]{2,1,0:T(8,128)(2,1)S(1)}, u32[]{:S(2)}, u32[]{:S(2)}) collective-permute-start(bf16[2,320,256]{2,1,0:T(8,128)(2,1)S(1)} %get-tuple-element.89.own.refs_0_), channel_id=1, source_target_pairs={{0,1},{1,0},{2,3},{3,2},{4,5},{5,4},{6,7},{7,6},{8,9},{9,8},{10,11... | collective-permute-start | bytes 983048 | tf_op jit(solution)/shard_map/ppermute | solution.py:377
  20.8 9.6 %collective-permute-start.17 = (bf16[2,320,256]{2,1,0:T(8,128)(2,1)S(1)}, bf16[2,320,256]{2,1,0:T(8,128)(2,1)S(1)}, u32[]{:S(2)}, u32[]{:S(2)}) collective-permute-start(bf16[2,320,256]{2,1,0:T(8,128)(2,1)S(1)} %get-tuple-element.93.own.refs_1_), channel_id=1, source_target_pairs={{0,2},{1,3},{2,0},{3,1},{4,6},{5,7},{6,4},{7,5},{8,10},{9,11},{10,... | collective-permute-start | bytes 983048 | tf_op jit(solution)/shard_map/ppermute | solution.py:380
  29.5 9.0 %collective-permute-start.16 = (bf16[2,320,256]{2,1,0:T(8,128)(2,1)S(1)}, bf16[2,320,256]{2,1,0:T(8,128)(2,1)S(1)}, u32[]{:S(2)}, u32[]{:S(2)}) collective-permute-start(bf16[2,320,256]{2,1,0:T(8,128)(2,1)S(1)} %collective-permute-done.14.over_x), channel_id=1, source_target_pairs={{0,1},{1,0},{2,3},{3,2},{4,5},{5,4},{6,7},{7,6},{8,9},{9,8},{10,11... | collective-permute-start | bytes 983048 | tf_op jit(solution)/shard_map/ppermute | solution.py:377
  30.4 10.2 %collective-permute-start.13 = (bf16[80,1280]{1,0:T(8,128)(2,1)S(1)}, bf16[80,1280]{1,0:T(8,128)(2,1)S(1)}, u32[]{:S(2)}, u32[]{:S(2)}) collective-permute-start(bf16[80,1280]{1,0:T(8,128)(2,1)S(1)} %collective-permute-done.9.refs_11_), channel_id=1, source_target_pairs={{8,0},{16,8},{24,16},{28,24},{20,28},{12,20},{4,12},{0,4},{9,1},{1... | collective-permute-start | bytes 614408 | tf_op jit(solution)/shard_map/ppermute | solution.py:344
  31.6 13.5 %collective-permute-start.18 = (bf16[2,320,256]{2,1,0:T(8,128)(2,1)S(1)}, bf16[2,320,256]{2,1,0:T(8,128)(2,1)S(1)}, u32[]{:S(2)}, u32[]{:S(2)}) collective-permute-start(bf16[2,320,256]{2,1,0:T(8,128)(2,1)S(1)} %get-tuple-element.93.own.refs_1_), channel_id=1, source_target_pairs={{0,1},{1,0},{2,3},{3,2},{4,5},{5,4},{6,7},{7,6},{8,9},{9,8},{10,11... | collective-permute-start | bytes 983048 | tf_op jit(solution)/shard_map/ppermute | solution.py:377
  34.4 11.1 %collective-permute-start.19 = (bf16[2,320,256]{2,1,0:T(8,128)(2,1)S(1)}, bf16[2,320,256]{2,1,0:T(8,128)(2,1)S(1)}, u32[]{:S(2)}, u32[]{:S(2)}) collective-permute-start(bf16[2,320,256]{2,1,0:T(8,128)(2,1)S(1)} %collective-permute-done.17.over_x), channel_id=1, source_target_pairs={{0,1},{1,0},{2,3},{3,2},{4,5},{5,4},{6,7},{7,6},{8,9},{9,8},{10,11... | collective-permute-start | bytes 983048 | tf_op jit(solution)/shard_map/ppermute | solution.py:377
  40.6 10.3 %collective-permute-start.21 = (bf16[80,1280]{1,0:T(8,128)(2,1)S(1)}, bf16[80,1280]{1,0:T(8,128)(2,1)S(1)}, u32[]{:S(2)}, u32[]{:S(2)}) collective-permute-start(bf16[80,1280]{1,0:T(8,128)(2,1)S(1)} %get-tuple-element.108.refs_5_), channel_id=1, source_target_pairs={{0,8},{8,16},{16,24},{24,28},{28,20},{20,12},{12,4},{4,0},{1,9},{9... | collective-permute-start | bytes 614408 | tf_op jit(solution)/shard_map/ppermute | solution.py:343
  45.1 11.0 %collective-permute-start.25 = (bf16[80,1280]{1,0:T(8,128)(2,1)S(1)}, bf16[80,1280]{1,0:T(8,128)(2,1)S(1)}, u32[]{:S(2)}, u32[]{:S(2)}) collective-permute-start(bf16[80,1280]{1,0:T(8,128)(2,1)S(1)} %collective-permute-done.22.refs_8_), channel_id=1, source_target_pairs={{8,0},{16,8},{24,16},{28,24},{20,28},{12,20},{4,12},{0,4},{9,1},{1... | collective-permute-start | bytes 614408 | tf_op jit(solution)/shard_map/ppermute | solution.py:344
  47.0 11.6 %collective-permute-start.20 = (bf16[80,1280]{1,0:T(8,128)(2,1)S(1)}, bf16[80,1280]{1,0:T(8,128)(2,1)S(1)}, u32[]{:S(2)}, u32[]{:S(2)}) collective-permute-start(bf16[80,1280]{1,0:T(8,128)(2,1)S(1)} %get-tuple-element.99.refs_6_), channel_id=1, source_target_pairs={{0,8},{8,16},{16,24},{24,28},{28,20},{20,12},{12,4},{4,0},{1,9},{9... | collective-permute-start | bytes 614408 | tf_op jit(solution)/shard_map/ppermute | solution.py:343
  50.9 9.3 %collective-permute-start.24 = (bf16[80,1280]{1,0:T(8,128)(2,1)S(1)}, bf16[80,1280]{1,0:T(8,128)(2,1)S(1)}, u32[]{:S(2)}, u32[]{:S(2)}) collective-permute-start(bf16[80,1280]{1,0:T(8,128)(2,1)S(1)} %collective-permute-done.21.refs_7_), channel_id=1, source_target_pairs={{0,8},{8,16},{16,24},{24,28},{28,20},{20,12},{12,4},{4,0},{1,9},{9... | collective-permute-start | bytes 614408 | tf_op jit(solution)/shard_map/ppermute | solution.py:343
  51.7 8.8 %collective-permute-start.29 = (bf16[80,1280]{1,0:T(8,128)(2,1)S(1)}, bf16[80,1280]{1,0:T(8,128)(2,1)S(1)}, u32[]{:S(2)}, u32[]{:S(2)}) collective-permute-start(bf16[80,1280]{1,0:T(8,128)(2,1)S(1)} %collective-permute-done.28.refs_10_), channel_id=1, source_target_pairs={{8,0},{16,8},{24,16},{28,24},{20,28},{12,20},{4,12},{0,4},{9,1},{1... | collective-permute-start | bytes 614408 | tf_op jit(solution)/shard_map/ppermute | solution.py:344
  56.1 8.8 %collective-permute-start.33 = (bf16[80,1280]{1,0:T(8,128)(2,1)S(1)}, bf16[80,1280]{1,0:T(8,128)(2,1)S(1)}, u32[]{:S(2)}, u32[]{:S(2)}) collective-permute-start(bf16[80,1280]{1,0:T(8,128)(2,1)S(1)} %collective-permute-done.25.refs_12_), channel_id=1, source_target_pairs={{8,0},{16,8},{24,16},{28,24},{20,28},{12,20},{4,12},{0,4},{9,1},{1... | collective-permute-start | bytes 614408 | tf_op jit(solution)/shard_map/ppermute | solution.py:344
  58.5 8.8 %collective-permute-start.23 = (bf16[80,1280]{1,0:T(8,128)(2,1)S(1)}, bf16[80,1280]{1,0:T(8,128)(2,1)S(1)}, u32[]{:S(2)}, u32[]{:S(2)}) collective-permute-start(bf16[80,1280]{1,0:T(8,128)(2,1)S(1)} %collective-permute-done.20.refs_9_), channel_id=1, source_target_pairs={{0,8},{8,16},{16,24},{24,28},{28,20},{20,12},{12,4},{4,0},{1,9},{9... | collective-permute-start | bytes 614408 | tf_op jit(solution)/shard_map/ppermute | solution.py:343
  60.5 8.8 %collective-permute-start.30 = (bf16[80,1280]{1,0:T(8,128)(2,1)S(1)}, bf16[80,1280]{1,0:T(8,128)(2,1)S(1)}, u32[]{:S(2)}, u32[]{:S(2)}) collective-permute-start(bf16[80,1280]{1,0:T(8,128)(2,1)S(1)} %collective-permute-done.29.refs_14_), channel_id=1, source_target_pairs={{8,0},{16,8},{24,16},{28,24},{20,28},{12,20},{4,12},{0,4},{9,1},{1... | collective-permute-start | bytes 614408 | tf_op jit(solution)/shard_map/ppermute | solution.py:344
  64.9 8.8 %collective-permute-start.35 = (bf16[80,1280]{1,0:T(8,128)(2,1)S(1)}, bf16[80,1280]{1,0:T(8,128)(2,1)S(1)}, u32[]{:S(2)}, u32[]{:S(2)}) collective-permute-start(bf16[80,1280]{1,0:T(8,128)(2,1)S(1)} %collective-permute-done.33.refs_16_), channel_id=1, source_target_pairs={{8,0},{16,8},{24,16},{28,24},{20,28},{12,20},{4,12},{0,4},{9,1},{1... | collective-permute-start | bytes 614408 | tf_op jit(solution)/shard_map/ppermute | solution.py:344
  69.3 10.6 %collective-permute-start.31 = (bf16[80,1280]{1,0:T(8,128)(2,1)S(1)}, bf16[80,1280]{1,0:T(8,128)(2,1)S(1)}, u32[]{:S(2)}, u32[]{:S(2)}) collective-permute-start(bf16[80,1280]{1,0:T(8,128)(2,1)S(1)} %get-tuple-element.129.refs_1_), channel_id=1, source_target_pairs={{8,0},{16,8},{24,16},{28,24},{20,28},{12,20},{4,12},{0,4},{9,1},{1... | collective-permute-start | bytes 614408 | tf_op jit(solution)/shard_map/ppermute | solution.py:344
  78.7 12.9 %collective-permute-start.40 = (bf16[320,512]{1,0:T(8,128)(2,1)S(1)}, bf16[320,512]{1,0:T(8,128)(2,1)S(1)}, u32[]{:S(2)}, u32[]{:S(2)}) collective-permute-start(bf16[320,512]{1,0:T(8,128)(2,1)S(1)} %get-tuple-element.128), channel_id=1, source_target_pairs={{0,1},{1,0},{2,3},{3,2},{4,5},{5,4},{6,7},{7,6},{8,9},{9,8},{10,11... | collective-permute-start | bytes 983048 | tf_op jit(solution)/shard_map/ppermute | solution.py:377
  78.7 13.4 %collective-permute-start.38 = (bf16[320,512]{1,0:T(8,128)(2,1)S(1)}, bf16[320,512]{1,0:T(8,128)(2,1)S(1)}, u32[]{:S(2)}, u32[]{:S(2)}) collective-permute-start(bf16[320,512]{1,0:T(8,128)(2,1)S(1)} %get-tuple-element.125), channel_id=1, source_target_pairs={{0,1},{1,0},{2,3},{3,2},{4,5},{5,4},{6,7},{7,6},{8,9},{9,8},{10,11... | collective-permute-start | bytes 983048 | tf_op jit(solution)/shard_map/ppermute | solution.py:377
  79.9 10.8 %collective-permute-start.42 = (bf16[80,1280]{1,0:T(8,128)(2,1)S(1)}, bf16[80,1280]{1,0:T(8,128)(2,1)S(1)}, u32[]{:S(2)}, u32[]{:S(2)}) collective-permute-start(bf16[80,1280]{1,0:T(8,128)(2,1)S(1)} %get-tuple-element.129.refs_1_), channel_id=1, source_target_pairs={{0,8},{8,16},{16,24},{24,28},{28,20},{20,12},{12,4},{4,0},{1,9},{9... | collective-permute-start | bytes 614408 | tf_op jit(solution)/shard_map/ppermute | solution.py:343
  80.2 11.3 %collective-permute-start.45 = (bf16[80,1280]{1,0:T(8,128)(2,1)S(1)}, bf16[80,1280]{1,0:T(8,128)(2,1)S(1)}, u32[]{:S(2)}, u32[]{:S(2)}) collective-permute-start(bf16[80,1280]{1,0:T(8,128)(2,1)S(1)} %collective-permute-done.31.refs_3_), channel_id=1, source_target_pairs={{8,0},{16,8},{24,16},{28,24},{20,28},{12,20},{4,12},{0,4},{9,1},{1... | collective-permute-start | bytes 614408 | tf_op jit(solution)/shard_map/ppermute | solution.py:344
  91.5 10.2 %collective-permute-start.36 = (bf16[320,512]{1,0:T(8,128)(2,1)S(1)}, bf16[320,512]{1,0:T(8,128)(2,1)S(1)}, u32[]{:S(2)}, u32[]{:S(2)}) collective-permute-start(bf16[320,512]{1,0:T(8,128)(2,1)S(1)} %get-tuple-element.121), channel_id=1, source_target_pairs={{0,1},{1,0},{2,3},{3,2},{4,5},{5,4},{6,7},{7,6},{8,9},{9,8},{10,11... | collective-permute-start | bytes 983048 | tf_op jit(solution)/shard_map/ppermute | solution.py:377
  91.5 10.8 %collective-permute-start.37 = (bf16[320,512]{1,0:T(8,128)(2,1)S(1)}, bf16[320,512]{1,0:T(8,128)(2,1)S(1)}, u32[]{:S(2)}, u32[]{:S(2)}) collective-permute-start(bf16[320,512]{1,0:T(8,128)(2,1)S(1)} %get-tuple-element.122), channel_id=1, source_target_pairs={{0,1},{1,0},{2,3},{3,2},{4,5},{5,4},{6,7},{7,6},{8,9},{9,8},{10,11... | collective-permute-start | bytes 983048 | tf_op jit(solution)/shard_map/ppermute | solution.py:377
  92.1 11.6 %collective-permute-start.41 = (bf16[320,512]{1,0:T(8,128)(2,1)S(1)}, bf16[320,512]{1,0:T(8,128)(2,1)S(1)}, u32[]{:S(2)}, u32[]{:S(2)}) collective-permute-start(bf16[320,512]{1,0:T(8,128)(2,1)S(1)} %add.4), channel_id=1, source_target_pairs={{0,2},{1,3},{2,0},{3,1},{4,6},{5,7},{6,4},{7,5},{8,10},{9,11},{10,... | collective-permute-start | bytes 983048 | tf_op jit(solution)/shard_map/ppermute | solution.py:380
  98.1 10.7 %collective-permute-start.39 = (bf16[320,512]{1,0:T(8,128)(2,1)S(1)}, bf16[320,512]{1,0:T(8,128)(2,1)S(1)}, u32[]{:S(2)}, u32[]{:S(2)}) collective-permute-start(bf16[320,512]{1,0:T(8,128)(2,1)S(1)} %add.3), channel_id=1, source_target_pairs={{0,2},{1,3},{2,0},{3,1},{4,6},{5,7},{6,4},{7,5},{8,10},{9,11},{10,... | collective-permute-start | bytes 983048 | tf_op jit(solution)/shard_map/ppermute | solution.py:380
  101.7 9.8 %collective-permute-start.51 = (bf16[80,1280]{1,0:T(8,128)(2,1)S(1)}, bf16[80,1280]{1,0:T(8,128)(2,1)S(1)}, u32[]{:S(2)}, u32[]{:S(2)}) collective-permute-start(bf16[80,1280]{1,0:T(8,128)(2,1)S(1)} %collective-permute-done.47.refs_9_), channel_id=1, source_target_pairs={{8,0},{16,8},{24,16},{28,24},{20,28},{12,20},{4,12},{0,4},{9,1},{1... | collective-permute-start | bytes 614408 | tf_op jit(solution)/shard_map/ppermute | solution.py:344
  102.3 9.2 %collective-permute-start.48 = (bf16[80,1280]{1,0:T(8,128)(2,1)S(1)}, bf16[80,1280]{1,0:T(8,128)(2,1)S(1)}, u32[]{:S(2)}, u32[]{:S(2)}) collective-permute-start(bf16[80,1280]{1,0:T(8,128)(2,1)S(1)} %collective-permute-done.44.refs_6_), channel_id=1, source_target_pairs={{0,8},{8,16},{16,24},{24,28},{28,20},{20,12},{12,4},{4,0},{1,9},{9... | collective-permute-start | bytes 614408 | tf_op jit(solution)/shard_map/ppermute | solution.py:343
  103.7 8.9 %collective-permute-start.50 = (bf16[80,1280]{1,0:T(8,128)(2,1)S(1)}, bf16[80,1280]{1,0:T(8,128)(2,1)S(1)}, u32[]{:S(2)}, u32[]{:S(2)}) collective-permute-start(bf16[80,1280]{1,0:T(8,128)(2,1)S(1)} %collective-permute-done.46.refs_8_), channel_id=1, source_target_pairs={{0,8},{8,16},{16,24},{24,28},{28,20},{20,12},{12,4},{4,0},{1,9},{9... | collective-permute-start | bytes 614408 | tf_op jit(solution)/shard_map/ppermute | solution.py:343
  116.2 12.7 %collective-permute-start.53 = (bf16[320,256]{1,0:T(8,128)(2,1)S(1)}, bf16[320,256]{1,0:T(8,128)(2,1)S(1)}, u32[]{:S(2)}, u32[]{:S(2)}) collective-permute-start(bf16[320,256]{1,0:T(8,128)(2,1)S(1)} %add.5), channel_id=1, source_target_pairs={{0,2},{1,3},{2,0},{3,1},{4,6},{5,7},{6,4},{7,5},{8,10},{9,11},{10,... | collective-permute-start | bytes 491528 | tf_op jit(solution)/shard_map/ppermute | solution.py:380
  (37 other events, 359.3 us)

commit v4 on v3

--- a/solution.py
+++ b/solution.py
@@ -10,6 +10,7 @@
 F32 = jnp.float32
 BF16 = jnp.bfloat16
 WINDOW = 4
+LATE = (1, 2, 3)
 VMEM = pl.BlockSpec(memory_space=pltpu.VMEM)
 
 
@@ -199,17 +200,13 @@
         give[c][:, at : at + step] = total[block:]
 
 
-def proj_kernel(pieces, missing, count, shard_rows, merged, *refs):
+def proj_kernel(pieces, count, shard_rows, merged, *refs):
     sources, (keep, give, part) = refs[:-3], refs[-3:]
     block = keep.shape[1]
     for p in pieces:
         x, core, inside = p.block_row(count, shard_rows, block)
         at = rows_at(core * 2 * block + x * block + inside, p.rows)
         part[at, :] = sources[p.array][p.start : p.start + p.rows, :]
-    if missing is not None:
-        x, core, inside = missing.block_row(count, shard_rows, block)
-        at = rows_at(core * 2 * block + x * block + inside, missing.rows)
-        part[at, :] = jnp.zeros((missing.rows, part.shape[1]), BF16)
     for core, target in ((1, give), (0, keep)):
         v = jnp.dot(
             part[core * 2 * block : (core + 1) * 2 * block, :],
@@ -220,23 +217,17 @@
         target[1] = v[block:]
 
 
-def last_kernel(first, second, merged, o_ref):
-    rows = first.shape[0]
-    whole = jnp.concatenate([first[...], second[...]], axis=0)
-    o_ref[...] = jnp.dot(whole, merged[...], preferred_element_type=F32).astype(BF16)
-
-
 def stream_kernel(chunks, bias, *refs):
     o_ref = refs[-1]
-    own, keep, near, far = (refs[i * chunks : (i + 1) * chunks] for i in range(4))
+    own = refs[:chunks]
+    keep, near, far = (
+        refs[chunks + i * WINDOW : chunks + (i + 1) * WINDOW] for i in range(3)
+    )
     each, rows, windows = own[0].shape
-    for c in range(chunks):
-        total = keep[c][...].astype(F32) + near[c][...].astype(F32) + far[c][...].astype(F32)
-        total = total + bias[...]
-        for j in range(each):
-            v = own[c][j].astype(F32) + total[:, j * windows : (j + 1) * windows]
-            p = c * each + j
-            o_ref[p * rows : (p + 1) * rows, :] = v.astype(BF16)
+    for p in range(WINDOW):
+        total = keep[p][...].astype(F32) + near[p][...].astype(F32) + far[p][...].astype(F32)
+        v = own[p // each][p % each].astype(F32) + (total + bias[...])
+        o_ref[p * rows : (p + 1) * rows, :] = v.astype(BF16)
 
 
 LANES = 128
@@ -247,21 +238,9 @@
     return rest > 0 and LANES % rest == 0 and bucket % (16 * (LANES // rest)) == 0
 
 
-def pack_kernel(missing, count, shard_rows, groups, extra, slots_of, keep, near, far, bias, *refs):
-    late, o_ref, total = refs[:extra], refs[-2], refs[-1]
-    total[...] = keep[0].astype(F32) + near[0].astype(F32) + far[...].astype(F32)
-    if extra:
-        x, core, inside = missing.block_row(count, shard_rows, total.shape[0])
-
-        @pl.when(x + core == 0)
-        def _():
-            at = pl.ds(pl.multiple_of(inside, 16), missing.rows)
-            added = late[0][...].astype(F32)
-            for r in late[1:]:
-                added = added + r[...].astype(F32)
-            total[at, :] = total[at, :] + added
-
-    vision = (total[...] + bias[...]).astype(BF16)
+def pack_kernel(groups, slots_of, keep, near, far, bias, o_ref):
+    total = keep[0].astype(F32) + near[0].astype(F32) + far[...].astype(F32)
+    vision = (total + bias[...]).astype(BF16)
     width = vision.shape[0]
     bucket = o_ref.shape[1] * o_ref.shape[2] // width
     slot = lax.broadcasted_iota(jnp.int32, (groups * bucket, vision.shape[1]), 0)
@@ -337,8 +316,9 @@
         t = len(self.done)
         waits = [x for at, x in self.work if at == t - 2]
         if t >= 2:
-            to_right = after(to_right, self.done[t - 2][0], *waits)
-            to_left = after(to_left, self.done[t - 2][1])
+            before = [self.done[t - 3][1]] if t >= 3 else []
+            to_right = after(to_right, self.done[t - 2][0], *before, *waits)
+            to_left = after(to_left, *self.done[t - 2])
         pair = (
             lax.ppermute(to_right, "wide", self.right),
             lax.ppermute(to_left, "wide", self.left),
@@ -353,6 +333,9 @@
 
     def add_work(self, x):
         self.work.append((len(self.done) - 1, x))
+
+    def add_late(self, x, steps):
+        self.work.append((len(self.done) - 1 + steps, x))
 
 
 def per_device(
@@ -416,12 +399,12 @@
     def mlp_out(pieces, arrays, hiddens, over_x):
         outs = call(
             functools.partial(
-                out_kernel, pieces, groups, shard_rows[1], over_x, len(hiddens), chunks
+                out_kernel, pieces, groups, shard_rows[1], over_x, len(hiddens), WINDOW
             ),
-            (*hiddens, *arrays), [shape(width, tokens // chunks)] * (2 * chunks),
+            (*hiddens, *arrays), [shape(width, windows)] * (2 * WINDOW),
             scratch=[pltpu.VMEM((2 * width, ff), BF16)], name="mlp_out",
         )
-        return outs[:chunks], outs[chunks:]
+        return outs[:WINDOW], outs[WINDOW:]
 
     def add(keep, other):
         return call(add_kernel, (keep, other), shape(*keep.shape), name="add")
@@ -433,21 +416,21 @@
             shape(WINDOW * width, windows), name="stream",
         )
 
-    def proj(pieces, missing, arrays, merged):
-        return call(
-            functools.partial(proj_kernel, pieces, missing, groups, shard_rows[2]),
+    def proj(pieces, arrays, merged):
+        return call(
+            functools.partial(proj_kernel, pieces, groups, shard_rows[2]),
             (merged, *arrays), [shape(2, width, windows)] * 2,
             scratch=[pltpu.VMEM((full, WINDOW * width), BF16)], name="proj",
         )
 
-    def pack(slots_of, missing, keep, core_sums, x_sums, late):
+    def pack(slots_of, keep, core_sums, x_sums):
         block = (bucket, width)
         if compact(width, bucket):
             block = (bucket * width // LANES, LANES)
         return call(
-            functools.partial(pack_kernel, missing, groups, shard_rows[2], groups, len(late)),
-            (slots_of, keep, core_sums, x_sums, b_proj[:, None], *late), shape(groups, *block),
-            scratch=[pltpu.VMEM((width, windows), F32)], name="pack",
+            functools.partial(pack_kernel, groups),
+            (slots_of, keep, core_sums, x_sums, b_proj[:, None]), shape(groups, *block),
+            name="pack",
         )
 
     def exchange_and_place(buffer, targets):
@@ -470,10 +453,10 @@
         x_sums = [far(add(k, near(g))) for k, g in zip(keep_x, give_x)]
         merged = stream(own, keep, [near(g) for g in give], x_sums)
         slots_of, targets = route()
-        keep, give = proj(pieces, None, wholes[2:], merged)
+        keep, give = proj(pieces, wholes[2:], merged)
         core_sums = near(give)
         x_sums = far(add(keep[1], core_sums[1]))
-        return exchange_and_place(pack(slots_of, None, keep, core_sums, x_sums, ()), targets)
+        return exchange_and_place(pack(slots_of, keep, core_sums, x_sums), targets)
 
 
     ring = Ring(groups)
@@ -559,6 +542,8 @@
         core = [ring.now(got["core", 1][0]), *got["core", 1][1:]]
         sums = [add(k, c) for k, c in zip(got["keep", 1], core)]
         got["x_sums"] = [far(x) for x in sums]
+        for i, x in enumerate(got["x_sums"][:-1]):
+            ring.add_late(x, LATE[i])
         ring.add_work(sums[0])
         start_out(0)
 
@@ -567,28 +552,10 @@
     )
 
     merged = stream(own, got["keep", 0], got["core", 0], got["x_sums"])
-    missing = Piece(0, 0, shard_rows[2], last, 0)
-    keep, give = proj(pieces_proj[:-2], missing, arrays_proj[:-2], merged)
+    keep, give = proj(pieces_proj, arrays_proj, merged)
     core_sums = near(give)
     x_sums = far(add(keep[1], core_sums[1]))
-
-    halves = sorted(pieces_proj[-2:], key=lambda p: p.base)
-    late = call(
-        last_kernel, (*[arrays_proj[p.array] for p in halves], merged),
-        shape(shard_rows[2], windows), name="proj_last",
-    )
-    order_of = ring_order(groups)
-    keeper = [
-        order_of[(order_of.index(w) + last) % groups] * shard_rows[2] // width
-        for w in range(groups)
-    ]
-    lates = [late]
-    for flip in range(1, parts):
-        pairs = [(w * parts + (keeper[w] ^ flip), w * parts + keeper[w]) for w in range(groups)]
-        lates.append(lax.ppermute(late, ("wide", "narrow"), pairs))
-
-    buffer = pack(got["slots_of"], missing, keep, core_sums, x_sums, lates)
-    return exchange_and_place(buffer, got["targets"])
+    return exchange_and_place(pack(got["slots_of"], keep, core_sums, x_sums), got["targets"])
 
 
 def solution(mesh):

time: 146 us -> 139 us (0.952)
  waiting for transfers between devices: 55.8 us -> 51.1 us
  starting transfers between devices: 53.4 us -> 51.4 us
    ppermute x21, waiting for transfers between devices: 28.4 us -> 7.31 us  [step(): lax.ppermute(to_left, 'wide', self.left)]
    ppermute x21, waiting for transfers between devices: 22.4 us -> 30.2 us  [step(): lax.ppermute(to_right, 'wide', self.right)]
    ppermute x5 -> x7, waiting for transfers between devices: 3.43 us -> 10 us  [far(): return lax.ppermute(x, 'narrow', far_pairs)]
    ppermute x3 -> x0, starting transfers between devices: 4.99 us -> none  [per_device(): lates.append(lax.ppermute(late, ('wide', 'narrow'), pairs))]
    ppermute x21, starting transfers between devices: 14.1 us -> 10.4 us  [step(): lax.ppermute(to_right, 'wide', self.right)]
    ppermute x5 -> x7, starting transfers between devices: 4.83 us -> 8.47 us  [far(): return lax.ppermute(x, 'narrow', far_pairs)]
    ppermute x9 -> x13, waiting for transfers between devices: 0.02 us -> 3.6 us  [near(): return lax.ppermute(x, 'narrow', near_pairs)]
    ppermute x21, starting transfers between devices: 28.3 us -> 31.7 us  [step(): lax.ppermute(to_left, 'wide', self.left)]
  transfers between devices with their start and end apart: 59 -> 62, of which waited for: 26 -> 37; matrix products, arithmetic and copies ran while one was open for 0% -> 0% of each run, Pallas kernels for 10% -> 10%
where the time goes in v4:
time: 139 us
  starting transfers between devices  51.4 us (37%)
  waiting for transfers between devices  51.1 us (37%)
  Pallas kernels  17.2 us (12%)
  blocking collectives  15.1 us (11%)
  local copies, waits for them, and re-layouts  3.47 us (2%)
    ppermute x21, starting transfers between devices, step(): lax.ppermute(to_left, 'wide', self.left)  31.7 us
    ppermute x21, waiting for transfers between devices, step(): lax.ppermute(to_right, 'wide', self.right)  30.2 us
    pallas_call x21, Pallas kernels, call(): pl.pallas_call(kernel, out_shape=outs, in_specs=[VMEM] * len(operands), o...  17.2 us
    all_to_all x1, blocking collectives, exchange_and_place(): lax.all_to_all(buffer, 'wide', split_axis=0, concat_axis=0, tiled=True)  15.1 us
    ppermute x21, starting transfers between devices, step(): lax.ppermute(to_right, 'wide', self.right)  10.4 us
    ppermute x7, waiting for transfers between devices, far(): return lax.ppermute(x, 'narrow', far_pairs)  10 us
    ppermute x7, starting transfers between devices, far(): return lax.ppermute(x, 'narrow', far_pairs)  8.47 us
    ppermute x21, waiting for transfers between devices, step(): lax.ppermute(to_left, 'wide', self.left)  7.31 us
  transfers between devices with their start and end apart: 62, of which 37 were waited for; matrix products, arithmetic and copies ran while one was open for 0% of the time, Pallas kernels for 10%

profile of v4, /device:TPU:0, one launch (start us, length us, event | category | flops | bytes accessed | tf_op | source)
XLA Modules:
  0.0 138.6 jit_solution(7063969387953105929)
XLA Ops:
  1.1 3.0 %collective-permute-start.1 = (bf16[80,1280]{1,0:T(8,128)(2,1)S(1)}, bf16[80,1280]{1,0:T(8,128)(2,1)S(1)}, u32[]{:S(2)}, u32[]{:S(2)}) collective-permute-start(bf16[80,1280]{1,0:T(8,128)(2,1)S(1)} %get-tuple-element.159.refs_1_), channel_id=1, source_target_pairs={{8,0},{16,8},{24,16},{28,24},{20,28},{12,20},{4,12},{0,4},{9,1},{1... | collective-permute-start | bytes 614408 | tf_op jit(solution)/shard_map/ppermute | solution.py:324
  4.3 2.0 %collective-permute-start.2 = (bf16[80,1280]{1,0:T(8,128)(2,1)S(1)}, bf16[80,1280]{1,0:T(8,128)(2,1)S(1)}, u32[]{:S(2)}, u32[]{:S(2)}) collective-permute-start(bf16[80,1280]{1,0:T(8,128)(2,1)S(1)} %get-tuple-element.159.refs_1_), channel_id=1, source_target_pairs={{0,8},{8,16},{16,24},{24,28},{28,20},{20,12},{12,4},{4,0},{1,9},{9... | collective-permute-start | bytes 614408 | tf_op jit(solution)/shard_map/ppermute | solution.py:323
  8.2 1.9 %collective-permute-start.14 = (bf16[2,320,256]{2,1,0:T(8,128)(2,1)S(1)}, bf16[2,320,256]{2,1,0:T(8,128)(2,1)S(1)}, u32[]{:S(2)}, u32[]{:S(2)}) collective-permute-start(bf16[2,320,256]{2,1,0:T(8,128)(2,1)S(1)} %get-tuple-element.97.own.refs_0_), channel_id=1, source_target_pairs={{0,2},{1,3},{2,0},{3,1},{4,6},{5,7},{6,4},{7,5},{8,10},{9,11},{10,... | collective-permute-start | bytes 983048 | tf_op jit(solution)/shard_map/ppermute | solution.py:363
  10.2 2.0 %collective-permute-done.refs_2_ = bf16[80,1280]{1,0:T(8,128)(2,1)S(1)} collective-permute-done((bf16[80,1280]{1,0:T(8,128)(2,1)S(1)}, bf16[80,1280]{1,0:T(8,128)(2,1)S(1)}, u32[]{:S(2)}, u32[]{:S(2)}) %collective-permute-start) | collective-permute-done | bytes 204832 | tf_op jit(solution)/shard_map/ppermute | solution.py:323
  12.1 1.6 %collective-permute-start.5 = (bf16[80,1280]{1,0:T(8,128)(2,1)S(1)}, bf16[80,1280]{1,0:T(8,128)(2,1)S(1)}, u32[]{:S(2)}, u32[]{:S(2)}) collective-permute-start(bf16[80,1280]{1,0:T(8,128)(2,1)S(1)} %collective-permute-done.1.refs_3_), channel_id=1, source_target_pairs={{8,0},{16,8},{24,16},{28,24},{20,28},{12,20},{4,12},{0,4},{9,1},{1... | collective-permute-start | bytes 614408 | tf_op jit(solution)/shard_map/ppermute | solution.py:324
  16.6 1.9 %collective-permute-start.17 = (bf16[2,320,256]{2,1,0:T(8,128)(2,1)S(1)}, bf16[2,320,256]{2,1,0:T(8,128)(2,1)S(1)}, u32[]{:S(2)}, u32[]{:S(2)}) collective-permute-start(bf16[2,320,256]{2,1,0:T(8,128)(2,1)S(1)} %get-tuple-element.101.own.refs_1_), channel_id=1, source_target_pairs={{0,2},{1,3},{2,0},{3,1},{4,6},{5,7},{6,4},{7,5},{8,10},{9,11},{10,... | collective-permute-start | bytes 983048 | tf_op jit(solution)/shard_map/ppermute | solution.py:363
  20.1 1.6 %collective-permute-done.4.refs_6_ = bf16[80,1280]{1,0:T(8,128)(2,1)S(1)} collective-permute-done((bf16[80,1280]{1,0:T(8,128)(2,1)S(1)}, bf16[80,1280]{1,0:T(8,128)(2,1)S(1)}, u32[]{:S(2)}, u32[]{:S(2)}) %collective-permute-start.4) | collective-permute-done | bytes 204832 | tf_op jit(solution)/shard_map/ppermute | solution.py:323
  22.1 1.8 %collective-permute-done.6.refs_8_ = bf16[80,1280]{1,0:T(8,128)(2,1)S(1)} collective-permute-done((bf16[80,1280]{1,0:T(8,128)(2,1)S(1)}, bf16[80,1280]{1,0:T(8,128)(2,1)S(1)}, u32[]{:S(2)}, u32[]{:S(2)}) %collective-permute-start.6) | collective-permute-done | bytes 204832 | tf_op jit(solution)/shard_map/ppermute | solution.py:323
  23.8 1.6 %collective-permute-start.9 = (bf16[80,1280]{1,0:T(8,128)(2,1)S(1)}, bf16[80,1280]{1,0:T(8,128)(2,1)S(1)}, u32[]{:S(2)}, u32[]{:S(2)}) collective-permute-start(bf16[80,1280]{1,0:T(8,128)(2,1)S(1)} %collective-permute-done.5.refs_7_), channel_id=1, source_target_pairs={{8,0},{16,8},{24,16},{28,24},{20,28},{12,20},{4,12},{0,4},{9,1},{1... | collective-permute-start | bytes 614408 | tf_op jit(solution)/shard_map/ppermute | solution.py:324
  25.9 3.6 %collective-permute-done.8.refs_10_ = bf16[80,1280]{1,0:T(8,128)(2,1)S(1)} collective-permute-done((bf16[80,1280]{1,0:T(8,128)(2,1)S(1)}, bf16[80,1280]{1,0:T(8,128)(2,1)S(1)}, u32[]{:S(2)}, u32[]{:S(2)}) %collective-permute-start.8) | collective-permute-done | bytes 204832 | tf_op jit(solution)/shard_map/ppermute | solution.py:323
  30.1 1.6 %collective-permute-start.11 = (bf16[80,1280]{1,0:T(8,128)(2,1)S(1)}, bf16[80,1280]{1,0:T(8,128)(2,1)S(1)}, u32[]{:S(2)}, u32[]{:S(2)}) collective-permute-start(bf16[80,1280]{1,0:T(8,128)(2,1)S(1)} %collective-permute-done.7.refs_9_), channel_id=1, source_target_pairs={{8,0},{16,8},{24,16},{28,24},{20,28},{12,20},{4,12},{0,4},{9,1},{1... | collective-permute-start | bytes 614408 | tf_op jit(solution)/shard_map/ppermute | solution.py:324
  31.6 1.9 %collective-permute-done.10.refs_12_ = bf16[80,1280]{1,0:T(8,128)(2,1)S(1)} collective-permute-done((bf16[80,1280]{1,0:T(8,128)(2,1)S(1)}, bf16[80,1280]{1,0:T(8,128)(2,1)S(1)}, u32[]{:S(2)}, u32[]{:S(2)}) %collective-permute-start.10) | collective-permute-done | bytes 204832 | tf_op jit(solution)/shard_map/ppermute | solution.py:323
  33.9 1.6 %collective-permute-start.13 = (bf16[80,1280]{1,0:T(8,128)(2,1)S(1)}, bf16[80,1280]{1,0:T(8,128)(2,1)S(1)}, u32[]{:S(2)}, u32[]{:S(2)}) collective-permute-start(bf16[80,1280]{1,0:T(8,128)(2,1)S(1)} %collective-permute-done.9.refs_11_), channel_id=1, source_target_pairs={{8,0},{16,8},{24,16},{28,24},{20,28},{12,20},{4,12},{0,4},{9,1},{1... | collective-permute-start | bytes 614408 | tf_op jit(solution)/shard_map/ppermute | solution.py:324
  38.4 1.7 %collective-permute-start.21 = (bf16[80,1280]{1,0:T(8,128)(2,1)S(1)}, bf16[80,1280]{1,0:T(8,128)(2,1)S(1)}, u32[]{:S(2)}, u32[]{:S(2)}) collective-permute-start(bf16[80,1280]{1,0:T(8,128)(2,1)S(1)} %get-tuple-element.106.refs_6_), channel_id=1, source_target_pairs={{8,0},{16,8},{24,16},{28,24},{20,28},{12,20},{4,12},{0,4},{9,1},{1... | collective-permute-start | bytes 614408 | tf_op jit(solution)/shard_map/ppermute | solution.py:324
  46.8 1.6 %collective-permute-start.24 = (bf16[80,1280]{1,0:T(8,128)(2,1)S(1)}, bf16[80,1280]{1,0:T(8,128)(2,1)S(1)}, u32[]{:S(2)}, u32[]{:S(2)}) collective-permute-start(bf16[80,1280]{1,0:T(8,128)(2,1)S(1)} %collective-permute-done.21.refs_8_), channel_id=1, source_target_pairs={{8,0},{16,8},{24,16},{28,24},{20,28},{12,20},{4,12},{0,4},{9,1},{1... | collective-permute-start | bytes 614408 | tf_op jit(solution)/shard_map/ppermute | solution.py:324
  51.2 1.6 %collective-permute-start.30 = (bf16[80,1280]{1,0:T(8,128)(2,1)S(1)}, bf16[80,1280]{1,0:T(8,128)(2,1)S(1)}, u32[]{:S(2)}, u32[]{:S(2)}) collective-permute-start(bf16[80,1280]{1,0:T(8,128)(2,1)S(1)} %collective-permute-done.29.refs_10_), channel_id=1, source_target_pairs={{8,0},{16,8},{24,16},{28,24},{20,28},{12,20},{4,12},{0,4},{9,1},{1... | collective-permute-start | bytes 614408 | tf_op jit(solution)/shard_map/ppermute | solution.py:324
  65.9 2.0 %collective-permute-done.26.refs_17_ = bf16[80,1280]{1,0:T(8,128)(2,1)S(1)} collective-permute-done((bf16[80,1280]{1,0:T(8,128)(2,1)S(1)}, bf16[80,1280]{1,0:T(8,128)(2,1)S(1)}, u32[]{:S(2)}, u32[]{:S(2)}) %collective-permute-start.26) | collective-permute-done | bytes 204832 | tf_op jit(solution)/shard_map/ppermute | solution.py:323
  70.3 2.0 %collective-permute-done.34.refs_19_ = bf16[80,1280]{1,0:T(8,128)(2,1)S(1)} collective-permute-done((bf16[80,1280]{1,0:T(8,128)(2,1)S(1)}, bf16[80,1280]{1,0:T(8,128)(2,1)S(1)}, u32[]{:S(2)}, u32[]{:S(2)}) %collective-permute-start.34) | collective-permute-done | bytes 204832 | tf_op jit(solution)/shard_map/ppermute | solution.py:323
  73.1 2.3 %mlp_out.3 = (bf16[320,256]{1,0:T(8,128)(2,1)S(1)}, bf16[320,256]{1,0:T(8,128)(2,1)S(1)}, bf16[320,256]{1,0:T(8,128)(2,1)S(1)}, bf16[320,256]{1,0:T(8,128)(2,1)S...) custom-call(bf16[1024,256]{1,0:T(8,128)(2,1)S(1)} %hidden.5.refs_0_,, ...), custom_call_target="tpu_custom_call" | custom-call | tf_op jit(solution)/shard_map/mlp_out/pallas_call | solution.py:19
  75.5 1.7 %collective-permute-start.49 = (bf16[80,1280]{1,0:T(8,128)(2,1)S(1)}, bf16[80,1280]{1,0:T(8,128)(2,1)S(1)}, u32[]{:S(2)}, u32[]{:S(2)}) collective-permute-start(bf16[80,1280]{1,0:T(8,128)(2,1)S(1)} %get-tuple-element.146.refs_0_), channel_id=1, source_target_pairs={{8,0},{16,8},{24,16},{28,24},{20,28},{12,20},{4,12},{0,4},{9,1},{1... | collective-permute-start | bytes 614408 | tf_op jit(solution)/shard_map/ppermute | solution.py:324
  78.5 1.6 %collective-permute-start.51 = (bf16[80,1280]{1,0:T(8,128)(2,1)S(1)}, bf16[80,1280]{1,0:T(8,128)(2,1)S(1)}, u32[]{:S(2)}, u32[]{:S(2)}) collective-permute-start(bf16[80,1280]{1,0:T(8,128)(2,1)S(1)} %collective-permute-done.32.refs_3_), channel_id=1, source_target_pairs={{8,0},{16,8},{24,16},{28,24},{20,28},{12,20},{4,12},{0,4},{9,1},{1... | collective-permute-start | bytes 614408 | tf_op jit(solution)/shard_map/ppermute | solution.py:324
  81.7 1.7 %collective-permute-done.49.refs_5_ = bf16[80,1280]{1,0:T(8,128)(2,1)S(1)} collective-permute-done((bf16[80,1280]{1,0:T(8,128)(2,1)S(1)}, bf16[80,1280]{1,0:T(8,128)(2,1)S(1)}, u32[]{:S(2)}, u32[]{:S(2)}) %collective-permute-start.49) | collective-permute-done | bytes 204832 | tf_op jit(solution)/shard_map/ppermute | solution.py:324
  83.5 1.7 %collective-permute-start.43 = (bf16[320,256]{1,0:T(8,128)(2,1)S(1)}, bf16[320,256]{1,0:T(8,128)(2,1)S(1)}, u32[]{:S(2)}, u32[]{:S(2)}) collective-permute-start(bf16[320,256]{1,0:T(8,128)(2,1)S(1)} %add.6), channel_id=1, source_target_pairs={{0,2},{1,3},{2,0},{3,1},{4,6},{5,7},{6,4},{7,5},{8,10},{9,11},{10,... | collective-permute-start | bytes 491528 | tf_op jit(solution)/shard_map/ppermute | solution.py:363
  85.2 2.2 %mlp_out.2 = (bf16[320,256]{1,0:T(8,128)(2,1)S(1)}, bf16[320,256]{1,0:T(8,128)(2,1)S(1)}, bf16[320,256]{1,0:T(8,128)(2,1)S(1)}, bf16[320,256]{1,0:T(8,128)(2,1)S...) custom-call(bf16[1024,256]{1,0:T(8,128)(2,1)S(1)} %hidden.5.refs_0_,, ...), custom_call_target="tpu_custom_call" | custom-call | tf_op jit(solution)/shard_map/mlp_out/pallas_call | solution.py:19
  87.4 1.6 %collective-permute-start.53 = (bf16[80,1280]{1,0:T(8,128)(2,1)S(1)}, bf16[80,1280]{1,0:T(8,128)(2,1)S(1)}, u32[]{:S(2)}, u32[]{:S(2)}) collective-permute-start(bf16[80,1280]{1,0:T(8,128)(2,1)S(1)} %collective-permute-done.49.refs_5_), channel_id=1, source_target_pairs={{8,0},{16,8},{24,16},{28,24},{20,28},{12,20},{4,12},{0,4},{9,1},{1... | collective-permute-start | bytes 614408 | tf_op jit(solution)/shard_map/ppermute | solution.py:324
  92.0 4.1 %collective-permute-done.45.refs_12_ = bf16[320,256]{1,0:T(8,128)(2,1)S(1)} collective-permute-done((bf16[320,256]{1,0:T(8,128)(2,1)S(1)}, bf16[320,256]{1,0:T(8,128)(2,1)S(1)}, u32[]{:S(2)}, u32[]{:S(2)}) %collective-permute-start.45) | collective-permute-done | bytes 163872 | tf_op jit(solution)/shard_map/ppermute | solution.py:363
  97.0 3.3 %collective-permute-done.54.refs_10_ = bf16[80,1280]{1,0:T(8,128)(2,1)S(1)} collective-permute-done((bf16[80,1280]{1,0:T(8,128)(2,1)S(1)}, bf16[80,1280]{1,0:T(8,128)(2,1)S(1)}, u32[]{:S(2)}, u32[]{:S(2)}) %collective-permute-start.54) | collective-permute-done | bytes 204832 | tf_op jit(solution)/shard_map/ppermute | solution.py:323
  106.3 1.9 %collective-permute-done.56.refs_12_ = bf16[80,1280]{1,0:T(8,128)(2,1)S(1)} collective-permute-done((bf16[80,1280]{1,0:T(8,128)(2,1)S(1)}, bf16[80,1280]{1,0:T(8,128)(2,1)S(1)}, u32[]{:S(2)}, u32[]{:S(2)}) %collective-permute-start.56) | collective-permute-done | bytes 204832 | tf_op jit(solution)/shard_map/ppermute | solution.py:323
  109.3 2.9 %collective-permute-done.58.refs_14_ = bf16[80,1280]{1,0:T(8,128)(2,1)S(1)} collective-permute-done((bf16[80,1280]{1,0:T(8,128)(2,1)S(1)}, bf16[80,1280]{1,0:T(8,128)(2,1)S(1)}, u32[]{:S(2)}, u32[]{:S(2)}) %collective-permute-start.58) | collective-permute-done | bytes 204832 | tf_op jit(solution)/shard_map/ppermute | solution.py:323
  113.8 1.6 %collective-permute-done.60.near = bf16[2,320,256]{2,1,0:T(8,128)(2,1)S(1)} collective-permute-done((bf16[2,320,256]{2,1,0:T(8,128)(2,1)S(1)}, bf16[2,320,256]{2,1,0:T(8,128)(2,1)S(1)}, u32[]{:S(2)}, u32[]{:S(2)}) %collective-permute-start.60) | collective-permute-done | bytes 327712 | tf_op jit(solution)/shard_map/ppermute | solution.py:360
  116.4 5.4 %collective-permute-done.61.far = bf16[320,256]{1,0:T(8,128)(2,1)S(1)} collective-permute-done((bf16[320,256]{1,0:T(8,128)(2,1)S(1)}, bf16[320,256]{1,0:T(8,128)(2,1)S(1)}, u32[]{:S(2)}, u32[]{:S(2)}) %collective-permute-start.61) | collective-permute-done | bytes 163872 | tf_op jit(solution)/shard_map/ppermute | solution.py:363
  122.2 15.1 %all_to_all.5.arrived = bf16[8,160,128]{2,1,0:T(8,128)(2,1)S(1)} all-to-all(bf16[8,160,128]{2,1,0:T(8,128)(2,1)S(1)} %pack.1), channel_id=1, replica_groups=mesh['wide'=8,'narrow'=4] {'wide'}, dimensions={0} | all-to-all | bytes 655360 | tf_op jit(solution)/shard_map/all_to_all | solution.py:437
  (143 shorter events, 56.2 us)
Async XLA Ops:
  1.1 9.1 %collective-permute-start.1 = (bf16[80,1280]{1,0:T(8,128)(2,1)S(1)}, bf16[80,1280]{1,0:T(8,128)(2,1)S(1)}, u32[]{:S(2)}, u32[]{:S(2)}) collective-permute-start(bf16[80,1280]{1,0:T(8,128)(2,1)S(1)} %get-tuple-element.159.refs_1_), channel_id=1, source_target_pairs={{8,0},{16,8},{24,16},{28,24},{20,28},{12,20},{4,12},{0,4},{9,1},{1... | collective-permute-start | bytes 614408 | tf_op jit(solution)/shard_map/ppermute | solution.py:324
  4.3 12.3 %collective-permute-start.2 = (bf16[80,1280]{1,0:T(8,128)(2,1)S(1)}, bf16[80,1280]{1,0:T(8,128)(2,1)S(1)}, u32[]{:S(2)}, u32[]{:S(2)}) collective-permute-start(bf16[80,1280]{1,0:T(8,128)(2,1)S(1)} %get-tuple-element.159.refs_1_), channel_id=1, source_target_pairs={{0,8},{8,16},{16,24},{24,28},{28,20},{20,12},{12,4},{4,0},{1,9},{9... | collective-permute-start | bytes 614408 | tf_op jit(solution)/shard_map/ppermute | solution.py:323
  6.2 10.4 %collective-permute-start.3 = (bf16[80,1280]{1,0:T(8,128)(2,1)S(1)}, bf16[80,1280]{1,0:T(8,128)(2,1)S(1)}, u32[]{:S(2)}, u32[]{:S(2)}) collective-permute-start(bf16[80,1280]{1,0:T(8,128)(2,1)S(1)} %get-tuple-element.160.refs_0_), channel_id=1, source_target_pairs={{8,0},{16,8},{24,16},{28,24},{20,28},{12,20},{4,12},{0,4},{9,1},{1... | collective-permute-start | bytes 614408 | tf_op jit(solution)/shard_map/ppermute | solution.py:324
  8.2 13.4 %collective-permute-start.14 = (bf16[2,320,256]{2,1,0:T(8,128)(2,1)S(1)}, bf16[2,320,256]{2,1,0:T(8,128)(2,1)S(1)}, u32[]{:S(2)}, u32[]{:S(2)}) collective-permute-start(bf16[2,320,256]{2,1,0:T(8,128)(2,1)S(1)} %get-tuple-element.97.own.refs_0_), channel_id=1, source_target_pairs={{0,2},{1,3},{2,0},{3,1},{4,6},{5,7},{6,4},{7,5},{8,10},{9,11},{10,... | collective-permute-start | bytes 983048 | tf_op jit(solution)/shard_map/ppermute | solution.py:363
  16.6 9.3 %collective-permute-start.17 = (bf16[2,320,256]{2,1,0:T(8,128)(2,1)S(1)}, bf16[2,320,256]{2,1,0:T(8,128)(2,1)S(1)}, u32[]{:S(2)}, u32[]{:S(2)}) collective-permute-start(bf16[2,320,256]{2,1,0:T(8,128)(2,1)S(1)} %get-tuple-element.101.own.refs_1_), channel_id=1, source_target_pairs={{0,2},{1,3},{2,0},{3,1},{4,6},{5,7},{6,4},{7,5},{8,10},{9,11},{10,... | collective-permute-start | bytes 983048 | tf_op jit(solution)/shard_map/ppermute | solution.py:363
  21.7 8.4 %collective-permute-start.15 = (bf16[2,320,256]{2,1,0:T(8,128)(2,1)S(1)}, bf16[2,320,256]{2,1,0:T(8,128)(2,1)S(1)}, u32[]{:S(2)}, u32[]{:S(2)}) collective-permute-start(bf16[2,320,256]{2,1,0:T(8,128)(2,1)S(1)} %get-tuple-element.97.own.refs_0_), channel_id=1, source_target_pairs={{0,1},{1,0},{2,3},{3,2},{4,5},{5,4},{6,7},{7,6},{8,9},{9,8},{10,11... | collective-permute-start | bytes 983048 | tf_op jit(solution)/shard_map/ppermute | solution.py:360
  25.4 8.1 %collective-permute-start.10 = (bf16[80,1280]{1,0:T(8,128)(2,1)S(1)}, bf16[80,1280]{1,0:T(8,128)(2,1)S(1)}, u32[]{:S(2)}, u32[]{:S(2)}) collective-permute-start(bf16[80,1280]{1,0:T(8,128)(2,1)S(1)} %collective-permute-done.6.refs_8_), channel_id=1, source_target_pairs={{0,8},{8,16},{16,24},{24,28},{28,20},{20,12},{12,4},{4,0},{1,9},{9... | collective-permute-start | bytes 614408 | tf_op jit(solution)/shard_map/ppermute | solution.py:323
  29.5 8.8 %collective-permute-start.18 = (bf16[2,320,256]{2,1,0:T(8,128)(2,1)S(1)}, bf16[2,320,256]{2,1,0:T(8,128)(2,1)S(1)}, u32[]{:S(2)}, u32[]{:S(2)}) collective-permute-start(bf16[2,320,256]{2,1,0:T(8,128)(2,1)S(1)} %get-tuple-element.101.own.refs_1_), channel_id=1, source_target_pairs={{0,1},{1,0},{2,3},{3,2},{4,5},{5,4},{6,7},{7,6},{8,9},{9,8},{10,11... | collective-permute-start | bytes 983048 | tf_op jit(solution)/shard_map/ppermute | solution.py:360
  29.6 10.4 %collective-permute-start.19 = (bf16[2,320,256]{2,1,0:T(8,128)(2,1)S(1)}, bf16[2,320,256]{2,1,0:T(8,128)(2,1)S(1)}, u32[]{:S(2)}, u32[]{:S(2)}) collective-permute-start(bf16[2,320,256]{2,1,0:T(8,128)(2,1)S(1)} %collective-permute-done.17.over_x), channel_id=1, source_target_pairs={{0,1},{1,0},{2,3},{3,2},{4,5},{5,4},{6,7},{7,6},{8,9},{9,8},{10,11... | collective-permute-start | bytes 983048 | tf_op jit(solution)/shard_map/ppermute | solution.py:360
  33.9 8.4 %collective-permute-start.13 = (bf16[80,1280]{1,0:T(8,128)(2,1)S(1)}, bf16[80,1280]{1,0:T(8,128)(2,1)S(1)}, u32[]{:S(2)}, u32[]{:S(2)}) collective-permute-start(bf16[80,1280]{1,0:T(8,128)(2,1)S(1)} %collective-permute-done.9.refs_11_), channel_id=1, source_target_pairs={{8,0},{16,8},{24,16},{28,24},{20,28},{12,20},{4,12},{0,4},{9,1},{1... | collective-permute-start | bytes 614408 | tf_op jit(solution)/shard_map/ppermute | solution.py:324
  38.4 8.4 %collective-permute-start.21 = (bf16[80,1280]{1,0:T(8,128)(2,1)S(1)}, bf16[80,1280]{1,0:T(8,128)(2,1)S(1)}, u32[]{:S(2)}, u32[]{:S(2)}) collective-permute-start(bf16[80,1280]{1,0:T(8,128)(2,1)S(1)} %get-tuple-element.106.refs_6_), channel_id=1, source_target_pairs={{8,0},{16,8},{24,16},{28,24},{20,28},{12,20},{4,12},{0,4},{9,1},{1... | collective-permute-start | bytes 614408 | tf_op jit(solution)/shard_map/ppermute | solution.py:324
  41.5 8.9 %collective-permute-start.20 = (bf16[80,1280]{1,0:T(8,128)(2,1)S(1)}, bf16[80,1280]{1,0:T(8,128)(2,1)S(1)}, u32[]{:S(2)}, u32[]{:S(2)}) collective-permute-start(bf16[80,1280]{1,0:T(8,128)(2,1)S(1)} %get-tuple-element.106.refs_6_), channel_id=1, source_target_pairs={{0,8},{8,16},{16,24},{24,28},{28,20},{20,12},{12,4},{4,0},{1,9},{9... | collective-permute-start | bytes 614408 | tf_op jit(solution)/shard_map/ppermute | solution.py:323
  42.4 8.8 %collective-permute-start.29 = (bf16[80,1280]{1,0:T(8,128)(2,1)S(1)}, bf16[80,1280]{1,0:T(8,128)(2,1)S(1)}, u32[]{:S(2)}, u32[]{:S(2)}) collective-permute-start(bf16[80,1280]{1,0:T(8,128)(2,1)S(1)} %get-tuple-element.117.refs_5_), channel_id=1, source_target_pairs={{8,0},{16,8},{24,16},{28,24},{20,28},{12,20},{4,12},{0,4},{9,1},{1... | collective-permute-start | bytes 614408 | tf_op jit(solution)/shard_map/ppermute | solution.py:324
  46.0 8.8 %collective-permute-start.25 = (bf16[80,1280]{1,0:T(8,128)(2,1)S(1)}, bf16[80,1280]{1,0:T(8,128)(2,1)S(1)}, u32[]{:S(2)}, u32[]{:S(2)}) collective-permute-start(bf16[80,1280]{1,0:T(8,128)(2,1)S(1)} %collective-permute-done.22.refs_7_), channel_id=1, source_target_pairs={{0,8},{8,16},{16,24},{24,28},{28,20},{20,12},{12,4},{4,0},{1,9},{9... | collective-permute-start | bytes 614408 | tf_op jit(solution)/shard_map/ppermute | solution.py:323
  46.8 8.8 %collective-permute-start.24 = (bf16[80,1280]{1,0:T(8,128)(2,1)S(1)}, bf16[80,1280]{1,0:T(8,128)(2,1)S(1)}, u32[]{:S(2)}, u32[]{:S(2)}) collective-permute-start(bf16[80,1280]{1,0:T(8,128)(2,1)S(1)} %collective-permute-done.21.refs_8_), channel_id=1, source_target_pairs={{8,0},{16,8},{24,16},{28,24},{20,28},{12,20},{4,12},{0,4},{9,1},{1... | collective-permute-start | bytes 614408 | tf_op jit(solution)/shard_map/ppermute | solution.py:324
  50.4 8.8 %collective-permute-start.23 = (bf16[80,1280]{1,0:T(8,128)(2,1)S(1)}, bf16[80,1280]{1,0:T(8,128)(2,1)S(1)}, u32[]{:S(2)}, u32[]{:S(2)}) collective-permute-start(bf16[80,1280]{1,0:T(8,128)(2,1)S(1)} %collective-permute-done.20.refs_9_), channel_id=1, source_target_pairs={{0,8},{8,16},{16,24},{24,28},{28,20},{20,12},{12,4},{4,0},{1,9},{9... | collective-permute-start | bytes 614408 | tf_op jit(solution)/shard_map/ppermute | solution.py:323
  51.2 8.8 %collective-permute-start.30 = (bf16[80,1280]{1,0:T(8,128)(2,1)S(1)}, bf16[80,1280]{1,0:T(8,128)(2,1)S(1)}, u32[]{:S(2)}, u32[]{:S(2)}) collective-permute-start(bf16[80,1280]{1,0:T(8,128)(2,1)S(1)} %collective-permute-done.29.refs_10_), channel_id=1, source_target_pairs={{8,0},{16,8},{24,16},{28,24},{20,28},{12,20},{4,12},{0,4},{9,1},{1... | collective-permute-start | bytes 614408 | tf_op jit(solution)/shard_map/ppermute | solution.py:324
  54.8 8.8 %collective-permute-start.33 = (bf16[80,1280]{1,0:T(8,128)(2,1)S(1)}, bf16[80,1280]{1,0:T(8,128)(2,1)S(1)}, u32[]{:S(2)}, u32[]{:S(2)}) collective-permute-start(bf16[80,1280]{1,0:T(8,128)(2,1)S(1)} %collective-permute-done.25.refs_11_), channel_id=1, source_target_pairs={{0,8},{8,16},{16,24},{24,28},{28,20},{20,12},{12,4},{4,0},{1,9},{9... | collective-permute-start | bytes 614408 | tf_op jit(solution)/shard_map/ppermute | solution.py:323
  55.5 8.8 %collective-permute-start.27 = (bf16[80,1280]{1,0:T(8,128)(2,1)S(1)}, bf16[80,1280]{1,0:T(8,128)(2,1)S(1)}, u32[]{:S(2)}, u32[]{:S(2)}) collective-permute-start(bf16[80,1280]{1,0:T(8,128)(2,1)S(1)} %collective-permute-done.24.refs_12_), channel_id=1, source_target_pairs={{8,0},{16,8},{24,16},{28,24},{20,28},{12,20},{4,12},{0,4},{9,1},{1... | collective-permute-start | bytes 614408 | tf_op jit(solution)/shard_map/ppermute | solution.py:324
  59.2 8.8 %collective-permute-start.26 = (bf16[80,1280]{1,0:T(8,128)(2,1)S(1)}, bf16[80,1280]{1,0:T(8,128)(2,1)S(1)}, u32[]{:S(2)}, u32[]{:S(2)}) collective-permute-start(bf16[80,1280]{1,0:T(8,128)(2,1)S(1)} %collective-permute-done.23.refs_13_), channel_id=1, source_target_pairs={{0,8},{8,16},{16,24},{24,28},{28,20},{20,12},{12,4},{4,0},{1,9},{9... | collective-permute-start | bytes 614408 | tf_op jit(solution)/shard_map/ppermute | solution.py:323
  59.9 8.8 %collective-permute-start.31 = (bf16[80,1280]{1,0:T(8,128)(2,1)S(1)}, bf16[80,1280]{1,0:T(8,128)(2,1)S(1)}, u32[]{:S(2)}, u32[]{:S(2)}) collective-permute-start(bf16[80,1280]{1,0:T(8,128)(2,1)S(1)} %collective-permute-done.30.refs_14_), channel_id=1, source_target_pairs={{8,0},{16,8},{24,16},{28,24},{20,28},{12,20},{4,12},{0,4},{9,1},{1... | collective-permute-start | bytes 614408 | tf_op jit(solution)/shard_map/ppermute | solution.py:324
  63.6 8.8 %collective-permute-start.34 = (bf16[80,1280]{1,0:T(8,128)(2,1)S(1)}, bf16[80,1280]{1,0:T(8,128)(2,1)S(1)}, u32[]{:S(2)}, u32[]{:S(2)}) collective-permute-start(bf16[80,1280]{1,0:T(8,128)(2,1)S(1)} %collective-permute-done.33.refs_15_), channel_id=1, source_target_pairs={{0,8},{8,16},{16,24},{24,28},{28,20},{20,12},{12,4},{4,0},{1,9},{9... | collective-permute-start | bytes 614408 | tf_op jit(solution)/shard_map/ppermute | solution.py:323
  64.3 8.8 %collective-permute-start.35 = (bf16[80,1280]{1,0:T(8,128)(2,1)S(1)}, bf16[80,1280]{1,0:T(8,128)(2,1)S(1)}, u32[]{:S(2)}, u32[]{:S(2)}) collective-permute-start(bf16[80,1280]{1,0:T(8,128)(2,1)S(1)} %collective-permute-done.27.refs_16_), channel_id=1, source_target_pairs={{8,0},{16,8},{24,16},{28,24},{20,28},{12,20},{4,12},{0,4},{9,1},{1... | collective-permute-start | bytes 614408 | tf_op jit(solution)/shard_map/ppermute | solution.py:324
  67.9 9.2 %collective-permute-start.28 = (bf16[80,1280]{1,0:T(8,128)(2,1)S(1)}, bf16[80,1280]{1,0:T(8,128)(2,1)S(1)}, u32[]{:S(2)}, u32[]{:S(2)}) collective-permute-start(bf16[80,1280]{1,0:T(8,128)(2,1)S(1)} %get-tuple-element.146.refs_0_), channel_id=1, source_target_pairs={{0,8},{8,16},{16,24},{24,28},{28,20},{20,12},{12,4},{4,0},{1,9},{9... | collective-permute-start | bytes 614408 | tf_op jit(solution)/shard_map/ppermute | solution.py:323
  68.7 8.6 %collective-permute-start.32 = (bf16[80,1280]{1,0:T(8,128)(2,1)S(1)}, bf16[80,1280]{1,0:T(8,128)(2,1)S(1)}, u32[]{:S(2)}, u32[]{:S(2)}) collective-permute-start(bf16[80,1280]{1,0:T(8,128)(2,1)S(1)} %get-tuple-element.145.refs_1_), channel_id=1, source_target_pairs={{8,0},{16,8},{24,16},{28,24},{20,28},{12,20},{4,12},{0,4},{9,1},{1... | collective-permute-start | bytes 614408 | tf_op jit(solution)/shard_map/ppermute | solution.py:324
  77.3 11.7 %collective-permute-start.50 = (bf16[80,1280]{1,0:T(8,128)(2,1)S(1)}, bf16[80,1280]{1,0:T(8,128)(2,1)S(1)}, u32[]{:S(2)}, u32[]{:S(2)}) collective-permute-start(bf16[80,1280]{1,0:T(8,128)(2,1)S(1)} %collective-permute-done.28.refs_2_), channel_id=1, source_target_pairs={{0,8},{8,16},{16,24},{24,28},{28,20},{20,12},{12,4},{4,0},{1,9},{9... | collective-permute-start | bytes 614408 | tf_op jit(solution)/shard_map/ppermute | solution.py:323
  78.5 11.9 %collective-permute-start.51 = (bf16[80,1280]{1,0:T(8,128)(2,1)S(1)}, bf16[80,1280]{1,0:T(8,128)(2,1)S(1)}, u32[]{:S(2)}, u32[]{:S(2)}) collective-permute-start(bf16[80,1280]{1,0:T(8,128)(2,1)S(1)} %collective-permute-done.32.refs_3_), channel_id=1, source_target_pairs={{8,0},{16,8},{24,16},{28,24},{20,28},{12,20},{4,12},{0,4},{9,1},{1... | collective-permute-start | bytes 614408 | tf_op jit(solution)/shard_map/ppermute | solution.py:324
  87.4 9.1 %collective-permute-start.53 = (bf16[80,1280]{1,0:T(8,128)(2,1)S(1)}, bf16[80,1280]{1,0:T(8,128)(2,1)S(1)}, u32[]{:S(2)}, u32[]{:S(2)}) collective-permute-start(bf16[80,1280]{1,0:T(8,128)(2,1)S(1)} %collective-permute-done.49.refs_5_), channel_id=1, source_target_pairs={{8,0},{16,8},{24,16},{28,24},{20,28},{12,20},{4,12},{0,4},{9,1},{1... | collective-permute-start | bytes 614408 | tf_op jit(solution)/shard_map/ppermute | solution.py:324
  89.5 10.9 %collective-permute-start.54 = (bf16[80,1280]{1,0:T(8,128)(2,1)S(1)}, bf16[80,1280]{1,0:T(8,128)(2,1)S(1)}, u32[]{:S(2)}, u32[]{:S(2)}) collective-permute-start(bf16[80,1280]{1,0:T(8,128)(2,1)S(1)} %collective-permute-done.50.refs_6_), channel_id=1, source_target_pairs={{0,8},{8,16},{16,24},{24,28},{28,20},{20,12},{12,4},{4,0},{1,9},{9... | collective-permute-start | bytes 614408 | tf_op jit(solution)/shard_map/ppermute | solution.py:323
  91.0 9.4 %collective-permute-start.55 = (bf16[80,1280]{1,0:T(8,128)(2,1)S(1)}, bf16[80,1280]{1,0:T(8,128)(2,1)S(1)}, u32[]{:S(2)}, u32[]{:S(2)}) collective-permute-start(bf16[80,1280]{1,0:T(8,128)(2,1)S(1)} %collective-permute-done.51.refs_7_), channel_id=1, source_target_pairs={{8,0},{16,8},{24,16},{28,24},{20,28},{12,20},{4,12},{0,4},{9,1},{1... | collective-permute-start | bytes 614408 | tf_op jit(solution)/shard_map/ppermute | solution.py:324
  102.4 9.8 %collective-permute-start.58 = (bf16[80,1280]{1,0:T(8,128)(2,1)S(1)}, bf16[80,1280]{1,0:T(8,128)(2,1)S(1)}, u32[]{:S(2)}, u32[]{:S(2)}) collective-permute-start(bf16[80,1280]{1,0:T(8,128)(2,1)S(1)} %collective-permute-done.54.refs_10_), channel_id=1, source_target_pairs={{0,8},{8,16},{16,24},{24,28},{28,20},{20,12},{12,4},{4,0},{1,9},{9... | collective-permute-start | bytes 614408 | tf_op jit(solution)/shard_map/ppermute | solution.py:323
  103.4 9.0 %collective-permute-start.59 = (bf16[80,1280]{1,0:T(8,128)(2,1)S(1)}, bf16[80,1280]{1,0:T(8,128)(2,1)S(1)}, u32[]{:S(2)}, u32[]{:S(2)}) collective-permute-start(bf16[80,1280]{1,0:T(8,128)(2,1)S(1)} %collective-permute-done.55.refs_11_), channel_id=1, source_target_pairs={{8,0},{16,8},{24,16},{28,24},{20,28},{12,20},{4,12},{0,4},{9,1},{1... | collective-permute-start | bytes 614408 | tf_op jit(solution)/shard_map/ppermute | solution.py:324
  (40 other events, 344.0 us)

commit v5 on v4

--- a/solution.py
+++ b/solution.py
@@ -10,7 +10,8 @@
 F32 = jnp.float32
 BF16 = jnp.bfloat16
 WINDOW = 4
-LATE = (1, 2, 3)
+LATE = (2, 3, 4)
+OWN_AT = 3
 VMEM = pl.BlockSpec(memory_space=pltpu.VMEM)
 
 
@@ -200,21 +201,31 @@
         give[c][:, at : at + step] = total[block:]
 
 
-def proj_kernel(pieces, count, shard_rows, merged, *refs):
-    sources, (keep, give, part) = refs[:-3], refs[-3:]
-    block = keep.shape[1]
+def proj_kernel(pieces, missing, count, shard_rows, merged, *refs):
+    sources, outs, part = refs[:-5], refs[-5:-1], refs[-1]
+    block = outs[0].shape[0]
+
+    def at(piece):
+        x, core, inside = piece.block_row(count, shard_rows, block)
+        return rows_at((core * 2 + x) * block + inside, piece.rows)
+
     for p in pieces:
-        x, core, inside = p.block_row(count, shard_rows, block)
-        at = rows_at(core * 2 * block + x * block + inside, p.rows)
-        part[at, :] = sources[p.array][p.start : p.start + p.rows, :]
-    for core, target in ((1, give), (0, keep)):
+        part[at(p), :] = sources[p.array][p.start : p.start + p.rows, :]
+    if missing is not None:
+        part[at(missing), :] = jnp.zeros((missing.rows, part.shape[1]), BF16)
+    for half in (1, 0):
         v = jnp.dot(
-            part[core * 2 * block : (core + 1) * 2 * block, :],
+            part[half * 2 * block : (half + 1) * 2 * block, :],
             merged[...],
             preferred_element_type=F32,
         ).astype(BF16)
-        target[0] = v[:block]
-        target[1] = v[block:]
+        outs[2 * half][...] = v[:block]
+        outs[2 * half + 1][...] = v[block:]
+
+
+def last_kernel(first, second, merged, o_ref):
+    whole = jnp.concatenate([first[...], second[...]], axis=0)
+    o_ref[...] = jnp.dot(whole, merged[...], preferred_element_type=F32).astype(BF16)
 
 
 def stream_kernel(chunks, bias, *refs):
@@ -238,9 +249,24 @@
     return rest > 0 and LANES % rest == 0 and bucket % (16 * (LANES // rest)) == 0
 
 
-def pack_kernel(groups, slots_of, keep, near, far, bias, o_ref):
-    total = keep[0].astype(F32) + near[0].astype(F32) + far[...].astype(F32)
-    vision = (total + bias[...]).astype(BF16)
+def pack_kernel(missing, count, shard_rows, groups, terms, slots_of, bias, *refs):
+    total, o_ref = refs[-1], refs[-2]
+    total[...] = refs[0][...].astype(F32)
+    for r in refs[1:terms]:
+        total[...] = total[...] + r[...].astype(F32)
+    late = refs[terms:-2]
+    if late:
+        x, core, inside = missing.block_row(count, shard_rows, total.shape[0])
+
+        @pl.when(x + core == 0)
+        def _():
+            at = rows_at(inside, missing.rows)
+            added = late[0][...].astype(F32)
+            for r in late[1:]:
+                added = added + r[...].astype(F32)
+            total[at, :] = total[at, :] + added
+
+    vision = (total[...] + bias[...]).astype(BF16)
     width = vision.shape[0]
     bucket = o_ref.shape[1] * o_ref.shape[2] // width
     slot = lax.broadcasted_iota(jnp.int32, (groups * bucket, vision.shape[1]), 0)
@@ -362,6 +388,9 @@
     def far(x):
         return lax.ppermute(x, "narrow", far_pairs)
 
+    def both(x):
+        return lax.ppermute(x, "narrow", [(i, i ^ 3) for i in range(parts)])
+
 
     def order(x):
         return call(
@@ -416,21 +445,21 @@
             shape(WINDOW * width, windows), name="stream",
         )
 
-    def proj(pieces, arrays, merged):
-        return call(
-            functools.partial(proj_kernel, pieces, groups, shard_rows[2]),
-            (merged, *arrays), [shape(2, width, windows)] * 2,
+    def proj(pieces, missing, arrays, merged):
+        return call(
+            functools.partial(proj_kernel, pieces, missing, groups, shard_rows[2]),
+            (merged, *arrays), [shape(width, windows)] * parts,
             scratch=[pltpu.VMEM((full, WINDOW * width), BF16)], name="proj",
         )
 
-    def pack(slots_of, keep, core_sums, x_sums):
+    def pack(slots_of, missing, terms, late):
         block = (bucket, width)
         if compact(width, bucket):
             block = (bucket * width // LANES, LANES)
         return call(
-            functools.partial(pack_kernel, groups),
-            (slots_of, keep, core_sums, x_sums, b_proj[:, None]), shape(groups, *block),
-            name="pack",
+            functools.partial(pack_kernel, missing, groups, shard_rows[2], groups, len(terms)),
+            (slots_of, b_proj[:, None], *terms, *late), shape(groups, *block),
+            scratch=[pltpu.VMEM((width, windows), F32)], name="pack",
         )
 
     def exchange_and_place(buffer, targets):
@@ -453,10 +482,9 @@
         x_sums = [far(add(k, near(g))) for k, g in zip(keep_x, give_x)]
         merged = stream(own, keep, [near(g) for g in give], x_sums)
         slots_of, targets = route()
-        keep, give = proj(pieces, wholes[2:], merged)
-        core_sums = near(give)
-        x_sums = far(add(keep[1], core_sums[1]))
-        return exchange_and_place(pack(slots_of, keep, core_sums, x_sums), targets)
+        mine, give_x, give_core, give_both = proj(pieces, None, wholes[2:], merged)
+        terms = [mine, far(give_x), near(give_core), both(give_both)]
+        return exchange_and_place(pack(slots_of, None, terms, ()), targets)
 
 
     ring = Ring(groups)
@@ -542,20 +570,28 @@
         core = [ring.now(got["core", 1][0]), *got["core", 1][1:]]
         sums = [add(k, c) for k, c in zip(got["keep", 1], core)]
         got["x_sums"] = [far(x) for x in sums]
-        for i, x in enumerate(got["x_sums"][:-1]):
+        for i, x in zip(range(len(LATE)), got["x_sums"]):
             ring.add_late(x, LATE[i])
         ring.add_work(sums[0])
-        start_out(0)
 
     pieces_proj, arrays_proj = gather(
-        got["shards"][2:], {0: lambda: start_out(1), 1: start_sums}
+        got["shards"][2:], {0: lambda: start_out(1), 1: start_sums, OWN_AT: lambda: start_out(0)}
     )
 
     merged = stream(own, got["keep", 0], got["core", 0], got["x_sums"])
-    keep, give = proj(pieces_proj, arrays_proj, merged)
-    core_sums = near(give)
-    x_sums = far(add(keep[1], core_sums[1]))
-    return exchange_and_place(pack(got["slots_of"], keep, core_sums, x_sums), got["targets"])
+    missing = Piece(0, 0, shard_rows[2], last, 0)
+    mine, give_x, give_core, give_both = proj(pieces_proj[:-2], missing, arrays_proj[:-2], merged)
+    terms = [mine, far(give_x), near(give_core), both(give_both)]
+
+    halves = sorted(pieces_proj[-2:], key=lambda p: p.base)
+    late = call(
+        last_kernel, (*[arrays_proj[p.array] for p in halves], merged),
+        shape(shard_rows[2], windows), name="proj_last",
+    )
+    late = add(late, near(late))
+    return exchange_and_place(
+        pack(got["slots_of"], missing, terms, [late, far(late)]), got["targets"]
+    )
 
 
 def solution(mesh):

time: 139 us -> 145 us (1.043)
  starting transfers between devices: 51.4 us -> 59.7 us
  waiting for transfers between devices: 51.1 us -> 46.8 us
    ppermute x21, starting transfers between devices: 10.4 us -> 31.3 us  [step(): lax.ppermute(to_right, 'wide', self.right)]
    ppermute x21, starting transfers between devices: 31.7 us -> 16.8 us  [step(): lax.ppermute(to_left, 'wide', self.left)]
    ppermute x21, waiting for transfers between devices: 30.2 us -> 23.2 us  [step(): lax.ppermute(to_right, 'wide', self.right)]
    ppermute x21, waiting for transfers between devices: 7.31 us -> 11.8 us  [step(): lax.ppermute(to_left, 'wide', self.left)]
    ppermute x0 -> x1, waiting for transfers between devices: none -> 3.34 us  [both(): return lax.ppermute(x, 'narrow', [(i, i ^ 3) for i in range(parts)])]
    ppermute x7 -> x8, waiting for transfers between devices: 10 us -> 6.93 us  [far(): return lax.ppermute(x, 'narrow', far_pairs)]
    ppermute x13 -> x14, waiting for transfers between devices: 3.6 us -> 1.44 us  [near(): return lax.ppermute(x, 'narrow', near_pairs)]
    ppermute x7 -> x8, starting transfers between devices: 8.47 us -> 9.56 us  [far(): return lax.ppermute(x, 'narrow', far_pairs)]
  transfers between devices with their start and end apart: 62 -> 65, of which waited for: 37 -> 31; matrix products, arithmetic and copies ran while one was open for 0% -> 0% of each run, Pallas kernels for 10% -> 11%
where the time goes in v5:
time: 145 us; the launch traced here: 144 us
  starting transfers between devices  59.7 us (41%)
  waiting for transfers between devices  46.8 us (32%)
  Pallas kernels  17.6 us (12%)
  blocking collectives  16.4 us (11%)
  local copies, waits for them, and re-layouts  3.45 us (2%)
    ppermute x21, starting transfers between devices, step(): lax.ppermute(to_right, 'wide', self.right)  31.3 us
    ppermute x21, waiting for transfers between devices, step(): lax.ppermute(to_right, 'wide', self.right)  23.2 us
    pallas_call x22, Pallas kernels, call(): pl.pallas_call(kernel, out_shape=outs, in_specs=[VMEM] * len(operands), o...  17.6 us
    ppermute x21, starting transfers between devices, step(): lax.ppermute(to_left, 'wide', self.left)  16.8 us
    all_to_all x1, blocking collectives, exchange_and_place(): lax.all_to_all(buffer, 'wide', split_axis=0, concat_axis=0, tiled=True)  16.4 us
    ppermute x21, waiting for transfers between devices, step(): lax.ppermute(to_left, 'wide', self.left)  11.8 us
    ppermute x8, starting transfers between devices, far(): return lax.ppermute(x, 'narrow', far_pairs)  9.56 us
    ppermute x8, waiting for transfers between devices, far(): return lax.ppermute(x, 'narrow', far_pairs)  6.93 us
  transfers between devices with their start and end apart: 65, of which 31 were waited for; matrix products, arithmetic and copies ran while one was open for 0% of the time, Pallas kernels for 11%

profile of v5, /device:TPU:0, one launch (start us, length us, event | category | flops | bytes accessed | tf_op | source)
XLA Modules:
  0.0 144.2 jit_solution(14423128549446368456)
XLA Ops:
  1.1 3.1 %collective-permute-start = (bf16[80,1280]{1,0:T(8,128)(2,1)S(1)}, bf16[80,1280]{1,0:T(8,128)(2,1)S(1)}, u32[]{:S(2)}, u32[]{:S(2)}) collective-permute-start(bf16[80,1280]{1,0:T(8,128)(2,1)S(1)} %get-tuple-element.164.refs_0_), channel_id=1, source_target_pairs={{0,8},{8,16},{16,24},{24,28},{28,20},{20,12},{12,4},{4,0},{1,9},{9... | collective-permute-start | bytes 614408 | tf_op jit(solution)/shard_map/ppermute | solution.py:349
  4.2 2.0 %collective-permute-start.2 = (bf16[80,1280]{1,0:T(8,128)(2,1)S(1)}, bf16[80,1280]{1,0:T(8,128)(2,1)S(1)}, u32[]{:S(2)}, u32[]{:S(2)}) collective-permute-start(bf16[80,1280]{1,0:T(8,128)(2,1)S(1)} %get-tuple-element.163.refs_1_), channel_id=1, source_target_pairs={{0,8},{8,16},{16,24},{24,28},{28,20},{20,12},{12,4},{4,0},{1,9},{9... | collective-permute-start | bytes 614408 | tf_op jit(solution)/shard_map/ppermute | solution.py:349
  8.2 1.6 %collective-permute-start.14 = (bf16[2,320,256]{2,1,0:T(8,128)(2,1)S(1)}, bf16[2,320,256]{2,1,0:T(8,128)(2,1)S(1)}, u32[]{:S(2)}, u32[]{:S(2)}) collective-permute-start(bf16[2,320,256]{2,1,0:T(8,128)(2,1)S(1)} %get-tuple-element.99.own.refs_0_), channel_id=1, source_target_pairs={{0,2},{1,3},{2,0},{3,1},{4,6},{5,7},{6,4},{7,5},{8,10},{9,11},{10,... | collective-permute-start | bytes 983048 | tf_op jit(solution)/shard_map/ppermute | solution.py:389
  10.2 2.0 %collective-permute-start.4 = (bf16[80,1280]{1,0:T(8,128)(2,1)S(1)}, bf16[80,1280]{1,0:T(8,128)(2,1)S(1)}, u32[]{:S(2)}, u32[]{:S(2)}) collective-permute-start(bf16[80,1280]{1,0:T(8,128)(2,1)S(1)} %collective-permute-done.refs_2_), channel_id=1, source_target_pairs={{0,8},{8,16},{16,24},{24,28},{28,20},{20,12},{12,4},{4,0},{1,9},{9... | collective-permute-start | bytes 614408 | tf_op jit(solution)/shard_map/ppermute | solution.py:349
  12.2 2.2 %collective-permute-done.2.refs_4_ = bf16[80,1280]{1,0:T(8,128)(2,1)S(1)} collective-permute-done((bf16[80,1280]{1,0:T(8,128)(2,1)S(1)}, bf16[80,1280]{1,0:T(8,128)(2,1)S(1)}, u32[]{:S(2)}, u32[]{:S(2)}) %collective-permute-start.2) | collective-permute-done | bytes 204832 | tf_op jit(solution)/shard_map/ppermute | solution.py:349
  14.4 3.3 %collective-permute-done.3.refs_5_ = bf16[80,1280]{1,0:T(8,128)(2,1)S(1)} collective-permute-done((bf16[80,1280]{1,0:T(8,128)(2,1)S(1)}, bf16[80,1280]{1,0:T(8,128)(2,1)S(1)}, u32[]{:S(2)}, u32[]{:S(2)}) %collective-permute-start.3) | collective-permute-done | bytes 204832 | tf_op jit(solution)/shard_map/ppermute | solution.py:350
  19.4 2.1 %collective-permute-start.6 = (bf16[80,1280]{1,0:T(8,128)(2,1)S(1)}, bf16[80,1280]{1,0:T(8,128)(2,1)S(1)}, u32[]{:S(2)}, u32[]{:S(2)}) collective-permute-start(bf16[80,1280]{1,0:T(8,128)(2,1)S(1)} %collective-permute-done.2.refs_4_), channel_id=1, source_target_pairs={{0,8},{8,16},{16,24},{24,28},{28,20},{20,12},{12,4},{4,0},{1,9},{9... | collective-permute-start | bytes 614408 | tf_op jit(solution)/shard_map/ppermute | solution.py:349
  22.0 1.6 %collective-permute-start.8 = (bf16[80,1280]{1,0:T(8,128)(2,1)S(1)}, bf16[80,1280]{1,0:T(8,128)(2,1)S(1)}, u32[]{:S(2)}, u32[]{:S(2)}) collective-permute-start(bf16[80,1280]{1,0:T(8,128)(2,1)S(1)} %collective-permute-done.4.refs_6_), channel_id=1, source_target_pairs={{0,8},{8,16},{16,24},{24,28},{28,20},{20,12},{12,4},{4,0},{1,9},{9... | collective-permute-start | bytes 614408 | tf_op jit(solution)/shard_map/ppermute | solution.py:349
  25.8 2.5 %collective-permute-start.10 = (bf16[80,1280]{1,0:T(8,128)(2,1)S(1)}, bf16[80,1280]{1,0:T(8,128)(2,1)S(1)}, u32[]{:S(2)}, u32[]{:S(2)}) collective-permute-start(bf16[80,1280]{1,0:T(8,128)(2,1)S(1)} %collective-permute-done.6.refs_8_), channel_id=1, source_target_pairs={{0,8},{8,16},{16,24},{24,28},{28,20},{20,12},{12,4},{4,0},{1,9},{9... | collective-permute-start | bytes 614408 | tf_op jit(solution)/shard_map/ppermute | solution.py:349
  30.3 1.6 %collective-permute-start.11 = (bf16[80,1280]{1,0:T(8,128)(2,1)S(1)}, bf16[80,1280]{1,0:T(8,128)(2,1)S(1)}, u32[]{:S(2)}, u32[]{:S(2)}) collective-permute-start(bf16[80,1280]{1,0:T(8,128)(2,1)S(1)} %collective-permute-done.7.refs_9_), channel_id=1, source_target_pairs={{8,0},{16,8},{24,16},{28,24},{20,28},{12,20},{4,12},{0,4},{9,1},{1... | collective-permute-start | bytes 614408 | tf_op jit(solution)/shard_map/ppermute | solution.py:350
  31.9 3.0 %collective-permute-done.10.refs_12_ = bf16[80,1280]{1,0:T(8,128)(2,1)S(1)} collective-permute-done((bf16[80,1280]{1,0:T(8,128)(2,1)S(1)}, bf16[80,1280]{1,0:T(8,128)(2,1)S(1)}, u32[]{:S(2)}, u32[]{:S(2)}) %collective-permute-start.10) | collective-permute-done | bytes 204832 | tf_op jit(solution)/shard_map/ppermute | solution.py:349
  37.0 1.4 norm.2.refs_16_
  71.3 3.4 %collective-permute-done.31.refs_20_ = bf16[80,1280]{1,0:T(8,128)(2,1)S(1)} collective-permute-done((bf16[80,1280]{1,0:T(8,128)(2,1)S(1)}, bf16[80,1280]{1,0:T(8,128)(2,1)S(1)}, u32[]{:S(2)}, u32[]{:S(2)}) %collective-permute-start.31) | collective-permute-done | bytes 204832 | tf_op jit(solution)/shard_map/ppermute | solution.py:350
  74.8 2.3 %mlp_out.2 = (bf16[320,256]{1,0:T(8,128)(2,1)S(1)}, bf16[320,256]{1,0:T(8,128)(2,1)S(1)}, bf16[320,256]{1,0:T(8,128)(2,1)S(1)}, bf16[320,256]{1,0:T(8,128)(2,1)S...) custom-call(bf16[1024,256]{1,0:T(8,128)(2,1)S(1)} %hidden.5.refs_0_,, ...), custom_call_target="tpu_custom_call" | custom-call | tf_op jit(solution)/shard_map/mlp_out/pallas_call | solution.py:20
  79.3 1.8 %collective-permute-start.35 = (bf16[80,1280]{1,0:T(8,128)(2,1)S(1)}, bf16[80,1280]{1,0:T(8,128)(2,1)S(1)}, u32[]{:S(2)}, u32[]{:S(2)}) collective-permute-start(bf16[80,1280]{1,0:T(8,128)(2,1)S(1)} %collective-permute-done.28.refs_2_), channel_id=1, source_target_pairs={{0,8},{8,16},{16,24},{24,28},{28,20},{20,12},{12,4},{4,0},{1,9},{9... | collective-permute-start | bytes 614408 | tf_op jit(solution)/shard_map/ppermute | solution.py:349
  81.4 3.7 %collective-permute-done.50.refs_4_ = bf16[80,1280]{1,0:T(8,128)(2,1)S(1)} collective-permute-done((bf16[80,1280]{1,0:T(8,128)(2,1)S(1)}, bf16[80,1280]{1,0:T(8,128)(2,1)S(1)}, u32[]{:S(2)}, u32[]{:S(2)}) %collective-permute-start.50) | collective-permute-done | bytes 204832 | tf_op jit(solution)/shard_map/ppermute | solution.py:349
  85.2 1.5 %collective-permute-done.51.refs_5_ = bf16[80,1280]{1,0:T(8,128)(2,1)S(1)} collective-permute-done((bf16[80,1280]{1,0:T(8,128)(2,1)S(1)}, bf16[80,1280]{1,0:T(8,128)(2,1)S(1)}, u32[]{:S(2)}, u32[]{:S(2)}) %collective-permute-start.51) | collective-permute-done | bytes 204832 | tf_op jit(solution)/shard_map/ppermute | solution.py:350
  86.7 1.5 %collective-permute-start.45 = (bf16[320,256]{1,0:T(8,128)(2,1)S(1)}, bf16[320,256]{1,0:T(8,128)(2,1)S(1)}, u32[]{:S(2)}, u32[]{:S(2)}) collective-permute-start(bf16[320,256]{1,0:T(8,128)(2,1)S(1)} %add.6), channel_id=1, source_target_pairs={{0,2},{1,3},{2,0},{3,1},{4,6},{5,7},{6,4},{7,5},{8,10},{9,11},{10,... | collective-permute-start | bytes 491528 | tf_op jit(solution)/shard_map/ppermute | solution.py:389
  89.1 1.6 %collective-permute-start.53 = (bf16[80,1280]{1,0:T(8,128)(2,1)S(1)}, bf16[80,1280]{1,0:T(8,128)(2,1)S(1)}, u32[]{:S(2)}, u32[]{:S(2)}) collective-permute-start(bf16[80,1280]{1,0:T(8,128)(2,1)S(1)} %collective-permute-done.51.refs_5_), channel_id=1, source_target_pairs={{8,0},{16,8},{24,16},{28,24},{20,28},{12,20},{4,12},{0,4},{9,1},{1... | collective-permute-start | bytes 614408 | tf_op jit(solution)/shard_map/ppermute | solution.py:350
  91.1 1.6 %collective-permute-start.54 = (bf16[80,1280]{1,0:T(8,128)(2,1)S(1)}, bf16[80,1280]{1,0:T(8,128)(2,1)S(1)}, u32[]{:S(2)}, u32[]{:S(2)}) collective-permute-start(bf16[80,1280]{1,0:T(8,128)(2,1)S(1)} %collective-permute-done.35.refs_6_), channel_id=1, source_target_pairs={{0,8},{8,16},{16,24},{24,28},{28,20},{20,12},{12,4},{4,0},{1,9},{9... | collective-permute-start | bytes 614408 | tf_op jit(solution)/shard_map/ppermute | solution.py:349
  93.1 1.7 %collective-permute-start.43 = (bf16[320,256]{1,0:T(8,128)(2,1)S(1)}, bf16[320,256]{1,0:T(8,128)(2,1)S(1)}, u32[]{:S(2)}, u32[]{:S(2)}) collective-permute-start(bf16[320,256]{1,0:T(8,128)(2,1)S(1)} %add.5), channel_id=1, source_target_pairs={{0,2},{1,3},{2,0},{3,1},{4,6},{5,7},{6,4},{7,5},{8,10},{9,11},{10,... | collective-permute-start | bytes 491528 | tf_op jit(solution)/shard_map/ppermute | solution.py:389
  95.0 3.5 %collective-permute-done.43.refs_10_ = bf16[320,256]{1,0:T(8,128)(2,1)S(1)} collective-permute-done((bf16[320,256]{1,0:T(8,128)(2,1)S(1)}, bf16[320,256]{1,0:T(8,128)(2,1)S(1)}, u32[]{:S(2)}, u32[]{:S(2)}) %collective-permute-start.43) | collective-permute-done | bytes 163872 | tf_op jit(solution)/shard_map/ppermute | solution.py:389
  98.4 1.7 %collective-permute-start.47 = (bf16[320,256]{1,0:T(8,128)(2,1)S(1)}, bf16[320,256]{1,0:T(8,128)(2,1)S(1)}, u32[]{:S(2)}, u32[]{:S(2)}) collective-permute-start(bf16[320,256]{1,0:T(8,128)(2,1)S(1)} %add.7), channel_id=1, source_target_pairs={{0,2},{1,3},{2,0},{3,1},{4,6},{5,7},{6,4},{7,5},{8,10},{9,11},{10,... | collective-permute-start | bytes 491528 | tf_op jit(solution)/shard_map/ppermute | solution.py:389
  100.5 2.2 %mlp_out.3 = (bf16[320,256]{1,0:T(8,128)(2,1)S(1)}, bf16[320,256]{1,0:T(8,128)(2,1)S(1)}, bf16[320,256]{1,0:T(8,128)(2,1)S(1)}, bf16[320,256]{1,0:T(8,128)(2,1)S...) custom-call(bf16[1024,256]{1,0:T(8,128)(2,1)S(1)} %hidden.5.refs_0_,, ...), custom_call_target="tpu_custom_call" | custom-call | tf_op jit(solution)/shard_map/mlp_out/pallas_call | solution.py:20
  104.2 1.5 %collective-permute-start.57 = (bf16[80,1280]{1,0:T(8,128)(2,1)S(1)}, bf16[80,1280]{1,0:T(8,128)(2,1)S(1)}, u32[]{:S(2)}, u32[]{:S(2)}) collective-permute-start(bf16[80,1280]{1,0:T(8,128)(2,1)S(1)} %collective-permute-done.53.refs_9_), channel_id=1, source_target_pairs={{8,0},{16,8},{24,16},{28,24},{20,28},{12,20},{4,12},{0,4},{9,1},{1... | collective-permute-start | bytes 614408 | tf_op jit(solution)/shard_map/ppermute | solution.py:350
  105.9 1.8 %collective-permute-start.56 = (bf16[80,1280]{1,0:T(8,128)(2,1)S(1)}, bf16[80,1280]{1,0:T(8,128)(2,1)S(1)}, u32[]{:S(2)}, u32[]{:S(2)}) collective-permute-start(bf16[80,1280]{1,0:T(8,128)(2,1)S(1)} %collective-permute-done.52.refs_8_), channel_id=1, source_target_pairs={{0,8},{8,16},{16,24},{24,28},{28,20},{20,12},{12,4},{4,0},{1,9},{9... | collective-permute-start | bytes 614408 | tf_op jit(solution)/shard_map/ppermute | solution.py:349
  107.8 1.7 %collective-permute-start.61 = (bf16[80,1280]{1,0:T(8,128)(2,1)S(1)}, bf16[80,1280]{1,0:T(8,128)(2,1)S(1)}, u32[]{:S(2)}, u32[]{:S(2)}) collective-permute-start(bf16[80,1280]{1,0:T(8,128)(2,1)S(1)} %collective-permute-done.54.refs_10_), channel_id=1, source_target_pairs={{0,8},{8,16},{16,24},{24,28},{28,20},{20,12},{12,4},{4,0},{1,9},{9... | collective-permute-start | bytes 614408 | tf_op jit(solution)/shard_map/ppermute | solution.py:349
  112.0 2.0 %collective-permute-done.56.refs_12_ = bf16[80,1280]{1,0:T(8,128)(2,1)S(1)} collective-permute-done((bf16[80,1280]{1,0:T(8,128)(2,1)S(1)}, bf16[80,1280]{1,0:T(8,128)(2,1)S(1)}, u32[]{:S(2)}, u32[]{:S(2)}) %collective-permute-start.56) | collective-permute-done | bytes 204832 | tf_op jit(solution)/shard_map/ppermute | solution.py:349
  115.3 1.6 %collective-permute-start.58 = (bf16[320,256]{1,0:T(8,128)(2,1)S(1)}, bf16[320,256]{1,0:T(8,128)(2,1)S(1)}, u32[]{:S(2)}, u32[]{:S(2)}) collective-permute-start(bf16[320,256]{1,0:T(8,128)(2,1)S(1)} %get-tuple-element.158), channel_id=1, source_target_pairs={{0,2},{1,3},{2,0},{3,1},{4,6},{5,7},{6,4},{7,5},{8,10},{9,11},{10,... | collective-permute-start | bytes 491528 | tf_op jit(solution)/shard_map/ppermute | solution.py:389
  120.7 3.3 %collective-permute-done.60.refs_3_ = bf16[320,256]{1,0:T(8,128)(2,1)S(1)} collective-permute-done((bf16[320,256]{1,0:T(8,128)(2,1)S(1)}, bf16[320,256]{1,0:T(8,128)(2,1)S(1)}, u32[]{:S(2)}, u32[]{:S(2)}) %collective-permute-start.60) | collective-permute-done | bytes 163872 | tf_op jit(solution)/shard_map/ppermute | solution.py:392
  124.0 2.0 %collective-permute-done.64.refs_5_ = bf16[160,256]{1,0:T(8,128)(2,1)S(1)} collective-permute-done((bf16[160,256]{1,0:T(8,128)(2,1)S(1)}, bf16[160,256]{1,0:T(8,128)(2,1)S(1)}, u32[]{:S(2)}, u32[]{:S(2)}) %collective-permute-start.64) | collective-permute-done | bytes 81952 | tf_op jit(solution)/shard_map/ppermute | solution.py:389
  126.6 16.4 %all_to_all.5.arrived = bf16[8,160,128]{2,1,0:T(8,128)(2,1)S(1)} all-to-all(bf16[8,160,128]{2,1,0:T(8,128)(2,1)S(1)} %pack.1), channel_id=1, replica_groups=mesh['wide'=8,'narrow'=4] {'wide'}, dimensions={0} | all-to-all | bytes 655360 | tf_op jit(solution)/shard_map/all_to_all | solution.py:466
  (148 shorter events, 60.6 us)
Async XLA Ops:
  1.1 9.1 %collective-permute-start = (bf16[80,1280]{1,0:T(8,128)(2,1)S(1)}, bf16[80,1280]{1,0:T(8,128)(2,1)S(1)}, u32[]{:S(2)}, u32[]{:S(2)}) collective-permute-start(bf16[80,1280]{1,0:T(8,128)(2,1)S(1)} %get-tuple-element.164.refs_0_), channel_id=1, source_target_pairs={{0,8},{8,16},{16,24},{24,28},{28,20},{20,12},{12,4},{4,0},{1,9},{9... | collective-permute-start | bytes 614408 | tf_op jit(solution)/shard_map/ppermute | solution.py:349
  4.2 10.2 %collective-permute-start.2 = (bf16[80,1280]{1,0:T(8,128)(2,1)S(1)}, bf16[80,1280]{1,0:T(8,128)(2,1)S(1)}, u32[]{:S(2)}, u32[]{:S(2)}) collective-permute-start(bf16[80,1280]{1,0:T(8,128)(2,1)S(1)} %get-tuple-element.163.refs_1_), channel_id=1, source_target_pairs={{0,8},{8,16},{16,24},{24,28},{28,20},{20,12},{12,4},{4,0},{1,9},{9... | collective-permute-start | bytes 614408 | tf_op jit(solution)/shard_map/ppermute | solution.py:349
  8.2 11.3 %collective-permute-start.14 = (bf16[2,320,256]{2,1,0:T(8,128)(2,1)S(1)}, bf16[2,320,256]{2,1,0:T(8,128)(2,1)S(1)}, u32[]{:S(2)}, u32[]{:S(2)}) collective-permute-start(bf16[2,320,256]{2,1,0:T(8,128)(2,1)S(1)} %get-tuple-element.99.own.refs_0_), channel_id=1, source_target_pairs={{0,2},{1,3},{2,0},{3,1},{4,6},{5,7},{6,4},{7,5},{8,10},{9,11},{10,... | collective-permute-start | bytes 983048 | tf_op jit(solution)/shard_map/ppermute | solution.py:389
  10.2 11.3 %collective-permute-start.4 = (bf16[80,1280]{1,0:T(8,128)(2,1)S(1)}, bf16[80,1280]{1,0:T(8,128)(2,1)S(1)}, u32[]{:S(2)}, u32[]{:S(2)}) collective-permute-start(bf16[80,1280]{1,0:T(8,128)(2,1)S(1)} %collective-permute-done.refs_2_), channel_id=1, source_target_pairs={{0,8},{8,16},{16,24},{24,28},{28,20},{20,12},{12,4},{4,0},{1,9},{9... | collective-permute-start | bytes 614408 | tf_op jit(solution)/shard_map/ppermute | solution.py:349
  12.2 9.8 %collective-permute-start.5 = (bf16[80,1280]{1,0:T(8,128)(2,1)S(1)}, bf16[80,1280]{1,0:T(8,128)(2,1)S(1)}, u32[]{:S(2)}, u32[]{:S(2)}) collective-permute-start(bf16[80,1280]{1,0:T(8,128)(2,1)S(1)} %collective-permute-done.1.refs_3_), channel_id=1, source_target_pairs={{8,0},{16,8},{24,16},{28,24},{20,28},{12,20},{4,12},{0,4},{9,1},{1... | collective-permute-start | bytes 614408 | tf_op jit(solution)/shard_map/ppermute | solution.py:350
  21.5 8.8 %collective-permute-start.15 = (bf16[2,320,256]{2,1,0:T(8,128)(2,1)S(1)}, bf16[2,320,256]{2,1,0:T(8,128)(2,1)S(1)}, u32[]{:S(2)}, u32[]{:S(2)}) collective-permute-start(bf16[2,320,256]{2,1,0:T(8,128)(2,1)S(1)} %get-tuple-element.99.own.refs_0_), channel_id=1, source_target_pairs={{0,1},{1,0},{2,3},{3,2},{4,5},{5,4},{6,7},{7,6},{8,9},{9,8},{10,11... | collective-permute-start | bytes 983048 | tf_op jit(solution)/shard_map/ppermute | solution.py:386
  25.8 10.2 %collective-permute-start.16 = (bf16[2,320,256]{2,1,0:T(8,128)(2,1)S(1)}, bf16[2,320,256]{2,1,0:T(8,128)(2,1)S(1)}, u32[]{:S(2)}, u32[]{:S(2)}) collective-permute-start(bf16[2,320,256]{2,1,0:T(8,128)(2,1)S(1)} %collective-permute-done.14.over_x), channel_id=1, source_target_pairs={{0,1},{1,0},{2,3},{3,2},{4,5},{5,4},{6,7},{7,6},{8,9},{9,8},{10,11... | collective-permute-start | bytes 983048 | tf_op jit(solution)/shard_map/ppermute | solution.py:386
  25.8 9.2 %collective-permute-start.10 = (bf16[80,1280]{1,0:T(8,128)(2,1)S(1)}, bf16[80,1280]{1,0:T(8,128)(2,1)S(1)}, u32[]{:S(2)}, u32[]{:S(2)}) collective-permute-start(bf16[80,1280]{1,0:T(8,128)(2,1)S(1)} %collective-permute-done.6.refs_8_), channel_id=1, source_target_pairs={{0,8},{8,16},{16,24},{24,28},{28,20},{20,12},{12,4},{4,0},{1,9},{9... | collective-permute-start | bytes 614408 | tf_op jit(solution)/shard_map/ppermute | solution.py:349
  29.6 9.9 %collective-permute-start.18 = (bf16[2,320,256]{2,1,0:T(8,128)(2,1)S(1)}, bf16[2,320,256]{2,1,0:T(8,128)(2,1)S(1)}, u32[]{:S(2)}, u32[]{:S(2)}) collective-permute-start(bf16[2,320,256]{2,1,0:T(8,128)(2,1)S(1)} %get-tuple-element.103.own.refs_1_), channel_id=1, source_target_pairs={{0,1},{1,0},{2,3},{3,2},{4,5},{5,4},{6,7},{7,6},{8,9},{9,8},{10,11... | collective-permute-start | bytes 983048 | tf_op jit(solution)/shard_map/ppermute | solution.py:386
  30.3 10.2 %collective-permute-start.19 = (bf16[2,320,256]{2,1,0:T(8,128)(2,1)S(1)}, bf16[2,320,256]{2,1,0:T(8,128)(2,1)S(1)}, u32[]{:S(2)}, u32[]{:S(2)}) collective-permute-start(bf16[2,320,256]{2,1,0:T(8,128)(2,1)S(1)} %collective-permute-done.17.over_x), channel_id=1, source_target_pairs={{0,1},{1,0},{2,3},{3,2},{4,5},{5,4},{6,7},{7,6},{8,9},{9,8},{10,11... | collective-permute-start | bytes 983048 | tf_op jit(solution)/shard_map/ppermute | solution.py:386
  38.5 8.9 %collective-permute-start.22 = (bf16[80,1280]{1,0:T(8,128)(2,1)S(1)}, bf16[80,1280]{1,0:T(8,128)(2,1)S(1)}, u32[]{:S(2)}, u32[]{:S(2)}) collective-permute-start(bf16[80,1280]{1,0:T(8,128)(2,1)S(1)} %get-tuple-element.118.refs_5_), channel_id=1, source_target_pairs={{0,8},{8,16},{16,24},{24,28},{28,20},{20,12},{12,4},{4,0},{1,9},{9... | collective-permute-start | bytes 614408 | tf_op jit(solution)/shard_map/ppermute | solution.py:349
  39.6 8.9 %collective-permute-start.21 = (bf16[80,1280]{1,0:T(8,128)(2,1)S(1)}, bf16[80,1280]{1,0:T(8,128)(2,1)S(1)}, u32[]{:S(2)}, u32[]{:S(2)}) collective-permute-start(bf16[80,1280]{1,0:T(8,128)(2,1)S(1)} %get-tuple-element.108.refs_6_), channel_id=1, source_target_pairs={{8,0},{16,8},{24,16},{28,24},{20,28},{12,20},{4,12},{0,4},{9,1},{1... | collective-permute-start | bytes 614408 | tf_op jit(solution)/shard_map/ppermute | solution.py:350
  42.9 8.8 %collective-permute-start.20 = (bf16[80,1280]{1,0:T(8,128)(2,1)S(1)}, bf16[80,1280]{1,0:T(8,128)(2,1)S(1)}, u32[]{:S(2)}, u32[]{:S(2)}) collective-permute-start(bf16[80,1280]{1,0:T(8,128)(2,1)S(1)} %get-tuple-element.108.refs_6_), channel_id=1, source_target_pairs={{0,8},{8,16},{16,24},{24,28},{28,20},{20,12},{12,4},{4,0},{1,9},{9... | collective-permute-start | bytes 614408 | tf_op jit(solution)/shard_map/ppermute | solution.py:349
  44.0 8.8 %collective-permute-start.29 = (bf16[80,1280]{1,0:T(8,128)(2,1)S(1)}, bf16[80,1280]{1,0:T(8,128)(2,1)S(1)}, u32[]{:S(2)}, u32[]{:S(2)}) collective-permute-start(bf16[80,1280]{1,0:T(8,128)(2,1)S(1)} %get-tuple-element.118.refs_5_), channel_id=1, source_target_pairs={{8,0},{16,8},{24,16},{28,24},{20,28},{12,20},{4,12},{0,4},{9,1},{1... | collective-permute-start | bytes 614408 | tf_op jit(solution)/shard_map/ppermute | solution.py:350
  47.3 8.8 %collective-permute-start.25 = (bf16[80,1280]{1,0:T(8,128)(2,1)S(1)}, bf16[80,1280]{1,0:T(8,128)(2,1)S(1)}, u32[]{:S(2)}, u32[]{:S(2)}) collective-permute-start(bf16[80,1280]{1,0:T(8,128)(2,1)S(1)} %collective-permute-done.22.refs_7_), channel_id=1, source_target_pairs={{0,8},{8,16},{16,24},{24,28},{28,20},{20,12},{12,4},{4,0},{1,9},{9... | collective-permute-start | bytes 614408 | tf_op jit(solution)/shard_map/ppermute | solution.py:349
  48.4 8.8 %collective-permute-start.24 = (bf16[80,1280]{1,0:T(8,128)(2,1)S(1)}, bf16[80,1280]{1,0:T(8,128)(2,1)S(1)}, u32[]{:S(2)}, u32[]{:S(2)}) collective-permute-start(bf16[80,1280]{1,0:T(8,128)(2,1)S(1)} %collective-permute-done.21.refs_8_), channel_id=1, source_target_pairs={{8,0},{16,8},{24,16},{28,24},{20,28},{12,20},{4,12},{0,4},{9,1},{1... | collective-permute-start | bytes 614408 | tf_op jit(solution)/shard_map/ppermute | solution.py:350
  51.7 8.8 %collective-permute-start.23 = (bf16[80,1280]{1,0:T(8,128)(2,1)S(1)}, bf16[80,1280]{1,0:T(8,128)(2,1)S(1)}, u32[]{:S(2)}, u32[]{:S(2)}) collective-permute-start(bf16[80,1280]{1,0:T(8,128)(2,1)S(1)} %collective-permute-done.20.refs_9_), channel_id=1, source_target_pairs={{0,8},{8,16},{16,24},{24,28},{28,20},{20,12},{12,4},{4,0},{1,9},{9... | collective-permute-start | bytes 614408 | tf_op jit(solution)/shard_map/ppermute | solution.py:349
  52.8 8.8 %collective-permute-start.32 = (bf16[80,1280]{1,0:T(8,128)(2,1)S(1)}, bf16[80,1280]{1,0:T(8,128)(2,1)S(1)}, u32[]{:S(2)}, u32[]{:S(2)}) collective-permute-start(bf16[80,1280]{1,0:T(8,128)(2,1)S(1)} %collective-permute-done.29.refs_10_), channel_id=1, source_target_pairs={{8,0},{16,8},{24,16},{28,24},{20,28},{12,20},{4,12},{0,4},{9,1},{1... | collective-permute-start | bytes 614408 | tf_op jit(solution)/shard_map/ppermute | solution.py:350
  56.1 8.8 %collective-permute-start.30 = (bf16[80,1280]{1,0:T(8,128)(2,1)S(1)}, bf16[80,1280]{1,0:T(8,128)(2,1)S(1)}, u32[]{:S(2)}, u32[]{:S(2)}) collective-permute-start(bf16[80,1280]{1,0:T(8,128)(2,1)S(1)} %collective-permute-done.25.refs_11_), channel_id=1, source_target_pairs={{0,8},{8,16},{16,24},{24,28},{28,20},{20,12},{12,4},{4,0},{1,9},{9... | collective-permute-start | bytes 614408 | tf_op jit(solution)/shard_map/ppermute | solution.py:349
  57.2 8.8 %collective-permute-start.27 = (bf16[80,1280]{1,0:T(8,128)(2,1)S(1)}, bf16[80,1280]{1,0:T(8,128)(2,1)S(1)}, u32[]{:S(2)}, u32[]{:S(2)}) collective-permute-start(bf16[80,1280]{1,0:T(8,128)(2,1)S(1)} %collective-permute-done.24.refs_12_), channel_id=1, source_target_pairs={{8,0},{16,8},{24,16},{28,24},{20,28},{12,20},{4,12},{0,4},{9,1},{1... | collective-permute-start | bytes 614408 | tf_op jit(solution)/shard_map/ppermute | solution.py:350
  60.5 8.8 %collective-permute-start.26 = (bf16[80,1280]{1,0:T(8,128)(2,1)S(1)}, bf16[80,1280]{1,0:T(8,128)(2,1)S(1)}, u32[]{:S(2)}, u32[]{:S(2)}) collective-permute-start(bf16[80,1280]{1,0:T(8,128)(2,1)S(1)} %collective-permute-done.23.refs_13_), channel_id=1, source_target_pairs={{0,8},{8,16},{16,24},{24,28},{28,20},{20,12},{12,4},{4,0},{1,9},{9... | collective-permute-start | bytes 614408 | tf_op jit(solution)/shard_map/ppermute | solution.py:349
  61.6 8.8 %collective-permute-start.34 = (bf16[80,1280]{1,0:T(8,128)(2,1)S(1)}, bf16[80,1280]{1,0:T(8,128)(2,1)S(1)}, u32[]{:S(2)}, u32[]{:S(2)}) collective-permute-start(bf16[80,1280]{1,0:T(8,128)(2,1)S(1)} %collective-permute-done.32.refs_14_), channel_id=1, source_target_pairs={{8,0},{16,8},{24,16},{28,24},{20,28},{12,20},{4,12},{0,4},{9,1},{1... | collective-permute-start | bytes 614408 | tf_op jit(solution)/shard_map/ppermute | solution.py:350
  69.3 10.0 %collective-permute-start.28 = (bf16[80,1280]{1,0:T(8,128)(2,1)S(1)}, bf16[80,1280]{1,0:T(8,128)(2,1)S(1)}, u32[]{:S(2)}, u32[]{:S(2)}) collective-permute-start(bf16[80,1280]{1,0:T(8,128)(2,1)S(1)} %get-tuple-element.150.refs_0_), channel_id=1, source_target_pairs={{0,8},{8,16},{16,24},{24,28},{28,20},{20,12},{12,4},{4,0},{1,9},{9... | collective-permute-start | bytes 614408 | tf_op jit(solution)/shard_map/ppermute | solution.py:349
  70.4 8.9 %collective-permute-start.36 = (bf16[80,1280]{1,0:T(8,128)(2,1)S(1)}, bf16[80,1280]{1,0:T(8,128)(2,1)S(1)}, u32[]{:S(2)}, u32[]{:S(2)}) collective-permute-start(bf16[80,1280]{1,0:T(8,128)(2,1)S(1)} %get-tuple-element.149.refs_1_), channel_id=1, source_target_pairs={{8,0},{16,8},{24,16},{28,24},{20,28},{12,20},{4,12},{0,4},{9,1},{1... | collective-permute-start | bytes 614408 | tf_op jit(solution)/shard_map/ppermute | solution.py:350
  79.3 9.8 %collective-permute-start.35 = (bf16[80,1280]{1,0:T(8,128)(2,1)S(1)}, bf16[80,1280]{1,0:T(8,128)(2,1)S(1)}, u32[]{:S(2)}, u32[]{:S(2)}) collective-permute-start(bf16[80,1280]{1,0:T(8,128)(2,1)S(1)} %collective-permute-done.28.refs_2_), channel_id=1, source_target_pairs={{0,8},{8,16},{16,24},{24,28},{28,20},{20,12},{12,4},{4,0},{1,9},{9... | collective-permute-start | bytes 614408 | tf_op jit(solution)/shard_map/ppermute | solution.py:349
  81.0 10.1 %collective-permute-start.37 = (bf16[80,1280]{1,0:T(8,128)(2,1)S(1)}, bf16[80,1280]{1,0:T(8,128)(2,1)S(1)}, u32[]{:S(2)}, u32[]{:S(2)}) collective-permute-start(bf16[80,1280]{1,0:T(8,128)(2,1)S(1)} %collective-permute-done.36.refs_3_), channel_id=1, source_target_pairs={{8,0},{16,8},{24,16},{28,24},{20,28},{12,20},{4,12},{0,4},{9,1},{1... | collective-permute-start | bytes 614408 | tf_op jit(solution)/shard_map/ppermute | solution.py:350
  81.4 9.3 %collective-permute-start.46 = (bf16[320,256]{1,0:T(8,128)(2,1)S(1)}, bf16[320,256]{1,0:T(8,128)(2,1)S(1)}, u32[]{:S(2)}, u32[]{:S(2)}) collective-permute-start(bf16[320,256]{1,0:T(8,128)(2,1)S(1)} %get-tuple-element.146), channel_id=1, source_target_pairs={{0,1},{1,0},{2,3},{3,2},{4,5},{5,4},{6,7},{7,6},{8,9},{9,8},{10,11... | collective-permute-start | bytes 491528 | tf_op jit(solution)/shard_map/ppermute | solution.py:386
  89.1 11.1 %collective-permute-start.53 = (bf16[80,1280]{1,0:T(8,128)(2,1)S(1)}, bf16[80,1280]{1,0:T(8,128)(2,1)S(1)}, u32[]{:S(2)}, u32[]{:S(2)}) collective-permute-start(bf16[80,1280]{1,0:T(8,128)(2,1)S(1)} %collective-permute-done.51.refs_5_), channel_id=1, source_target_pairs={{8,0},{16,8},{24,16},{28,24},{20,28},{12,20},{4,12},{0,4},{9,1},{1... | collective-permute-start | bytes 614408 | tf_op jit(solution)/shard_map/ppermute | solution.py:350
  90.7 12.0 %collective-permute-start.52 = (bf16[80,1280]{1,0:T(8,128)(2,1)S(1)}, bf16[80,1280]{1,0:T(8,128)(2,1)S(1)}, u32[]{:S(2)}, u32[]{:S(2)}) collective-permute-start(bf16[80,1280]{1,0:T(8,128)(2,1)S(1)} %collective-permute-done.50.refs_4_), channel_id=1, source_target_pairs={{0,8},{8,16},{16,24},{24,28},{28,20},{20,12},{12,4},{4,0},{1,9},{9... | collective-permute-start | bytes 614408 | tf_op jit(solution)/shard_map/ppermute | solution.py:349
  91.1 11.7 %collective-permute-start.54 = (bf16[80,1280]{1,0:T(8,128)(2,1)S(1)}, bf16[80,1280]{1,0:T(8,128)(2,1)S(1)}, u32[]{:S(2)}, u32[]{:S(2)}) collective-permute-start(bf16[80,1280]{1,0:T(8,128)(2,1)S(1)} %collective-permute-done.35.refs_6_), channel_id=1, source_target_pairs={{0,8},{8,16},{16,24},{24,28},{28,20},{20,12},{12,4},{4,0},{1,9},{9... | collective-permute-start | bytes 614408 | tf_op jit(solution)/shard_map/ppermute | solution.py:349
  92.7 10.6 %collective-permute-start.55 = (bf16[80,1280]{1,0:T(8,128)(2,1)S(1)}, bf16[80,1280]{1,0:T(8,128)(2,1)S(1)}, u32[]{:S(2)}, u32[]{:S(2)}) collective-permute-start(bf16[80,1280]{1,0:T(8,128)(2,1)S(1)} %collective-permute-done.37.refs_7_), channel_id=1, source_target_pairs={{8,0},{16,8},{24,16},{28,24},{20,28},{12,20},{4,12},{0,4},{9,1},{1... | collective-permute-start | bytes 614408 | tf_op jit(solution)/shard_map/ppermute | solution.py:350
  107.8 9.2 %collective-permute-start.61 = (bf16[80,1280]{1,0:T(8,128)(2,1)S(1)}, bf16[80,1280]{1,0:T(8,128)(2,1)S(1)}, u32[]{:S(2)}, u32[]{:S(2)}) collective-permute-start(bf16[80,1280]{1,0:T(8,128)(2,1)S(1)} %collective-permute-done.54.refs_10_), channel_id=1, source_target_pairs={{0,8},{8,16},{16,24},{24,28},{28,20},{20,12},{12,4},{4,0},{1,9},{9... | collective-permute-start | bytes 614408 | tf_op jit(solution)/shard_map/ppermute | solution.py:349
  (43 other events, 360.7 us)

commit v6 on v4

--- a/solution.py
+++ b/solution.py
@@ -10,7 +10,12 @@
 F32 = jnp.float32
 BF16 = jnp.bfloat16
 WINDOW = 4
-LATE = (1, 2, 3)
+NORM_AT = 5
+HIDDEN_AT = 0
+SUMS = 2
+ADD_LATE = (1, 1)
+LATE = ()
+OWN_AT = 2
 VMEM = pl.BlockSpec(memory_space=pltpu.VMEM)
 
 
@@ -57,13 +62,15 @@
             return self.index * self.rows
         return ring_owner(lax.axis_index("wide"), self.shift, count) * shard_rows + self.base
 
+    def block(self, count, shard_rows, block):
+        if self.shift is None:
+            return self.index, 0
+        owner = ring_owner(lax.axis_index("wide"), self.shift, count)
+        per_block = block // shard_rows
+        return owner // per_block, (owner % per_block) * shard_rows + self.base
+
     def block_row(self, count, shard_rows, block):
-        if self.shift is None:
-            of, inside = self.index, 0
-        else:
-            owner = ring_owner(lax.axis_index("wide"), self.shift, count)
-            per_block = block // shard_rows
-            of, inside = owner // per_block, (owner % per_block) * shard_rows + self.base
+        of, inside = self.block(count, shard_rows, block)
         mine = lax.axis_index("narrow")
         over_x = jnp.where(of // 2 == mine // 2, 0, 1)
         over_core = jnp.where(of % 2 == mine % 2, 0, 1)
@@ -74,17 +81,14 @@
     return pl.ds(pl.multiple_of(start, 16), rows)
 
 
-def order_kernel(x_ref, *outs):
+def order_kernel(x_ref, o_ref):
     tokens = x_ref.shape[1]
     windows = tokens // WINDOW
     source = lax.broadcasted_iota(jnp.int32, (tokens, windows), 0)
     window = lax.broadcasted_iota(jnp.int32, (tokens, windows), 1)
-    each = WINDOW // len(outs)
     for p in range(WINDOW):
         pick = jnp.where(source == WINDOW * window + p, 1.0, 0.0).astype(BF16)
-        outs[p // each][p % each] = jnp.dot(
-            x_ref[...], pick, preferred_element_type=F32
-        ).astype(BF16)
+        o_ref[p] = jnp.dot(x_ref[...], pick, preferred_element_type=F32).astype(BF16)
 
 
 def shards_kernel(w_out, w_proj, *outs):
@@ -130,16 +134,14 @@
     slots_of[...] = jnp.where(mine >= 0, mine * bucket + rank - 1, groups * bucket)
 
 
-def norm_kernel(own, over_x, over_core, over_both, gain, bias, o_ref, whole):
-    parts = (own, over_x, over_core, over_both)
-    each, rows, windows = own.shape
-    tokens = each * windows
-    mine = lax.axis_index("narrow")
-    for part, flip in zip(parts, (0, 2, 1, 3)):
-        at = (mine ^ flip) * rows
-        for j in range(each):
-            whole[rows_at(at, rows), j * windows : (j + 1) * windows] = part[j]
-    width = whole.shape[0]
+def norm_kernel(first, each, blocks, gain, bias, o_ref, whole):
+    rows, windows = blocks.shape[3:]
+    for core in range(blocks.shape[0]):
+        for x in range(blocks.shape[1]):
+            at = (2 * x + core) * rows
+            for j in range(each):
+                whole[at : at + rows, j * windows : (j + 1) * windows] = blocks[core, x, first + j]
+    width, tokens = whole.shape
     step = 128
     for t in range(0, tokens, step):
         values = whole[:, t : t + step].astype(F32)
@@ -217,17 +219,16 @@
         target[1] = v[block:]
 
 
-def stream_kernel(chunks, bias, *refs):
-    o_ref = refs[-1]
-    own = refs[:chunks]
-    keep, near, far = (
-        refs[chunks + i * WINDOW : chunks + (i + 1) * WINDOW] for i in range(3)
-    )
-    each, rows, windows = own[0].shape
+def stream_kernel(own, bias, *refs):
+    parts, o_ref = refs[:-1], refs[-1]
+    count = len(parts) // 3
+    rows, windows = own.shape[1:]
+    each = WINDOW // count
     for p in range(WINDOW):
-        total = keep[p][...].astype(F32) + near[p][...].astype(F32) + far[p][...].astype(F32)
-        v = own[p // each][p % each].astype(F32) + (total + bias[...])
-        o_ref[p * rows : (p + 1) * rows, :] = v.astype(BF16)
+        at = slice(p % each * windows, (p % each + 1) * windows)
+        terms = [parts[i * count + p // each][:, at].astype(F32) for i in range(3)]
+        total = terms[0] + terms[1] + terms[2] + bias[...]
+        o_ref[p * rows : (p + 1) * rows, :] = (own[p].astype(F32) + total).astype(BF16)
 
 
 LANES = 128
@@ -351,7 +352,9 @@
     slots = groups * bucket
     shard_rows = [w_in.shape[0], w_out.shape[1], w_proj.shape[2]]
     small = groups == 8 and all(r % 32 == 0 for r in shard_rows)
-    chunks = 2
+    halves = 2
+    x_groups = [[i, i + 2] for i in range(parts // 2)]
+    core_groups = [[i, i + 1] for i in range(0, parts, 2)]
 
     near_pairs = [(i, i ^ 1) for i in range(parts)]
     far_pairs = [(i, i ^ 2) for i in range(parts)]
@@ -365,8 +368,7 @@
 
     def order(x):
         return call(
-            order_kernel, (x,), [shape(WINDOW // chunks, width, windows)] * chunks,
-            name="order_tokens",
+            order_kernel, (x,), shape(WINDOW, width, windows), name="order_tokens",
         )
 
     def shards(count):
@@ -382,10 +384,16 @@
             [shape(1, windows, dtype=jnp.int32), shape(slots, 1, dtype=jnp.int32)], name="route",
         )
 
-    def norm(blocks):
-        count = tokens // chunks
-        return call(
-            norm_kernel, (*blocks, norm_gain[None], norm_bias[None]), shape(count, full),
+    def gather(x):
+        x = lax.all_gather(x, "narrow", axis_index_groups=x_groups)
+        return lax.all_gather(x, "narrow", axis_index_groups=core_groups)
+
+    def norm(blocks, half):
+        each = WINDOW // halves
+        count = each * windows
+        return call(
+            functools.partial(norm_kernel, half * each, each),
+            (blocks, norm_gain[None], norm_bias[None]), shape(count, full),
             scratch=[pltpu.VMEM((full, count), BF16)], name="norm",
         )
 
@@ -399,21 +407,20 @@
     def mlp_out(pieces, arrays, hiddens, over_x):
         outs = call(
             functools.partial(
-                out_kernel, pieces, groups, shard_rows[1], over_x, len(hiddens), WINDOW
+                out_kernel, pieces, groups, shard_rows[1], over_x, len(hiddens), SUMS
             ),
-            (*hiddens, *arrays), [shape(width, windows)] * (2 * WINDOW),
+            (*hiddens, *arrays), [shape(width, tokens // SUMS)] * (2 * SUMS),
             scratch=[pltpu.VMEM((2 * width, ff), BF16)], name="mlp_out",
         )
-        return outs[:WINDOW], outs[WINDOW:]
+        return outs[:SUMS], outs[SUMS:]
 
     def add(keep, other):
         return call(add_kernel, (keep, other), shape(*keep.shape), name="add")
 
-    def stream(own, keep, core_sums, x_sums):
-        return call(
-            functools.partial(stream_kernel, chunks),
-            (b_out[:, None], *own, *keep, *core_sums, *x_sums),
-            shape(WINDOW * width, windows), name="stream",
+    def stream(own, sums):
+        return call(
+            stream_kernel, (own, b_out[:, None], *sums), shape(WINDOW * width, windows),
+            name="stream",
         )
 
     def proj(pieces, arrays, merged):
@@ -445,13 +452,13 @@
         wholes = [lax.all_gather(s, "wide", axis=0, tiled=True) for s in shard]
         pieces = [Piece(0, k * width, width, None, 0, k) for k in range(parts)]
         own = order(patches.T)
-        over_x = [far(x) for x in own]
-        normed = [norm((x, y, near(x), near(y))) for x, y in zip(own, over_x)]
+        blocks = gather(own)
+        normed = [norm(blocks, i) for i in range(halves)]
         act = hidden(pieces, wholes[:1], normed, 0, ff)
         keep_x, give_x = mlp_out(pieces, wholes[1:2], [act], 1)
         keep, give = mlp_out(pieces, wholes[1:2], [act], 0)
         x_sums = [far(add(k, near(g))) for k, g in zip(keep_x, give_x)]
-        merged = stream(own, keep, [near(g) for g in give], x_sums)
+        merged = stream(own, [*keep, *[near(g) for g in give], *x_sums])
         slots_of, targets = route()
         keep, give = proj(pieces, wholes[2:], merged)
         core_sums = near(give)
@@ -463,7 +470,7 @@
     half_rows = shard_rows[0] // 2
     last = groups // 2
 
-    def gather(halves, work):
+    def hops(halves, work):
         arrays = list(halves)
         pieces = [Piece(h, 0, half_rows, 0, h * half_rows) for h in (0, 1)]
         held = {(way, h): halves[h] for way in (0, 1) for h in (0, 1)}
@@ -483,40 +490,28 @@
                 t += 1
         return pieces, arrays
 
-    own, over_x, over_core, over_both, normed = [], [], [], [], []
-    got = {}
+    got, normed = {}, []
 
     def start_tokens():
-        own.extend(order(patches.T))
-        over_x.append(far(own[0]))
-        ring.add_work(own[0])
+        got["own"] = order(patches.T)
+        got["blocks"] = gather(got["own"])
+        ring.add_work(got["own"])
 
     def start_shards():
         got["shards"] = shards(2)
         ring.add_work(got["shards"][0])
-        over_core.extend(near(x) for x in own)
-
-    def send_second():
-        over_x.append(far(ring.now(own[1])))
+
+    def start_route():
         got["slots_of"], got["targets"] = route()
 
-    def send_both():
-        over_both.append(near(ring.now(over_x[len(over_both)])))
-
     def start_norm():
-        i = len(normed)
-        first = ring.now(own[i])
-        normed.append(norm((first, over_x[i], over_core[i], over_both[i])))
-        ring.add_work(normed[i])
-
-    def both_and_norm():
-        send_both()
-        start_norm()
-
-    pieces_in, arrays_in = gather(
+        normed.append(norm(ring.now(got["blocks"]), len(normed)))
+        ring.add_work(normed[-1])
+
+    pieces_in, arrays_in = hops(
         [w_in[:half_rows], w_in[half_rows:]],
-        {0: start_tokens, 1: start_shards, 2: send_second, 4: send_both, 5: both_and_norm,
-         6: start_norm},
+        {0: start_tokens, 1: start_shards, 2: start_route, NORM_AT: start_norm,
+         NORM_AT + 1: start_norm},
     )
 
     columns = 256
@@ -527,8 +522,8 @@
         hiddens.append(hidden(pieces_in, arrays_in, rows, len(hiddens) * columns, columns))
         ring.add_work(hiddens[-1])
 
-    pieces_out, arrays_out = gather(
-        got["shards"][:2], {t: start_hidden for t in range(ff // columns)}
+    pieces_out, arrays_out = hops(
+        got["shards"][:2], {t + HIDDEN_AT: start_hidden for t in range(ff // columns)}
     )
 
     def start_out(over_x):
@@ -539,19 +534,24 @@
         ring.add_work(keep[0])
 
     def start_sums():
-        core = [ring.now(got["core", 1][0]), *got["core", 1][1:]]
-        sums = [add(k, c) for k, c in zip(got["keep", 1], core)]
+        sums = [add(k, c) for k, c in zip(got["keep", 1], got["core", 1])]
         got["x_sums"] = [far(x) for x in sums]
-        for i, x in enumerate(got["x_sums"][:-1]):
-            ring.add_late(x, LATE[i])
-        ring.add_work(sums[0])
-        start_out(0)
-
-    pieces_proj, arrays_proj = gather(
-        got["shards"][2:], {0: lambda: start_out(1), 1: start_sums}
-    )
-
-    merged = stream(own, got["keep", 0], got["core", 0], got["x_sums"])
+        for steps, x in zip(ADD_LATE, sums):
+            ring.add_late(x, steps)
+        for steps, x in zip(LATE, got["x_sums"]):
+            ring.add_late(x, steps)
+
+    def start_first():
+        start_out(1)
+        start_sums()
+
+    pieces_proj, arrays_proj = hops(
+        got["shards"][2:], {0: start_first, OWN_AT: lambda: start_out(0)}
+    )
+
+    merged = stream(
+        got["own"], [*got["keep", 0], *got["core", 0], *got["x_sums"]]
+    )
     keep, give = proj(pieces_proj, arrays_proj, merged)
     core_sums = near(give)
     x_sums = far(add(keep[1], core_sums[1]))

time: 139 us -> 172 us (1.24)
  waiting for transfers between devices: 51.1 us -> 68.6 us
  between operations: 0.29 us -> 13.8 us
  Pallas kernels: 17.2 us -> 19.1 us
  local copies, waits for them, and re-layouts: 3.47 us -> 5.19 us
    all_gather x0 -> x2, waiting for transfers between devices: none -> 27.1 us  [the longest x1 27.1 us: gather(): x = lax.all_gather(x, 'narrow', axis_index_groups=x_groups)]
    ppermute x21, starting transfers between devices: 10.4 us -> 32.3 us  [step(): lax.ppermute(to_right, 'wide', self.right)]
    ppermute x21, starting transfers between devices: 31.7 us -> 13.4 us  [step(): lax.ppermute(to_left, 'wide', self.left)]
    ppermute x7 -> x3, starting transfers between devices: 8.47 us -> 3.66 us  [far(): return lax.ppermute(x, 'narrow', far_pairs)]
    ppermute x21, waiting for transfers between devices: 30.2 us -> 26.1 us  [step(): lax.ppermute(to_right, 'wide', self.right)]
    ppermute x7 -> x3, waiting for transfers between devices: 10 us -> 6.38 us  [far(): return lax.ppermute(x, 'narrow', far_pairs)]
    unnamed x20 -> x36, local copies, waits for them, and re-layouts: 2.13 us -> 4.93 us
    ppermute x13 -> x5, waiting for transfers between devices: 3.6 us -> 1.61 us  [near(): return lax.ppermute(x, 'narrow', near_pairs)]
  transfers between devices with their start and end apart: 62 -> 52, of which waited for: 37 -> 29; matrix products, arithmetic and copies ran while one was open for 0% -> 0% of each run, Pallas kernels for 10% -> 8%
where the time goes in v6:
time: 172 us
  waiting for transfers between devices  68.6 us (40%)
  starting transfers between devices  50.6 us (29%)
  Pallas kernels  19.1 us (11%)
  blocking collectives  14.7 us (9%)
  between operations  13.8 us (8%)
  local copies, waits for them, and re-layouts  5.19 us (3%)
    ppermute x21, starting transfers between devices, step(): lax.ppermute(to_right, 'wide', self.right)  32.3 us
    all_gather x1, waiting for transfers between devices, gather(): x = lax.all_gather(x, 'narrow', axis_index_groups=x_groups)  27.1 us
    ppermute x21, waiting for transfers between devices, step(): lax.ppermute(to_right, 'wide', self.right)  26.1 us
    pallas_call x19, Pallas kernels, call(): pl.pallas_call(kernel, out_shape=outs, in_specs=[VMEM] * len(operands), o...  19.1 us
    all_to_all x1, blocking collectives, exchange_and_place(): lax.all_to_all(buffer, 'wide', split_axis=0, concat_axis=0, tiled=True)  14.7 us
    ppermute x21, starting transfers between devices, step(): lax.ppermute(to_left, 'wide', self.left)  13.4 us
    ppermute x21, waiting for transfers between devices, step(): lax.ppermute(to_left, 'wide', self.left)  7.46 us
    ppermute x3, waiting for transfers between devices, far(): return lax.ppermute(x, 'narrow', far_pairs)  6.38 us
  transfers between devices with their start and end apart: 52, of which 29 were waited for; matrix products, arithmetic and copies ran while one was open for 0% of the time, Pallas kernels for 8%

profile of v6, /device:TPU:0, one launch (start us, length us, event | category | flops | bytes accessed | tf_op | source)
XLA Modules:
  0.0 171.9 jit_solution(2112511639061392084)
XLA Ops:
  7.6 1.7 order_tokens.1.own
  9.4 27.1 %all-gather.5.cloned.1.call-done = bf16[8,320,256]{2,1,0:T(8,128)(2,1)} async-done(((bf16[4,320,256]{2,1,0:T(8,128)(2,1)}), bf16[8,320,256]{2,1,0:T(8,128)(2,1)}) %all-gather.5.cloned.1.call-update) | async-done | bytes 1310736 | tf_op jit(solution)/shard_map/all_gather | solution.py:388
  36.5 1.5 collective-permute-start
  38.6 1.5 collective-permute-start.2
  40.7 3.9 %collective-permute-done.refs_2_ = bf16[80,1280]{1,0:T(8,128)(2,1)S(1)} collective-permute-done((bf16[80,1280]{1,0:T(8,128)(2,1)S(1)}, bf16[80,1280]{1,0:T(8,128)(2,1)S(1)}, u32[]{:S(2)}, u32[]{:S(2)}) %collective-permute-start) | collective-permute-done | bytes 204832 | tf_op jit(solution)/shard_map/ppermute | solution.py:324
  44.6 1.5 collective-permute-start.4
  49.0 1.5 collective-permute-start.6
  51.0 2.3 %collective-permute-done.4.refs_6_ = bf16[80,1280]{1,0:T(8,128)(2,1)S(1)} collective-permute-done((bf16[80,1280]{1,0:T(8,128)(2,1)S(1)}, bf16[80,1280]{1,0:T(8,128)(2,1)S(1)}, u32[]{:S(2)}, u32[]{:S(2)}) %collective-permute-start.4) | collective-permute-done | bytes 204832 | tf_op jit(solution)/shard_map/ppermute | solution.py:324
  55.4 2.3 %collective-permute-done.6.refs_8_ = bf16[80,1280]{1,0:T(8,128)(2,1)S(1)} collective-permute-done((bf16[80,1280]{1,0:T(8,128)(2,1)S(1)}, bf16[80,1280]{1,0:T(8,128)(2,1)S(1)}, u32[]{:S(2)}, u32[]{:S(2)}) %collective-permute-start.6) | collective-permute-done | bytes 204832 | tf_op jit(solution)/shard_map/ppermute | solution.py:324
  57.7 1.5 collective-permute-start.10
  59.8 2.3 %collective-permute-done.8.refs_10_ = bf16[80,1280]{1,0:T(8,128)(2,1)S(1)} collective-permute-done((bf16[80,1280]{1,0:T(8,128)(2,1)S(1)}, bf16[80,1280]{1,0:T(8,128)(2,1)S(1)}, u32[]{:S(2)}, u32[]{:S(2)}) %collective-permute-start.8) | collective-permute-done | bytes 204832 | tf_op jit(solution)/shard_map/ppermute | solution.py:324
  64.2 1.7 %copy-done = bf16[4,4,320,256]{3,2,1,0:T(8,128)(2,1)S(1)} copy-done((bf16[4,4,320,256]{3,2,1,0:T(8,128)(2,1)S(1)}, bf16[4,4,320,256]{3,2,1,0:T(8,128)(2,1)}, u32[]{:S(2)}) %copy-start) | copy-done | bytes 2621464
  67.4 1.5 collective-permute-start.14
  70.9 1.5 collective-permute-start.17
  95.1 2.3 %collective-permute-done.29.refs_17_ = bf16[80,1280]{1,0:T(8,128)(2,1)S(1)} collective-permute-done((bf16[80,1280]{1,0:T(8,128)(2,1)S(1)}, bf16[80,1280]{1,0:T(8,128)(2,1)S(1)}, u32[]{:S(2)}, u32[]{:S(2)}) %collective-permute-start.29) | collective-permute-done | bytes 204832 | tf_op jit(solution)/shard_map/ppermute | solution.py:324
  97.4 1.5 collective-permute-start.36
  99.5 2.3 %collective-permute-done.22.refs_19_ = bf16[80,1280]{1,0:T(8,128)(2,1)S(1)} collective-permute-done((bf16[80,1280]{1,0:T(8,128)(2,1)S(1)}, bf16[80,1280]{1,0:T(8,128)(2,1)S(1)}, u32[]{:S(2)}, u32[]{:S(2)}) %collective-permute-start.22) | collective-permute-done | bytes 204832 | tf_op jit(solution)/shard_map/ppermute | solution.py:324
  103.8 2.3 %mlp_out.3 = (bf16[320,512]{1,0:T(8,128)(2,1)S(1)}, bf16[320,512]{1,0:T(8,128)(2,1)S(1)}, bf16[320,512]{1,0:T(8,128)(2,1)S(1)}, bf16[320,512]{1,0:T(8,128)(2,1)S(1)}) custom-call(bf16[1024,256]{1,0:T(8,128)(2,1)S(1)} %hidden.5.refs_0_, bf16[1024,256]{1,0:T(8,128)(2,1)S(1)} %hidden.7.refs_1_, bf16[1024,256]{1,0:T(8,128)(2,1)S(1)} %hidden.6.refs_2_, ...), custom_call_target="tpu_custom_call" | custom-call | tf_op jit(solution)/shard_map/mlp_out/pallas_call | solution.py:24
  107.7 1.5 collective-permute-start.38
  112.2 2.2 %mlp_out.2 = (bf16[320,512]{1,0:T(8,128)(2,1)S(1)}, bf16[320,512]{1,0:T(8,128)(2,1)S(1)}, bf16[320,512]{1,0:T(8,128)(2,1)S(1)}, bf16[320,512]{1,0:T(8,128)(2,1)S(1)}) custom-call(bf16[1024,256]{1,0:T(8,128)(2,1)S(1)} %hidden.5.refs_0_, bf16[1024,256]{1,0:T(8,128)(2,1)S(1)} %hidden.7.refs_1_, bf16[1024,256]{1,0:T(8,128)(2,1)S(1)} %hidden.6.refs_2_, ...), custom_call_target="tpu_custom_call" | custom-call | tf_op jit(solution)/shard_map/mlp_out/pallas_call | solution.py:24
  115.3 1.9 %collective-permute-done.39.refs_7_ = bf16[80,1280]{1,0:T(8,128)(2,1)S(1)} collective-permute-done((bf16[80,1280]{1,0:T(8,128)(2,1)S(1)}, bf16[80,1280]{1,0:T(8,128)(2,1)S(1)}, u32[]{:S(2)}, u32[]{:S(2)}) %collective-permute-start.39) | collective-permute-done | bytes 204832 | tf_op jit(solution)/shard_map/ppermute | solution.py:325
  119.3 2.3 %collective-permute-done.41.refs_9_ = bf16[80,1280]{1,0:T(8,128)(2,1)S(1)} collective-permute-done((bf16[80,1280]{1,0:T(8,128)(2,1)S(1)}, bf16[80,1280]{1,0:T(8,128)(2,1)S(1)}, u32[]{:S(2)}, u32[]{:S(2)}) %collective-permute-start.41) | collective-permute-done | bytes 204832 | tf_op jit(solution)/shard_map/ppermute | solution.py:325
  122.3 1.6 collective-permute-start.40
  125.3 3.7 %collective-permute-done.40.refs_8_ = bf16[80,1280]{1,0:T(8,128)(2,1)S(1)} collective-permute-done((bf16[80,1280]{1,0:T(8,128)(2,1)S(1)}, bf16[80,1280]{1,0:T(8,128)(2,1)S(1)}, u32[]{:S(2)}, u32[]{:S(2)}) %collective-permute-start.40) | collective-permute-done | bytes 204832 | tf_op jit(solution)/shard_map/ppermute | solution.py:324
  129.0 2.4 %collective-permute-start.46 = (bf16[80,1280]{1,0:T(8,128)(2,1)S(1)}, bf16[80,1280]{1,0:T(8,128)(2,1)S(1)}, u32[]{:S(2)}, u32[]{:S(2)}) collective-permute-start(bf16[80,1280]{1,0:T(8,128)(2,1)S(1)} %collective-permute-done.42.refs_10_), channel_id=1, source_target_pairs={{0,8},{8,16},{16,24},{24,28},{28,20},{20,12},{12,4},{4,0},{1,9},{9... | collective-permute-start | bytes 614408 | tf_op jit(solution)/shard_map/ppermute | solution.py:324
  131.4 2.0 %collective-permute-start.44 = (bf16[80,1280]{1,0:T(8,128)(2,1)S(1)}, bf16[80,1280]{1,0:T(8,128)(2,1)S(1)}, u32[]{:S(2)}, u32[]{:S(2)}) collective-permute-start(bf16[80,1280]{1,0:T(8,128)(2,1)S(1)} %collective-permute-done.40.refs_8_), channel_id=1, source_target_pairs={{0,8},{8,16},{16,24},{24,28},{28,20},{20,12},{12,4},{4,0},{1,9},{9... | collective-permute-start | bytes 614408 | tf_op jit(solution)/shard_map/ppermute | solution.py:324
  133.9 2.3 %collective-permute-done.35.refs_5_ = bf16[320,512]{1,0:T(8,128)(2,1)S(1)} collective-permute-done((bf16[320,512]{1,0:T(8,128)(2,1)S(1)}, bf16[320,512]{1,0:T(8,128)(2,1)S(1)}, u32[]{:S(2)}, u32[]{:S(2)}) %collective-permute-start.35) | collective-permute-done | bytes 327712 | tf_op jit(solution)/shard_map/ppermute | solution.py:366
  137.6 1.7 collective-permute-done.45.refs_13_
  140.8 1.6 collective-permute-done.48.near
  142.4 1.7 collective-permute-start.49
  144.6 4.1 %collective-permute-done.49.far = bf16[320,256]{1,0:T(8,128)(2,1)S(1)} collective-permute-done((bf16[320,256]{1,0:T(8,128)(2,1)S(1)}, bf16[320,256]{1,0:T(8,128)(2,1)S(1)}, u32[]{:S(2)}, u32[]{:S(2)}) %collective-permute-start.49) | collective-permute-done | bytes 163872 | tf_op jit(solution)/shard_map/ppermute | solution.py:366
  149.1 14.7 %all_to_all.5.arrived = bf16[8,160,128]{2,1,0:T(8,128)(2,1)S(1)} all-to-all(bf16[8,160,128]{2,1,0:T(8,128)(2,1)S(1)} %pack.1), channel_id=1, replica_groups=mesh['wide'=8,'narrow'=4] {'wide'}, dimensions={0} | all-to-all | bytes 655360 | tf_op jit(solution)/shard_map/all_to_all | solution.py:444
  (139 shorter events, 54.2 us)
Async XLA Ops:
  6.5 29.9 %all-gather.5.cloned.1.call-start = ((), (), s32[]{:S(2)}) async-start(), calls=%async_computation.1 | async-start | bytes 1966080 | tf_op jit(solution)/shard_map/all_gather | solution.py:388
  9.4 54.9 %all-gather.7.cloned.1.call-start = ((), (), s32[]{:S(2)}) async-start(), calls=%async_computation.2 | async-start | bytes 3932160 | tf_op jit(solution)/shard_map/all_gather | solution.py:389
  38.6 10.3 %collective-permute-start.2 = (bf16[80,1280]{1,0:T(8,128)(2,1)S(1)}, bf16[80,1280]{1,0:T(8,128)(2,1)S(1)}, u32[]{:S(2)}, u32[]{:S(2)}) collective-permute-start(bf16[80,1280]{1,0:T(8,128)(2,1)S(1)} %get-tuple-element.131.refs_1_), channel_id=1, source_target_pairs={{0,8},{8,16},{16,24},{24,28},{28,20},{20,12},{12,4},{4,0},{1,9},{9... | collective-permute-start | bytes 614408 | tf_op jit(solution)/shard_map/ppermute | solution.py:324
  40.1 10.3 %collective-permute-start.3 = (bf16[80,1280]{1,0:T(8,128)(2,1)S(1)}, bf16[80,1280]{1,0:T(8,128)(2,1)S(1)}, u32[]{:S(2)}, u32[]{:S(2)}) collective-permute-start(bf16[80,1280]{1,0:T(8,128)(2,1)S(1)} %get-tuple-element.132.refs_0_), channel_id=1, source_target_pairs={{8,0},{16,8},{24,16},{28,24},{20,28},{12,20},{4,12},{0,4},{9,1},{1... | collective-permute-start | bytes 614408 | tf_op jit(solution)/shard_map/ppermute | solution.py:325
  44.6 8.8 %collective-permute-start.4 = (bf16[80,1280]{1,0:T(8,128)(2,1)S(1)}, bf16[80,1280]{1,0:T(8,128)(2,1)S(1)}, u32[]{:S(2)}, u32[]{:S(2)}) collective-permute-start(bf16[80,1280]{1,0:T(8,128)(2,1)S(1)} %collective-permute-done.refs_2_), channel_id=1, source_target_pairs={{0,8},{8,16},{16,24},{24,28},{28,20},{20,12},{12,4},{4,0},{1,9},{9... | collective-permute-start | bytes 614408 | tf_op jit(solution)/shard_map/ppermute | solution.py:324
  46.1 8.8 %collective-permute-start.5 = (bf16[80,1280]{1,0:T(8,128)(2,1)S(1)}, bf16[80,1280]{1,0:T(8,128)(2,1)S(1)}, u32[]{:S(2)}, u32[]{:S(2)}) collective-permute-start(bf16[80,1280]{1,0:T(8,128)(2,1)S(1)} %collective-permute-done.1.refs_3_), channel_id=1, source_target_pairs={{8,0},{16,8},{24,16},{28,24},{20,28},{12,20},{4,12},{0,4},{9,1},{1... | collective-permute-start | bytes 614408 | tf_op jit(solution)/shard_map/ppermute | solution.py:325
  49.0 8.8 %collective-permute-start.6 = (bf16[80,1280]{1,0:T(8,128)(2,1)S(1)}, bf16[80,1280]{1,0:T(8,128)(2,1)S(1)}, u32[]{:S(2)}, u32[]{:S(2)}) collective-permute-start(bf16[80,1280]{1,0:T(8,128)(2,1)S(1)} %collective-permute-done.2.refs_4_), channel_id=1, source_target_pairs={{0,8},{8,16},{16,24},{24,28},{28,20},{20,12},{12,4},{4,0},{1,9},{9... | collective-permute-start | bytes 614408 | tf_op jit(solution)/shard_map/ppermute | solution.py:324
  50.5 8.8 %collective-permute-start.7 = (bf16[80,1280]{1,0:T(8,128)(2,1)S(1)}, bf16[80,1280]{1,0:T(8,128)(2,1)S(1)}, u32[]{:S(2)}, u32[]{:S(2)}) collective-permute-start(bf16[80,1280]{1,0:T(8,128)(2,1)S(1)} %collective-permute-done.3.refs_5_), channel_id=1, source_target_pairs={{8,0},{16,8},{24,16},{28,24},{20,28},{12,20},{4,12},{0,4},{9,1},{1... | collective-permute-start | bytes 614408 | tf_op jit(solution)/shard_map/ppermute | solution.py:325
  53.3 8.8 %collective-permute-start.8 = (bf16[80,1280]{1,0:T(8,128)(2,1)S(1)}, bf16[80,1280]{1,0:T(8,128)(2,1)S(1)}, u32[]{:S(2)}, u32[]{:S(2)}) collective-permute-start(bf16[80,1280]{1,0:T(8,128)(2,1)S(1)} %collective-permute-done.4.refs_6_), channel_id=1, source_target_pairs={{0,8},{8,16},{16,24},{24,28},{28,20},{20,12},{12,4},{4,0},{1,9},{9... | collective-permute-start | bytes 614408 | tf_op jit(solution)/shard_map/ppermute | solution.py:324
  54.9 8.8 %collective-permute-start.9 = (bf16[80,1280]{1,0:T(8,128)(2,1)S(1)}, bf16[80,1280]{1,0:T(8,128)(2,1)S(1)}, u32[]{:S(2)}, u32[]{:S(2)}) collective-permute-start(bf16[80,1280]{1,0:T(8,128)(2,1)S(1)} %collective-permute-done.5.refs_7_), channel_id=1, source_target_pairs={{8,0},{16,8},{24,16},{28,24},{20,28},{12,20},{4,12},{0,4},{9,1},{1... | collective-permute-start | bytes 614408 | tf_op jit(solution)/shard_map/ppermute | solution.py:325
  57.7 9.6 %collective-permute-start.10 = (bf16[80,1280]{1,0:T(8,128)(2,1)S(1)}, bf16[80,1280]{1,0:T(8,128)(2,1)S(1)}, u32[]{:S(2)}, u32[]{:S(2)}) collective-permute-start(bf16[80,1280]{1,0:T(8,128)(2,1)S(1)} %collective-permute-done.6.refs_8_), channel_id=1, source_target_pairs={{0,8},{8,16},{16,24},{24,28},{28,20},{20,12},{12,4},{4,0},{1,9},{9... | collective-permute-start | bytes 614408 | tf_op jit(solution)/shard_map/ppermute | solution.py:324
  59.3 9.7 %collective-permute-start.11 = (bf16[80,1280]{1,0:T(8,128)(2,1)S(1)}, bf16[80,1280]{1,0:T(8,128)(2,1)S(1)}, u32[]{:S(2)}, u32[]{:S(2)}) collective-permute-start(bf16[80,1280]{1,0:T(8,128)(2,1)S(1)} %collective-permute-done.7.refs_9_), channel_id=1, source_target_pairs={{8,0},{16,8},{24,16},{28,24},{20,28},{12,20},{4,12},{0,4},{9,1},{1... | collective-permute-start | bytes 614408 | tf_op jit(solution)/shard_map/ppermute | solution.py:325
  62.1 8.8 %collective-permute-start.12 = (bf16[80,1280]{1,0:T(8,128)(2,1)S(1)}, bf16[80,1280]{1,0:T(8,128)(2,1)S(1)}, u32[]{:S(2)}, u32[]{:S(2)}) collective-permute-start(bf16[80,1280]{1,0:T(8,128)(2,1)S(1)} %collective-permute-done.8.refs_10_), channel_id=1, source_target_pairs={{0,8},{8,16},{16,24},{24,28},{28,20},{20,12},{12,4},{4,0},{1,9},{9... | collective-permute-start | bytes 614408 | tf_op jit(solution)/shard_map/ppermute | solution.py:324
  63.6 8.8 %collective-permute-start.13 = (bf16[80,1280]{1,0:T(8,128)(2,1)S(1)}, bf16[80,1280]{1,0:T(8,128)(2,1)S(1)}, u32[]{:S(2)}, u32[]{:S(2)}) collective-permute-start(bf16[80,1280]{1,0:T(8,128)(2,1)S(1)} %collective-permute-done.9.refs_11_), channel_id=1, source_target_pairs={{8,0},{16,8},{24,16},{28,24},{20,28},{12,20},{4,12},{0,4},{9,1},{1... | collective-permute-start | bytes 614408 | tf_op jit(solution)/shard_map/ppermute | solution.py:325
  70.9 8.9 %collective-permute-start.17 = (bf16[80,1280]{1,0:T(8,128)(2,1)S(1)}, bf16[80,1280]{1,0:T(8,128)(2,1)S(1)}, u32[]{:S(2)}, u32[]{:S(2)}) collective-permute-start(bf16[80,1280]{1,0:T(8,128)(2,1)S(1)} %copy-done.2), channel_id=1, source_target_pairs={{0,8},{8,16},{16,24},{24,28},{28,20},{20,12},{12,4},{4,0},{1,9},{9... | collective-permute-start | bytes 614408 | tf_op jit(solution)/shard_map/ppermute | solution.py:324
  72.4 8.9 %collective-permute-start.16 = (bf16[80,1280]{1,0:T(8,128)(2,1)S(1)}, bf16[80,1280]{1,0:T(8,128)(2,1)S(1)}, u32[]{:S(2)}, u32[]{:S(2)}) collective-permute-start(bf16[80,1280]{1,0:T(8,128)(2,1)S(1)} %get-tuple-element.87.refs_5_), channel_id=1, source_target_pairs={{8,0},{16,8},{24,16},{28,24},{20,28},{12,20},{4,12},{0,4},{9,1},{1... | collective-permute-start | bytes 614408 | tf_op jit(solution)/shard_map/ppermute | solution.py:325
  75.4 8.8 %collective-permute-start.15 = (bf16[80,1280]{1,0:T(8,128)(2,1)S(1)}, bf16[80,1280]{1,0:T(8,128)(2,1)S(1)}, u32[]{:S(2)}, u32[]{:S(2)}) collective-permute-start(bf16[80,1280]{1,0:T(8,128)(2,1)S(1)} %collective-permute-done.14.refs_7_), channel_id=1, source_target_pairs={{0,8},{8,16},{16,24},{24,28},{28,20},{20,12},{12,4},{4,0},{1,9},{9... | collective-permute-start | bytes 614408 | tf_op jit(solution)/shard_map/ppermute | solution.py:324
  77.0 8.8 %collective-permute-start.25 = (bf16[80,1280]{1,0:T(8,128)(2,1)S(1)}, bf16[80,1280]{1,0:T(8,128)(2,1)S(1)}, u32[]{:S(2)}, u32[]{:S(2)}) collective-permute-start(bf16[80,1280]{1,0:T(8,128)(2,1)S(1)} %collective-permute-done.20.refs_8_), channel_id=1, source_target_pairs={{8,0},{16,8},{24,16},{28,24},{20,28},{12,20},{4,12},{0,4},{9,1},{1... | collective-permute-start | bytes 614408 | tf_op jit(solution)/shard_map/ppermute | solution.py:325
  79.8 8.8 %collective-permute-start.21 = (bf16[80,1280]{1,0:T(8,128)(2,1)S(1)}, bf16[80,1280]{1,0:T(8,128)(2,1)S(1)}, u32[]{:S(2)}, u32[]{:S(2)}) collective-permute-start(bf16[80,1280]{1,0:T(8,128)(2,1)S(1)} %collective-permute-done.17.refs_9_), channel_id=1, source_target_pairs={{0,8},{8,16},{16,24},{24,28},{28,20},{20,12},{12,4},{4,0},{1,9},{9... | collective-permute-start | bytes 614408 | tf_op jit(solution)/shard_map/ppermute | solution.py:324
  81.4 8.8 %collective-permute-start.19 = (bf16[80,1280]{1,0:T(8,128)(2,1)S(1)}, bf16[80,1280]{1,0:T(8,128)(2,1)S(1)}, u32[]{:S(2)}, u32[]{:S(2)}) collective-permute-start(bf16[80,1280]{1,0:T(8,128)(2,1)S(1)} %collective-permute-done.16.refs_10_), channel_id=1, source_target_pairs={{8,0},{16,8},{24,16},{28,24},{20,28},{12,20},{4,12},{0,4},{9,1},{1... | collective-permute-start | bytes 614408 | tf_op jit(solution)/shard_map/ppermute | solution.py:325
  84.2 8.8 %collective-permute-start.18 = (bf16[80,1280]{1,0:T(8,128)(2,1)S(1)}, bf16[80,1280]{1,0:T(8,128)(2,1)S(1)}, u32[]{:S(2)}, u32[]{:S(2)}) collective-permute-start(bf16[80,1280]{1,0:T(8,128)(2,1)S(1)} %collective-permute-done.15.refs_11_), channel_id=1, source_target_pairs={{0,8},{8,16},{16,24},{24,28},{28,20},{20,12},{12,4},{4,0},{1,9},{9... | collective-permute-start | bytes 614408 | tf_op jit(solution)/shard_map/ppermute | solution.py:324
  85.8 8.8 %collective-permute-start.26 = (bf16[80,1280]{1,0:T(8,128)(2,1)S(1)}, bf16[80,1280]{1,0:T(8,128)(2,1)S(1)}, u32[]{:S(2)}, u32[]{:S(2)}) collective-permute-start(bf16[80,1280]{1,0:T(8,128)(2,1)S(1)} %collective-permute-done.25.refs_12_), channel_id=1, source_target_pairs={{8,0},{16,8},{24,16},{28,24},{20,28},{12,20},{4,12},{0,4},{9,1},{1... | collective-permute-start | bytes 614408 | tf_op jit(solution)/shard_map/ppermute | solution.py:325
  88.6 8.8 %collective-permute-start.29 = (bf16[80,1280]{1,0:T(8,128)(2,1)S(1)}, bf16[80,1280]{1,0:T(8,128)(2,1)S(1)}, u32[]{:S(2)}, u32[]{:S(2)}) collective-permute-start(bf16[80,1280]{1,0:T(8,128)(2,1)S(1)} %collective-permute-done.21.refs_13_), channel_id=1, source_target_pairs={{0,8},{8,16},{16,24},{24,28},{28,20},{20,12},{12,4},{4,0},{1,9},{9... | collective-permute-start | bytes 614408 | tf_op jit(solution)/shard_map/ppermute | solution.py:324
  94.5 8.8 %collective-permute-start.27 = (bf16[80,1280]{1,0:T(8,128)(2,1)S(1)}, bf16[80,1280]{1,0:T(8,128)(2,1)S(1)}, u32[]{:S(2)}, u32[]{:S(2)}) collective-permute-start(bf16[80,1280]{1,0:T(8,128)(2,1)S(1)} %collective-permute-done.26.refs_16_), channel_id=1, source_target_pairs={{8,0},{16,8},{24,16},{28,24},{20,28},{12,20},{4,12},{0,4},{9,1},{1... | collective-permute-start | bytes 614408 | tf_op jit(solution)/shard_map/ppermute | solution.py:325
  97.4 8.9 %collective-permute-start.36 = (bf16[80,1280]{1,0:T(8,128)(2,1)S(1)}, bf16[80,1280]{1,0:T(8,128)(2,1)S(1)}, u32[]{:S(2)}, u32[]{:S(2)}) collective-permute-start(bf16[80,1280]{1,0:T(8,128)(2,1)S(1)} %copy-done.8), channel_id=1, source_target_pairs={{0,8},{8,16},{16,24},{24,28},{28,20},{20,12},{12,4},{4,0},{1,9},{9... | collective-permute-start | bytes 614408 | tf_op jit(solution)/shard_map/ppermute | solution.py:324
  106.2 12.6 %collective-permute-start.32 = (bf16[320,512]{1,0:T(8,128)(2,1)S(1)}, bf16[320,512]{1,0:T(8,128)(2,1)S(1)}, u32[]{:S(2)}, u32[]{:S(2)}) collective-permute-start(bf16[320,512]{1,0:T(8,128)(2,1)S(1)} %get-tuple-element.114), channel_id=1, source_target_pairs={{0,1},{1,0},{2,3},{3,2},{4,5},{5,4},{6,7},{7,6},{8,9},{9,8},{10,11... | collective-permute-start | bytes 983048 | tf_op jit(solution)/shard_map/ppermute | solution.py:363
  106.2 12.5 %collective-permute-start.34 = (bf16[320,512]{1,0:T(8,128)(2,1)S(1)}, bf16[320,512]{1,0:T(8,128)(2,1)S(1)}, u32[]{:S(2)}, u32[]{:S(2)}) collective-permute-start(bf16[320,512]{1,0:T(8,128)(2,1)S(1)} %get-tuple-element.116), channel_id=1, source_target_pairs={{0,1},{1,0},{2,3},{3,2},{4,5},{5,4},{6,7},{7,6},{8,9},{9,8},{10,11... | collective-permute-start | bytes 983048 | tf_op jit(solution)/shard_map/ppermute | solution.py:363
  110.7 10.9 %collective-permute-start.41 = (bf16[80,1280]{1,0:T(8,128)(2,1)S(1)}, bf16[80,1280]{1,0:T(8,128)(2,1)S(1)}, u32[]{:S(2)}, u32[]{:S(2)}) collective-permute-start(bf16[80,1280]{1,0:T(8,128)(2,1)S(1)} %collective-permute-done.28.refs_5_), channel_id=1, source_target_pairs={{8,0},{16,8},{24,16},{28,24},{20,28},{12,20},{4,12},{0,4},{9,1},{1... | collective-permute-start | bytes 614408 | tf_op jit(solution)/shard_map/ppermute | solution.py:325
  118.7 12.6 %collective-permute-start.30 = (bf16[320,512]{1,0:T(8,128)(2,1)S(1)}, bf16[320,512]{1,0:T(8,128)(2,1)S(1)}, u32[]{:S(2)}, u32[]{:S(2)}) collective-permute-start(bf16[320,512]{1,0:T(8,128)(2,1)S(1)} %get-tuple-element.110), channel_id=1, source_target_pairs={{0,1},{1,0},{2,3},{3,2},{4,5},{5,4},{6,7},{7,6},{8,9},{9,8},{10,11... | collective-permute-start | bytes 983048 | tf_op jit(solution)/shard_map/ppermute | solution.py:363
  118.8 12.6 %collective-permute-start.31 = (bf16[320,512]{1,0:T(8,128)(2,1)S(1)}, bf16[320,512]{1,0:T(8,128)(2,1)S(1)}, u32[]{:S(2)}, u32[]{:S(2)}) collective-permute-start(bf16[320,512]{1,0:T(8,128)(2,1)S(1)} %get-tuple-element.111), channel_id=1, source_target_pairs={{0,1},{1,0},{2,3},{3,2},{4,5},{5,4},{6,7},{7,6},{8,9},{9,8},{10,11... | collective-permute-start | bytes 983048 | tf_op jit(solution)/shard_map/ppermute | solution.py:363
  121.7 11.8 %collective-permute-start.33 = (bf16[320,512]{1,0:T(8,128)(2,1)S(1)}, bf16[320,512]{1,0:T(8,128)(2,1)S(1)}, u32[]{:S(2)}, u32[]{:S(2)}) collective-permute-start(bf16[320,512]{1,0:T(8,128)(2,1)S(1)} %add.3), channel_id=1, source_target_pairs={{0,2},{1,3},{2,0},{3,1},{4,6},{5,7},{6,4},{7,5},{8,10},{9,11},{10,... | collective-permute-start | bytes 983048 | tf_op jit(solution)/shard_map/ppermute | solution.py:366
  123.8 12.3 %collective-permute-start.35 = (bf16[320,512]{1,0:T(8,128)(2,1)S(1)}, bf16[320,512]{1,0:T(8,128)(2,1)S(1)}, u32[]{:S(2)}, u32[]{:S(2)}) collective-permute-start(bf16[320,512]{1,0:T(8,128)(2,1)S(1)} %add.4), channel_id=1, source_target_pairs={{0,2},{1,3},{2,0},{3,1},{4,6},{5,7},{6,4},{7,5},{8,10},{9,11},{10,... | collective-permute-start | bytes 983048 | tf_op jit(solution)/shard_map/ppermute | solution.py:366
  (38 other events, 388.9 us)
Sparse Core Ops, SparseCore 0:
  9.5 26.9 all-gather.4
  38.0 11.3 all-gather.6

commit v7 on v6

--- a/solution.py
+++ b/solution.py
@@ -10,10 +10,10 @@
 F32 = jnp.float32
 BF16 = jnp.bfloat16
 WINDOW = 4
-NORM_AT = 5
-HIDDEN_AT = 0
+NORM_AT = 0
+HIDDEN_AT = 2
 SUMS = 2
-ADD_LATE = (1, 1)
+ADD_LATE = ()
 LATE = ()
 OWN_AT = 2
 VMEM = pl.BlockSpec(memory_space=pltpu.VMEM)
@@ -135,12 +135,10 @@
 
 
 def norm_kernel(first, each, blocks, gain, bias, o_ref, whole):
-    rows, windows = blocks.shape[3:]
-    for core in range(blocks.shape[0]):
-        for x in range(blocks.shape[1]):
-            at = (2 * x + core) * rows
-            for j in range(each):
-                whole[at : at + rows, j * windows : (j + 1) * windows] = blocks[core, x, first + j]
+    rows, windows = blocks.shape[2:]
+    for k in range(blocks.shape[0]):
+        for j in range(each):
+            whole[k * rows : (k + 1) * rows, j * windows : (j + 1) * windows] = blocks[k, first + j]
     width, tokens = whole.shape
     step = 128
     for t in range(0, tokens, step):
@@ -353,8 +351,6 @@
     shard_rows = [w_in.shape[0], w_out.shape[1], w_proj.shape[2]]
     small = groups == 8 and all(r % 32 == 0 for r in shard_rows)
     halves = 2
-    x_groups = [[i, i + 2] for i in range(parts // 2)]
-    core_groups = [[i, i + 1] for i in range(0, parts, 2)]
 
     near_pairs = [(i, i ^ 1) for i in range(parts)]
     far_pairs = [(i, i ^ 2) for i in range(parts)]
@@ -383,10 +379,6 @@
             functools.partial(route_kernel, seq_rows, bucket), (place.reshape(groups, windows),),
             [shape(1, windows, dtype=jnp.int32), shape(slots, 1, dtype=jnp.int32)], name="route",
         )
-
-    def gather(x):
-        x = lax.all_gather(x, "narrow", axis_index_groups=x_groups)
-        return lax.all_gather(x, "narrow", axis_index_groups=core_groups)
 
     def norm(blocks, half):
         each = WINDOW // halves
@@ -452,7 +444,7 @@
         wholes = [lax.all_gather(s, "wide", axis=0, tiled=True) for s in shard]
         pieces = [Piece(0, k * width, width, None, 0, k) for k in range(parts)]
         own = order(patches.T)
-        blocks = gather(own)
+        blocks = lax.all_gather(own, "narrow")
         normed = [norm(blocks, i) for i in range(halves)]
         act = hidden(pieces, wholes[:1], normed, 0, ff)
         keep_x, give_x = mlp_out(pieces, wholes[1:2], [act], 1)
@@ -494,7 +486,7 @@
 
     def start_tokens():
         got["own"] = order(patches.T)
-        got["blocks"] = gather(got["own"])
+        got["blocks"] = lax.all_gather(got["own"], "narrow")
         ring.add_work(got["own"])
 
     def start_shards():
@@ -510,24 +502,26 @@
 
     pieces_in, arrays_in = hops(
         [w_in[:half_rows], w_in[half_rows:]],
-        {0: start_tokens, 1: start_shards, 2: start_route, NORM_AT: start_norm,
-         NORM_AT + 1: start_norm},
+        {0: start_tokens, 1: start_shards, 2: start_route},
     )
 
-    columns = 256
     hiddens = []
+    second = {NORM_AT: start_norm, NORM_AT + 1: start_norm}
 
     def start_hidden():
         rows = [ring.now(normed[0]), *normed[1:]]
         hiddens.append(hidden(pieces_in, arrays_in, rows, len(hiddens) * columns, columns))
         ring.add_work(hiddens[-1])
 
-    pieces_out, arrays_out = hops(
-        got["shards"][:2], {t + HIDDEN_AT: start_hidden for t in range(ff // columns)}
-    )
+    columns = 256
+    for t in range(ff // columns):
+        second[HIDDEN_AT + t] = start_hidden
+    pieces_out, arrays_out = hops(got["shards"][:2], second)
 
     def start_out(over_x):
         acts = [ring.now(hiddens[0]), *hiddens[1:]]
+        if over_x == 0:
+            acts[0] = after(acts[0], *got["sums"])
         keep, give = mlp_out(pieces_out, arrays_out, acts, over_x)
         got["keep", over_x] = keep
         got["core", over_x] = [near(g) for g in give]
@@ -536,6 +530,7 @@
     def start_sums():
         sums = [add(k, c) for k, c in zip(got["keep", 1], got["core", 1])]
         got["x_sums"] = [far(x) for x in sums]
+        got["sums"] = sums
         for steps, x in zip(ADD_LATE, sums):
             ring.add_late(x, steps)
         for steps, x in zip(LATE, got["x_sums"]):

time: 172 us -> 152 us (0.88)
  waiting for transfers between devices: 68.6 us -> 46.6 us
  Pallas kernels: 19.1 us -> 22.4 us
    all_gather x2 -> x1, waiting for transfers between devices: 27.1 us -> 0.02 us  [start_tokens(): got['blocks'] = lax.all_gather(got['own'], 'narrow')]
    ppermute x21, waiting for transfers between devices: 7.46 us -> 16.4 us  [step(): lax.ppermute(to_left, 'wide', self.left)]
    ppermute x21, starting transfers between devices: 13.4 us -> 9.5 us  [step(): lax.ppermute(to_left, 'wide', self.left)]
    pallas_call x19, Pallas kernels: 19.1 us -> 22.4 us  [call(): pl.pallas_call(kernel, out_shape=outs, in_specs=[VMEM] * len(operands), o...]
    ppermute x21, starting transfers between devices: 32.3 us -> 35.3 us  [step(): lax.ppermute(to_right, 'wide', self.right)]
    ppermute x21, waiting for transfers between devices: 26.1 us -> 23.4 us  [step(): lax.ppermute(to_right, 'wide', self.right)]
    unnamed x36 -> x32, local copies, waits for them, and re-layouts: 4.93 us -> 4.25 us
  transfers between devices with their start and end apart: 52 -> 51, of which waited for: 29 -> 21; matrix products, arithmetic and copies ran while one was open for 0% -> 0% of each run, Pallas kernels for 8% -> 12%
where the time goes in v7:
time: 152 us; the launch traced here: 151 us
  starting transfers between devices  49.9 us (33%)
  waiting for transfers between devices  46.6 us (31%)
  Pallas kernels  22.4 us (15%)
  blocking collectives  14.2 us (9%)
  between operations  13.7 us (9%)
  local copies, waits for them, and re-layouts  4.51 us (3%)
    ppermute x21, starting transfers between devices, step(): lax.ppermute(to_right, 'wide', self.right)  35.3 us
    ppermute x21, waiting for transfers between devices, step(): lax.ppermute(to_right, 'wide', self.right)  23.4 us
    pallas_call x19, Pallas kernels, call(): pl.pallas_call(kernel, out_shape=outs, in_specs=[VMEM] * len(operands), o...  22.4 us
    ppermute x21, waiting for transfers between devices, step(): lax.ppermute(to_left, 'wide', self.left)  16.4 us
    all_to_all x1, blocking collectives, exchange_and_place(): lax.all_to_all(buffer, 'wide', split_axis=0, concat_axis=0, tiled=True)  14.2 us
    ppermute x21, starting transfers between devices, step(): lax.ppermute(to_left, 'wide', self.left)  9.5 us
    ppermute x3, waiting for transfers between devices, far(): return lax.ppermute(x, 'narrow', far_pairs)  5.22 us
    unnamed x32, local copies, waits for them, and re-layouts  4.25 us
  transfers between devices with their start and end apart: 51, of which 21 were waited for; matrix products, arithmetic and copies ran while one was open for 0% of the time, Pallas kernels for 12%

profile of v7, /device:TPU:0, one launch (start us, length us, event | category | flops | bytes accessed | tf_op | source)
XLA Modules:
  0.0 151.3 jit_solution(4016831555543957116)
XLA Ops:
  7.6 1.7 %order_tokens.1.own = bf16[4,320,256]{2,1,0:T(8,128)(2,1)} custom-call(bf16[320,1024]{1,0:T(8,128)(2,1)S(1)} %bitcast.12), custom_call_target="tpu_custom_call" | custom-call | tf_op jit(solution)/shard_map/order_tokens/pallas_call | solution.py:24
  9.4 3.1 %collective-permute-start = (bf16[80,1280]{1,0:T(8,128)(2,1)S(1)}, bf16[80,1280]{1,0:T(8,128)(2,1)S(1)}, u32[]{:S(2)}, u32[]{:S(2)}) collective-permute-start(bf16[80,1280]{1,0:T(8,128)(2,1)S(1)} %get-tuple-element.134.refs_0_), channel_id=1, source_target_pairs={{0,8},{8,16},{16,24},{24,28},{28,20},{20,12},{12,4},{4,0},{1,9},{9... | collective-permute-start | bytes 614408 | tf_op jit(solution)/shard_map/ppermute | solution.py:322
  12.5 2.0 %collective-permute-start.2 = (bf16[80,1280]{1,0:T(8,128)(2,1)S(1)}, bf16[80,1280]{1,0:T(8,128)(2,1)S(1)}, u32[]{:S(2)}, u32[]{:S(2)}) collective-permute-start(bf16[80,1280]{1,0:T(8,128)(2,1)S(1)} %get-tuple-element.133.refs_1_), channel_id=1, source_target_pairs={{0,8},{8,16},{16,24},{24,28},{28,20},{20,12},{12,4},{4,0},{1,9},{9... | collective-permute-start | bytes 614408 | tf_op jit(solution)/shard_map/ppermute | solution.py:322
  14.5 3.8 %collective-permute-done.refs_2_ = bf16[80,1280]{1,0:T(8,128)(2,1)S(1)} collective-permute-done((bf16[80,1280]{1,0:T(8,128)(2,1)S(1)}, bf16[80,1280]{1,0:T(8,128)(2,1)S(1)}, u32[]{:S(2)}, u32[]{:S(2)}) %collective-permute-start) | collective-permute-done | bytes 204832 | tf_op jit(solution)/shard_map/ppermute | solution.py:322
  18.3 2.1 %collective-permute-start.4 = (bf16[80,1280]{1,0:T(8,128)(2,1)S(1)}, bf16[80,1280]{1,0:T(8,128)(2,1)S(1)}, u32[]{:S(2)}, u32[]{:S(2)}) collective-permute-start(bf16[80,1280]{1,0:T(8,128)(2,1)S(1)} %collective-permute-done.refs_2_), channel_id=1, source_target_pairs={{0,8},{8,16},{16,24},{24,28},{28,20},{20,12},{12,4},{4,0},{1,9},{9... | collective-permute-start | bytes 614408 | tf_op jit(solution)/shard_map/ppermute | solution.py:322
  22.7 2.1 %collective-permute-start.6 = (bf16[80,1280]{1,0:T(8,128)(2,1)S(1)}, bf16[80,1280]{1,0:T(8,128)(2,1)S(1)}, u32[]{:S(2)}, u32[]{:S(2)}) collective-permute-start(bf16[80,1280]{1,0:T(8,128)(2,1)S(1)} %collective-permute-done.2.refs_4_), channel_id=1, source_target_pairs={{0,8},{8,16},{16,24},{24,28},{28,20},{20,12},{12,4},{4,0},{1,9},{9... | collective-permute-start | bytes 614408 | tf_op jit(solution)/shard_map/ppermute | solution.py:322
  24.9 2.2 %collective-permute-done.4.refs_6_ = bf16[80,1280]{1,0:T(8,128)(2,1)S(1)} collective-permute-done((bf16[80,1280]{1,0:T(8,128)(2,1)S(1)}, bf16[80,1280]{1,0:T(8,128)(2,1)S(1)}, u32[]{:S(2)}, u32[]{:S(2)}) %collective-permute-start.4) | collective-permute-done | bytes 204832 | tf_op jit(solution)/shard_map/ppermute | solution.py:322
  27.1 2.1 %collective-permute-start.8 = (bf16[80,1280]{1,0:T(8,128)(2,1)S(1)}, bf16[80,1280]{1,0:T(8,128)(2,1)S(1)}, u32[]{:S(2)}, u32[]{:S(2)}) collective-permute-start(bf16[80,1280]{1,0:T(8,128)(2,1)S(1)} %collective-permute-done.4.refs_6_), channel_id=1, source_target_pairs={{0,8},{8,16},{16,24},{24,28},{28,20},{20,12},{12,4},{4,0},{1,9},{9... | collective-permute-start | bytes 614408 | tf_op jit(solution)/shard_map/ppermute | solution.py:322
  29.3 2.2 %collective-permute-done.6.refs_8_ = bf16[80,1280]{1,0:T(8,128)(2,1)S(1)} collective-permute-done((bf16[80,1280]{1,0:T(8,128)(2,1)S(1)}, bf16[80,1280]{1,0:T(8,128)(2,1)S(1)}, u32[]{:S(2)}, u32[]{:S(2)}) %collective-permute-start.6) | collective-permute-done | bytes 204832 | tf_op jit(solution)/shard_map/ppermute | solution.py:322
  31.5 2.1 %collective-permute-start.10 = (bf16[80,1280]{1,0:T(8,128)(2,1)S(1)}, bf16[80,1280]{1,0:T(8,128)(2,1)S(1)}, u32[]{:S(2)}, u32[]{:S(2)}) collective-permute-start(bf16[80,1280]{1,0:T(8,128)(2,1)S(1)} %collective-permute-done.6.refs_8_), channel_id=1, source_target_pairs={{0,8},{8,16},{16,24},{24,28},{28,20},{20,12},{12,4},{4,0},{1,9},{9... | collective-permute-start | bytes 614408 | tf_op jit(solution)/shard_map/ppermute | solution.py:322
  33.7 2.2 %collective-permute-done.8.refs_10_ = bf16[80,1280]{1,0:T(8,128)(2,1)S(1)} collective-permute-done((bf16[80,1280]{1,0:T(8,128)(2,1)S(1)}, bf16[80,1280]{1,0:T(8,128)(2,1)S(1)}, u32[]{:S(2)}, u32[]{:S(2)}) %collective-permute-start.8) | collective-permute-done | bytes 204832 | tf_op jit(solution)/shard_map/ppermute | solution.py:322
  35.9 2.1 %collective-permute-start.12 = (bf16[80,1280]{1,0:T(8,128)(2,1)S(1)}, bf16[80,1280]{1,0:T(8,128)(2,1)S(1)}, u32[]{:S(2)}, u32[]{:S(2)}) collective-permute-start(bf16[80,1280]{1,0:T(8,128)(2,1)S(1)} %collective-permute-done.8.refs_10_), channel_id=1, source_target_pairs={{0,8},{8,16},{16,24},{24,28},{28,20},{20,12},{12,4},{4,0},{1,9},{9... | collective-permute-start | bytes 614408 | tf_op jit(solution)/shard_map/ppermute | solution.py:322
  38.0 2.2 %collective-permute-done.10.refs_12_ = bf16[80,1280]{1,0:T(8,128)(2,1)S(1)} collective-permute-done((bf16[80,1280]{1,0:T(8,128)(2,1)S(1)}, bf16[80,1280]{1,0:T(8,128)(2,1)S(1)}, u32[]{:S(2)}, u32[]{:S(2)}) %collective-permute-start.10) | collective-permute-done | bytes 204832 | tf_op jit(solution)/shard_map/ppermute | solution.py:322
  40.3 2.1 %collective-permute-start.16 = (bf16[80,1280]{1,0:T(8,128)(2,1)S(1)}, bf16[80,1280]{1,0:T(8,128)(2,1)}, u32[]{:S(2)}, u32[]{:S(2)}) collective-permute-start(bf16[80,1280]{1,0:T(8,128)(2,1)S(1)} %get-tuple-element.87.refs_5_), channel_id=1, source_target_pairs={{0,8},{8,16},{16,24},{24,28},{28,20},{20,12},{12,4},{4,0},{1,9},{9... | collective-permute-start | bytes 614408 | tf_op jit(solution)/shard_map/ppermute | solution.py:322
  42.4 2.2 %collective-permute-done.12.refs_14_ = bf16[80,1280]{1,0:T(8,128)(2,1)S(1)} collective-permute-done((bf16[80,1280]{1,0:T(8,128)(2,1)S(1)}, bf16[80,1280]{1,0:T(8,128)(2,1)S(1)}, u32[]{:S(2)}, u32[]{:S(2)}) %collective-permute-start.12) | collective-permute-done | bytes 204832 | tf_op jit(solution)/shard_map/ppermute | solution.py:322
  44.7 2.1 %collective-permute-done.13.refs_15_ = bf16[80,1280]{1,0:T(8,128)(2,1)S(1)} collective-permute-done((bf16[80,1280]{1,0:T(8,128)(2,1)S(1)}, bf16[80,1280]{1,0:T(8,128)(2,1)S(1)}, u32[]{:S(2)}, u32[]{:S(2)}) %collective-permute-start.13) | collective-permute-done | bytes 204832 | tf_op jit(solution)/shard_map/ppermute | solution.py:323
  48.9 1.7 %copy-done = bf16[16,320,256]{2,1,0:T(8,128)(2,1)S(1)} copy-done((bf16[16,320,256]{2,1,0:T(8,128)(2,1)S(1)}, bf16[16,320,256]{2,1,0:T(8,128)(2,1)}, u32[]{:S(2)}) %copy-start) | copy-done | bytes 2621464
  52.0 1.6 %collective-permute-start.18 = (bf16[80,1280]{1,0:T(8,128)(2,1)}, bf16[80,1280]{1,0:T(8,128)(2,1)S(1)}, u32[]{:S(2)}, u32[]{:S(2)}) collective-permute-start(bf16[80,1280]{1,0:T(8,128)(2,1)} %collective-permute-done.16.refs_7_), channel_id=1, source_target_pairs={{0,8},{8,16},{16,24},{24,28},{28,20},{20,12},{12,4},{4,0},{1,9},{9... | collective-permute-start | bytes 614408 | tf_op jit(solution)/shard_map/ppermute | solution.py:322
  57.5 1.6 %collective-permute-start.21 = (bf16[80,1280]{1,0:T(8,128)(2,1)}, bf16[80,1280]{1,0:T(8,128)(2,1)S(1)}, u32[]{:S(2)}, u32[]{:S(2)}) collective-permute-start(bf16[80,1280]{1,0:T(8,128)(2,1)} %collective-permute-done.14.refs_9_), channel_id=1, source_target_pairs={{0,8},{8,16},{16,24},{24,28},{28,20},{20,12},{12,4},{4,0},{1,9},{9... | collective-permute-start | bytes 614408 | tf_op jit(solution)/shard_map/ppermute | solution.py:322
  62.2 3.2 %collective-permute-done.20.refs_14_ = bf16[80,1280]{1,0:T(8,128)(2,1)S(1)} collective-permute-done((bf16[80,1280]{1,0:T(8,128)(2,1)}, bf16[80,1280]{1,0:T(8,128)(2,1)S(1)}, u32[]{:S(2)}, u32[]{:S(2)}) %collective-permute-start.20) | collective-permute-done | bytes 204832 | tf_op jit(solution)/shard_map/ppermute | solution.py:323
  71.6 2.6 %collective-permute-done.23.refs_18_ = bf16[80,1280]{1,0:T(8,128)(2,1)S(1)} collective-permute-done((bf16[80,1280]{1,0:T(8,128)(2,1)S(1)}, bf16[80,1280]{1,0:T(8,128)(2,1)S(1)}, u32[]{:S(2)}, u32[]{:S(2)}) %collective-permute-start.23) | collective-permute-done | bytes 204832 | tf_op jit(solution)/shard_map/ppermute | solution.py:323
  80.5 3.6 %mlp_out.2 = (bf16[320,512]{1,0:T(8,128)(2,1)S(1)}, bf16[320,512]{1,0:T(8,128)(2,1)S(1)}, bf16[320,512]{1,0:T(8,128)(2,1)S(1)}, bf16[320,512]{1,0:T(8,128)(2,1)S(1)}) custom-call(bf16[1024,256]{1,0:T(8,128)(2,1)S(1)} %hidden.5.refs_0_, bf16[1024,256]{1,0:T(8,128)(2,1)S(1)} %hidden.7.refs_1_, bf16[1024,256]{1,0:T(8,128)(2,1)S(1)} %hidden.6.refs_2_, ...), custom_call_target="tpu_custom_call" | custom-call | tf_op jit(solution)/shard_map/mlp_out/pallas_call | solution.py:24
  88.3 3.4 %collective-permute-done.39.refs_7_ = bf16[80,1280]{1,0:T(8,128)(2,1)S(1)} collective-permute-done((bf16[80,1280]{1,0:T(8,128)(2,1)S(1)}, bf16[80,1280]{1,0:T(8,128)(2,1)S(1)}, u32[]{:S(2)}, u32[]{:S(2)}) %collective-permute-start.39) | collective-permute-done | bytes 204832 | tf_op jit(solution)/shard_map/ppermute | solution.py:323
  94.4 1.7 %collective-permute-start.34 = (bf16[320,512]{1,0:T(8,128)(2,1)S(1)}, bf16[320,512]{1,0:T(8,128)(2,1)S(1)}, u32[]{:S(2)}, u32[]{:S(2)}) collective-permute-start(bf16[320,512]{1,0:T(8,128)(2,1)S(1)} %add.3), channel_id=1, source_target_pairs={{0,2},{1,3},{2,0},{3,1},{4,6},{5,7},{6,4},{7,5},{8,10},{9,11},{10,... | collective-permute-start | bytes 983048 | tf_op jit(solution)/shard_map/ppermute | solution.py:362
  96.2 3.5 %mlp_out.3 = (bf16[320,512]{1,0:T(8,128)(2,1)S(1)}, bf16[320,512]{1,0:T(8,128)(2,1)S(1)}, bf16[320,512]{1,0:T(8,128)(2,1)S(1)}, bf16[320,512]{1,0:T(8,128)(2,1)S(1)}) custom-call(bf16[1024,256]{1,0:T(8,128)(2,1)S(1)} %hidden.5.refs_0_, bf16[1024,256]{1,0:T(8,128)(2,1)S(1)} %hidden.7.refs_1_, bf16[1024,256]{1,0:T(8,128)(2,1)S(1)} %hidden.6.refs_2_, ...), custom_call_target="tpu_custom_call" | custom-call | tf_op jit(solution)/shard_map/mlp_out/pallas_call | solution.py:24
  102.3 1.6 %collective-permute-start.35 = (bf16[320,512]{1,0:T(8,128)(2,1)S(1)}, bf16[320,512]{1,0:T(8,128)(2,1)S(1)}, u32[]{:S(2)}, u32[]{:S(2)}) collective-permute-start(bf16[320,512]{1,0:T(8,128)(2,1)S(1)} %add.4), channel_id=1, source_target_pairs={{0,2},{1,3},{2,0},{3,1},{4,6},{5,7},{6,4},{7,5},{8,10},{9,11},{10,... | collective-permute-start | bytes 983048 | tf_op jit(solution)/shard_map/ppermute | solution.py:362
  103.9 3.5 %collective-permute-done.42.refs_10_ = bf16[80,1280]{1,0:T(8,128)(2,1)S(1)} collective-permute-done((bf16[80,1280]{1,0:T(8,128)(2,1)S(1)}, bf16[80,1280]{1,0:T(8,128)(2,1)S(1)}, u32[]{:S(2)}, u32[]{:S(2)}) %collective-permute-start.42) | collective-permute-done | bytes 204832 | tf_op jit(solution)/shard_map/ppermute | solution.py:322
  113.1 2.3 %collective-permute-done.45.refs_13_ = bf16[80,1280]{1,0:T(8,128)(2,1)S(1)} collective-permute-done((bf16[80,1280]{1,0:T(8,128)(2,1)S(1)}, bf16[80,1280]{1,0:T(8,128)(2,1)S(1)}, u32[]{:S(2)}, u32[]{:S(2)}) %collective-permute-start.45) | collective-permute-done | bytes 204832 | tf_op jit(solution)/shard_map/ppermute | solution.py:323
  116.9 2.3 %collective-permute-done.46.refs_14_ = bf16[80,1280]{1,0:T(8,128)(2,1)S(1)} collective-permute-done((bf16[80,1280]{1,0:T(8,128)(2,1)S(1)}, bf16[80,1280]{1,0:T(8,128)(2,1)S(1)}, u32[]{:S(2)}, u32[]{:S(2)}) %collective-permute-start.46) | collective-permute-done | bytes 204832 | tf_op jit(solution)/shard_map/ppermute | solution.py:322
  120.6 1.6 %collective-permute-done.48.near = bf16[2,320,256]{2,1,0:T(8,128)(2,1)S(1)} collective-permute-done((bf16[2,320,256]{2,1,0:T(8,128)(2,1)S(1)}, bf16[2,320,256]{2,1,0:T(8,128)(2,1)S(1)}, u32[]{:S(2)}, u32[]{:S(2)}) %collective-permute-start.48) | collective-permute-done | bytes 327712 | tf_op jit(solution)/shard_map/ppermute | solution.py:359
  123.4 5.2 %collective-permute-done.49.far = bf16[320,256]{1,0:T(8,128)(2,1)S(1)} collective-permute-done((bf16[320,256]{1,0:T(8,128)(2,1)S(1)}, bf16[320,256]{1,0:T(8,128)(2,1)S(1)}, u32[]{:S(2)}, u32[]{:S(2)}) %collective-permute-start.49) | collective-permute-done | bytes 163872 | tf_op jit(solution)/shard_map/ppermute | solution.py:362
  129.0 14.2 %all_to_all.5.arrived = bf16[8,160,128]{2,1,0:T(8,128)(2,1)S(1)} all-to-all(bf16[8,160,128]{2,1,0:T(8,128)(2,1)S(1)} %pack.1), channel_id=1, replica_groups=mesh['wide'=8,'narrow'=4] {'wide'}, dimensions={0} | all-to-all | bytes 655360 | tf_op jit(solution)/shard_map/all_to_all | solution.py:436
  (132 shorter events, 47.2 us)
Async XLA Ops:
  6.5 42.4 %all-gather.3.cloned.1.call-start = ((), (), s32[]{:S(2)}) async-start(), calls=%async_computation.1 | async-start | bytes 3276800 | tf_op jit(solution)/shard_map/all_gather | solution.py:489
  9.4 8.9 %collective-permute-start = (bf16[80,1280]{1,0:T(8,128)(2,1)S(1)}, bf16[80,1280]{1,0:T(8,128)(2,1)S(1)}, u32[]{:S(2)}, u32[]{:S(2)}) collective-permute-start(bf16[80,1280]{1,0:T(8,128)(2,1)S(1)} %get-tuple-element.134.refs_0_), channel_id=1, source_target_pairs={{0,8},{8,16},{16,24},{24,28},{28,20},{20,12},{12,4},{4,0},{1,9},{9... | collective-permute-start | bytes 614408 | tf_op jit(solution)/shard_map/ppermute | solution.py:322
  12.5 10.2 %collective-permute-start.2 = (bf16[80,1280]{1,0:T(8,128)(2,1)S(1)}, bf16[80,1280]{1,0:T(8,128)(2,1)S(1)}, u32[]{:S(2)}, u32[]{:S(2)}) collective-permute-start(bf16[80,1280]{1,0:T(8,128)(2,1)S(1)} %get-tuple-element.133.refs_1_), channel_id=1, source_target_pairs={{0,8},{8,16},{16,24},{24,28},{28,20},{20,12},{12,4},{4,0},{1,9},{9... | collective-permute-start | bytes 614408 | tf_op jit(solution)/shard_map/ppermute | solution.py:322
  14.5 10.4 %collective-permute-start.3 = (bf16[80,1280]{1,0:T(8,128)(2,1)S(1)}, bf16[80,1280]{1,0:T(8,128)(2,1)S(1)}, u32[]{:S(2)}, u32[]{:S(2)}) collective-permute-start(bf16[80,1280]{1,0:T(8,128)(2,1)S(1)} %get-tuple-element.134.refs_0_), channel_id=1, source_target_pairs={{8,0},{16,8},{24,16},{28,24},{20,28},{12,20},{4,12},{0,4},{9,1},{1... | collective-permute-start | bytes 614408 | tf_op jit(solution)/shard_map/ppermute | solution.py:323
  18.3 8.8 %collective-permute-start.4 = (bf16[80,1280]{1,0:T(8,128)(2,1)S(1)}, bf16[80,1280]{1,0:T(8,128)(2,1)S(1)}, u32[]{:S(2)}, u32[]{:S(2)}) collective-permute-start(bf16[80,1280]{1,0:T(8,128)(2,1)S(1)} %collective-permute-done.refs_2_), channel_id=1, source_target_pairs={{0,8},{8,16},{16,24},{24,28},{28,20},{20,12},{12,4},{4,0},{1,9},{9... | collective-permute-start | bytes 614408 | tf_op jit(solution)/shard_map/ppermute | solution.py:322
  20.5 8.8 %collective-permute-start.5 = (bf16[80,1280]{1,0:T(8,128)(2,1)S(1)}, bf16[80,1280]{1,0:T(8,128)(2,1)S(1)}, u32[]{:S(2)}, u32[]{:S(2)}) collective-permute-start(bf16[80,1280]{1,0:T(8,128)(2,1)S(1)} %collective-permute-done.1.refs_3_), channel_id=1, source_target_pairs={{8,0},{16,8},{24,16},{28,24},{20,28},{12,20},{4,12},{0,4},{9,1},{1... | collective-permute-start | bytes 614408 | tf_op jit(solution)/shard_map/ppermute | solution.py:323
  22.7 8.8 %collective-permute-start.6 = (bf16[80,1280]{1,0:T(8,128)(2,1)S(1)}, bf16[80,1280]{1,0:T(8,128)(2,1)S(1)}, u32[]{:S(2)}, u32[]{:S(2)}) collective-permute-start(bf16[80,1280]{1,0:T(8,128)(2,1)S(1)} %collective-permute-done.2.refs_4_), channel_id=1, source_target_pairs={{0,8},{8,16},{16,24},{24,28},{28,20},{20,12},{12,4},{4,0},{1,9},{9... | collective-permute-start | bytes 614408 | tf_op jit(solution)/shard_map/ppermute | solution.py:322
  24.9 8.8 %collective-permute-start.7 = (bf16[80,1280]{1,0:T(8,128)(2,1)S(1)}, bf16[80,1280]{1,0:T(8,128)(2,1)S(1)}, u32[]{:S(2)}, u32[]{:S(2)}) collective-permute-start(bf16[80,1280]{1,0:T(8,128)(2,1)S(1)} %collective-permute-done.3.refs_5_), channel_id=1, source_target_pairs={{8,0},{16,8},{24,16},{28,24},{20,28},{12,20},{4,12},{0,4},{9,1},{1... | collective-permute-start | bytes 614408 | tf_op jit(solution)/shard_map/ppermute | solution.py:323
  27.1 8.8 %collective-permute-start.8 = (bf16[80,1280]{1,0:T(8,128)(2,1)S(1)}, bf16[80,1280]{1,0:T(8,128)(2,1)S(1)}, u32[]{:S(2)}, u32[]{:S(2)}) collective-permute-start(bf16[80,1280]{1,0:T(8,128)(2,1)S(1)} %collective-permute-done.4.refs_6_), channel_id=1, source_target_pairs={{0,8},{8,16},{16,24},{24,28},{28,20},{20,12},{12,4},{4,0},{1,9},{9... | collective-permute-start | bytes 614408 | tf_op jit(solution)/shard_map/ppermute | solution.py:322
  29.3 8.8 %collective-permute-start.9 = (bf16[80,1280]{1,0:T(8,128)(2,1)S(1)}, bf16[80,1280]{1,0:T(8,128)(2,1)S(1)}, u32[]{:S(2)}, u32[]{:S(2)}) collective-permute-start(bf16[80,1280]{1,0:T(8,128)(2,1)S(1)} %collective-permute-done.5.refs_7_), channel_id=1, source_target_pairs={{8,0},{16,8},{24,16},{28,24},{20,28},{12,20},{4,12},{0,4},{9,1},{1... | collective-permute-start | bytes 614408 | tf_op jit(solution)/shard_map/ppermute | solution.py:323
  31.5 8.8 %collective-permute-start.10 = (bf16[80,1280]{1,0:T(8,128)(2,1)S(1)}, bf16[80,1280]{1,0:T(8,128)(2,1)S(1)}, u32[]{:S(2)}, u32[]{:S(2)}) collective-permute-start(bf16[80,1280]{1,0:T(8,128)(2,1)S(1)} %collective-permute-done.6.refs_8_), channel_id=1, source_target_pairs={{0,8},{8,16},{16,24},{24,28},{28,20},{20,12},{12,4},{4,0},{1,9},{9... | collective-permute-start | bytes 614408 | tf_op jit(solution)/shard_map/ppermute | solution.py:322
  33.6 8.8 %collective-permute-start.11 = (bf16[80,1280]{1,0:T(8,128)(2,1)S(1)}, bf16[80,1280]{1,0:T(8,128)(2,1)S(1)}, u32[]{:S(2)}, u32[]{:S(2)}) collective-permute-start(bf16[80,1280]{1,0:T(8,128)(2,1)S(1)} %collective-permute-done.7.refs_9_), channel_id=1, source_target_pairs={{8,0},{16,8},{24,16},{28,24},{20,28},{12,20},{4,12},{0,4},{9,1},{1... | collective-permute-start | bytes 614408 | tf_op jit(solution)/shard_map/ppermute | solution.py:323
  35.9 8.8 %collective-permute-start.12 = (bf16[80,1280]{1,0:T(8,128)(2,1)S(1)}, bf16[80,1280]{1,0:T(8,128)(2,1)S(1)}, u32[]{:S(2)}, u32[]{:S(2)}) collective-permute-start(bf16[80,1280]{1,0:T(8,128)(2,1)S(1)} %collective-permute-done.8.refs_10_), channel_id=1, source_target_pairs={{0,8},{8,16},{16,24},{24,28},{28,20},{20,12},{12,4},{4,0},{1,9},{9... | collective-permute-start | bytes 614408 | tf_op jit(solution)/shard_map/ppermute | solution.py:322
  38.0 8.8 %collective-permute-start.13 = (bf16[80,1280]{1,0:T(8,128)(2,1)S(1)}, bf16[80,1280]{1,0:T(8,128)(2,1)S(1)}, u32[]{:S(2)}, u32[]{:S(2)}) collective-permute-start(bf16[80,1280]{1,0:T(8,128)(2,1)S(1)} %collective-permute-done.9.refs_11_), channel_id=1, source_target_pairs={{8,0},{16,8},{24,16},{28,24},{20,28},{12,20},{4,12},{0,4},{9,1},{1... | collective-permute-start | bytes 614408 | tf_op jit(solution)/shard_map/ppermute | solution.py:323
  40.3 11.8 %collective-permute-start.16 = (bf16[80,1280]{1,0:T(8,128)(2,1)S(1)}, bf16[80,1280]{1,0:T(8,128)(2,1)}, u32[]{:S(2)}, u32[]{:S(2)}) collective-permute-start(bf16[80,1280]{1,0:T(8,128)(2,1)S(1)} %get-tuple-element.87.refs_5_), channel_id=1, source_target_pairs={{0,8},{8,16},{16,24},{24,28},{28,20},{20,12},{12,4},{4,0},{1,9},{9... | collective-permute-start | bytes 614408 | tf_op jit(solution)/shard_map/ppermute | solution.py:322
  42.4 11.2 %collective-permute-start.17 = (bf16[80,1280]{1,0:T(8,128)(2,1)}, bf16[80,1280]{1,0:T(8,128)(2,1)}, u32[]{:S(2)}, u32[]{:S(2)}) collective-permute-start(bf16[80,1280]{1,0:T(8,128)(2,1)} %get-tuple-element.88.refs_6_), channel_id=1, source_target_pairs={{8,0},{16,8},{24,16},{28,24},{20,28},{12,20},{4,12},{0,4},{9,1},{1... | collective-permute-start | bytes 614408 | tf_op jit(solution)/shard_map/ppermute | solution.py:323
  55.6 9.8 %collective-permute-start.20 = (bf16[80,1280]{1,0:T(8,128)(2,1)}, bf16[80,1280]{1,0:T(8,128)(2,1)S(1)}, u32[]{:S(2)}, u32[]{:S(2)}) collective-permute-start(bf16[80,1280]{1,0:T(8,128)(2,1)} %collective-permute-done.15.refs_10_), channel_id=1, source_target_pairs={{8,0},{16,8},{24,16},{28,24},{20,28},{12,20},{4,12},{0,4},{9,1},{1... | collective-permute-start | bytes 614408 | tf_op jit(solution)/shard_map/ppermute | solution.py:323
  60.1 9.4 %collective-permute-start.19 = (bf16[80,1280]{1,0:T(8,128)(2,1)S(1)}, bf16[80,1280]{1,0:T(8,128)(2,1)S(1)}, u32[]{:S(2)}, u32[]{:S(2)}) collective-permute-start(bf16[80,1280]{1,0:T(8,128)(2,1)S(1)} %collective-permute-done.18.refs_11_), channel_id=1, source_target_pairs={{0,8},{8,16},{16,24},{24,28},{28,20},{20,12},{12,4},{4,0},{1,9},{9... | collective-permute-start | bytes 614408 | tf_op jit(solution)/shard_map/ppermute | solution.py:322
  61.7 9.3 %collective-permute-start.27 = (bf16[80,1280]{1,0:T(8,128)(2,1)S(1)}, bf16[80,1280]{1,0:T(8,128)(2,1)S(1)}, u32[]{:S(2)}, u32[]{:S(2)}) collective-permute-start(bf16[80,1280]{1,0:T(8,128)(2,1)S(1)} %collective-permute-done.24.refs_12_), channel_id=1, source_target_pairs={{8,0},{16,8},{24,16},{28,24},{20,28},{12,20},{4,12},{0,4},{9,1},{1... | collective-permute-start | bytes 614408 | tf_op jit(solution)/shard_map/ppermute | solution.py:323
  65.5 8.8 %collective-permute-start.23 = (bf16[80,1280]{1,0:T(8,128)(2,1)S(1)}, bf16[80,1280]{1,0:T(8,128)(2,1)S(1)}, u32[]{:S(2)}, u32[]{:S(2)}) collective-permute-start(bf16[80,1280]{1,0:T(8,128)(2,1)S(1)} %collective-permute-done.20.refs_14_), channel_id=1, source_target_pairs={{8,0},{16,8},{24,16},{28,24},{20,28},{12,20},{4,12},{0,4},{9,1},{1... | collective-permute-start | bytes 614408 | tf_op jit(solution)/shard_map/ppermute | solution.py:323
  69.5 8.8 %collective-permute-start.22 = (bf16[80,1280]{1,0:T(8,128)(2,1)S(1)}, bf16[80,1280]{1,0:T(8,128)(2,1)S(1)}, u32[]{:S(2)}, u32[]{:S(2)}) collective-permute-start(bf16[80,1280]{1,0:T(8,128)(2,1)S(1)} %collective-permute-done.19.refs_15_), channel_id=1, source_target_pairs={{0,8},{8,16},{16,24},{24,28},{28,20},{20,12},{12,4},{4,0},{1,9},{9... | collective-permute-start | bytes 614408 | tf_op jit(solution)/shard_map/ppermute | solution.py:322
  71.0 9.0 %collective-permute-start.28 = (bf16[80,1280]{1,0:T(8,128)(2,1)S(1)}, bf16[80,1280]{1,0:T(8,128)(2,1)S(1)}, u32[]{:S(2)}, u32[]{:S(2)}) collective-permute-start(bf16[80,1280]{1,0:T(8,128)(2,1)S(1)} %collective-permute-done.27.refs_16_), channel_id=1, source_target_pairs={{8,0},{16,8},{24,16},{28,24},{20,28},{12,20},{4,12},{0,4},{9,1},{1... | collective-permute-start | bytes 614408 | tf_op jit(solution)/shard_map/ppermute | solution.py:323
  74.2 9.9 %collective-permute-start.37 = (bf16[80,1280]{1,0:T(8,128)(2,1)S(1)}, bf16[80,1280]{1,0:T(8,128)(2,1)S(1)}, u32[]{:S(2)}, u32[]{:S(2)}) collective-permute-start(bf16[80,1280]{1,0:T(8,128)(2,1)S(1)} %copy-done.8), channel_id=1, source_target_pairs={{8,0},{16,8},{24,16},{28,24},{20,28},{12,20},{4,12},{0,4},{9,1},{1... | collective-permute-start | bytes 614408 | tf_op jit(solution)/shard_map/ppermute | solution.py:323
  84.1 10.2 %collective-permute-start.30 = (bf16[320,512]{1,0:T(8,128)(2,1)S(1)}, bf16[320,512]{1,0:T(8,128)(2,1)S(1)}, u32[]{:S(2)}, u32[]{:S(2)}) collective-permute-start(bf16[320,512]{1,0:T(8,128)(2,1)S(1)} %get-tuple-element.111), channel_id=1, source_target_pairs={{0,1},{1,0},{2,3},{3,2},{4,5},{5,4},{6,7},{7,6},{8,9},{9,8},{10,11... | collective-permute-start | bytes 983048 | tf_op jit(solution)/shard_map/ppermute | solution.py:359
  84.1 12.0 %collective-permute-start.31 = (bf16[320,512]{1,0:T(8,128)(2,1)S(1)}, bf16[320,512]{1,0:T(8,128)(2,1)S(1)}, u32[]{:S(2)}, u32[]{:S(2)}) collective-permute-start(bf16[320,512]{1,0:T(8,128)(2,1)S(1)} %get-tuple-element.113), channel_id=1, source_target_pairs={{0,1},{1,0},{2,3},{3,2},{4,5},{5,4},{6,7},{7,6},{8,9},{9,8},{10,11... | collective-permute-start | bytes 983048 | tf_op jit(solution)/shard_map/ppermute | solution.py:359
  86.7 13.2 %collective-permute-start.40 = (bf16[80,1280]{1,0:T(8,128)(2,1)S(1)}, bf16[80,1280]{1,0:T(8,128)(2,1)S(1)}, u32[]{:S(2)}, u32[]{:S(2)}) collective-permute-start(bf16[80,1280]{1,0:T(8,128)(2,1)S(1)} %collective-permute-done.26.refs_4_), channel_id=1, source_target_pairs={{0,8},{8,16},{16,24},{24,28},{28,20},{20,12},{12,4},{4,0},{1,9},{9... | collective-permute-start | bytes 614408 | tf_op jit(solution)/shard_map/ppermute | solution.py:322
  93.4 8.9 %collective-permute-start.43 = (bf16[80,1280]{1,0:T(8,128)(2,1)S(1)}, bf16[80,1280]{1,0:T(8,128)(2,1)S(1)}, u32[]{:S(2)}, u32[]{:S(2)}) collective-permute-start(bf16[80,1280]{1,0:T(8,128)(2,1)S(1)} %collective-permute-done.39.refs_7_), channel_id=1, source_target_pairs={{8,0},{16,8},{24,16},{28,24},{20,28},{12,20},{4,12},{0,4},{9,1},{1... | collective-permute-start | bytes 614408 | tf_op jit(solution)/shard_map/ppermute | solution.py:323
  94.4 14.5 %collective-permute-start.34 = (bf16[320,512]{1,0:T(8,128)(2,1)S(1)}, bf16[320,512]{1,0:T(8,128)(2,1)S(1)}, u32[]{:S(2)}, u32[]{:S(2)}) collective-permute-start(bf16[320,512]{1,0:T(8,128)(2,1)S(1)} %add.3), channel_id=1, source_target_pairs={{0,2},{1,3},{2,0},{3,1},{4,6},{5,7},{6,4},{7,5},{8,10},{9,11},{10,... | collective-permute-start | bytes 983048 | tf_op jit(solution)/shard_map/ppermute | solution.py:362
  99.7 9.7 %collective-permute-start.32 = (bf16[320,512]{1,0:T(8,128)(2,1)S(1)}, bf16[320,512]{1,0:T(8,128)(2,1)S(1)}, u32[]{:S(2)}, u32[]{:S(2)}) collective-permute-start(bf16[320,512]{1,0:T(8,128)(2,1)S(1)} %get-tuple-element.117), channel_id=1, source_target_pairs={{0,1},{1,0},{2,3},{3,2},{4,5},{5,4},{6,7},{7,6},{8,9},{9,8},{10,11... | collective-permute-start | bytes 983048 | tf_op jit(solution)/shard_map/ppermute | solution.py:359
  99.8 10.7 %collective-permute-start.33 = (bf16[320,512]{1,0:T(8,128)(2,1)S(1)}, bf16[320,512]{1,0:T(8,128)(2,1)S(1)}, u32[]{:S(2)}, u32[]{:S(2)}) collective-permute-start(bf16[320,512]{1,0:T(8,128)(2,1)S(1)} %get-tuple-element.118), channel_id=1, source_target_pairs={{0,1},{1,0},{2,3},{3,2},{4,5},{5,4},{6,7},{7,6},{8,9},{9,8},{10,11... | collective-permute-start | bytes 983048 | tf_op jit(solution)/shard_map/ppermute | solution.py:359
  102.3 9.2 %collective-permute-start.35 = (bf16[320,512]{1,0:T(8,128)(2,1)S(1)}, bf16[320,512]{1,0:T(8,128)(2,1)S(1)}, u32[]{:S(2)}, u32[]{:S(2)}) collective-permute-start(bf16[320,512]{1,0:T(8,128)(2,1)S(1)} %add.4), channel_id=1, source_target_pairs={{0,2},{1,3},{2,0},{3,1},{4,6},{5,7},{6,4},{7,5},{8,10},{9,11},{10,... | collective-permute-start | bytes 983048 | tf_op jit(solution)/shard_map/ppermute | solution.py:362
  109.4 9.8 %collective-permute-start.46 = (bf16[80,1280]{1,0:T(8,128)(2,1)S(1)}, bf16[80,1280]{1,0:T(8,128)(2,1)S(1)}, u32[]{:S(2)}, u32[]{:S(2)}) collective-permute-start(bf16[80,1280]{1,0:T(8,128)(2,1)S(1)} %collective-permute-done.42.refs_10_), channel_id=1, source_target_pairs={{0,8},{8,16},{16,24},{24,28},{28,20},{20,12},{12,4},{4,0},{1,9},{9... | collective-permute-start | bytes 614408 | tf_op jit(solution)/shard_map/ppermute | solution.py:322
  (35 other events, 322.0 us)
Sparse Core Ops, SparseCore 0:
  9.5 28.2 all-gather.2

commit v8 on v7

--- a/solution.py
+++ b/solution.py
@@ -81,14 +81,17 @@
     return pl.ds(pl.multiple_of(start, 16), rows)
 
 
-def order_kernel(x_ref, o_ref):
+def order_kernel(x_ref, *outs):
     tokens = x_ref.shape[1]
     windows = tokens // WINDOW
     source = lax.broadcasted_iota(jnp.int32, (tokens, windows), 0)
     window = lax.broadcasted_iota(jnp.int32, (tokens, windows), 1)
+    each = WINDOW // len(outs)
     for p in range(WINDOW):
         pick = jnp.where(source == WINDOW * window + p, 1.0, 0.0).astype(BF16)
-        o_ref[p] = jnp.dot(x_ref[...], pick, preferred_element_type=F32).astype(BF16)
+        outs[p // each][p % each] = jnp.dot(
+            x_ref[...], pick, preferred_element_type=F32
+        ).astype(BF16)
 
 
 def shards_kernel(w_out, w_proj, *outs):
@@ -134,11 +137,13 @@
     slots_of[...] = jnp.where(mine >= 0, mine * bucket + rank - 1, groups * bucket)
 
 
-def norm_kernel(first, each, blocks, gain, bias, o_ref, whole):
-    rows, windows = blocks.shape[2:]
-    for k in range(blocks.shape[0]):
+def norm_kernel(own, over_x, over_core, over_both, gain, bias, o_ref, whole):
+    each, rows, windows = own.shape
+    mine = lax.axis_index("narrow")
+    for part, flip in zip((own, over_x, over_core, over_both), (0, 2, 1, 3)):
+        at = rows_at((mine ^ flip) * rows, rows)
         for j in range(each):
-            whole[k * rows : (k + 1) * rows, j * windows : (j + 1) * windows] = blocks[k, first + j]
+            whole[at, j * windows : (j + 1) * windows] = part[j]
     width, tokens = whole.shape
     step = 128
     for t in range(0, tokens, step):
@@ -217,16 +222,17 @@
         target[1] = v[block:]
 
 
-def stream_kernel(own, bias, *refs):
-    parts, o_ref = refs[:-1], refs[-1]
+def stream_kernel(own_count, bias, *refs):
+    own, parts, o_ref = refs[:own_count], refs[own_count:-1], refs[-1]
     count = len(parts) // 3
-    rows, windows = own.shape[1:]
-    each = WINDOW // count
+    rows, windows = own[0].shape[1:]
+    each, own_each = WINDOW // count, WINDOW // own_count
     for p in range(WINDOW):
         at = slice(p % each * windows, (p % each + 1) * windows)
         terms = [parts[i * count + p // each][:, at].astype(F32) for i in range(3)]
         total = terms[0] + terms[1] + terms[2] + bias[...]
-        o_ref[p * rows : (p + 1) * rows, :] = (own[p].astype(F32) + total).astype(BF16)
+        v = own[p // own_each][p % own_each].astype(F32) + total
+        o_ref[p * rows : (p + 1) * rows, :] = v.astype(BF16)
 
 
 LANES = 128
@@ -364,7 +370,8 @@
 
     def order(x):
         return call(
-            order_kernel, (x,), shape(WINDOW, width, windows), name="order_tokens",
+            order_kernel, (x,), [shape(WINDOW // halves, width, windows)] * halves,
+            name="order_tokens",
         )
 
     def shards(count):
@@ -380,12 +387,10 @@
             [shape(1, windows, dtype=jnp.int32), shape(slots, 1, dtype=jnp.int32)], name="route",
         )
 
-    def norm(blocks, half):
-        each = WINDOW // halves
-        count = each * windows
-        return call(
-            functools.partial(norm_kernel, half * each, each),
-            (blocks, norm_gain[None], norm_bias[None]), shape(count, full),
+    def norm(*blocks):
+        count = tokens // halves
+        return call(
+            norm_kernel, (*blocks, norm_gain[None], norm_bias[None]), shape(count, full),
             scratch=[pltpu.VMEM((full, count), BF16)], name="norm",
         )
 
@@ -411,7 +416,7 @@
 
     def stream(own, sums):
         return call(
-            stream_kernel, (own, b_out[:, None], *sums), shape(WINDOW * width, windows),
+            functools.partial(stream_kernel, halves), (b_out[:, None], *own, *sums), shape(WINDOW * width, windows),
             name="stream",
         )
 
@@ -444,8 +449,8 @@
         wholes = [lax.all_gather(s, "wide", axis=0, tiled=True) for s in shard]
         pieces = [Piece(0, k * width, width, None, 0, k) for k in range(parts)]
         own = order(patches.T)
-        blocks = lax.all_gather(own, "narrow")
-        normed = [norm(blocks, i) for i in range(halves)]
+        over_x = [far(x) for x in own]
+        normed = [norm(x, y, near(x), near(y)) for x, y in zip(own, over_x)]
         act = hidden(pieces, wholes[:1], normed, 0, ff)
         keep_x, give_x = mlp_out(pieces, wholes[1:2], [act], 1)
         keep, give = mlp_out(pieces, wholes[1:2], [act], 0)
@@ -484,25 +489,38 @@
 
     got, normed = {}, []
 
+    over_x, over_core, over_both = [], [], []
+
     def start_tokens():
         got["own"] = order(patches.T)
-        got["blocks"] = lax.all_gather(got["own"], "narrow")
-        ring.add_work(got["own"])
+        over_x.append(far(got["own"][0]))
+        ring.add_work(got["own"][0])
 
     def start_shards():
         got["shards"] = shards(2)
         ring.add_work(got["shards"][0])
 
-    def start_route():
+    def send_second():
+        over_x.append(far(ring.now(got["own"][1])))
         got["slots_of"], got["targets"] = route()
 
+    def send_core():
+        over_core.append(near(ring.now(got["own"][len(over_core)])))
+
+    def send_both():
+        over_both.append(near(ring.now(over_x[len(over_both)])))
+
     def start_norm():
-        normed.append(norm(ring.now(got["blocks"]), len(normed)))
+        i = len(normed)
+        normed.append(
+            norm(ring.now(got["own"][i]), over_x[i], over_core[i], over_both[i])
+        )
         ring.add_work(normed[-1])
 
     pieces_in, arrays_in = hops(
         [w_in[:half_rows], w_in[half_rows:]],
-        {0: start_tokens, 1: start_shards, 2: start_route},
+        {0: start_tokens, 1: start_shards, 2: send_second, 3: send_core, 4: send_both,
+         5: send_core, 6: send_both},
     )
 
     hiddens = []

time: 152 us -> 143 us (0.941)
  between operations: 13.7 us -> 0.33 us
  waiting for transfers between devices: 46.6 us -> 54.2 us
  Pallas kernels: 22.4 us -> 17.5 us
  starting transfers between devices: 49.9 us -> 52.7 us
    ppermute x21, waiting for transfers between devices: 23.4 us -> 28.5 us  [step(): lax.ppermute(to_right, 'wide', self.right)]
    pallas_call x19, Pallas kernels: 22.4 us -> 17.5 us  [call(): pl.pallas_call(kernel, out_shape=outs, in_specs=[VMEM] * len(operands), o...]
    ppermute x21, starting transfers between devices: 9.5 us -> 12.4 us  [step(): lax.ppermute(to_left, 'wide', self.left)]
    ppermute x21, waiting for transfers between devices: 16.4 us -> 18.6 us  [step(): lax.ppermute(to_left, 'wide', self.left)]
    unnamed x32 -> x20, local copies, waits for them, and re-layouts: 4.25 us -> 2.13 us
    ppermute x3 -> x5, starting transfers between devices: 3.91 us -> 4.78 us  [far(): return lax.ppermute(x, 'narrow', far_pairs)]
    ppermute x3 -> x5, waiting for transfers between devices: 5.22 us -> 5.42 us  [far(): return lax.ppermute(x, 'narrow', far_pairs)]
  transfers between devices with their start and end apart: 51 -> 56, of which waited for: 21 -> 27; matrix products, arithmetic and copies ran while one was open for 0% -> 0% of each run, Pallas kernels for 12% -> 10%
where the time goes in v8:
time: 143 us
  waiting for transfers between devices  54.2 us (38%)
  starting transfers between devices  52.7 us (37%)
  Pallas kernels  17.5 us (12%)
  blocking collectives  14.8 us (10%)
  local copies, waits for them, and re-layouts  3.48 us (2%)
    ppermute x21, starting transfers between devices, step(): lax.ppermute(to_right, 'wide', self.right)  34.9 us
    ppermute x21, waiting for transfers between devices, step(): lax.ppermute(to_right, 'wide', self.right)  28.5 us
    ppermute x21, waiting for transfers between devices, step(): lax.ppermute(to_left, 'wide', self.left)  18.6 us
    pallas_call x19, Pallas kernels, call(): pl.pallas_call(kernel, out_shape=outs, in_specs=[VMEM] * len(operands), o...  17.5 us
    all_to_all x1, blocking collectives, exchange_and_place(): lax.all_to_all(buffer, 'wide', split_axis=0, concat_axis=0, tiled=True)  14.8 us
    ppermute x21, starting transfers between devices, step(): lax.ppermute(to_left, 'wide', self.left)  12.4 us
    ppermute x5, waiting for transfers between devices, far(): return lax.ppermute(x, 'narrow', far_pairs)  5.42 us
    ppermute x5, starting transfers between devices, far(): return lax.ppermute(x, 'narrow', far_pairs)  4.78 us
  transfers between devices with their start and end apart: 56, of which 27 were waited for; matrix products, arithmetic and copies ran while one was open for 0% of the time, Pallas kernels for 10%

profile of v8, /device:TPU:0, one launch (start us, length us, event | category | flops | bytes accessed | tf_op | source)
XLA Modules:
  0.0 143.0 jit_solution(4929892255649480275)
XLA Ops:
  1.1 3.1 %collective-permute-start = (bf16[80,1280]{1,0:T(8,128)(2,1)S(1)}, bf16[80,1280]{1,0:T(8,128)(2,1)S(1)}, u32[]{:S(2)}, u32[]{:S(2)}) collective-permute-start(bf16[80,1280]{1,0:T(8,128)(2,1)S(1)} %get-tuple-element.148.refs_0_), channel_id=1, source_target_pairs={{0,8},{8,16},{16,24},{24,28},{28,20},{20,12},{12,4},{4,0},{1,9},{9... | collective-permute-start | bytes 614408 | tf_op jit(solution)/shard_map/ppermute | solution.py:328
  4.2 2.0 %collective-permute-start.2 = (bf16[80,1280]{1,0:T(8,128)(2,1)S(1)}, bf16[80,1280]{1,0:T(8,128)(2,1)S(1)}, u32[]{:S(2)}, u32[]{:S(2)}) collective-permute-start(bf16[80,1280]{1,0:T(8,128)(2,1)S(1)} %get-tuple-element.147.refs_1_), channel_id=1, source_target_pairs={{0,8},{8,16},{16,24},{24,28},{28,20},{20,12},{12,4},{4,0},{1,9},{9... | collective-permute-start | bytes 614408 | tf_op jit(solution)/shard_map/ppermute | solution.py:328
  8.2 2.0 %collective-permute-start.14 = (bf16[2,320,256]{2,1,0:T(8,128)(2,1)S(1)}, bf16[2,320,256]{2,1,0:T(8,128)(2,1)S(1)}, u32[]{:S(2)}, u32[]{:S(2)}) collective-permute-start(bf16[2,320,256]{2,1,0:T(8,128)(2,1)S(1)} %get-tuple-element.92.own.refs_0_), channel_id=1, source_target_pairs={{0,2},{1,3},{2,0},{3,1},{4,6},{5,7},{6,4},{7,5},{8,10},{9,11},{10,... | collective-permute-start | bytes 983048 | tf_op jit(solution)/shard_map/ppermute | solution.py:368
  10.2 2.0 %collective-permute-start.4 = (bf16[80,1280]{1,0:T(8,128)(2,1)S(1)}, bf16[80,1280]{1,0:T(8,128)(2,1)S(1)}, u32[]{:S(2)}, u32[]{:S(2)}) collective-permute-start(bf16[80,1280]{1,0:T(8,128)(2,1)S(1)} %collective-permute-done.refs_2_), channel_id=1, source_target_pairs={{0,8},{8,16},{16,24},{24,28},{28,20},{20,12},{12,4},{4,0},{1,9},{9... | collective-permute-start | bytes 614408 | tf_op jit(solution)/shard_map/ppermute | solution.py:328
  14.4 2.1 %collective-permute-start.6 = (bf16[80,1280]{1,0:T(8,128)(2,1)S(1)}, bf16[80,1280]{1,0:T(8,128)(2,1)S(1)}, u32[]{:S(2)}, u32[]{:S(2)}) collective-permute-start(bf16[80,1280]{1,0:T(8,128)(2,1)S(1)} %collective-permute-done.2.refs_4_), channel_id=1, source_target_pairs={{0,8},{8,16},{16,24},{24,28},{28,20},{20,12},{12,4},{4,0},{1,9},{9... | collective-permute-start | bytes 614408 | tf_op jit(solution)/shard_map/ppermute | solution.py:328
  16.6 2.2 %collective-permute-done.4.refs_6_ = bf16[80,1280]{1,0:T(8,128)(2,1)S(1)} collective-permute-done((bf16[80,1280]{1,0:T(8,128)(2,1)S(1)}, bf16[80,1280]{1,0:T(8,128)(2,1)S(1)}, u32[]{:S(2)}, u32[]{:S(2)}) %collective-permute-start.4) | collective-permute-done | bytes 204832 | tf_op jit(solution)/shard_map/ppermute | solution.py:328
  18.8 2.1 %collective-permute-start.8 = (bf16[80,1280]{1,0:T(8,128)(2,1)S(1)}, bf16[80,1280]{1,0:T(8,128)(2,1)S(1)}, u32[]{:S(2)}, u32[]{:S(2)}) collective-permute-start(bf16[80,1280]{1,0:T(8,128)(2,1)S(1)} %collective-permute-done.4.refs_6_), channel_id=1, source_target_pairs={{0,8},{8,16},{16,24},{24,28},{28,20},{20,12},{12,4},{4,0},{1,9},{9... | collective-permute-start | bytes 614408 | tf_op jit(solution)/shard_map/ppermute | solution.py:328
  21.0 2.2 %collective-permute-done.6.refs_8_ = bf16[80,1280]{1,0:T(8,128)(2,1)S(1)} collective-permute-done((bf16[80,1280]{1,0:T(8,128)(2,1)S(1)}, bf16[80,1280]{1,0:T(8,128)(2,1)S(1)}, u32[]{:S(2)}, u32[]{:S(2)}) %collective-permute-start.6) | collective-permute-done | bytes 204832 | tf_op jit(solution)/shard_map/ppermute | solution.py:328
  23.2 2.0 %collective-permute-start.21 = (bf16[2,320,256]{2,1,0:T(8,128)(2,1)S(1)}, bf16[2,320,256]{2,1,0:T(8,128)(2,1)S(1)}, u32[]{:S(2)}, u32[]{:S(2)}) collective-permute-start(bf16[2,320,256]{2,1,0:T(8,128)(2,1)S(1)} %get-tuple-element.102.own.refs_1_), channel_id=1, source_target_pairs={{0,2},{1,3},{2,0},{3,1},{4,6},{5,7},{6,4},{7,5},{8,10},{9,11},{10,... | collective-permute-start | bytes 983048 | tf_op jit(solution)/shard_map/ppermute | solution.py:368
  27.6 2.1 %collective-permute-start.11 = (bf16[80,1280]{1,0:T(8,128)(2,1)S(1)}, bf16[80,1280]{1,0:T(8,128)(2,1)S(1)}, u32[]{:S(2)}, u32[]{:S(2)}) collective-permute-start(bf16[80,1280]{1,0:T(8,128)(2,1)S(1)} %collective-permute-done.7.refs_9_), channel_id=1, source_target_pairs={{8,0},{16,8},{24,16},{28,24},{20,28},{12,20},{4,12},{0,4},{9,1},{1... | collective-permute-start | bytes 614408 | tf_op jit(solution)/shard_map/ppermute | solution.py:329
  29.9 2.3 %collective-permute-done.10.refs_12_ = bf16[80,1280]{1,0:T(8,128)(2,1)S(1)} collective-permute-done((bf16[80,1280]{1,0:T(8,128)(2,1)S(1)}, bf16[80,1280]{1,0:T(8,128)(2,1)S(1)}, u32[]{:S(2)}, u32[]{:S(2)}) %collective-permute-start.10) | collective-permute-done | bytes 204832 | tf_op jit(solution)/shard_map/ppermute | solution.py:328
  32.2 2.0 %collective-permute-start.13 = (bf16[80,1280]{1,0:T(8,128)(2,1)S(1)}, bf16[80,1280]{1,0:T(8,128)(2,1)S(1)}, u32[]{:S(2)}, u32[]{:S(2)}) collective-permute-start(bf16[80,1280]{1,0:T(8,128)(2,1)S(1)} %collective-permute-done.9.refs_11_), channel_id=1, source_target_pairs={{8,0},{16,8},{24,16},{28,24},{20,28},{12,20},{4,12},{0,4},{9,1},{1... | collective-permute-start | bytes 614408 | tf_op jit(solution)/shard_map/ppermute | solution.py:329
  36.2 2.0 %collective-permute-start.19 = (bf16[80,1280]{1,0:T(8,128)(2,1)S(1)}, bf16[80,1280]{1,0:T(8,128)(2,1)S(1)}, u32[]{:S(2)}, u32[]{:S(2)}) collective-permute-start(bf16[80,1280]{1,0:T(8,128)(2,1)S(1)} %get-tuple-element.98.refs_5_), channel_id=1, source_target_pairs={{0,8},{8,16},{16,24},{24,28},{28,20},{20,12},{12,4},{4,0},{1,9},{9... | collective-permute-start | bytes 614408 | tf_op jit(solution)/shard_map/ppermute | solution.py:328
  38.7 4.5 %collective-permute-done.19.refs_7_ = bf16[80,1280]{1,0:T(8,128)(2,1)S(1)} collective-permute-done((bf16[80,1280]{1,0:T(8,128)(2,1)S(1)}, bf16[80,1280]{1,0:T(8,128)(2,1)S(1)}, u32[]{:S(2)}, u32[]{:S(2)}) %collective-permute-start.19) | collective-permute-done | bytes 204832 | tf_op jit(solution)/shard_map/ppermute | solution.py:328
  43.3 2.0 %collective-permute-start.17 = (bf16[80,1280]{1,0:T(8,128)(2,1)S(1)}, bf16[80,1280]{1,0:T(8,128)(2,1)S(1)}, u32[]{:S(2)}, u32[]{:S(2)}) collective-permute-start(bf16[80,1280]{1,0:T(8,128)(2,1)S(1)} %get-tuple-element.99.refs_6_), channel_id=1, source_target_pairs={{0,8},{8,16},{16,24},{24,28},{28,20},{20,12},{12,4},{4,0},{1,9},{9... | collective-permute-start | bytes 614408 | tf_op jit(solution)/shard_map/ppermute | solution.py:328
  50.3 3.0 %collective-permute-done.18.refs_10_ = bf16[80,1280]{1,0:T(8,128)(2,1)S(1)} collective-permute-done((bf16[80,1280]{1,0:T(8,128)(2,1)S(1)}, bf16[80,1280]{1,0:T(8,128)(2,1)S(1)}, u32[]{:S(2)}, u32[]{:S(2)}) %collective-permute-start.18) | collective-permute-done | bytes 204832 | tf_op jit(solution)/shard_map/ppermute | solution.py:329
  53.3 2.0 %collective-permute-start.27 = (bf16[80,1280]{1,0:T(8,128)(2,1)S(1)}, bf16[80,1280]{1,0:T(8,128)(2,1)S(1)}, u32[]{:S(2)}, u32[]{:S(2)}) collective-permute-start(bf16[80,1280]{1,0:T(8,128)(2,1)S(1)} %collective-permute-done.17.refs_9_), channel_id=1, source_target_pairs={{0,8},{8,16},{16,24},{24,28},{28,20},{20,12},{12,4},{4,0},{1,9},{9... | collective-permute-start | bytes 614408 | tf_op jit(solution)/shard_map/ppermute | solution.py:328
  55.3 2.4 %collective-permute-done.30.refs_12_ = bf16[80,1280]{1,0:T(8,128)(2,1)S(1)} collective-permute-done((bf16[80,1280]{1,0:T(8,128)(2,1)S(1)}, bf16[80,1280]{1,0:T(8,128)(2,1)S(1)}, u32[]{:S(2)}, u32[]{:S(2)}) %collective-permute-start.30) | collective-permute-done | bytes 204832 | tf_op jit(solution)/shard_map/ppermute | solution.py:329
  58.7 2.1 %collective-permute-start.25 = (bf16[80,1280]{1,0:T(8,128)(2,1)S(1)}, bf16[80,1280]{1,0:T(8,128)(2,1)S(1)}, u32[]{:S(2)}, u32[]{:S(2)}) collective-permute-start(bf16[80,1280]{1,0:T(8,128)(2,1)S(1)} %collective-permute-done.24.refs_11_), channel_id=1, source_target_pairs={{0,8},{8,16},{16,24},{24,28},{28,20},{20,12},{12,4},{4,0},{1,9},{9... | collective-permute-start | bytes 614408 | tf_op jit(solution)/shard_map/ppermute | solution.py:328
  64.1 2.4 %collective-permute-done.33.refs_16_ = bf16[80,1280]{1,0:T(8,128)(2,1)S(1)} collective-permute-done((bf16[80,1280]{1,0:T(8,128)(2,1)S(1)}, bf16[80,1280]{1,0:T(8,128)(2,1)S(1)}, u32[]{:S(2)}, u32[]{:S(2)}) %collective-permute-start.33) | collective-permute-done | bytes 204832 | tf_op jit(solution)/shard_map/ppermute | solution.py:329
  76.3 2.5 %mlp_out.2 = (bf16[320,512]{1,0:T(8,128)(2,1)S(1)}, bf16[320,512]{1,0:T(8,128)(2,1)S(1)}, bf16[320,512]{1,0:T(8,128)(2,1)S(1)}, bf16[320,512]{1,0:T(8,128)(2,1)S(1)}) custom-call(bf16[1024,256]{1,0:T(8,128)(2,1)S(1)} %hidden.5.refs_0_, bf16[1024,256]{1,0:T(8,128)(2,1)S(1)} %hidden.7.refs_1_, bf16[1024,256]{1,0:T(8,128)(2,1)S(1)} %hidden.6.refs_2_, ...), custom_call_target="tpu_custom_call" | custom-call | tf_op jit(solution)/shard_map/mlp_out/pallas_call | solution.py:24
  78.8 1.6 %collective-permute-start.32 = (bf16[80,1280]{1,0:T(8,128)(2,1)S(1)}, bf16[80,1280]{1,0:T(8,128)(2,1)S(1)}, u32[]{:S(2)}, u32[]{:S(2)}) collective-permute-start(bf16[80,1280]{1,0:T(8,128)(2,1)S(1)} %get-tuple-element.134.refs_1_), channel_id=1, source_target_pairs={{0,8},{8,16},{16,24},{24,28},{28,20},{20,12},{12,4},{4,0},{1,9},{9... | collective-permute-start | bytes 614408 | tf_op jit(solution)/shard_map/ppermute | solution.py:328
  82.2 4.1 %collective-permute-done.32.refs_4_ = bf16[80,1280]{1,0:T(8,128)(2,1)S(1)} collective-permute-done((bf16[80,1280]{1,0:T(8,128)(2,1)S(1)}, bf16[80,1280]{1,0:T(8,128)(2,1)S(1)}, u32[]{:S(2)}, u32[]{:S(2)}) %collective-permute-start.32) | collective-permute-done | bytes 204832 | tf_op jit(solution)/shard_map/ppermute | solution.py:328
  90.8 2.3 %mlp_out.3 = (bf16[320,512]{1,0:T(8,128)(2,1)S(1)}, bf16[320,512]{1,0:T(8,128)(2,1)S(1)}, bf16[320,512]{1,0:T(8,128)(2,1)S(1)}, bf16[320,512]{1,0:T(8,128)(2,1)S(1)}) custom-call(bf16[1024,256]{1,0:T(8,128)(2,1)S(1)} %hidden.5.refs_0_, bf16[1024,256]{1,0:T(8,128)(2,1)S(1)} %hidden.7.refs_1_, bf16[1024,256]{1,0:T(8,128)(2,1)S(1)} %hidden.6.refs_2_, ...), custom_call_target="tpu_custom_call" | custom-call | tf_op jit(solution)/shard_map/mlp_out/pallas_call | solution.py:24
  95.6 1.8 %collective-permute-done.46.refs_8_ = bf16[80,1280]{1,0:T(8,128)(2,1)S(1)} collective-permute-done((bf16[80,1280]{1,0:T(8,128)(2,1)S(1)}, bf16[80,1280]{1,0:T(8,128)(2,1)S(1)}, u32[]{:S(2)}, u32[]{:S(2)}) %collective-permute-start.46) | collective-permute-done | bytes 204832 | tf_op jit(solution)/shard_map/ppermute | solution.py:328
  100.9 3.9 %collective-permute-done.48.refs_10_ = bf16[80,1280]{1,0:T(8,128)(2,1)S(1)} collective-permute-done((bf16[80,1280]{1,0:T(8,128)(2,1)S(1)}, bf16[80,1280]{1,0:T(8,128)(2,1)S(1)}, u32[]{:S(2)}, u32[]{:S(2)}) %collective-permute-start.48) | collective-permute-done | bytes 204832 | tf_op jit(solution)/shard_map/ppermute | solution.py:328
  109.4 3.4 %collective-permute-done.50.refs_12_ = bf16[80,1280]{1,0:T(8,128)(2,1)S(1)} collective-permute-done((bf16[80,1280]{1,0:T(8,128)(2,1)S(1)}, bf16[80,1280]{1,0:T(8,128)(2,1)S(1)}, u32[]{:S(2)}, u32[]{:S(2)}) %collective-permute-start.50) | collective-permute-done | bytes 204832 | tf_op jit(solution)/shard_map/ppermute | solution.py:328
  112.8 1.6 %collective-permute-done.51.refs_13_ = bf16[80,1280]{1,0:T(8,128)(2,1)S(1)} collective-permute-done((bf16[80,1280]{1,0:T(8,128)(2,1)S(1)}, bf16[80,1280]{1,0:T(8,128)(2,1)S(1)}, u32[]{:S(2)}, u32[]{:S(2)}) %collective-permute-start.51) | collective-permute-done | bytes 204832 | tf_op jit(solution)/shard_map/ppermute | solution.py:329
  115.5 1.6 %collective-permute-done.53.refs_15_ = bf16[80,1280]{1,0:T(8,128)(2,1)S(1)} collective-permute-done((bf16[80,1280]{1,0:T(8,128)(2,1)S(1)}, bf16[80,1280]{1,0:T(8,128)(2,1)S(1)}, u32[]{:S(2)}, u32[]{:S(2)}) %collective-permute-start.53) | collective-permute-done | bytes 204832 | tf_op jit(solution)/shard_map/ppermute | solution.py:329
  118.5 1.6 %collective-permute-done.54.near = bf16[2,320,256]{2,1,0:T(8,128)(2,1)S(1)} collective-permute-done((bf16[2,320,256]{2,1,0:T(8,128)(2,1)S(1)}, bf16[2,320,256]{2,1,0:T(8,128)(2,1)S(1)}, u32[]{:S(2)}, u32[]{:S(2)}) %collective-permute-start.54) | collective-permute-done | bytes 327712 | tf_op jit(solution)/shard_map/ppermute | solution.py:365
  121.1 5.4 %collective-permute-done.55.far = bf16[320,256]{1,0:T(8,128)(2,1)S(1)} collective-permute-done((bf16[320,256]{1,0:T(8,128)(2,1)S(1)}, bf16[320,256]{1,0:T(8,128)(2,1)S(1)}, u32[]{:S(2)}, u32[]{:S(2)}) %collective-permute-start.55) | collective-permute-done | bytes 163872 | tf_op jit(solution)/shard_map/ppermute | solution.py:368
  126.9 14.8 %all_to_all.5.arrived = bf16[8,160,128]{2,1,0:T(8,128)(2,1)S(1)} all-to-all(bf16[8,160,128]{2,1,0:T(8,128)(2,1)S(1)} %pack.1), channel_id=1, replica_groups=mesh['wide'=8,'narrow'=4] {'wide'}, dimensions={0} | all-to-all | bytes 655360 | tf_op jit(solution)/shard_map/all_to_all | solution.py:441
  (129 shorter events, 51.6 us)
Async XLA Ops:
  1.1 9.1 %collective-permute-start = (bf16[80,1280]{1,0:T(8,128)(2,1)S(1)}, bf16[80,1280]{1,0:T(8,128)(2,1)S(1)}, u32[]{:S(2)}, u32[]{:S(2)}) collective-permute-start(bf16[80,1280]{1,0:T(8,128)(2,1)S(1)} %get-tuple-element.148.refs_0_), channel_id=1, source_target_pairs={{0,8},{8,16},{16,24},{24,28},{28,20},{20,12},{12,4},{4,0},{1,9},{9... | collective-permute-start | bytes 614408 | tf_op jit(solution)/shard_map/ppermute | solution.py:328
  4.2 10.2 %collective-permute-start.2 = (bf16[80,1280]{1,0:T(8,128)(2,1)S(1)}, bf16[80,1280]{1,0:T(8,128)(2,1)S(1)}, u32[]{:S(2)}, u32[]{:S(2)}) collective-permute-start(bf16[80,1280]{1,0:T(8,128)(2,1)S(1)} %get-tuple-element.147.refs_1_), channel_id=1, source_target_pairs={{0,8},{8,16},{16,24},{24,28},{28,20},{20,12},{12,4},{4,0},{1,9},{9... | collective-permute-start | bytes 614408 | tf_op jit(solution)/shard_map/ppermute | solution.py:328
  6.2 10.4 %collective-permute-start.3 = (bf16[80,1280]{1,0:T(8,128)(2,1)S(1)}, bf16[80,1280]{1,0:T(8,128)(2,1)S(1)}, u32[]{:S(2)}, u32[]{:S(2)}) collective-permute-start(bf16[80,1280]{1,0:T(8,128)(2,1)S(1)} %get-tuple-element.148.refs_0_), channel_id=1, source_target_pairs={{8,0},{16,8},{24,16},{28,24},{20,28},{12,20},{4,12},{0,4},{9,1},{1... | collective-permute-start | bytes 614408 | tf_op jit(solution)/shard_map/ppermute | solution.py:329
  8.2 17.1 %collective-permute-start.14 = (bf16[2,320,256]{2,1,0:T(8,128)(2,1)S(1)}, bf16[2,320,256]{2,1,0:T(8,128)(2,1)S(1)}, u32[]{:S(2)}, u32[]{:S(2)}) collective-permute-start(bf16[2,320,256]{2,1,0:T(8,128)(2,1)S(1)} %get-tuple-element.92.own.refs_0_), channel_id=1, source_target_pairs={{0,2},{1,3},{2,0},{3,1},{4,6},{5,7},{6,4},{7,5},{8,10},{9,11},{10,... | collective-permute-start | bytes 983048 | tf_op jit(solution)/shard_map/ppermute | solution.py:368
  10.2 8.6 %collective-permute-start.4 = (bf16[80,1280]{1,0:T(8,128)(2,1)S(1)}, bf16[80,1280]{1,0:T(8,128)(2,1)S(1)}, u32[]{:S(2)}, u32[]{:S(2)}) collective-permute-start(bf16[80,1280]{1,0:T(8,128)(2,1)S(1)} %collective-permute-done.refs_2_), channel_id=1, source_target_pairs={{0,8},{8,16},{16,24},{24,28},{28,20},{20,12},{12,4},{4,0},{1,9},{9... | collective-permute-start | bytes 614408 | tf_op jit(solution)/shard_map/ppermute | solution.py:328
  12.2 8.8 %collective-permute-start.5 = (bf16[80,1280]{1,0:T(8,128)(2,1)S(1)}, bf16[80,1280]{1,0:T(8,128)(2,1)S(1)}, u32[]{:S(2)}, u32[]{:S(2)}) collective-permute-start(bf16[80,1280]{1,0:T(8,128)(2,1)S(1)} %collective-permute-done.1.refs_3_), channel_id=1, source_target_pairs={{8,0},{16,8},{24,16},{28,24},{20,28},{12,20},{4,12},{0,4},{9,1},{1... | collective-permute-start | bytes 614408 | tf_op jit(solution)/shard_map/ppermute | solution.py:329
  14.4 8.8 %collective-permute-start.6 = (bf16[80,1280]{1,0:T(8,128)(2,1)S(1)}, bf16[80,1280]{1,0:T(8,128)(2,1)S(1)}, u32[]{:S(2)}, u32[]{:S(2)}) collective-permute-start(bf16[80,1280]{1,0:T(8,128)(2,1)S(1)} %collective-permute-done.2.refs_4_), channel_id=1, source_target_pairs={{0,8},{8,16},{16,24},{24,28},{28,20},{20,12},{12,4},{4,0},{1,9},{9... | collective-permute-start | bytes 614408 | tf_op jit(solution)/shard_map/ppermute | solution.py:328
  16.6 10.2 %collective-permute-start.7 = (bf16[80,1280]{1,0:T(8,128)(2,1)S(1)}, bf16[80,1280]{1,0:T(8,128)(2,1)S(1)}, u32[]{:S(2)}, u32[]{:S(2)}) collective-permute-start(bf16[80,1280]{1,0:T(8,128)(2,1)S(1)} %collective-permute-done.3.refs_5_), channel_id=1, source_target_pairs={{8,0},{16,8},{24,16},{28,24},{20,28},{12,20},{4,12},{0,4},{9,1},{1... | collective-permute-start | bytes 614408 | tf_op jit(solution)/shard_map/ppermute | solution.py:329
  18.8 8.8 %collective-permute-start.8 = (bf16[80,1280]{1,0:T(8,128)(2,1)S(1)}, bf16[80,1280]{1,0:T(8,128)(2,1)S(1)}, u32[]{:S(2)}, u32[]{:S(2)}) collective-permute-start(bf16[80,1280]{1,0:T(8,128)(2,1)S(1)} %collective-permute-done.4.refs_6_), channel_id=1, source_target_pairs={{0,8},{8,16},{16,24},{24,28},{28,20},{20,12},{12,4},{4,0},{1,9},{9... | collective-permute-start | bytes 614408 | tf_op jit(solution)/shard_map/ppermute | solution.py:328
  21.0 8.7 %collective-permute-start.9 = (bf16[80,1280]{1,0:T(8,128)(2,1)S(1)}, bf16[80,1280]{1,0:T(8,128)(2,1)S(1)}, u32[]{:S(2)}, u32[]{:S(2)}) collective-permute-start(bf16[80,1280]{1,0:T(8,128)(2,1)S(1)} %collective-permute-done.5.refs_7_), channel_id=1, source_target_pairs={{8,0},{16,8},{24,16},{28,24},{20,28},{12,20},{4,12},{0,4},{9,1},{1... | collective-permute-start | bytes 614408 | tf_op jit(solution)/shard_map/ppermute | solution.py:329
  23.2 12.5 %collective-permute-start.21 = (bf16[2,320,256]{2,1,0:T(8,128)(2,1)S(1)}, bf16[2,320,256]{2,1,0:T(8,128)(2,1)S(1)}, u32[]{:S(2)}, u32[]{:S(2)}) collective-permute-start(bf16[2,320,256]{2,1,0:T(8,128)(2,1)S(1)} %get-tuple-element.102.own.refs_1_), channel_id=1, source_target_pairs={{0,2},{1,3},{2,0},{3,1},{4,6},{5,7},{6,4},{7,5},{8,10},{9,11},{10,... | collective-permute-start | bytes 983048 | tf_op jit(solution)/shard_map/ppermute | solution.py:368
  26.8 9.4 %collective-permute-start.15 = (bf16[2,320,256]{2,1,0:T(8,128)(2,1)S(1)}, bf16[2,320,256]{2,1,0:T(8,128)(2,1)S(1)}, u32[]{:S(2)}, u32[]{:S(2)}) collective-permute-start(bf16[2,320,256]{2,1,0:T(8,128)(2,1)S(1)} %get-tuple-element.92.own.refs_0_), channel_id=1, source_target_pairs={{0,1},{1,0},{2,3},{3,2},{4,5},{5,4},{6,7},{7,6},{8,9},{9,8},{10,11... | collective-permute-start | bytes 983048 | tf_op jit(solution)/shard_map/ppermute | solution.py:365
  29.7 8.6 %collective-permute-start.12 = (bf16[80,1280]{1,0:T(8,128)(2,1)S(1)}, bf16[80,1280]{1,0:T(8,128)(2,1)S(1)}, u32[]{:S(2)}, u32[]{:S(2)}) collective-permute-start(bf16[80,1280]{1,0:T(8,128)(2,1)S(1)} %collective-permute-done.8.refs_10_), channel_id=1, source_target_pairs={{0,8},{8,16},{16,24},{24,28},{28,20},{20,12},{12,4},{4,0},{1,9},{9... | collective-permute-start | bytes 614408 | tf_op jit(solution)/shard_map/ppermute | solution.py:328
  35.7 9.7 %collective-permute-start.16 = (bf16[2,320,256]{2,1,0:T(8,128)(2,1)S(1)}, bf16[2,320,256]{2,1,0:T(8,128)(2,1)S(1)}, u32[]{:S(2)}, u32[]{:S(2)}) collective-permute-start(bf16[2,320,256]{2,1,0:T(8,128)(2,1)S(1)} %collective-permute-done.14.over_x), channel_id=1, source_target_pairs={{0,1},{1,0},{2,3},{3,2},{4,5},{5,4},{6,7},{7,6},{8,9},{9,8},{10,11... | collective-permute-start | bytes 983048 | tf_op jit(solution)/shard_map/ppermute | solution.py:365
  35.7 12.6 %collective-permute-start.22 = (bf16[2,320,256]{2,1,0:T(8,128)(2,1)S(1)}, bf16[2,320,256]{2,1,0:T(8,128)(2,1)S(1)}, u32[]{:S(2)}, u32[]{:S(2)}) collective-permute-start(bf16[2,320,256]{2,1,0:T(8,128)(2,1)S(1)} %get-tuple-element.102.own.refs_1_), channel_id=1, source_target_pairs={{0,1},{1,0},{2,3},{3,2},{4,5},{5,4},{6,7},{7,6},{8,9},{9,8},{10,11... | collective-permute-start | bytes 983048 | tf_op jit(solution)/shard_map/ppermute | solution.py:365
  38.7 10.2 %collective-permute-start.23 = (bf16[2,320,256]{2,1,0:T(8,128)(2,1)S(1)}, bf16[2,320,256]{2,1,0:T(8,128)(2,1)S(1)}, u32[]{:S(2)}, u32[]{:S(2)}) collective-permute-start(bf16[2,320,256]{2,1,0:T(8,128)(2,1)S(1)} %collective-permute-done.21.over_x), channel_id=1, source_target_pairs={{0,1},{1,0},{2,3},{3,2},{4,5},{5,4},{6,7},{7,6},{8,9},{9,8},{10,11... | collective-permute-start | bytes 983048 | tf_op jit(solution)/shard_map/ppermute | solution.py:365
  45.4 12.3 %collective-permute-start.30 = (bf16[80,1280]{1,0:T(8,128)(2,1)S(1)}, bf16[80,1280]{1,0:T(8,128)(2,1)S(1)}, u32[]{:S(2)}, u32[]{:S(2)}) collective-permute-start(bf16[80,1280]{1,0:T(8,128)(2,1)S(1)} %collective-permute-done.20.refs_8_), channel_id=1, source_target_pairs={{8,0},{16,8},{24,16},{28,24},{20,28},{12,20},{4,12},{0,4},{9,1},{1... | collective-permute-start | bytes 614408 | tf_op jit(solution)/shard_map/ppermute | solution.py:329
  48.3 9.4 %collective-permute-start.24 = (bf16[80,1280]{1,0:T(8,128)(2,1)S(1)}, bf16[80,1280]{1,0:T(8,128)(2,1)S(1)}, u32[]{:S(2)}, u32[]{:S(2)}) collective-permute-start(bf16[80,1280]{1,0:T(8,128)(2,1)S(1)} %collective-permute-done.19.refs_7_), channel_id=1, source_target_pairs={{0,8},{8,16},{16,24},{24,28},{28,20},{20,12},{12,4},{4,0},{1,9},{9... | collective-permute-start | bytes 614408 | tf_op jit(solution)/shard_map/ppermute | solution.py:328
  53.3 8.8 %collective-permute-start.26 = (bf16[80,1280]{1,0:T(8,128)(2,1)S(1)}, bf16[80,1280]{1,0:T(8,128)(2,1)S(1)}, u32[]{:S(2)}, u32[]{:S(2)}) collective-permute-start(bf16[80,1280]{1,0:T(8,128)(2,1)S(1)} %collective-permute-done.18.refs_10_), channel_id=1, source_target_pairs={{8,0},{16,8},{24,16},{28,24},{20,28},{12,20},{4,12},{0,4},{9,1},{1... | collective-permute-start | bytes 614408 | tf_op jit(solution)/shard_map/ppermute | solution.py:329
  53.3 8.8 %collective-permute-start.27 = (bf16[80,1280]{1,0:T(8,128)(2,1)S(1)}, bf16[80,1280]{1,0:T(8,128)(2,1)S(1)}, u32[]{:S(2)}, u32[]{:S(2)}) collective-permute-start(bf16[80,1280]{1,0:T(8,128)(2,1)S(1)} %collective-permute-done.17.refs_9_), channel_id=1, source_target_pairs={{0,8},{8,16},{16,24},{24,28},{28,20},{20,12},{12,4},{4,0},{1,9},{9... | collective-permute-start | bytes 614408 | tf_op jit(solution)/shard_map/ppermute | solution.py:328
  57.7 8.8 %collective-permute-start.33 = (bf16[80,1280]{1,0:T(8,128)(2,1)S(1)}, bf16[80,1280]{1,0:T(8,128)(2,1)S(1)}, u32[]{:S(2)}, u32[]{:S(2)}) collective-permute-start(bf16[80,1280]{1,0:T(8,128)(2,1)S(1)} %collective-permute-done.30.refs_12_), channel_id=1, source_target_pairs={{8,0},{16,8},{24,16},{28,24},{20,28},{12,20},{4,12},{0,4},{9,1},{1... | collective-permute-start | bytes 614408 | tf_op jit(solution)/shard_map/ppermute | solution.py:329
  62.1 8.8 %collective-permute-start.29 = (bf16[80,1280]{1,0:T(8,128)(2,1)S(1)}, bf16[80,1280]{1,0:T(8,128)(2,1)S(1)}, u32[]{:S(2)}, u32[]{:S(2)}) collective-permute-start(bf16[80,1280]{1,0:T(8,128)(2,1)S(1)} %collective-permute-done.26.refs_14_), channel_id=1, source_target_pairs={{8,0},{16,8},{24,16},{28,24},{20,28},{12,20},{4,12},{0,4},{9,1},{1... | collective-permute-start | bytes 614408 | tf_op jit(solution)/shard_map/ppermute | solution.py:329
  66.5 8.8 %collective-permute-start.34 = (bf16[80,1280]{1,0:T(8,128)(2,1)S(1)}, bf16[80,1280]{1,0:T(8,128)(2,1)S(1)}, u32[]{:S(2)}, u32[]{:S(2)}) collective-permute-start(bf16[80,1280]{1,0:T(8,128)(2,1)S(1)} %collective-permute-done.33.refs_16_), channel_id=1, source_target_pairs={{8,0},{16,8},{24,16},{28,24},{20,28},{12,20},{4,12},{0,4},{9,1},{1... | collective-permute-start | bytes 614408 | tf_op jit(solution)/shard_map/ppermute | solution.py:329
  70.9 10.0 %collective-permute-start.43 = (bf16[80,1280]{1,0:T(8,128)(2,1)S(1)}, bf16[80,1280]{1,0:T(8,128)(2,1)S(1)}, u32[]{:S(2)}, u32[]{:S(2)}) collective-permute-start(bf16[80,1280]{1,0:T(8,128)(2,1)S(1)} %get-tuple-element.134.refs_1_), channel_id=1, source_target_pairs={{8,0},{16,8},{24,16},{28,24},{20,28},{12,20},{4,12},{0,4},{9,1},{1... | collective-permute-start | bytes 614408 | tf_op jit(solution)/shard_map/ppermute | solution.py:329
  78.7 11.2 %collective-permute-start.36 = (bf16[320,512]{1,0:T(8,128)(2,1)S(1)}, bf16[320,512]{1,0:T(8,128)(2,1)S(1)}, u32[]{:S(2)}, u32[]{:S(2)}) collective-permute-start(bf16[320,512]{1,0:T(8,128)(2,1)S(1)} %get-tuple-element.125), channel_id=1, source_target_pairs={{0,1},{1,0},{2,3},{3,2},{4,5},{5,4},{6,7},{7,6},{8,9},{9,8},{10,11... | collective-permute-start | bytes 983048 | tf_op jit(solution)/shard_map/ppermute | solution.py:365
  80.9 9.6 %collective-permute-start.37 = (bf16[320,512]{1,0:T(8,128)(2,1)S(1)}, bf16[320,512]{1,0:T(8,128)(2,1)S(1)}, u32[]{:S(2)}, u32[]{:S(2)}) collective-permute-start(bf16[320,512]{1,0:T(8,128)(2,1)S(1)} %get-tuple-element.127), channel_id=1, source_target_pairs={{0,1},{1,0},{2,3},{3,2},{4,5},{5,4},{6,7},{7,6},{8,9},{9,8},{10,11... | collective-permute-start | bytes 983048 | tf_op jit(solution)/shard_map/ppermute | solution.py:365
  80.9 12.2 %collective-permute-start.45 = (bf16[80,1280]{1,0:T(8,128)(2,1)S(1)}, bf16[80,1280]{1,0:T(8,128)(2,1)S(1)}, u32[]{:S(2)}, u32[]{:S(2)}) collective-permute-start(bf16[80,1280]{1,0:T(8,128)(2,1)S(1)} %collective-permute-done.43.refs_3_), channel_id=1, source_target_pairs={{8,0},{16,8},{24,16},{28,24},{20,28},{12,20},{4,12},{0,4},{9,1},{1... | collective-permute-start | bytes 614408 | tf_op jit(solution)/shard_map/ppermute | solution.py:329
  88.4 9.0 %collective-permute-start.46 = (bf16[80,1280]{1,0:T(8,128)(2,1)S(1)}, bf16[80,1280]{1,0:T(8,128)(2,1)S(1)}, u32[]{:S(2)}, u32[]{:S(2)}) collective-permute-start(bf16[80,1280]{1,0:T(8,128)(2,1)S(1)} %collective-permute-done.32.refs_4_), channel_id=1, source_target_pairs={{0,8},{8,16},{16,24},{24,28},{28,20},{20,12},{12,4},{4,0},{1,9},{9... | collective-permute-start | bytes 614408 | tf_op jit(solution)/shard_map/ppermute | solution.py:328
  90.5 15.9 %collective-permute-start.40 = (bf16[320,512]{1,0:T(8,128)(2,1)S(1)}, bf16[320,512]{1,0:T(8,128)(2,1)S(1)}, u32[]{:S(2)}, u32[]{:S(2)}) collective-permute-start(bf16[320,512]{1,0:T(8,128)(2,1)S(1)} %add.3), channel_id=1, source_target_pairs={{0,2},{1,3},{2,0},{3,1},{4,6},{5,7},{6,4},{7,5},{8,10},{9,11},{10,... | collective-permute-start | bytes 983048 | tf_op jit(solution)/shard_map/ppermute | solution.py:368
  95.6 11.3 %collective-permute-start.38 = (bf16[320,512]{1,0:T(8,128)(2,1)S(1)}, bf16[320,512]{1,0:T(8,128)(2,1)S(1)}, u32[]{:S(2)}, u32[]{:S(2)}) collective-permute-start(bf16[320,512]{1,0:T(8,128)(2,1)S(1)} %get-tuple-element.131), channel_id=1, source_target_pairs={{0,1},{1,0},{2,3},{3,2},{4,5},{5,4},{6,7},{7,6},{8,9},{9,8},{10,11... | collective-permute-start | bytes 983048 | tf_op jit(solution)/shard_map/ppermute | solution.py:365
  97.3 11.1 %collective-permute-start.39 = (bf16[320,512]{1,0:T(8,128)(2,1)S(1)}, bf16[320,512]{1,0:T(8,128)(2,1)S(1)}, u32[]{:S(2)}, u32[]{:S(2)}) collective-permute-start(bf16[320,512]{1,0:T(8,128)(2,1)S(1)} %get-tuple-element.132), channel_id=1, source_target_pairs={{0,1},{1,0},{2,3},{3,2},{4,5},{5,4},{6,7},{7,6},{8,9},{9,8},{10,11... | collective-permute-start | bytes 983048 | tf_op jit(solution)/shard_map/ppermute | solution.py:365
  108.5 8.6 %collective-permute-start.53 = (bf16[80,1280]{1,0:T(8,128)(2,1)S(1)}, bf16[80,1280]{1,0:T(8,128)(2,1)S(1)}, u32[]{:S(2)}, u32[]{:S(2)}) collective-permute-start(bf16[80,1280]{1,0:T(8,128)(2,1)S(1)} %collective-permute-done.49.refs_11_), channel_id=1, source_target_pairs={{8,0},{16,8},{24,16},{28,24},{20,28},{12,20},{4,12},{0,4},{9,1},{1... | collective-permute-start | bytes 614408 | tf_op jit(solution)/shard_map/ppermute | solution.py:329
  (34 other events, 349.2 us)

commit v9 on v4

--- a/solution.py
+++ b/solution.py
@@ -10,7 +10,10 @@
 F32 = jnp.float32
 BF16 = jnp.bfloat16
 WINDOW = 4
-LATE = (1, 2, 3)
+LATE = (1, 2, 2)
+HIDDEN_AT = (7, 7, 8, 8, 8)
+OUT_AT = 1
+SUMS_AT = 2
 VMEM = pl.BlockSpec(memory_space=pltpu.VMEM)
 
 
@@ -87,13 +90,11 @@
         ).astype(BF16)
 
 
-def shards_kernel(w_out, w_proj, *outs):
-    rows, width = w_proj.shape[1], w_proj.shape[2]
-    half = rows // (len(outs) // 2)
+def shards_kernel(w_proj, *outs):
+    half = w_proj.shape[1] // len(outs)
     flat = jnp.concatenate([w_proj[p] for p in range(WINDOW)], axis=1)
-    for i in range(len(outs) // 2):
-        outs[i][...] = w_out[i * half : (i + 1) * half, :]
-        outs[len(outs) // 2 + i][...] = flat[i * half : (i + 1) * half, :]
+    for i, o_ref in enumerate(outs):
+        o_ref[...] = flat[i * half : (i + 1) * half, :]
 
 
 def route_kernel(seq_rows, bucket, place, slots_of, targets):
@@ -370,10 +371,10 @@
         )
 
     def shards(count):
-        rows = shard_rows[1] // count
-        return call(
-            shards_kernel, (w_out.T, jnp.transpose(w_proj, (0, 2, 1))),
-            [shape(rows, full)] * (2 * count), name="shards",
+        rows = shard_rows[2] // count
+        return call(
+            shards_kernel, (jnp.transpose(w_proj, (0, 2, 1)),),
+            [shape(rows, WINDOW * width)] * count, name="shards",
         )
 
     def route():
@@ -441,7 +442,7 @@
 
 
     if not small:
-        shard = [w_in, *shards(1)]
+        shard = [w_in, w_out.T, *shards(1)]
         wholes = [lax.all_gather(s, "wide", axis=0, tiled=True) for s in shard]
         pieces = [Piece(0, k * width, width, None, 0, k) for k in range(parts)]
         own = order(patches.T)
@@ -483,6 +484,30 @@
                 t += 1
         return pieces, arrays
 
+    def hops_of_two(shards, work):
+        arrays = [[x] for x in shards]
+        pieces = [[Piece(0, 0, 2 * half_rows, 0, 0)] for _ in shards]
+        held = {(way, k): x for way in (0, 1) for k, x in enumerate(shards)}
+        t = 0
+        for step in range(1, last + 1):
+            for k in range(len(shards)):
+                sent = [held[0, k], held[1, k]]
+                rows, bases = 2 * half_rows, (0, 0)
+                if step == last:
+                    sent = [sent[0][:half_rows], sent[1][half_rows:]]
+                    rows, bases = half_rows, (0, half_rows)
+                pair = ring.step(*sent)
+                for way in (0, 1):
+                    held[way, k] = pair[way]
+                    shift = -step if way == 0 else step
+                    pieces[k].append(Piece(len(arrays[k]), 0, rows, shift, bases[way]))
+                    arrays[k].append(pair[way])
+                if t in work:
+                    for run in work[t]:
+                        run(pieces, arrays)
+                t += 1
+        return pieces, arrays
+
     own, over_x, over_core, over_both, normed = [], [], [], [], []
     got = {}
 
@@ -513,12 +538,6 @@
         send_both()
         start_norm()
 
-    pieces_in, arrays_in = gather(
-        [w_in[:half_rows], w_in[half_rows:]],
-        {0: start_tokens, 1: start_shards, 2: send_second, 4: send_both, 5: both_and_norm,
-         6: start_norm},
-    )
-
     columns = 256
     hiddens = []
 
@@ -527,9 +546,20 @@
         hiddens.append(hidden(pieces_in, arrays_in, rows, len(hiddens) * columns, columns))
         ring.add_work(hiddens[-1])
 
-    pieces_out, arrays_out = gather(
-        got["shards"][:2], {t: start_hidden for t in range(ff // columns)}
-    )
+    early = {0: start_tokens, 1: send_second, 2: start_shards, 3: send_both, 4: both_and_norm,
+             5: start_norm}
+    work = {t: [lambda p, a, run=run: run()] for t, run in early.items()}
+    first_of_last = 2 * last
+
+    def hidden_in_pair(pieces, arrays):
+        rows = [ring.now(normed[0]), *normed[1:]]
+        hiddens.append(hidden(pieces[0], arrays[0], rows, len(hiddens) * columns, columns))
+        ring.add_work(hiddens[-1])
+
+    for t in HIDDEN_AT:
+        if t < first_of_last:
+            work.setdefault(t, []).append(hidden_in_pair)
+    (pieces_in, pieces_out), (arrays_in, arrays_out) = hops_of_two([w_in, w_out.T], work)
 
     def start_out(over_x):
         acts = [ring.now(hiddens[0]), *hiddens[1:]]
@@ -547,8 +577,21 @@
         ring.add_work(sums[0])
         start_out(0)
 
+    plan = {}
+    for t in HIDDEN_AT:
+        if t >= first_of_last:
+            plan.setdefault(t - first_of_last, []).append(start_hidden)
+    plan.setdefault(OUT_AT, []).append(lambda: start_out(1))
+    plan.setdefault(SUMS_AT, []).append(start_sums)
+
+    def run_all(steps):
+        def run():
+            for step in steps:
+                step()
+        return run
+
     pieces_proj, arrays_proj = gather(
-        got["shards"][2:], {0: lambda: start_out(1), 1: start_sums}
+        got["shards"], {t: run_all(steps) for t, steps in plan.items()}
     )
 
     merged = stream(own, got["keep", 0], got["core", 0], got["x_sums"])

time: 139 us -> 138 us (level)
  starting transfers between devices: 51.4 us -> 48.9 us
    ppermute x21 -> x15, starting transfers between devices: 31.7 us -> 21.9 us  [step(): lax.ppermute(to_left, 'wide', self.left)]
    ppermute x21 -> x15, starting transfers between devices: 10.4 us -> 14.8 us  [step(): lax.ppermute(to_right, 'wide', self.right)]
    ppermute x7, waiting for transfers between devices: 10 us -> 14.3 us  [far(): return lax.ppermute(x, 'narrow', far_pairs)]
    ppermute x7, starting transfers between devices: 8.47 us -> 11 us  [far(): return lax.ppermute(x, 'narrow', far_pairs)]
    ppermute x13, waiting for transfers between devices: 3.6 us -> 1.63 us  [near(): return lax.ppermute(x, 'narrow', near_pairs)]
    ppermute x21 -> x15, waiting for transfers between devices: 7.31 us -> 5.76 us  [step(): lax.ppermute(to_left, 'wide', self.left)]
    ppermute x21 -> x15, waiting for transfers between devices: 30.2 us -> 30.4 us  [step(): lax.ppermute(to_right, 'wide', self.right)]
  transfers between devices with their start and end apart: 62 -> 50, of which waited for: 37 -> 18; matrix products, arithmetic and copies ran while one was open for 0% -> 1% of each run, Pallas kernels for 10% -> 10%
where the time goes in v9:
time: 138 us
  waiting for transfers between devices  52.1 us (38%)
  starting transfers between devices  48.9 us (35%)
  Pallas kernels  17.4 us (13%)
  blocking collectives  15.2 us (11%)
  local copies, waits for them, and re-layouts  3.84 us (3%)
    ppermute x15, waiting for transfers between devices, step(): lax.ppermute(to_right, 'wide', self.right)  30.4 us
    ppermute x15, starting transfers between devices, step(): lax.ppermute(to_left, 'wide', self.left)  21.9 us
    pallas_call x21, Pallas kernels, call(): pl.pallas_call(kernel, out_shape=outs, in_specs=[VMEM] * len(operands), o...  17.4 us
    all_to_all x1, blocking collectives, exchange_and_place(): lax.all_to_all(buffer, 'wide', split_axis=0, concat_axis=0, tiled=True)  15.2 us
    ppermute x15, starting transfers between devices, step(): lax.ppermute(to_right, 'wide', self.right)  14.8 us
    ppermute x7, waiting for transfers between devices, far(): return lax.ppermute(x, 'narrow', far_pairs)  14.3 us
    ppermute x7, starting transfers between devices, far(): return lax.ppermute(x, 'narrow', far_pairs)  11 us
    ppermute x15, waiting for transfers between devices, step(): lax.ppermute(to_left, 'wide', self.left)  5.76 us
  transfers between devices with their start and end apart: 50, of which 18 were waited for; matrix products, arithmetic and copies ran while one was open for 1% of the time, Pallas kernels for 10%

profile of v9, /device:TPU:0, one launch (start us, length us, event | category | flops | bytes accessed | tf_op | source)
XLA Modules:
  0.0 137.8 jit_solution(3798726145090924671)
XLA Ops:
  0.0 3.0 %collective-permute-start = (bf16[160,1280]{1,0:T(8,128)(2,1)}, bf16[160,1280]{1,0:T(8,128)(2,1)S(1)}, u32[]{:S(2)}, u32[]{:S(2)}) collective-permute-start(bf16[160,1280]{1,0:T(8,128)(2,1)} %refs_0_.9), channel_id=1, source_target_pairs={{0,8},{8,16},{16,24},{24,28},{28,20},{20,12},{12,4},{4,0},{1,9},{9... | collective-permute-start | bytes 1228808 | tf_op jit(solution)/shard_map/ppermute | solution.py:324
  3.0 2.0 %collective-permute-start.7 = (bf16[160,1280]{1,0:T(8,128)(2,1)}, bf16[160,1280]{1,0:T(8,128)(2,1)S(1)}, u32[]{:S(2)}, u32[]{:S(2)}) collective-permute-start(bf16[160,1280]{1,0:T(8,128)(2,1)} %bitcast.9), channel_id=1, source_target_pairs={{0,8},{8,16},{16,24},{24,28},{28,20},{20,12},{12,4},{4,0},{1,9},{9... | collective-permute-start | bytes 1228808 | tf_op jit(solution)/shard_map/ppermute | solution.py:324
  7.0 6.5 %collective-permute-done.refs_1_ = bf16[160,1280]{1,0:T(8,128)(2,1)S(1)} collective-permute-done((bf16[160,1280]{1,0:T(8,128)(2,1)}, bf16[160,1280]{1,0:T(8,128)(2,1)S(1)}, u32[]{:S(2)}, u32[]{:S(2)}) %collective-permute-start) | collective-permute-done | bytes 409632 | tf_op jit(solution)/shard_map/ppermute | solution.py:324
  13.5 2.1 %collective-permute-start.2 = (bf16[160,1280]{1,0:T(8,128)(2,1)S(1)}, bf16[160,1280]{1,0:T(8,128)(2,1)S(1)}, u32[]{:S(2)}, u32[]{:S(2)}) collective-permute-start(bf16[160,1280]{1,0:T(8,128)(2,1)S(1)} %collective-permute-done.refs_1_), channel_id=1, source_target_pairs={{0,8},{8,16},{16,24},{24,28},{28,20},{20,12},{12,4},{4,0},{1,9},{9... | collective-permute-start | bytes 1228808 | tf_op jit(solution)/shard_map/ppermute | solution.py:324
  15.6 1.9 %collective-permute-start.10 = (bf16[2,320,256]{2,1,0:T(8,128)(2,1)S(1)}, bf16[2,320,256]{2,1,0:T(8,128)(2,1)S(1)}, u32[]{:S(2)}, u32[]{:S(2)}) collective-permute-start(bf16[2,320,256]{2,1,0:T(8,128)(2,1)S(1)} %get-tuple-element.76.own.refs_0_), channel_id=1, source_target_pairs={{0,2},{1,3},{2,0},{3,1},{4,6},{5,7},{6,4},{7,5},{8,10},{9,11},{10,... | collective-permute-start | bytes 983048 | tf_op jit(solution)/shard_map/ppermute | solution.py:364
  17.6 4.7 %collective-permute-done.7.refs_6_ = bf16[160,1280]{1,0:T(8,128)(2,1)S(1)} collective-permute-done((bf16[160,1280]{1,0:T(8,128)(2,1)}, bf16[160,1280]{1,0:T(8,128)(2,1)S(1)}, u32[]{:S(2)}, u32[]{:S(2)}) %collective-permute-start.7) | collective-permute-done | bytes 409632 | tf_op jit(solution)/shard_map/ppermute | solution.py:324
  22.2 2.2 %collective-permute-done.4.refs_7_ = bf16[160,1280]{1,0:T(8,128)(2,1)S(1)} collective-permute-done((bf16[160,1280]{1,0:T(8,128)(2,1)}, bf16[160,1280]{1,0:T(8,128)(2,1)S(1)}, u32[]{:S(2)}, u32[]{:S(2)}) %collective-permute-start.4) | collective-permute-done | bytes 409632 | tf_op jit(solution)/shard_map/ppermute | solution.py:325
  26.0 5.0 %collective-permute-done.2.refs_3_ = bf16[160,1280]{1,0:T(8,128)(2,1)S(1)} collective-permute-done((bf16[160,1280]{1,0:T(8,128)(2,1)S(1)}, bf16[160,1280]{1,0:T(8,128)(2,1)S(1)}, u32[]{:S(2)}, u32[]{:S(2)}) %collective-permute-start.2) | collective-permute-done | bytes 409632 | tf_op jit(solution)/shard_map/ppermute | solution.py:324
  31.0 2.1 %collective-permute-start.8 = (bf16[160,1280]{1,0:T(8,128)(2,1)S(1)}, bf16[160,1280]{1,0:T(8,128)(2,1)S(1)}, u32[]{:S(2)}, u32[]{:S(2)}) collective-permute-start(bf16[160,1280]{1,0:T(8,128)(2,1)S(1)} %collective-permute-done.4.refs_7_), channel_id=1, source_target_pairs={{8,0},{16,8},{24,16},{28,24},{20,28},{12,20},{4,12},{0,4},{9,1},{1... | collective-permute-start | bytes 1228808 | tf_op jit(solution)/shard_map/ppermute | solution.py:325
  34.4 1.9 %collective-permute-start.15 = (bf16[2,320,256]{2,1,0:T(8,128)(2,1)S(1)}, bf16[2,320,256]{2,1,0:T(8,128)(2,1)S(1)}, u32[]{:S(2)}, u32[]{:S(2)}) collective-permute-start(bf16[2,320,256]{2,1,0:T(8,128)(2,1)S(1)} %get-tuple-element.82.own.refs_1_), channel_id=1, source_target_pairs={{0,2},{1,3},{2,0},{3,1},{4,6},{5,7},{6,4},{7,5},{8,10},{9,11},{10,... | collective-permute-start | bytes 983048 | tf_op jit(solution)/shard_map/ppermute | solution.py:364
  36.3 3.5 %collective-permute-done.9.refs_8_ = bf16[160,1280]{1,0:T(8,128)(2,1)S(1)} collective-permute-done((bf16[160,1280]{1,0:T(8,128)(2,1)S(1)}, bf16[160,1280]{1,0:T(8,128)(2,1)S(1)}, u32[]{:S(2)}, u32[]{:S(2)}) %collective-permute-start.9) | collective-permute-done | bytes 409632 | tf_op jit(solution)/shard_map/ppermute | solution.py:324
  39.8 2.1 %collective-permute-start.6 = (bf16[160,1280]{1,0:T(8,128)(2,1)S(1)}, bf16[160,1280]{1,0:T(8,128)(2,1)S(1)}, u32[]{:S(2)}, u32[]{:S(2)}) collective-permute-start(bf16[160,1280]{1,0:T(8,128)(2,1)S(1)} %collective-permute-done.3.refs_4_), channel_id=1, source_target_pairs={{8,0},{16,8},{24,16},{28,24},{20,28},{12,20},{4,12},{0,4},{9,1},{1... | collective-permute-start | bytes 1228808 | tf_op jit(solution)/shard_map/ppermute | solution.py:325
  43.9 4.7 %collective-permute-done.5.refs_5_ = bf16[160,1280]{1,0:T(8,128)(2,1)S(1)} collective-permute-done((bf16[160,1280]{1,0:T(8,128)(2,1)S(1)}, bf16[160,1280]{1,0:T(8,128)(2,1)S(1)}, u32[]{:S(2)}, u32[]{:S(2)}) %collective-permute-start.5) | collective-permute-done | bytes 409632 | tf_op jit(solution)/shard_map/ppermute | solution.py:324
  52.3 2.0 %collective-permute-start.13 = (bf16[80,1280]{1,0:T(8,128)(2,1)S(1)}, bf16[80,1280]{1,0:T(8,128)(2,1)S(1)}, u32[]{:S(2)}, u32[]{:S(2)}) collective-permute-start(bf16[80,1280]{1,0:T(8,128)(2,1)S(1)} %slice.24), channel_id=1, source_target_pairs={{0,8},{8,16},{16,24},{24,28},{28,20},{20,12},{12,4},{4,0},{1,9},{9... | collective-permute-start | bytes 614408 | tf_op jit(solution)/shard_map/ppermute | solution.py:324
  54.3 3.0 %collective-permute-done.18.refs_10_ = bf16[160,1280]{1,0:T(8,128)(2,1)S(1)} collective-permute-done((bf16[160,1280]{1,0:T(8,128)(2,1)S(1)}, bf16[160,1280]{1,0:T(8,128)(2,1)S(1)}, u32[]{:S(2)}, u32[]{:S(2)}) %collective-permute-start.18) | collective-permute-done | bytes 409632 | tf_op jit(solution)/shard_map/ppermute | solution.py:324
  57.4 2.1 %collective-permute-start.14 = (bf16[80,1280]{1,0:T(8,128)(2,1)S(1)}, bf16[80,1280]{1,0:T(8,128)(2,1)S(1)}, u32[]{:S(2)}, u32[]{:S(2)}) collective-permute-start(bf16[80,1280]{1,0:T(8,128)(2,1)S(1)} %slice.25), channel_id=1, source_target_pairs={{8,0},{16,8},{24,16},{28,24},{20,28},{12,20},{4,12},{0,4},{9,1},{1... | collective-permute-start | bytes 614408 | tf_op jit(solution)/shard_map/ppermute | solution.py:325
  61.0 2.0 %collective-permute-start.22 = (bf16[80,1280]{1,0:T(8,128)(2,1)S(1)}, bf16[80,1280]{1,0:T(8,128)(2,1)S(1)}, u32[]{:S(2)}, u32[]{:S(2)}) collective-permute-start(bf16[80,1280]{1,0:T(8,128)(2,1)S(1)} %slice.27), channel_id=1, source_target_pairs={{8,0},{16,8},{24,16},{28,24},{20,28},{12,20},{4,12},{0,4},{9,1},{1... | collective-permute-start | bytes 614408 | tf_op jit(solution)/shard_map/ppermute | solution.py:325
  65.0 2.3 %collective-permute-start.29 = (bf16[80,1280]{1,0:T(8,128)(2,1)S(1)}, bf16[80,1280]{1,0:T(8,128)(2,1)S(1)}, u32[]{:S(2)}, u32[]{:S(2)}) collective-permute-start(bf16[80,1280]{1,0:T(8,128)(2,1)S(1)} %get-tuple-element.102.refs_1_), channel_id=1, source_target_pairs={{8,0},{16,8},{24,16},{28,24},{20,28},{12,20},{4,12},{0,4},{9,1},{1... | collective-permute-start | bytes 614408 | tf_op jit(solution)/shard_map/ppermute | solution.py:325
  69.5 2.2 %collective-permute-start.23 = (bf16[80,1280]{1,0:T(8,128)(2,1)S(1)}, bf16[80,1280]{1,0:T(8,128)(2,1)S(1)}, u32[]{:S(2)}, u32[]{:S(2)}) collective-permute-start(bf16[80,1280]{1,0:T(8,128)(2,1)S(1)} %get-tuple-element.101.refs_0_), channel_id=1, source_target_pairs={{8,0},{16,8},{24,16},{28,24},{20,28},{12,20},{4,12},{0,4},{9,1},{1... | collective-permute-start | bytes 614408 | tf_op jit(solution)/shard_map/ppermute | solution.py:325
  74.9 2.2 %mlp_out.3 = (bf16[320,256]{1,0:T(8,128)(2,1)S(1)}, bf16[320,256]{1,0:T(8,128)(2,1)S(1)}, bf16[320,256]{1,0:T(8,128)(2,1)S(1)}, bf16[320,256]{1,0:T(8,128)(2,1)S...) custom-call(bf16[1024,256]{1,0:T(8,128)(2,1)S(1)} %hidden.5.refs_0_,, ...), custom_call_target="tpu_custom_call" | custom-call | tf_op jit(solution)/shard_map/mlp_out/pallas_call | solution.py:22
  77.2 1.9 %collective-permute-start.39 = (bf16[80,1280]{1,0:T(8,128)(2,1)S(1)}, bf16[80,1280]{1,0:T(8,128)(2,1)S(1)}, u32[]{:S(2)}, u32[]{:S(2)}) collective-permute-start(bf16[80,1280]{1,0:T(8,128)(2,1)S(1)} %collective-permute-done.29.refs_3_), channel_id=1, source_target_pairs={{8,0},{16,8},{24,16},{28,24},{20,28},{12,20},{4,12},{0,4},{9,1},{1... | collective-permute-start | bytes 614408 | tf_op jit(solution)/shard_map/ppermute | solution.py:325
  79.3 1.9 %collective-permute-start.41 = (bf16[80,1280]{1,0:T(8,128)(2,1)S(1)}, bf16[80,1280]{1,0:T(8,128)(2,1)S(1)}, u32[]{:S(2)}, u32[]{:S(2)}) collective-permute-start(bf16[80,1280]{1,0:T(8,128)(2,1)S(1)} %collective-permute-done.23.refs_5_), channel_id=1, source_target_pairs={{8,0},{16,8},{24,16},{28,24},{20,28},{12,20},{4,12},{0,4},{9,1},{1... | collective-permute-start | bytes 614408 | tf_op jit(solution)/shard_map/ppermute | solution.py:325
  81.7 2.4 %mlp_out.2 = (bf16[320,256]{1,0:T(8,128)(2,1)S(1)}, bf16[320,256]{1,0:T(8,128)(2,1)S(1)}, bf16[320,256]{1,0:T(8,128)(2,1)S(1)}, bf16[320,256]{1,0:T(8,128)(2,1)S...) custom-call(bf16[1024,256]{1,0:T(8,128)(2,1)S(1)} %hidden.5.refs_0_,, ...), custom_call_target="tpu_custom_call" | custom-call | tf_op jit(solution)/shard_map/mlp_out/pallas_call | solution.py:22
  85.2 1.8 %collective-permute-start.31 = (bf16[320,256]{1,0:T(8,128)(2,1)S(1)}, bf16[320,256]{1,0:T(8,128)(2,1)S(1)}, u32[]{:S(2)}, u32[]{:S(2)}) collective-permute-start(bf16[320,256]{1,0:T(8,128)(2,1)S(1)} %add.5), channel_id=1, source_target_pairs={{0,2},{1,3},{2,0},{3,1},{4,6},{5,7},{6,4},{7,5},{8,10},{9,11},{10,... | collective-permute-start | bytes 491528 | tf_op jit(solution)/shard_map/ppermute | solution.py:364
  87.3 1.8 %collective-permute-start.43 = (bf16[80,1280]{1,0:T(8,128)(2,1)S(1)}, bf16[80,1280]{1,0:T(8,128)(2,1)S(1)}, u32[]{:S(2)}, u32[]{:S(2)}) collective-permute-start(bf16[80,1280]{1,0:T(8,128)(2,1)S(1)} %collective-permute-done.39.refs_7_), channel_id=1, source_target_pairs={{8,0},{16,8},{24,16},{28,24},{20,28},{12,20},{4,12},{0,4},{9,1},{1... | collective-permute-start | bytes 614408 | tf_op jit(solution)/shard_map/ppermute | solution.py:325
  89.6 1.8 %collective-permute-start.35 = (bf16[320,256]{1,0:T(8,128)(2,1)S(1)}, bf16[320,256]{1,0:T(8,128)(2,1)S(1)}, u32[]{:S(2)}, u32[]{:S(2)}) collective-permute-start(bf16[320,256]{1,0:T(8,128)(2,1)S(1)} %add.7), channel_id=1, source_target_pairs={{0,2},{1,3},{2,0},{3,1},{4,6},{5,7},{6,4},{7,5},{8,10},{9,11},{10,... | collective-permute-start | bytes 491528 | tf_op jit(solution)/shard_map/ppermute | solution.py:364
  92.4 3.5 %collective-permute-done.33.refs_11_ = bf16[320,256]{1,0:T(8,128)(2,1)S(1)} collective-permute-done((bf16[320,256]{1,0:T(8,128)(2,1)S(1)}, bf16[320,256]{1,0:T(8,128)(2,1)S(1)}, u32[]{:S(2)}, u32[]{:S(2)}) %collective-permute-start.33) | collective-permute-done | bytes 163872 | tf_op jit(solution)/shard_map/ppermute | solution.py:364
  95.9 2.0 %collective-permute-done.35.refs_12_ = bf16[320,256]{1,0:T(8,128)(2,1)S(1)} collective-permute-done((bf16[320,256]{1,0:T(8,128)(2,1)S(1)}, bf16[320,256]{1,0:T(8,128)(2,1)S(1)}, u32[]{:S(2)}, u32[]{:S(2)}) %collective-permute-start.35) | collective-permute-done | bytes 163872 | tf_op jit(solution)/shard_map/ppermute | solution.py:364
  104.3 3.7 %collective-permute-done.37.refs_13_ = bf16[320,256]{1,0:T(8,128)(2,1)S(1)} collective-permute-done((bf16[320,256]{1,0:T(8,128)(2,1)S(1)}, bf16[320,256]{1,0:T(8,128)(2,1)S(1)}, u32[]{:S(2)}, u32[]{:S(2)}) %collective-permute-start.37) | collective-permute-done | bytes 163872 | tf_op jit(solution)/shard_map/ppermute | solution.py:364
  108.5 3.0 %collective-permute-done.46.refs_14_ = bf16[80,1280]{1,0:T(8,128)(2,1)S(1)} collective-permute-done((bf16[80,1280]{1,0:T(8,128)(2,1)S(1)}, bf16[80,1280]{1,0:T(8,128)(2,1)S(1)}, u32[]{:S(2)}, u32[]{:S(2)}) %collective-permute-start.46) | collective-permute-done | bytes 204832 | tf_op jit(solution)/shard_map/ppermute | solution.py:324
  116.7 4.2 %collective-permute-done.49.far = bf16[320,256]{1,0:T(8,128)(2,1)S(1)} collective-permute-done((bf16[320,256]{1,0:T(8,128)(2,1)S(1)}, bf16[320,256]{1,0:T(8,128)(2,1)S(1)}, u32[]{:S(2)}, u32[]{:S(2)}) %collective-permute-start.49) | collective-permute-done | bytes 163872 | tf_op jit(solution)/shard_map/ppermute | solution.py:364
  121.3 15.2 %all_to_all.5.arrived = bf16[8,160,128]{2,1,0:T(8,128)(2,1)S(1)} all-to-all(bf16[8,160,128]{2,1,0:T(8,128)(2,1)S(1)} %pack.1), channel_id=1, replica_groups=mesh['wide'=8,'narrow'=4] {'wide'}, dimensions={0} | all-to-all | bytes 655360 | tf_op jit(solution)/shard_map/all_to_all | solution.py:438
  (120 shorter events, 36.7 us)
Async XLA Ops:
  0.0 13.5 %collective-permute-start = (bf16[160,1280]{1,0:T(8,128)(2,1)}, bf16[160,1280]{1,0:T(8,128)(2,1)S(1)}, u32[]{:S(2)}, u32[]{:S(2)}) collective-permute-start(bf16[160,1280]{1,0:T(8,128)(2,1)} %refs_0_.9), channel_id=1, source_target_pairs={{0,8},{8,16},{16,24},{24,28},{28,20},{20,12},{12,4},{4,0},{1,9},{9... | collective-permute-start | bytes 1228808 | tf_op jit(solution)/shard_map/ppermute | solution.py:324
  3.0 12.6 %collective-permute-start.1 = (bf16[160,1280]{1,0:T(8,128)(2,1)}, bf16[160,1280]{1,0:T(8,128)(2,1)S(1)}, u32[]{:S(2)}, u32[]{:S(2)}) collective-permute-start(bf16[160,1280]{1,0:T(8,128)(2,1)} %refs_0_.9), channel_id=1, source_target_pairs={{8,0},{16,8},{24,16},{28,24},{20,28},{12,20},{4,12},{0,4},{9,1},{1... | collective-permute-start | bytes 1228808 | tf_op jit(solution)/shard_map/ppermute | solution.py:325
  3.0 19.2 %collective-permute-start.7 = (bf16[160,1280]{1,0:T(8,128)(2,1)}, bf16[160,1280]{1,0:T(8,128)(2,1)S(1)}, u32[]{:S(2)}, u32[]{:S(2)}) collective-permute-start(bf16[160,1280]{1,0:T(8,128)(2,1)} %bitcast.9), channel_id=1, source_target_pairs={{0,8},{8,16},{16,24},{24,28},{28,20},{20,12},{12,4},{4,0},{1,9},{9... | collective-permute-start | bytes 1228808 | tf_op jit(solution)/shard_map/ppermute | solution.py:324
  5.1 19.4 %collective-permute-start.4 = (bf16[160,1280]{1,0:T(8,128)(2,1)}, bf16[160,1280]{1,0:T(8,128)(2,1)S(1)}, u32[]{:S(2)}, u32[]{:S(2)}) collective-permute-start(bf16[160,1280]{1,0:T(8,128)(2,1)} %bitcast.10), channel_id=1, source_target_pairs={{8,0},{16,8},{24,16},{28,24},{20,28},{12,20},{4,12},{0,4},{9,1},{1... | collective-permute-start | bytes 1228808 | tf_op jit(solution)/shard_map/ppermute | solution.py:325
  13.5 17.6 %collective-permute-start.2 = (bf16[160,1280]{1,0:T(8,128)(2,1)S(1)}, bf16[160,1280]{1,0:T(8,128)(2,1)S(1)}, u32[]{:S(2)}, u32[]{:S(2)}) collective-permute-start(bf16[160,1280]{1,0:T(8,128)(2,1)S(1)} %collective-permute-done.refs_1_), channel_id=1, source_target_pairs={{0,8},{8,16},{16,24},{24,28},{28,20},{20,12},{12,4},{4,0},{1,9},{9... | collective-permute-start | bytes 1228808 | tf_op jit(solution)/shard_map/ppermute | solution.py:324
  15.6 18.7 %collective-permute-start.3 = (bf16[160,1280]{1,0:T(8,128)(2,1)S(1)}, bf16[160,1280]{1,0:T(8,128)(2,1)S(1)}, u32[]{:S(2)}, u32[]{:S(2)}) collective-permute-start(bf16[160,1280]{1,0:T(8,128)(2,1)S(1)} %collective-permute-done.1.refs_2_), channel_id=1, source_target_pairs={{8,0},{16,8},{24,16},{28,24},{20,28},{12,20},{4,12},{0,4},{9,1},{1... | collective-permute-start | bytes 1228808 | tf_op jit(solution)/shard_map/ppermute | solution.py:325
  15.6 18.6 %collective-permute-start.10 = (bf16[2,320,256]{2,1,0:T(8,128)(2,1)S(1)}, bf16[2,320,256]{2,1,0:T(8,128)(2,1)S(1)}, u32[]{:S(2)}, u32[]{:S(2)}) collective-permute-start(bf16[2,320,256]{2,1,0:T(8,128)(2,1)S(1)} %get-tuple-element.76.own.refs_0_), channel_id=1, source_target_pairs={{0,2},{1,3},{2,0},{3,1},{4,6},{5,7},{6,4},{7,5},{8,10},{9,11},{10,... | collective-permute-start | bytes 983048 | tf_op jit(solution)/shard_map/ppermute | solution.py:364
  22.2 14.1 %collective-permute-start.11 = (bf16[2,320,256]{2,1,0:T(8,128)(2,1)S(1)}, bf16[2,320,256]{2,1,0:T(8,128)(2,1)S(1)}, u32[]{:S(2)}, u32[]{:S(2)}) collective-permute-start(bf16[2,320,256]{2,1,0:T(8,128)(2,1)S(1)} %get-tuple-element.76.own.refs_0_), channel_id=1, source_target_pairs={{0,1},{1,0},{2,3},{3,2},{4,5},{5,4},{6,7},{7,6},{8,9},{9,8},{10,11... | collective-permute-start | bytes 983048 | tf_op jit(solution)/shard_map/ppermute | solution.py:361
  24.4 15.4 %collective-permute-start.9 = (bf16[160,1280]{1,0:T(8,128)(2,1)S(1)}, bf16[160,1280]{1,0:T(8,128)(2,1)S(1)}, u32[]{:S(2)}, u32[]{:S(2)}) collective-permute-start(bf16[160,1280]{1,0:T(8,128)(2,1)S(1)} %collective-permute-done.7.refs_6_), channel_id=1, source_target_pairs={{0,8},{8,16},{16,24},{24,28},{28,20},{20,12},{12,4},{4,0},{1,9},{9... | collective-permute-start | bytes 1228808 | tf_op jit(solution)/shard_map/ppermute | solution.py:324
  31.0 10.8 %collective-permute-start.8 = (bf16[160,1280]{1,0:T(8,128)(2,1)S(1)}, bf16[160,1280]{1,0:T(8,128)(2,1)S(1)}, u32[]{:S(2)}, u32[]{:S(2)}) collective-permute-start(bf16[160,1280]{1,0:T(8,128)(2,1)S(1)} %collective-permute-done.4.refs_7_), channel_id=1, source_target_pairs={{8,0},{16,8},{24,16},{28,24},{20,28},{12,20},{4,12},{0,4},{9,1},{1... | collective-permute-start | bytes 1228808 | tf_op jit(solution)/shard_map/ppermute | solution.py:325
  34.3 14.3 %collective-permute-start.5 = (bf16[160,1280]{1,0:T(8,128)(2,1)S(1)}, bf16[160,1280]{1,0:T(8,128)(2,1)S(1)}, u32[]{:S(2)}, u32[]{:S(2)}) collective-permute-start(bf16[160,1280]{1,0:T(8,128)(2,1)S(1)} %collective-permute-done.2.refs_3_), channel_id=1, source_target_pairs={{0,8},{8,16},{16,24},{24,28},{28,20},{20,12},{12,4},{4,0},{1,9},{9... | collective-permute-start | bytes 1228808 | tf_op jit(solution)/shard_map/ppermute | solution.py:324
  39.8 12.5 %collective-permute-start.6 = (bf16[160,1280]{1,0:T(8,128)(2,1)S(1)}, bf16[160,1280]{1,0:T(8,128)(2,1)S(1)}, u32[]{:S(2)}, u32[]{:S(2)}) collective-permute-start(bf16[160,1280]{1,0:T(8,128)(2,1)S(1)} %collective-permute-done.3.refs_4_), channel_id=1, source_target_pairs={{8,0},{16,8},{24,16},{28,24},{20,28},{12,20},{4,12},{0,4},{9,1},{1... | collective-permute-start | bytes 1228808 | tf_op jit(solution)/shard_map/ppermute | solution.py:325
  41.9 15.5 %collective-permute-start.18 = (bf16[160,1280]{1,0:T(8,128)(2,1)S(1)}, bf16[160,1280]{1,0:T(8,128)(2,1)S(1)}, u32[]{:S(2)}, u32[]{:S(2)}) collective-permute-start(bf16[160,1280]{1,0:T(8,128)(2,1)S(1)} %collective-permute-done.9.refs_8_), channel_id=1, source_target_pairs={{0,8},{8,16},{16,24},{24,28},{28,20},{20,12},{12,4},{4,0},{1,9},{9... | collective-permute-start | bytes 1228808 | tf_op jit(solution)/shard_map/ppermute | solution.py:324
  42.3 18.7 %collective-permute-start.21 = (bf16[160,1280]{1,0:T(8,128)(2,1)S(1)}, bf16[160,1280]{1,0:T(8,128)(2,1)S(1)}, u32[]{:S(2)}, u32[]{:S(2)}) collective-permute-start(bf16[160,1280]{1,0:T(8,128)(2,1)S(1)} %collective-permute-done.8.refs_9_), channel_id=1, source_target_pairs={{8,0},{16,8},{24,16},{28,24},{20,28},{12,20},{4,12},{0,4},{9,1},{1... | collective-permute-start | bytes 1228808 | tf_op jit(solution)/shard_map/ppermute | solution.py:325
  43.9 15.6 %collective-permute-start.16 = (bf16[2,320,256]{2,1,0:T(8,128)(2,1)S(1)}, bf16[2,320,256]{2,1,0:T(8,128)(2,1)S(1)}, u32[]{:S(2)}, u32[]{:S(2)}) collective-permute-start(bf16[2,320,256]{2,1,0:T(8,128)(2,1)S(1)} %get-tuple-element.82.own.refs_1_), channel_id=1, source_target_pairs={{0,1},{1,0},{2,3},{3,2},{4,5},{5,4},{6,7},{7,6},{8,9},{9,8},{10,11... | collective-permute-start | bytes 983048 | tf_op jit(solution)/shard_map/ppermute | solution.py:361
  48.6 10.9 %collective-permute-start.17 = (bf16[2,320,256]{2,1,0:T(8,128)(2,1)S(1)}, bf16[2,320,256]{2,1,0:T(8,128)(2,1)S(1)}, u32[]{:S(2)}, u32[]{:S(2)}) collective-permute-start(bf16[2,320,256]{2,1,0:T(8,128)(2,1)S(1)} %collective-permute-done.15.over_x), channel_id=1, source_target_pairs={{0,1},{1,0},{2,3},{3,2},{4,5},{5,4},{6,7},{7,6},{8,9},{9,8},{10,11... | collective-permute-start | bytes 983048 | tf_op jit(solution)/shard_map/ppermute | solution.py:361
  52.3 10.7 %collective-permute-start.13 = (bf16[80,1280]{1,0:T(8,128)(2,1)S(1)}, bf16[80,1280]{1,0:T(8,128)(2,1)S(1)}, u32[]{:S(2)}, u32[]{:S(2)}) collective-permute-start(bf16[80,1280]{1,0:T(8,128)(2,1)S(1)} %slice.24), channel_id=1, source_target_pairs={{0,8},{8,16},{16,24},{24,28},{28,20},{20,12},{12,4},{4,0},{1,9},{9... | collective-permute-start | bytes 614408 | tf_op jit(solution)/shard_map/ppermute | solution.py:324
  60.9 8.5 %collective-permute-start.19 = (bf16[80,1280]{1,0:T(8,128)(2,1)S(1)}, bf16[80,1280]{1,0:T(8,128)(2,1)S(1)}, u32[]{:S(2)}, u32[]{:S(2)}) collective-permute-start(bf16[80,1280]{1,0:T(8,128)(2,1)S(1)} %slice.26), channel_id=1, source_target_pairs={{0,8},{8,16},{16,24},{24,28},{28,20},{20,12},{12,4},{4,0},{1,9},{9... | collective-permute-start | bytes 614408 | tf_op jit(solution)/shard_map/ppermute | solution.py:324
  61.0 8.5 %collective-permute-start.22 = (bf16[80,1280]{1,0:T(8,128)(2,1)S(1)}, bf16[80,1280]{1,0:T(8,128)(2,1)S(1)}, u32[]{:S(2)}, u32[]{:S(2)}) collective-permute-start(bf16[80,1280]{1,0:T(8,128)(2,1)S(1)} %slice.27), channel_id=1, source_target_pairs={{8,0},{16,8},{24,16},{28,24},{20,28},{12,20},{4,12},{0,4},{9,1},{1... | collective-permute-start | bytes 614408 | tf_op jit(solution)/shard_map/ppermute | solution.py:325
  63.1 11.8 %collective-permute-start.28 = (bf16[80,1280]{1,0:T(8,128)(2,1)S(1)}, bf16[80,1280]{1,0:T(8,128)(2,1)S(1)}, u32[]{:S(2)}, u32[]{:S(2)}) collective-permute-start(bf16[80,1280]{1,0:T(8,128)(2,1)S(1)} %get-tuple-element.101.refs_0_), channel_id=1, source_target_pairs={{0,8},{8,16},{16,24},{24,28},{28,20},{20,12},{12,4},{4,0},{1,9},{9... | collective-permute-start | bytes 614408 | tf_op jit(solution)/shard_map/ppermute | solution.py:324
  65.0 9.9 %collective-permute-start.29 = (bf16[80,1280]{1,0:T(8,128)(2,1)S(1)}, bf16[80,1280]{1,0:T(8,128)(2,1)S(1)}, u32[]{:S(2)}, u32[]{:S(2)}) collective-permute-start(bf16[80,1280]{1,0:T(8,128)(2,1)S(1)} %get-tuple-element.102.refs_1_), channel_id=1, source_target_pairs={{8,0},{16,8},{24,16},{28,24},{20,28},{12,20},{4,12},{0,4},{9,1},{1... | collective-permute-start | bytes 614408 | tf_op jit(solution)/shard_map/ppermute | solution.py:325
  69.4 9.7 %collective-permute-start.20 = (bf16[80,1280]{1,0:T(8,128)(2,1)S(1)}, bf16[80,1280]{1,0:T(8,128)(2,1)S(1)}, u32[]{:S(2)}, u32[]{:S(2)}) collective-permute-start(bf16[80,1280]{1,0:T(8,128)(2,1)S(1)} %get-tuple-element.102.refs_1_), channel_id=1, source_target_pairs={{0,8},{8,16},{16,24},{24,28},{28,20},{20,12},{12,4},{4,0},{1,9},{9... | collective-permute-start | bytes 614408 | tf_op jit(solution)/shard_map/ppermute | solution.py:324
  69.5 9.8 %collective-permute-start.23 = (bf16[80,1280]{1,0:T(8,128)(2,1)S(1)}, bf16[80,1280]{1,0:T(8,128)(2,1)S(1)}, u32[]{:S(2)}, u32[]{:S(2)}) collective-permute-start(bf16[80,1280]{1,0:T(8,128)(2,1)S(1)} %get-tuple-element.101.refs_0_), channel_id=1, source_target_pairs={{8,0},{16,8},{24,16},{28,24},{20,28},{12,20},{4,12},{0,4},{9,1},{1... | collective-permute-start | bytes 614408 | tf_op jit(solution)/shard_map/ppermute | solution.py:325
  79.3 10.3 %collective-permute-start.41 = (bf16[80,1280]{1,0:T(8,128)(2,1)S(1)}, bf16[80,1280]{1,0:T(8,128)(2,1)S(1)}, u32[]{:S(2)}, u32[]{:S(2)}) collective-permute-start(bf16[80,1280]{1,0:T(8,128)(2,1)S(1)} %collective-permute-done.23.refs_5_), channel_id=1, source_target_pairs={{8,0},{16,8},{24,16},{28,24},{20,28},{12,20},{4,12},{0,4},{9,1},{1... | collective-permute-start | bytes 614408 | tf_op jit(solution)/shard_map/ppermute | solution.py:325
  84.2 13.7 %collective-permute-start.42 = (bf16[80,1280]{1,0:T(8,128)(2,1)S(1)}, bf16[80,1280]{1,0:T(8,128)(2,1)S(1)}, u32[]{:S(2)}, u32[]{:S(2)}) collective-permute-start(bf16[80,1280]{1,0:T(8,128)(2,1)S(1)} %collective-permute-done.38.refs_6_), channel_id=1, source_target_pairs={{0,8},{8,16},{16,24},{24,28},{28,20},{20,12},{12,4},{4,0},{1,9},{9... | collective-permute-start | bytes 614408 | tf_op jit(solution)/shard_map/ppermute | solution.py:324
  87.1 8.8 %collective-permute-start.33 = (bf16[320,256]{1,0:T(8,128)(2,1)S(1)}, bf16[320,256]{1,0:T(8,128)(2,1)S(1)}, u32[]{:S(2)}, u32[]{:S(2)}) collective-permute-start(bf16[320,256]{1,0:T(8,128)(2,1)S(1)} %add.6), channel_id=1, source_target_pairs={{0,2},{1,3},{2,0},{3,1},{4,6},{5,7},{6,4},{7,5},{8,10},{9,11},{10,... | collective-permute-start | bytes 491528 | tf_op jit(solution)/shard_map/ppermute | solution.py:364
  87.3 11.1 %collective-permute-start.43 = (bf16[80,1280]{1,0:T(8,128)(2,1)S(1)}, bf16[80,1280]{1,0:T(8,128)(2,1)S(1)}, u32[]{:S(2)}, u32[]{:S(2)}) collective-permute-start(bf16[80,1280]{1,0:T(8,128)(2,1)S(1)} %collective-permute-done.39.refs_7_), channel_id=1, source_target_pairs={{8,0},{16,8},{24,16},{28,24},{20,28},{12,20},{4,12},{0,4},{9,1},{1... | collective-permute-start | bytes 614408 | tf_op jit(solution)/shard_map/ppermute | solution.py:325
  89.6 8.2 %collective-permute-start.35 = (bf16[320,256]{1,0:T(8,128)(2,1)S(1)}, bf16[320,256]{1,0:T(8,128)(2,1)S(1)}, u32[]{:S(2)}, u32[]{:S(2)}) collective-permute-start(bf16[320,256]{1,0:T(8,128)(2,1)S(1)} %add.7), channel_id=1, source_target_pairs={{0,2},{1,3},{2,0},{3,1},{4,6},{5,7},{6,4},{7,5},{8,10},{9,11},{10,... | collective-permute-start | bytes 491528 | tf_op jit(solution)/shard_map/ppermute | solution.py:364
  98.4 10.0 %collective-permute-start.45 = (bf16[80,1280]{1,0:T(8,128)(2,1)S(1)}, bf16[80,1280]{1,0:T(8,128)(2,1)S(1)}, u32[]{:S(2)}, u32[]{:S(2)}) collective-permute-start(bf16[80,1280]{1,0:T(8,128)(2,1)S(1)} %collective-permute-done.41.refs_9_), channel_id=1, source_target_pairs={{8,0},{16,8},{24,16},{28,24},{20,28},{12,20},{4,12},{0,4},{9,1},{1... | collective-permute-start | bytes 614408 | tf_op jit(solution)/shard_map/ppermute | solution.py:325
  100.0 8.5 %collective-permute-start.44 = (bf16[80,1280]{1,0:T(8,128)(2,1)S(1)}, bf16[80,1280]{1,0:T(8,128)(2,1)S(1)}, u32[]{:S(2)}, u32[]{:S(2)}) collective-permute-start(bf16[80,1280]{1,0:T(8,128)(2,1)S(1)} %collective-permute-done.40.refs_8_), channel_id=1, source_target_pairs={{0,8},{8,16},{16,24},{24,28},{28,20},{20,12},{12,4},{4,0},{1,9},{9... | collective-permute-start | bytes 614408 | tf_op jit(solution)/shard_map/ppermute | solution.py:324
  100.5 11.0 %collective-permute-start.46 = (bf16[80,1280]{1,0:T(8,128)(2,1)S(1)}, bf16[80,1280]{1,0:T(8,128)(2,1)S(1)}, u32[]{:S(2)}, u32[]{:S(2)}) collective-permute-start(bf16[80,1280]{1,0:T(8,128)(2,1)S(1)} %collective-permute-done.42.refs_10_), channel_id=1, source_target_pairs={{0,8},{8,16},{16,24},{24,28},{28,20},{20,12},{12,4},{4,0},{1,9},{9... | collective-permute-start | bytes 614408 | tf_op jit(solution)/shard_map/ppermute | solution.py:324
  102.1 9.4 %collective-permute-start.47 = (bf16[80,1280]{1,0:T(8,128)(2,1)S(1)}, bf16[80,1280]{1,0:T(8,128)(2,1)S(1)}, u32[]{:S(2)}, u32[]{:S(2)}) collective-permute-start(bf16[80,1280]{1,0:T(8,128)(2,1)S(1)} %collective-permute-done.43.refs_11_), channel_id=1, source_target_pairs={{8,0},{16,8},{24,16},{28,24},{20,28},{12,20},{4,12},{0,4},{9,1},{1... | collective-permute-start | bytes 614408 | tf_op jit(solution)/shard_map/ppermute | solution.py:325
  (27 other events, 177.6 us)

commit v10 on v9

--- a/solution.py
+++ b/solution.py
@@ -10,9 +10,10 @@
 F32 = jnp.float32
 BF16 = jnp.bfloat16
 WINDOW = 4
-LATE = (1, 2, 2)
+LATE = (1, 2, 3)
 HIDDEN_AT = (7, 7, 8, 8, 8)
 OUT_AT = 1
+OWN_PARTS = 1
 SUMS_AT = 2
 VMEM = pl.BlockSpec(memory_space=pltpu.VMEM)
 
@@ -220,13 +221,14 @@
 
 def stream_kernel(chunks, bias, *refs):
     o_ref = refs[-1]
-    own = refs[:chunks]
-    keep, near, far = (
-        refs[chunks + i * WINDOW : chunks + (i + 1) * WINDOW] for i in range(3)
-    )
+    own, refs = refs[:chunks], refs[chunks:-1]
+    keep, near, far = refs[:OWN_PARTS], refs[OWN_PARTS : 2 * OWN_PARTS], refs[2 * OWN_PARTS :]
+    of_own = WINDOW // OWN_PARTS
     each, rows, windows = own[0].shape
     for p in range(WINDOW):
-        total = keep[p][...].astype(F32) + near[p][...].astype(F32) + far[p][...].astype(F32)
+        at = slice(p % of_own * windows, (p % of_own + 1) * windows)
+        total = keep[p // of_own][:, at].astype(F32) + near[p // of_own][:, at].astype(F32)
+        total = total + far[p][...].astype(F32)
         v = own[p // each][p % each].astype(F32) + (total + bias[...])
         o_ref[p * rows : (p + 1) * rows, :] = v.astype(BF16)
 
@@ -398,14 +400,15 @@
         )
 
     def mlp_out(pieces, arrays, hiddens, over_x):
+        count = WINDOW if over_x else OWN_PARTS
         outs = call(
             functools.partial(
-                out_kernel, pieces, groups, shard_rows[1], over_x, len(hiddens), WINDOW
+                out_kernel, pieces, groups, shard_rows[1], over_x, len(hiddens), count
             ),
-            (*hiddens, *arrays), [shape(width, windows)] * (2 * WINDOW),
+            (*hiddens, *arrays), [shape(width, tokens // count)] * (2 * count),
             scratch=[pltpu.VMEM((2 * width, ff), BF16)], name="mlp_out",
         )
-        return outs[:WINDOW], outs[WINDOW:]
+        return outs[:count], outs[count:]
 
     def add(keep, other):
         return call(add_kernel, (keep, other), shape(*keep.shape), name="add")
@@ -572,8 +575,8 @@
         core = [ring.now(got["core", 1][0]), *got["core", 1][1:]]
         sums = [add(k, c) for k, c in zip(got["keep", 1], core)]
         got["x_sums"] = [far(x) for x in sums]
-        for i, x in enumerate(got["x_sums"][:-1]):
-            ring.add_late(x, LATE[i])
+        for steps, x in zip(LATE, got["x_sums"]):
+            ring.add_late(x, steps)
         ring.add_work(sums[0])
         start_out(0)
 

time: 138 us -> 134 us (0.971)
  waiting for transfers between devices: 52.1 us -> 47.7 us
    ppermute x7, waiting for transfers between devices: 14.3 us -> 6.03 us  [far(): return lax.ppermute(x, 'narrow', far_pairs)]
    ppermute x15, waiting for transfers between devices: 30.4 us -> 35.6 us  [step(): lax.ppermute(to_right, 'wide', self.right)]
    ppermute x15, starting transfers between devices: 14.8 us -> 18.1 us  [step(): lax.ppermute(to_right, 'wide', self.right)]
    ppermute x15, starting transfers between devices: 21.9 us -> 20 us  [step(): lax.ppermute(to_left, 'wide', self.left)]
  transfers between devices with their start and end apart: 50 -> 47, of which waited for: 18 -> 20; matrix products, arithmetic and copies ran while one was open for 1% -> 1% of each run, Pallas kernels for 10% -> 11%
where the time goes in v10:
time: 134 us
  starting transfers between devices  49.9 us (37%)
  waiting for transfers between devices  47.7 us (36%)
  Pallas kernels  17.5 us (13%)
  blocking collectives  14.6 us (11%)
  local copies, waits for them, and re-layouts  3.84 us (3%)
    ppermute x15, waiting for transfers between devices, step(): lax.ppermute(to_right, 'wide', self.right)  35.6 us
    ppermute x15, starting transfers between devices, step(): lax.ppermute(to_left, 'wide', self.left)  20 us
    ppermute x15, starting transfers between devices, step(): lax.ppermute(to_right, 'wide', self.right)  18.1 us
    pallas_call x21, Pallas kernels, call(): pl.pallas_call(kernel, out_shape=outs, in_specs=[VMEM] * len(operands), o...  17.5 us
    all_to_all x1, blocking collectives, exchange_and_place(): lax.all_to_all(buffer, 'wide', split_axis=0, concat_axis=0, tiled=True)  14.6 us
    ppermute x7, starting transfers between devices, far(): return lax.ppermute(x, 'narrow', far_pairs)  10.6 us
    ppermute x7, waiting for transfers between devices, far(): return lax.ppermute(x, 'narrow', far_pairs)  6.03 us
    ppermute x15, waiting for transfers between devices, step(): lax.ppermute(to_left, 'wide', self.left)  4.44 us
  transfers between devices with their start and end apart: 47, of which 20 were waited for; matrix products, arithmetic and copies ran while one was open for 1% of the time, Pallas kernels for 11%

profile of v10, /device:TPU:0, one launch (start us, length us, event | category | flops | bytes accessed | tf_op | source)
XLA Modules:
  0.0 134.0 jit_solution(6610709898781736768)
XLA Ops:
  0.0 3.0 %collective-permute-start = (bf16[160,1280]{1,0:T(8,128)(2,1)}, bf16[160,1280]{1,0:T(8,128)(2,1)S(1)}, u32[]{:S(2)}, u32[]{:S(2)}) collective-permute-start(bf16[160,1280]{1,0:T(8,128)(2,1)} %refs_0_.9), channel_id=1, source_target_pairs={{0,8},{8,16},{16,24},{24,28},{28,20},{20,12},{12,4},{4,0},{1,9},{9... | collective-permute-start | bytes 1228808 | tf_op jit(solution)/shard_map/ppermute | solution.py:326
  3.0 2.0 %collective-permute-start.7 = (bf16[160,1280]{1,0:T(8,128)(2,1)}, bf16[160,1280]{1,0:T(8,128)(2,1)S(1)}, u32[]{:S(2)}, u32[]{:S(2)}) collective-permute-start(bf16[160,1280]{1,0:T(8,128)(2,1)} %bitcast.9), channel_id=1, source_target_pairs={{0,8},{8,16},{16,24},{24,28},{28,20},{20,12},{12,4},{4,0},{1,9},{9... | collective-permute-start | bytes 1228808 | tf_op jit(solution)/shard_map/ppermute | solution.py:326
  7.0 6.5 %collective-permute-done.refs_1_ = bf16[160,1280]{1,0:T(8,128)(2,1)S(1)} collective-permute-done((bf16[160,1280]{1,0:T(8,128)(2,1)}, bf16[160,1280]{1,0:T(8,128)(2,1)S(1)}, u32[]{:S(2)}, u32[]{:S(2)}) %collective-permute-start) | collective-permute-done | bytes 409632 | tf_op jit(solution)/shard_map/ppermute | solution.py:326
  13.5 2.1 %collective-permute-start.2 = (bf16[160,1280]{1,0:T(8,128)(2,1)S(1)}, bf16[160,1280]{1,0:T(8,128)(2,1)S(1)}, u32[]{:S(2)}, u32[]{:S(2)}) collective-permute-start(bf16[160,1280]{1,0:T(8,128)(2,1)S(1)} %collective-permute-done.refs_1_), channel_id=1, source_target_pairs={{0,8},{8,16},{16,24},{24,28},{28,20},{20,12},{12,4},{4,0},{1,9},{9... | collective-permute-start | bytes 1228808 | tf_op jit(solution)/shard_map/ppermute | solution.py:326
  15.6 1.9 %collective-permute-start.10 = (bf16[2,320,256]{2,1,0:T(8,128)(2,1)S(1)}, bf16[2,320,256]{2,1,0:T(8,128)(2,1)S(1)}, u32[]{:S(2)}, u32[]{:S(2)}) collective-permute-start(bf16[2,320,256]{2,1,0:T(8,128)(2,1)S(1)} %get-tuple-element.70.own.refs_0_), channel_id=1, source_target_pairs={{0,2},{1,3},{2,0},{3,1},{4,6},{5,7},{6,4},{7,5},{8,10},{9,11},{10,... | collective-permute-start | bytes 983048 | tf_op jit(solution)/shard_map/ppermute | solution.py:366
  17.6 4.7 %collective-permute-done.7.refs_6_ = bf16[160,1280]{1,0:T(8,128)(2,1)S(1)} collective-permute-done((bf16[160,1280]{1,0:T(8,128)(2,1)}, bf16[160,1280]{1,0:T(8,128)(2,1)S(1)}, u32[]{:S(2)}, u32[]{:S(2)}) %collective-permute-start.7) | collective-permute-done | bytes 409632 | tf_op jit(solution)/shard_map/ppermute | solution.py:326
  22.2 2.2 %collective-permute-done.4.refs_7_ = bf16[160,1280]{1,0:T(8,128)(2,1)S(1)} collective-permute-done((bf16[160,1280]{1,0:T(8,128)(2,1)}, bf16[160,1280]{1,0:T(8,128)(2,1)S(1)}, u32[]{:S(2)}, u32[]{:S(2)}) %collective-permute-start.4) | collective-permute-done | bytes 409632 | tf_op jit(solution)/shard_map/ppermute | solution.py:327
  24.4 1.6 %collective-permute-start.9 = (bf16[160,1280]{1,0:T(8,128)(2,1)S(1)}, bf16[160,1280]{1,0:T(8,128)(2,1)S(1)}, u32[]{:S(2)}, u32[]{:S(2)}) collective-permute-start(bf16[160,1280]{1,0:T(8,128)(2,1)S(1)} %collective-permute-done.7.refs_6_), channel_id=1, source_target_pairs={{0,8},{8,16},{16,24},{24,28},{28,20},{20,12},{12,4},{4,0},{1,9},{9... | collective-permute-start | bytes 1228808 | tf_op jit(solution)/shard_map/ppermute | solution.py:326
  26.0 5.0 %collective-permute-done.2.refs_3_ = bf16[160,1280]{1,0:T(8,128)(2,1)S(1)} collective-permute-done((bf16[160,1280]{1,0:T(8,128)(2,1)S(1)}, bf16[160,1280]{1,0:T(8,128)(2,1)S(1)}, u32[]{:S(2)}, u32[]{:S(2)}) %collective-permute-start.2) | collective-permute-done | bytes 409632 | tf_op jit(solution)/shard_map/ppermute | solution.py:326
  31.0 2.1 %collective-permute-start.8 = (bf16[160,1280]{1,0:T(8,128)(2,1)S(1)}, bf16[160,1280]{1,0:T(8,128)(2,1)S(1)}, u32[]{:S(2)}, u32[]{:S(2)}) collective-permute-start(bf16[160,1280]{1,0:T(8,128)(2,1)S(1)} %collective-permute-done.4.refs_7_), channel_id=1, source_target_pairs={{8,0},{16,8},{24,16},{28,24},{20,28},{12,20},{4,12},{0,4},{9,1},{1... | collective-permute-start | bytes 1228808 | tf_op jit(solution)/shard_map/ppermute | solution.py:327
  34.4 1.9 %collective-permute-start.15 = (bf16[2,320,256]{2,1,0:T(8,128)(2,1)S(1)}, bf16[2,320,256]{2,1,0:T(8,128)(2,1)S(1)}, u32[]{:S(2)}, u32[]{:S(2)}) collective-permute-start(bf16[2,320,256]{2,1,0:T(8,128)(2,1)S(1)} %get-tuple-element.76.own.refs_1_), channel_id=1, source_target_pairs={{0,2},{1,3},{2,0},{3,1},{4,6},{5,7},{6,4},{7,5},{8,10},{9,11},{10,... | collective-permute-start | bytes 983048 | tf_op jit(solution)/shard_map/ppermute | solution.py:366
  36.3 3.5 %collective-permute-done.9.refs_8_ = bf16[160,1280]{1,0:T(8,128)(2,1)S(1)} collective-permute-done((bf16[160,1280]{1,0:T(8,128)(2,1)S(1)}, bf16[160,1280]{1,0:T(8,128)(2,1)S(1)}, u32[]{:S(2)}, u32[]{:S(2)}) %collective-permute-start.9) | collective-permute-done | bytes 409632 | tf_op jit(solution)/shard_map/ppermute | solution.py:326
  39.8 2.1 %collective-permute-start.6 = (bf16[160,1280]{1,0:T(8,128)(2,1)S(1)}, bf16[160,1280]{1,0:T(8,128)(2,1)S(1)}, u32[]{:S(2)}, u32[]{:S(2)}) collective-permute-start(bf16[160,1280]{1,0:T(8,128)(2,1)S(1)} %collective-permute-done.3.refs_4_), channel_id=1, source_target_pairs={{8,0},{16,8},{24,16},{28,24},{20,28},{12,20},{4,12},{0,4},{9,1},{1... | collective-permute-start | bytes 1228808 | tf_op jit(solution)/shard_map/ppermute | solution.py:327
  42.3 1.6 %collective-permute-start.21 = (bf16[160,1280]{1,0:T(8,128)(2,1)S(1)}, bf16[160,1280]{1,0:T(8,128)(2,1)S(1)}, u32[]{:S(2)}, u32[]{:S(2)}) collective-permute-start(bf16[160,1280]{1,0:T(8,128)(2,1)S(1)} %collective-permute-done.8.refs_9_), channel_id=1, source_target_pairs={{8,0},{16,8},{24,16},{28,24},{20,28},{12,20},{4,12},{0,4},{9,1},{1... | collective-permute-start | bytes 1228808 | tf_op jit(solution)/shard_map/ppermute | solution.py:327
  43.9 4.7 %collective-permute-done.5.refs_5_ = bf16[160,1280]{1,0:T(8,128)(2,1)S(1)} collective-permute-done((bf16[160,1280]{1,0:T(8,128)(2,1)S(1)}, bf16[160,1280]{1,0:T(8,128)(2,1)S(1)}, u32[]{:S(2)}, u32[]{:S(2)}) %collective-permute-start.5) | collective-permute-done | bytes 409632 | tf_op jit(solution)/shard_map/ppermute | solution.py:326
  52.3 2.0 %collective-permute-start.13 = (bf16[80,1280]{1,0:T(8,128)(2,1)S(1)}, bf16[80,1280]{1,0:T(8,128)(2,1)S(1)}, u32[]{:S(2)}, u32[]{:S(2)}) collective-permute-start(bf16[80,1280]{1,0:T(8,128)(2,1)S(1)} %slice.24), channel_id=1, source_target_pairs={{0,8},{8,16},{16,24},{24,28},{28,20},{20,12},{12,4},{4,0},{1,9},{9... | collective-permute-start | bytes 614408 | tf_op jit(solution)/shard_map/ppermute | solution.py:326
  54.3 3.0 %collective-permute-done.18.refs_10_ = bf16[160,1280]{1,0:T(8,128)(2,1)S(1)} collective-permute-done((bf16[160,1280]{1,0:T(8,128)(2,1)S(1)}, bf16[160,1280]{1,0:T(8,128)(2,1)S(1)}, u32[]{:S(2)}, u32[]{:S(2)}) %collective-permute-start.18) | collective-permute-done | bytes 409632 | tf_op jit(solution)/shard_map/ppermute | solution.py:326
  57.4 2.1 %collective-permute-start.14 = (bf16[80,1280]{1,0:T(8,128)(2,1)S(1)}, bf16[80,1280]{1,0:T(8,128)(2,1)S(1)}, u32[]{:S(2)}, u32[]{:S(2)}) collective-permute-start(bf16[80,1280]{1,0:T(8,128)(2,1)S(1)} %slice.25), channel_id=1, source_target_pairs={{8,0},{16,8},{24,16},{28,24},{20,28},{12,20},{4,12},{0,4},{9,1},{1... | collective-permute-start | bytes 614408 | tf_op jit(solution)/shard_map/ppermute | solution.py:327
  61.0 2.0 %collective-permute-start.22 = (bf16[80,1280]{1,0:T(8,128)(2,1)S(1)}, bf16[80,1280]{1,0:T(8,128)(2,1)S(1)}, u32[]{:S(2)}, u32[]{:S(2)}) collective-permute-start(bf16[80,1280]{1,0:T(8,128)(2,1)S(1)} %slice.27), channel_id=1, source_target_pairs={{8,0},{16,8},{24,16},{28,24},{20,28},{12,20},{4,12},{0,4},{9,1},{1... | collective-permute-start | bytes 614408 | tf_op jit(solution)/shard_map/ppermute | solution.py:327
  65.0 2.3 %collective-permute-start.26 = (bf16[80,1280]{1,0:T(8,128)(2,1)S(1)}, bf16[80,1280]{1,0:T(8,128)(2,1)S(1)}, u32[]{:S(2)}, u32[]{:S(2)}) collective-permute-start(bf16[80,1280]{1,0:T(8,128)(2,1)S(1)} %get-tuple-element.90.refs_1_), channel_id=1, source_target_pairs={{8,0},{16,8},{24,16},{28,24},{20,28},{12,20},{4,12},{0,4},{9,1},{1... | collective-permute-start | bytes 614408 | tf_op jit(solution)/shard_map/ppermute | solution.py:327
  69.5 2.2 %collective-permute-start.23 = (bf16[80,1280]{1,0:T(8,128)(2,1)S(1)}, bf16[80,1280]{1,0:T(8,128)(2,1)S(1)}, u32[]{:S(2)}, u32[]{:S(2)}) collective-permute-start(bf16[80,1280]{1,0:T(8,128)(2,1)S(1)} %get-tuple-element.89.refs_0_), channel_id=1, source_target_pairs={{8,0},{16,8},{24,16},{28,24},{20,28},{12,20},{4,12},{0,4},{9,1},{1... | collective-permute-start | bytes 614408 | tf_op jit(solution)/shard_map/ppermute | solution.py:327
  74.8 2.2 %mlp_out.3 = (bf16[320,256]{1,0:T(8,128)(2,1)S(1)}, bf16[320,256]{1,0:T(8,128)(2,1)S(1)}, bf16[320,256]{1,0:T(8,128)(2,1)S(1)}, bf16[320,256]{1,0:T(8,128)(2,1)S...) custom-call(bf16[1024,256]{1,0:T(8,128)(2,1)S(1)} %hidden.5.refs_0_,, ...), custom_call_target="tpu_custom_call" | custom-call | tf_op jit(solution)/shard_map/mlp_out/pallas_call | solution.py:23
  80.2 2.4 %mlp_out.2 = (bf16[320,1024]{1,0:T(8,128)(2,1)S(1)}, bf16[320,1024]{1,0:T(8,128)(2,1)S(1)}) custom-call(bf16[1024,256]{1,0:T(8,128)(2,1)S(1)} %hidden.5.refs_0_, bf16[1024,256]{1,0:T(8,128)(2,1)S(1)} %hidden.6.refs_1_, bf16[1024,256]{1,0:T(8,128)(2,1)S(1)} %hidden.7.refs_2_, bf16[1024,256]{1,0:T(8,128)(2,1)S(1)} %hidden.8.refs_3_, ...), custom_call_target="tpu_custom_call" | custom-call | tf_op jit(solution)/shard_map/mlp_out/pallas_call | solution.py:23
  87.7 2.5 %collective-permute-done.37.refs_8_ = bf16[80,1280]{1,0:T(8,128)(2,1)S(1)} collective-permute-done((bf16[80,1280]{1,0:T(8,128)(2,1)S(1)}, bf16[80,1280]{1,0:T(8,128)(2,1)S(1)}, u32[]{:S(2)}, u32[]{:S(2)}) %collective-permute-start.37) | collective-permute-done | bytes 204832 | tf_op jit(solution)/shard_map/ppermute | solution.py:326
  92.4 1.5 %collective-permute-start.32 = (bf16[320,256]{1,0:T(8,128)(2,1)S(1)}, bf16[320,256]{1,0:T(8,128)(2,1)S(1)}, u32[]{:S(2)}, u32[]{:S(2)}) collective-permute-start(bf16[320,256]{1,0:T(8,128)(2,1)S(1)} %add.7), channel_id=1, source_target_pairs={{0,2},{1,3},{2,0},{3,1},{4,6},{5,7},{6,4},{7,5},{8,10},{9,11},{10,... | collective-permute-start | bytes 491528 | tf_op jit(solution)/shard_map/ppermute | solution.py:366
  96.8 1.6 %collective-permute-start.42 = (bf16[80,1280]{1,0:T(8,128)(2,1)S(1)}, bf16[80,1280]{1,0:T(8,128)(2,1)S(1)}, u32[]{:S(2)}, u32[]{:S(2)}) collective-permute-start(bf16[80,1280]{1,0:T(8,128)(2,1)S(1)} %collective-permute-done.38.refs_9_), channel_id=1, source_target_pairs={{8,0},{16,8},{24,16},{28,24},{20,28},{12,20},{4,12},{0,4},{9,1},{1... | collective-permute-start | bytes 614408 | tf_op jit(solution)/shard_map/ppermute | solution.py:327
  101.4 1.6 %collective-permute-start.44 = (bf16[80,1280]{1,0:T(8,128)(2,1)S(1)}, bf16[80,1280]{1,0:T(8,128)(2,1)S(1)}, u32[]{:S(2)}, u32[]{:S(2)}) collective-permute-start(bf16[80,1280]{1,0:T(8,128)(2,1)S(1)} %collective-permute-done.40.refs_11_), channel_id=1, source_target_pairs={{8,0},{16,8},{24,16},{28,24},{20,28},{12,20},{4,12},{0,4},{9,1},{1... | collective-permute-start | bytes 614408 | tf_op jit(solution)/shard_map/ppermute | solution.py:327
  103.6 2.5 %collective-permute-done.41.refs_12_ = bf16[80,1280]{1,0:T(8,128)(2,1)S(1)} collective-permute-done((bf16[80,1280]{1,0:T(8,128)(2,1)S(1)}, bf16[80,1280]{1,0:T(8,128)(2,1)S(1)}, u32[]{:S(2)}, u32[]{:S(2)}) %collective-permute-start.41) | collective-permute-done | bytes 204832 | tf_op jit(solution)/shard_map/ppermute | solution.py:326
  106.0 2.2 %collective-permute-done.43.refs_14_ = bf16[80,1280]{1,0:T(8,128)(2,1)S(1)} collective-permute-done((bf16[80,1280]{1,0:T(8,128)(2,1)S(1)}, bf16[80,1280]{1,0:T(8,128)(2,1)S(1)}, u32[]{:S(2)}, u32[]{:S(2)}) %collective-permute-start.43) | collective-permute-done | bytes 204832 | tf_op jit(solution)/shard_map/ppermute | solution.py:326
  109.7 1.6 %collective-permute-done.45.near = bf16[2,320,256]{2,1,0:T(8,128)(2,1)S(1)} collective-permute-done((bf16[2,320,256]{2,1,0:T(8,128)(2,1)S(1)}, bf16[2,320,256]{2,1,0:T(8,128)(2,1)S(1)}, u32[]{:S(2)}, u32[]{:S(2)}) %collective-permute-start.45) | collective-permute-done | bytes 327712 | tf_op jit(solution)/shard_map/ppermute | solution.py:363
  113.3 4.3 %collective-permute-done.46.far = bf16[320,256]{1,0:T(8,128)(2,1)S(1)} collective-permute-done((bf16[320,256]{1,0:T(8,128)(2,1)S(1)}, bf16[320,256]{1,0:T(8,128)(2,1)S(1)}, u32[]{:S(2)}, u32[]{:S(2)}) %collective-permute-start.46) | collective-permute-done | bytes 163872 | tf_op jit(solution)/shard_map/ppermute | solution.py:366
  118.1 14.6 %all_to_all.5.arrived = bf16[8,160,128]{2,1,0:T(8,128)(2,1)S(1)} all-to-all(bf16[8,160,128]{2,1,0:T(8,128)(2,1)S(1)} %pack.1), channel_id=1, replica_groups=mesh['wide'=8,'narrow'=4] {'wide'}, dimensions={0} | all-to-all | bytes 655360 | tf_op jit(solution)/shard_map/all_to_all | solution.py:441
  (114 shorter events, 38.2 us)
Async XLA Ops:
  0.0 13.5 %collective-permute-start = (bf16[160,1280]{1,0:T(8,128)(2,1)}, bf16[160,1280]{1,0:T(8,128)(2,1)S(1)}, u32[]{:S(2)}, u32[]{:S(2)}) collective-permute-start(bf16[160,1280]{1,0:T(8,128)(2,1)} %refs_0_.9), channel_id=1, source_target_pairs={{0,8},{8,16},{16,24},{24,28},{28,20},{20,12},{12,4},{4,0},{1,9},{9... | collective-permute-start | bytes 1228808 | tf_op jit(solution)/shard_map/ppermute | solution.py:326
  3.0 12.6 %collective-permute-start.1 = (bf16[160,1280]{1,0:T(8,128)(2,1)}, bf16[160,1280]{1,0:T(8,128)(2,1)S(1)}, u32[]{:S(2)}, u32[]{:S(2)}) collective-permute-start(bf16[160,1280]{1,0:T(8,128)(2,1)} %refs_0_.9), channel_id=1, source_target_pairs={{8,0},{16,8},{24,16},{28,24},{20,28},{12,20},{4,12},{0,4},{9,1},{1... | collective-permute-start | bytes 1228808 | tf_op jit(solution)/shard_map/ppermute | solution.py:327
  3.0 19.2 %collective-permute-start.7 = (bf16[160,1280]{1,0:T(8,128)(2,1)}, bf16[160,1280]{1,0:T(8,128)(2,1)S(1)}, u32[]{:S(2)}, u32[]{:S(2)}) collective-permute-start(bf16[160,1280]{1,0:T(8,128)(2,1)} %bitcast.9), channel_id=1, source_target_pairs={{0,8},{8,16},{16,24},{24,28},{28,20},{20,12},{12,4},{4,0},{1,9},{9... | collective-permute-start | bytes 1228808 | tf_op jit(solution)/shard_map/ppermute | solution.py:326
  5.1 19.4 %collective-permute-start.4 = (bf16[160,1280]{1,0:T(8,128)(2,1)}, bf16[160,1280]{1,0:T(8,128)(2,1)S(1)}, u32[]{:S(2)}, u32[]{:S(2)}) collective-permute-start(bf16[160,1280]{1,0:T(8,128)(2,1)} %bitcast.10), channel_id=1, source_target_pairs={{8,0},{16,8},{24,16},{28,24},{20,28},{12,20},{4,12},{0,4},{9,1},{1... | collective-permute-start | bytes 1228808 | tf_op jit(solution)/shard_map/ppermute | solution.py:327
  13.5 17.6 %collective-permute-start.2 = (bf16[160,1280]{1,0:T(8,128)(2,1)S(1)}, bf16[160,1280]{1,0:T(8,128)(2,1)S(1)}, u32[]{:S(2)}, u32[]{:S(2)}) collective-permute-start(bf16[160,1280]{1,0:T(8,128)(2,1)S(1)} %collective-permute-done.refs_1_), channel_id=1, source_target_pairs={{0,8},{8,16},{16,24},{24,28},{28,20},{20,12},{12,4},{4,0},{1,9},{9... | collective-permute-start | bytes 1228808 | tf_op jit(solution)/shard_map/ppermute | solution.py:326
  15.6 18.7 %collective-permute-start.3 = (bf16[160,1280]{1,0:T(8,128)(2,1)S(1)}, bf16[160,1280]{1,0:T(8,128)(2,1)S(1)}, u32[]{:S(2)}, u32[]{:S(2)}) collective-permute-start(bf16[160,1280]{1,0:T(8,128)(2,1)S(1)} %collective-permute-done.1.refs_2_), channel_id=1, source_target_pairs={{8,0},{16,8},{24,16},{28,24},{20,28},{12,20},{4,12},{0,4},{9,1},{1... | collective-permute-start | bytes 1228808 | tf_op jit(solution)/shard_map/ppermute | solution.py:327
  15.6 18.6 %collective-permute-start.10 = (bf16[2,320,256]{2,1,0:T(8,128)(2,1)S(1)}, bf16[2,320,256]{2,1,0:T(8,128)(2,1)S(1)}, u32[]{:S(2)}, u32[]{:S(2)}) collective-permute-start(bf16[2,320,256]{2,1,0:T(8,128)(2,1)S(1)} %get-tuple-element.70.own.refs_0_), channel_id=1, source_target_pairs={{0,2},{1,3},{2,0},{3,1},{4,6},{5,7},{6,4},{7,5},{8,10},{9,11},{10,... | collective-permute-start | bytes 983048 | tf_op jit(solution)/shard_map/ppermute | solution.py:366
  22.2 14.1 %collective-permute-start.11 = (bf16[2,320,256]{2,1,0:T(8,128)(2,1)S(1)}, bf16[2,320,256]{2,1,0:T(8,128)(2,1)S(1)}, u32[]{:S(2)}, u32[]{:S(2)}) collective-permute-start(bf16[2,320,256]{2,1,0:T(8,128)(2,1)S(1)} %get-tuple-element.70.own.refs_0_), channel_id=1, source_target_pairs={{0,1},{1,0},{2,3},{3,2},{4,5},{5,4},{6,7},{7,6},{8,9},{9,8},{10,11... | collective-permute-start | bytes 983048 | tf_op jit(solution)/shard_map/ppermute | solution.py:363
  24.4 15.4 %collective-permute-start.9 = (bf16[160,1280]{1,0:T(8,128)(2,1)S(1)}, bf16[160,1280]{1,0:T(8,128)(2,1)S(1)}, u32[]{:S(2)}, u32[]{:S(2)}) collective-permute-start(bf16[160,1280]{1,0:T(8,128)(2,1)S(1)} %collective-permute-done.7.refs_6_), channel_id=1, source_target_pairs={{0,8},{8,16},{16,24},{24,28},{28,20},{20,12},{12,4},{4,0},{1,9},{9... | collective-permute-start | bytes 1228808 | tf_op jit(solution)/shard_map/ppermute | solution.py:326
  31.0 10.8 %collective-permute-start.8 = (bf16[160,1280]{1,0:T(8,128)(2,1)S(1)}, bf16[160,1280]{1,0:T(8,128)(2,1)S(1)}, u32[]{:S(2)}, u32[]{:S(2)}) collective-permute-start(bf16[160,1280]{1,0:T(8,128)(2,1)S(1)} %collective-permute-done.4.refs_7_), channel_id=1, source_target_pairs={{8,0},{16,8},{24,16},{28,24},{20,28},{12,20},{4,12},{0,4},{9,1},{1... | collective-permute-start | bytes 1228808 | tf_op jit(solution)/shard_map/ppermute | solution.py:327
  34.3 14.3 %collective-permute-start.5 = (bf16[160,1280]{1,0:T(8,128)(2,1)S(1)}, bf16[160,1280]{1,0:T(8,128)(2,1)S(1)}, u32[]{:S(2)}, u32[]{:S(2)}) collective-permute-start(bf16[160,1280]{1,0:T(8,128)(2,1)S(1)} %collective-permute-done.2.refs_3_), channel_id=1, source_target_pairs={{0,8},{8,16},{16,24},{24,28},{28,20},{20,12},{12,4},{4,0},{1,9},{9... | collective-permute-start | bytes 1228808 | tf_op jit(solution)/shard_map/ppermute | solution.py:326
  34.4 8.0 %collective-permute-start.15 = (bf16[2,320,256]{2,1,0:T(8,128)(2,1)S(1)}, bf16[2,320,256]{2,1,0:T(8,128)(2,1)S(1)}, u32[]{:S(2)}, u32[]{:S(2)}) collective-permute-start(bf16[2,320,256]{2,1,0:T(8,128)(2,1)S(1)} %get-tuple-element.76.own.refs_1_), channel_id=1, source_target_pairs={{0,2},{1,3},{2,0},{3,1},{4,6},{5,7},{6,4},{7,5},{8,10},{9,11},{10,... | collective-permute-start | bytes 983048 | tf_op jit(solution)/shard_map/ppermute | solution.py:366
  36.3 7.6 %collective-permute-start.12 = (bf16[2,320,256]{2,1,0:T(8,128)(2,1)S(1)}, bf16[2,320,256]{2,1,0:T(8,128)(2,1)S(1)}, u32[]{:S(2)}, u32[]{:S(2)}) collective-permute-start(bf16[2,320,256]{2,1,0:T(8,128)(2,1)S(1)} %collective-permute-done.10.over_x), channel_id=1, source_target_pairs={{0,1},{1,0},{2,3},{3,2},{4,5},{5,4},{6,7},{7,6},{8,9},{9,8},{10,11... | collective-permute-start | bytes 983048 | tf_op jit(solution)/shard_map/ppermute | solution.py:363
  39.8 12.5 %collective-permute-start.6 = (bf16[160,1280]{1,0:T(8,128)(2,1)S(1)}, bf16[160,1280]{1,0:T(8,128)(2,1)S(1)}, u32[]{:S(2)}, u32[]{:S(2)}) collective-permute-start(bf16[160,1280]{1,0:T(8,128)(2,1)S(1)} %collective-permute-done.3.refs_4_), channel_id=1, source_target_pairs={{8,0},{16,8},{24,16},{28,24},{20,28},{12,20},{4,12},{0,4},{9,1},{1... | collective-permute-start | bytes 1228808 | tf_op jit(solution)/shard_map/ppermute | solution.py:327
  41.9 15.5 %collective-permute-start.18 = (bf16[160,1280]{1,0:T(8,128)(2,1)S(1)}, bf16[160,1280]{1,0:T(8,128)(2,1)S(1)}, u32[]{:S(2)}, u32[]{:S(2)}) collective-permute-start(bf16[160,1280]{1,0:T(8,128)(2,1)S(1)} %collective-permute-done.9.refs_8_), channel_id=1, source_target_pairs={{0,8},{8,16},{16,24},{24,28},{28,20},{20,12},{12,4},{4,0},{1,9},{9... | collective-permute-start | bytes 1228808 | tf_op jit(solution)/shard_map/ppermute | solution.py:326
  42.3 18.7 %collective-permute-start.21 = (bf16[160,1280]{1,0:T(8,128)(2,1)S(1)}, bf16[160,1280]{1,0:T(8,128)(2,1)S(1)}, u32[]{:S(2)}, u32[]{:S(2)}) collective-permute-start(bf16[160,1280]{1,0:T(8,128)(2,1)S(1)} %collective-permute-done.8.refs_9_), channel_id=1, source_target_pairs={{8,0},{16,8},{24,16},{28,24},{20,28},{12,20},{4,12},{0,4},{9,1},{1... | collective-permute-start | bytes 1228808 | tf_op jit(solution)/shard_map/ppermute | solution.py:327
  43.9 15.6 %collective-permute-start.16 = (bf16[2,320,256]{2,1,0:T(8,128)(2,1)S(1)}, bf16[2,320,256]{2,1,0:T(8,128)(2,1)S(1)}, u32[]{:S(2)}, u32[]{:S(2)}) collective-permute-start(bf16[2,320,256]{2,1,0:T(8,128)(2,1)S(1)} %get-tuple-element.76.own.refs_1_), channel_id=1, source_target_pairs={{0,1},{1,0},{2,3},{3,2},{4,5},{5,4},{6,7},{7,6},{8,9},{9,8},{10,11... | collective-permute-start | bytes 983048 | tf_op jit(solution)/shard_map/ppermute | solution.py:363
  48.6 10.9 %collective-permute-start.17 = (bf16[2,320,256]{2,1,0:T(8,128)(2,1)S(1)}, bf16[2,320,256]{2,1,0:T(8,128)(2,1)S(1)}, u32[]{:S(2)}, u32[]{:S(2)}) collective-permute-start(bf16[2,320,256]{2,1,0:T(8,128)(2,1)S(1)} %collective-permute-done.15.over_x), channel_id=1, source_target_pairs={{0,1},{1,0},{2,3},{3,2},{4,5},{5,4},{6,7},{7,6},{8,9},{9,8},{10,11... | collective-permute-start | bytes 983048 | tf_op jit(solution)/shard_map/ppermute | solution.py:363
  52.3 10.7 %collective-permute-start.13 = (bf16[80,1280]{1,0:T(8,128)(2,1)S(1)}, bf16[80,1280]{1,0:T(8,128)(2,1)S(1)}, u32[]{:S(2)}, u32[]{:S(2)}) collective-permute-start(bf16[80,1280]{1,0:T(8,128)(2,1)S(1)} %slice.24), channel_id=1, source_target_pairs={{0,8},{8,16},{16,24},{24,28},{28,20},{20,12},{12,4},{4,0},{1,9},{9... | collective-permute-start | bytes 614408 | tf_op jit(solution)/shard_map/ppermute | solution.py:326
  57.4 7.7 %collective-permute-start.14 = (bf16[80,1280]{1,0:T(8,128)(2,1)S(1)}, bf16[80,1280]{1,0:T(8,128)(2,1)S(1)}, u32[]{:S(2)}, u32[]{:S(2)}) collective-permute-start(bf16[80,1280]{1,0:T(8,128)(2,1)S(1)} %slice.25), channel_id=1, source_target_pairs={{8,0},{16,8},{24,16},{28,24},{20,28},{12,20},{4,12},{0,4},{9,1},{1... | collective-permute-start | bytes 614408 | tf_op jit(solution)/shard_map/ppermute | solution.py:327
  60.9 8.5 %collective-permute-start.19 = (bf16[80,1280]{1,0:T(8,128)(2,1)S(1)}, bf16[80,1280]{1,0:T(8,128)(2,1)S(1)}, u32[]{:S(2)}, u32[]{:S(2)}) collective-permute-start(bf16[80,1280]{1,0:T(8,128)(2,1)S(1)} %slice.26), channel_id=1, source_target_pairs={{0,8},{8,16},{16,24},{24,28},{28,20},{20,12},{12,4},{4,0},{1,9},{9... | collective-permute-start | bytes 614408 | tf_op jit(solution)/shard_map/ppermute | solution.py:326
  61.0 8.5 %collective-permute-start.22 = (bf16[80,1280]{1,0:T(8,128)(2,1)S(1)}, bf16[80,1280]{1,0:T(8,128)(2,1)S(1)}, u32[]{:S(2)}, u32[]{:S(2)}) collective-permute-start(bf16[80,1280]{1,0:T(8,128)(2,1)S(1)} %slice.27), channel_id=1, source_target_pairs={{8,0},{16,8},{24,16},{28,24},{20,28},{12,20},{4,12},{0,4},{9,1},{1... | collective-permute-start | bytes 614408 | tf_op jit(solution)/shard_map/ppermute | solution.py:327
  63.1 11.8 %collective-permute-start.25 = (bf16[80,1280]{1,0:T(8,128)(2,1)S(1)}, bf16[80,1280]{1,0:T(8,128)(2,1)S(1)}, u32[]{:S(2)}, u32[]{:S(2)}) collective-permute-start(bf16[80,1280]{1,0:T(8,128)(2,1)S(1)} %get-tuple-element.89.refs_0_), channel_id=1, source_target_pairs={{0,8},{8,16},{16,24},{24,28},{28,20},{20,12},{12,4},{4,0},{1,9},{9... | collective-permute-start | bytes 614408 | tf_op jit(solution)/shard_map/ppermute | solution.py:326
  65.0 9.8 %collective-permute-start.26 = (bf16[80,1280]{1,0:T(8,128)(2,1)S(1)}, bf16[80,1280]{1,0:T(8,128)(2,1)S(1)}, u32[]{:S(2)}, u32[]{:S(2)}) collective-permute-start(bf16[80,1280]{1,0:T(8,128)(2,1)S(1)} %get-tuple-element.90.refs_1_), channel_id=1, source_target_pairs={{8,0},{16,8},{24,16},{28,24},{20,28},{12,20},{4,12},{0,4},{9,1},{1... | collective-permute-start | bytes 614408 | tf_op jit(solution)/shard_map/ppermute | solution.py:327
  69.4 8.3 %collective-permute-start.20 = (bf16[80,1280]{1,0:T(8,128)(2,1)S(1)}, bf16[80,1280]{1,0:T(8,128)(2,1)S(1)}, u32[]{:S(2)}, u32[]{:S(2)}) collective-permute-start(bf16[80,1280]{1,0:T(8,128)(2,1)S(1)} %get-tuple-element.90.refs_1_), channel_id=1, source_target_pairs={{0,8},{8,16},{16,24},{24,28},{28,20},{20,12},{12,4},{4,0},{1,9},{9... | collective-permute-start | bytes 614408 | tf_op jit(solution)/shard_map/ppermute | solution.py:326
  69.5 8.6 %collective-permute-start.23 = (bf16[80,1280]{1,0:T(8,128)(2,1)S(1)}, bf16[80,1280]{1,0:T(8,128)(2,1)S(1)}, u32[]{:S(2)}, u32[]{:S(2)}) collective-permute-start(bf16[80,1280]{1,0:T(8,128)(2,1)S(1)} %get-tuple-element.89.refs_0_), channel_id=1, source_target_pairs={{8,0},{16,8},{24,16},{28,24},{20,28},{12,20},{4,12},{0,4},{9,1},{1... | collective-permute-start | bytes 614408 | tf_op jit(solution)/shard_map/ppermute | solution.py:327
  82.6 20.5 %collective-permute-start.24 = (bf16[320,1024]{1,0:T(8,128)(2,1)S(1)}, bf16[320,1024]{1,0:T(8,128)(2,1)S(1)}, u32[]{:S(2)}, u32[]{:S(2)}) collective-permute-start(bf16[320,1024]{1,0:T(8,128)(2,1)S(1)} %get-tuple-element.88), channel_id=1, source_target_pairs={{0,1},{1,0},{2,3},{3,2},{4,5},{5,4},{6,7},{7,6},{8,9},{9,8},{10,11... | collective-permute-start | bytes 1966088 | tf_op jit(solution)/shard_map/ppermute | solution.py:363
  82.7 7.5 %collective-permute-start.37 = (bf16[80,1280]{1,0:T(8,128)(2,1)S(1)}, bf16[80,1280]{1,0:T(8,128)(2,1)S(1)}, u32[]{:S(2)}, u32[]{:S(2)}) collective-permute-start(bf16[80,1280]{1,0:T(8,128)(2,1)S(1)} %collective-permute-done.20.refs_4_), channel_id=1, source_target_pairs={{0,8},{8,16},{16,24},{24,28},{28,20},{20,12},{12,4},{4,0},{1,9},{9... | collective-permute-start | bytes 614408 | tf_op jit(solution)/shard_map/ppermute | solution.py:326
  83.9 7.4 %collective-permute-start.38 = (bf16[80,1280]{1,0:T(8,128)(2,1)S(1)}, bf16[80,1280]{1,0:T(8,128)(2,1)S(1)}, u32[]{:S(2)}, u32[]{:S(2)}) collective-permute-start(bf16[80,1280]{1,0:T(8,128)(2,1)S(1)} %collective-permute-done.23.refs_5_), channel_id=1, source_target_pairs={{8,0},{16,8},{24,16},{28,24},{20,28},{12,20},{4,12},{0,4},{9,1},{1... | collective-permute-start | bytes 614408 | tf_op jit(solution)/shard_map/ppermute | solution.py:327
  86.8 7.9 %collective-permute-start.30 = (bf16[320,256]{1,0:T(8,128)(2,1)S(1)}, bf16[320,256]{1,0:T(8,128)(2,1)S(1)}, u32[]{:S(2)}, u32[]{:S(2)}) collective-permute-start(bf16[320,256]{1,0:T(8,128)(2,1)S(1)} %add.6), channel_id=1, source_target_pairs={{0,2},{1,3},{2,0},{3,1},{4,6},{5,7},{6,4},{7,5},{8,10},{9,11},{10,... | collective-permute-start | bytes 491528 | tf_op jit(solution)/shard_map/ppermute | solution.py:366
  98.4 7.6 %collective-permute-start.41 = (bf16[80,1280]{1,0:T(8,128)(2,1)S(1)}, bf16[80,1280]{1,0:T(8,128)(2,1)S(1)}, u32[]{:S(2)}, u32[]{:S(2)}) collective-permute-start(bf16[80,1280]{1,0:T(8,128)(2,1)S(1)} %collective-permute-done.37.refs_8_), channel_id=1, source_target_pairs={{0,8},{8,16},{16,24},{24,28},{28,20},{20,12},{12,4},{4,0},{1,9},{9... | collective-permute-start | bytes 614408 | tf_op jit(solution)/shard_map/ppermute | solution.py:326
  99.5 8.7 %collective-permute-start.43 = (bf16[80,1280]{1,0:T(8,128)(2,1)S(1)}, bf16[80,1280]{1,0:T(8,128)(2,1)S(1)}, u32[]{:S(2)}, u32[]{:S(2)}) collective-permute-start(bf16[80,1280]{1,0:T(8,128)(2,1)S(1)} %collective-permute-done.39.refs_10_), channel_id=1, source_target_pairs={{0,8},{8,16},{16,24},{24,28},{28,20},{20,12},{12,4},{4,0},{1,9},{9... | collective-permute-start | bytes 614408 | tf_op jit(solution)/shard_map/ppermute | solution.py:326
  (24 other events, 169.4 us)

commit v11 on v10

--- a/solution.py
+++ b/solution.py
@@ -10,7 +10,7 @@
 F32 = jnp.float32
 BF16 = jnp.bfloat16
 WINDOW = 4
-LATE = (1, 2, 3)
+LATE = (2, 2, 3)
 HIDDEN_AT = (7, 7, 8, 8, 8)
 OUT_AT = 1
 OWN_PARTS = 1

time: 134 us -> 135 us (level)
    ppermute x15, waiting for transfers between devices: 35.6 us -> 34.1 us  [step(): lax.ppermute(to_right, 'wide', self.right)]
    ppermute x15, waiting for transfers between devices: 4.44 us -> 5.9 us  [step(): lax.ppermute(to_left, 'wide', self.left)]
  transfers between devices with their start and end apart: 47 -> 47, of which waited for: 20 -> 22; matrix products, arithmetic and copies ran while one was open for 1% -> 1% of each run, Pallas kernels for 11% -> 11%
where the time goes in v11:
time: 135 us
  starting transfers between devices  49.4 us (37%)
  waiting for transfers between devices  48.2 us (36%)
  Pallas kernels  17.5 us (13%)
  blocking collectives  15.3 us (11%)
  local copies, waits for them, and re-layouts  3.84 us (3%)
    ppermute x15, waiting for transfers between devices, step(): lax.ppermute(to_right, 'wide', self.right)  34.1 us
    ppermute x15, starting transfers between devices, step(): lax.ppermute(to_left, 'wide', self.left)  19.3 us
    ppermute x15, starting transfers between devices, step(): lax.ppermute(to_right, 'wide', self.right)  18.2 us
    pallas_call x21, Pallas kernels, call(): pl.pallas_call(kernel, out_shape=outs, in_specs=[VMEM] * len(operands), o...  17.5 us
    all_to_all x1, blocking collectives, exchange_and_place(): lax.all_to_all(buffer, 'wide', split_axis=0, concat_axis=0, tiled=True)  15.3 us
    ppermute x7, starting transfers between devices, far(): return lax.ppermute(x, 'narrow', far_pairs)  10.7 us
    ppermute x7, waiting for transfers between devices, far(): return lax.ppermute(x, 'narrow', far_pairs)  6.57 us
    ppermute x15, waiting for transfers between devices, step(): lax.ppermute(to_left, 'wide', self.left)  5.9 us
  transfers between devices with their start and end apart: 47, of which 22 were waited for; matrix products, arithmetic and copies ran while one was open for 1% of the time, Pallas kernels for 11%

profile of v11, /device:TPU:0, one launch (start us, length us, event | category | flops | bytes accessed | tf_op | source)
XLA Modules:
  0.0 134.6 jit_solution(3519996558223765180)
XLA Ops:
  0.0 3.0 %collective-permute-start = (bf16[160,1280]{1,0:T(8,128)(2,1)}, bf16[160,1280]{1,0:T(8,128)(2,1)S(1)}, u32[]{:S(2)}, u32[]{:S(2)}) collective-permute-start(bf16[160,1280]{1,0:T(8,128)(2,1)} %refs_0_.9), channel_id=1, source_target_pairs={{0,8},{8,16},{16,24},{24,28},{28,20},{20,12},{12,4},{4,0},{1,9},{9... | collective-permute-start | bytes 1228808 | tf_op jit(solution)/shard_map/ppermute | solution.py:326
  3.0 2.0 %collective-permute-start.7 = (bf16[160,1280]{1,0:T(8,128)(2,1)}, bf16[160,1280]{1,0:T(8,128)(2,1)S(1)}, u32[]{:S(2)}, u32[]{:S(2)}) collective-permute-start(bf16[160,1280]{1,0:T(8,128)(2,1)} %bitcast.9), channel_id=1, source_target_pairs={{0,8},{8,16},{16,24},{24,28},{28,20},{20,12},{12,4},{4,0},{1,9},{9... | collective-permute-start | bytes 1228808 | tf_op jit(solution)/shard_map/ppermute | solution.py:326
  7.0 6.5 %collective-permute-done.refs_1_ = bf16[160,1280]{1,0:T(8,128)(2,1)S(1)} collective-permute-done((bf16[160,1280]{1,0:T(8,128)(2,1)}, bf16[160,1280]{1,0:T(8,128)(2,1)S(1)}, u32[]{:S(2)}, u32[]{:S(2)}) %collective-permute-start) | collective-permute-done | bytes 409632 | tf_op jit(solution)/shard_map/ppermute | solution.py:326
  13.5 2.1 %collective-permute-start.2 = (bf16[160,1280]{1,0:T(8,128)(2,1)S(1)}, bf16[160,1280]{1,0:T(8,128)(2,1)S(1)}, u32[]{:S(2)}, u32[]{:S(2)}) collective-permute-start(bf16[160,1280]{1,0:T(8,128)(2,1)S(1)} %collective-permute-done.refs_1_), channel_id=1, source_target_pairs={{0,8},{8,16},{16,24},{24,28},{28,20},{20,12},{12,4},{4,0},{1,9},{9... | collective-permute-start | bytes 1228808 | tf_op jit(solution)/shard_map/ppermute | solution.py:326
  15.6 1.9 %collective-permute-start.10 = (bf16[2,320,256]{2,1,0:T(8,128)(2,1)S(1)}, bf16[2,320,256]{2,1,0:T(8,128)(2,1)S(1)}, u32[]{:S(2)}, u32[]{:S(2)}) collective-permute-start(bf16[2,320,256]{2,1,0:T(8,128)(2,1)S(1)} %get-tuple-element.70.own.refs_0_), channel_id=1, source_target_pairs={{0,2},{1,3},{2,0},{3,1},{4,6},{5,7},{6,4},{7,5},{8,10},{9,11},{10,... | collective-permute-start | bytes 983048 | tf_op jit(solution)/shard_map/ppermute | solution.py:366
  17.6 4.7 %collective-permute-done.7.refs_6_ = bf16[160,1280]{1,0:T(8,128)(2,1)S(1)} collective-permute-done((bf16[160,1280]{1,0:T(8,128)(2,1)}, bf16[160,1280]{1,0:T(8,128)(2,1)S(1)}, u32[]{:S(2)}, u32[]{:S(2)}) %collective-permute-start.7) | collective-permute-done | bytes 409632 | tf_op jit(solution)/shard_map/ppermute | solution.py:326
  22.2 2.2 %collective-permute-done.4.refs_7_ = bf16[160,1280]{1,0:T(8,128)(2,1)S(1)} collective-permute-done((bf16[160,1280]{1,0:T(8,128)(2,1)}, bf16[160,1280]{1,0:T(8,128)(2,1)S(1)}, u32[]{:S(2)}, u32[]{:S(2)}) %collective-permute-start.4) | collective-permute-done | bytes 409632 | tf_op jit(solution)/shard_map/ppermute | solution.py:327
  24.4 1.6 %collective-permute-start.9 = (bf16[160,1280]{1,0:T(8,128)(2,1)S(1)}, bf16[160,1280]{1,0:T(8,128)(2,1)S(1)}, u32[]{:S(2)}, u32[]{:S(2)}) collective-permute-start(bf16[160,1280]{1,0:T(8,128)(2,1)S(1)} %collective-permute-done.7.refs_6_), channel_id=1, source_target_pairs={{0,8},{8,16},{16,24},{24,28},{28,20},{20,12},{12,4},{4,0},{1,9},{9... | collective-permute-start | bytes 1228808 | tf_op jit(solution)/shard_map/ppermute | solution.py:326
  26.0 5.0 %collective-permute-done.2.refs_3_ = bf16[160,1280]{1,0:T(8,128)(2,1)S(1)} collective-permute-done((bf16[160,1280]{1,0:T(8,128)(2,1)S(1)}, bf16[160,1280]{1,0:T(8,128)(2,1)S(1)}, u32[]{:S(2)}, u32[]{:S(2)}) %collective-permute-start.2) | collective-permute-done | bytes 409632 | tf_op jit(solution)/shard_map/ppermute | solution.py:326
  31.0 2.1 %collective-permute-start.8 = (bf16[160,1280]{1,0:T(8,128)(2,1)S(1)}, bf16[160,1280]{1,0:T(8,128)(2,1)S(1)}, u32[]{:S(2)}, u32[]{:S(2)}) collective-permute-start(bf16[160,1280]{1,0:T(8,128)(2,1)S(1)} %collective-permute-done.4.refs_7_), channel_id=1, source_target_pairs={{8,0},{16,8},{24,16},{28,24},{20,28},{12,20},{4,12},{0,4},{9,1},{1... | collective-permute-start | bytes 1228808 | tf_op jit(solution)/shard_map/ppermute | solution.py:327
  34.4 1.9 %collective-permute-start.15 = (bf16[2,320,256]{2,1,0:T(8,128)(2,1)S(1)}, bf16[2,320,256]{2,1,0:T(8,128)(2,1)S(1)}, u32[]{:S(2)}, u32[]{:S(2)}) collective-permute-start(bf16[2,320,256]{2,1,0:T(8,128)(2,1)S(1)} %get-tuple-element.76.own.refs_1_), channel_id=1, source_target_pairs={{0,2},{1,3},{2,0},{3,1},{4,6},{5,7},{6,4},{7,5},{8,10},{9,11},{10,... | collective-permute-start | bytes 983048 | tf_op jit(solution)/shard_map/ppermute | solution.py:366
  36.3 3.5 %collective-permute-done.9.refs_8_ = bf16[160,1280]{1,0:T(8,128)(2,1)S(1)} collective-permute-done((bf16[160,1280]{1,0:T(8,128)(2,1)S(1)}, bf16[160,1280]{1,0:T(8,128)(2,1)S(1)}, u32[]{:S(2)}, u32[]{:S(2)}) %collective-permute-start.9) | collective-permute-done | bytes 409632 | tf_op jit(solution)/shard_map/ppermute | solution.py:326
  39.8 2.1 %collective-permute-start.6 = (bf16[160,1280]{1,0:T(8,128)(2,1)S(1)}, bf16[160,1280]{1,0:T(8,128)(2,1)S(1)}, u32[]{:S(2)}, u32[]{:S(2)}) collective-permute-start(bf16[160,1280]{1,0:T(8,128)(2,1)S(1)} %collective-permute-done.3.refs_4_), channel_id=1, source_target_pairs={{8,0},{16,8},{24,16},{28,24},{20,28},{12,20},{4,12},{0,4},{9,1},{1... | collective-permute-start | bytes 1228808 | tf_op jit(solution)/shard_map/ppermute | solution.py:327
  42.3 1.6 %collective-permute-start.21 = (bf16[160,1280]{1,0:T(8,128)(2,1)S(1)}, bf16[160,1280]{1,0:T(8,128)(2,1)S(1)}, u32[]{:S(2)}, u32[]{:S(2)}) collective-permute-start(bf16[160,1280]{1,0:T(8,128)(2,1)S(1)} %collective-permute-done.8.refs_9_), channel_id=1, source_target_pairs={{8,0},{16,8},{24,16},{28,24},{20,28},{12,20},{4,12},{0,4},{9,1},{1... | collective-permute-start | bytes 1228808 | tf_op jit(solution)/shard_map/ppermute | solution.py:327
  43.9 4.7 %collective-permute-done.5.refs_5_ = bf16[160,1280]{1,0:T(8,128)(2,1)S(1)} collective-permute-done((bf16[160,1280]{1,0:T(8,128)(2,1)S(1)}, bf16[160,1280]{1,0:T(8,128)(2,1)S(1)}, u32[]{:S(2)}, u32[]{:S(2)}) %collective-permute-start.5) | collective-permute-done | bytes 409632 | tf_op jit(solution)/shard_map/ppermute | solution.py:326
  52.3 2.0 %collective-permute-start.13 = (bf16[80,1280]{1,0:T(8,128)(2,1)S(1)}, bf16[80,1280]{1,0:T(8,128)(2,1)S(1)}, u32[]{:S(2)}, u32[]{:S(2)}) collective-permute-start(bf16[80,1280]{1,0:T(8,128)(2,1)S(1)} %slice.24), channel_id=1, source_target_pairs={{0,8},{8,16},{16,24},{24,28},{28,20},{20,12},{12,4},{4,0},{1,9},{9... | collective-permute-start | bytes 614408 | tf_op jit(solution)/shard_map/ppermute | solution.py:326
  54.3 3.0 %collective-permute-done.18.refs_10_ = bf16[160,1280]{1,0:T(8,128)(2,1)S(1)} collective-permute-done((bf16[160,1280]{1,0:T(8,128)(2,1)S(1)}, bf16[160,1280]{1,0:T(8,128)(2,1)S(1)}, u32[]{:S(2)}, u32[]{:S(2)}) %collective-permute-start.18) | collective-permute-done | bytes 409632 | tf_op jit(solution)/shard_map/ppermute | solution.py:326
  57.4 2.1 %collective-permute-start.14 = (bf16[80,1280]{1,0:T(8,128)(2,1)S(1)}, bf16[80,1280]{1,0:T(8,128)(2,1)S(1)}, u32[]{:S(2)}, u32[]{:S(2)}) collective-permute-start(bf16[80,1280]{1,0:T(8,128)(2,1)S(1)} %slice.25), channel_id=1, source_target_pairs={{8,0},{16,8},{24,16},{28,24},{20,28},{12,20},{4,12},{0,4},{9,1},{1... | collective-permute-start | bytes 614408 | tf_op jit(solution)/shard_map/ppermute | solution.py:327
  61.0 2.0 %collective-permute-start.22 = (bf16[80,1280]{1,0:T(8,128)(2,1)S(1)}, bf16[80,1280]{1,0:T(8,128)(2,1)S(1)}, u32[]{:S(2)}, u32[]{:S(2)}) collective-permute-start(bf16[80,1280]{1,0:T(8,128)(2,1)S(1)} %slice.27), channel_id=1, source_target_pairs={{8,0},{16,8},{24,16},{28,24},{20,28},{12,20},{4,12},{0,4},{9,1},{1... | collective-permute-start | bytes 614408 | tf_op jit(solution)/shard_map/ppermute | solution.py:327
  65.0 2.3 %collective-permute-start.26 = (bf16[80,1280]{1,0:T(8,128)(2,1)S(1)}, bf16[80,1280]{1,0:T(8,128)(2,1)S(1)}, u32[]{:S(2)}, u32[]{:S(2)}) collective-permute-start(bf16[80,1280]{1,0:T(8,128)(2,1)S(1)} %get-tuple-element.90.refs_1_), channel_id=1, source_target_pairs={{8,0},{16,8},{24,16},{28,24},{20,28},{12,20},{4,12},{0,4},{9,1},{1... | collective-permute-start | bytes 614408 | tf_op jit(solution)/shard_map/ppermute | solution.py:327
  69.5 2.2 %collective-permute-start.23 = (bf16[80,1280]{1,0:T(8,128)(2,1)S(1)}, bf16[80,1280]{1,0:T(8,128)(2,1)S(1)}, u32[]{:S(2)}, u32[]{:S(2)}) collective-permute-start(bf16[80,1280]{1,0:T(8,128)(2,1)S(1)} %get-tuple-element.89.refs_0_), channel_id=1, source_target_pairs={{8,0},{16,8},{24,16},{28,24},{20,28},{12,20},{4,12},{0,4},{9,1},{1... | collective-permute-start | bytes 614408 | tf_op jit(solution)/shard_map/ppermute | solution.py:327
  74.8 2.2 %mlp_out.3 = (bf16[320,256]{1,0:T(8,128)(2,1)S(1)}, bf16[320,256]{1,0:T(8,128)(2,1)S(1)}, bf16[320,256]{1,0:T(8,128)(2,1)S(1)}, bf16[320,256]{1,0:T(8,128)(2,1)S...) custom-call(bf16[1024,256]{1,0:T(8,128)(2,1)S(1)} %hidden.5.refs_0_,, ...), custom_call_target="tpu_custom_call" | custom-call | tf_op jit(solution)/shard_map/mlp_out/pallas_call | solution.py:23
  80.2 2.4 %mlp_out.2 = (bf16[320,1024]{1,0:T(8,128)(2,1)S(1)}, bf16[320,1024]{1,0:T(8,128)(2,1)S(1)}) custom-call(bf16[1024,256]{1,0:T(8,128)(2,1)S(1)} %hidden.5.refs_0_, bf16[1024,256]{1,0:T(8,128)(2,1)S(1)} %hidden.6.refs_1_, bf16[1024,256]{1,0:T(8,128)(2,1)S(1)} %hidden.7.refs_2_, bf16[1024,256]{1,0:T(8,128)(2,1)S(1)} %hidden.8.refs_3_, ...), custom_call_target="tpu_custom_call" | custom-call | tf_op jit(solution)/shard_map/mlp_out/pallas_call | solution.py:23
  85.2 1.5 %collective-permute-start.28 = (bf16[320,256]{1,0:T(8,128)(2,1)S(1)}, bf16[320,256]{1,0:T(8,128)(2,1)S(1)}, u32[]{:S(2)}, u32[]{:S(2)}) collective-permute-start(bf16[320,256]{1,0:T(8,128)(2,1)S(1)} %add.5), channel_id=1, source_target_pairs={{0,2},{1,3},{2,0},{3,1},{4,6},{5,7},{6,4},{7,5},{8,10},{9,11},{10,... | collective-permute-start | bytes 491528 | tf_op jit(solution)/shard_map/ppermute | solution.py:366
  87.7 2.5 %collective-permute-done.37.refs_8_ = bf16[80,1280]{1,0:T(8,128)(2,1)S(1)} collective-permute-done((bf16[80,1280]{1,0:T(8,128)(2,1)S(1)}, bf16[80,1280]{1,0:T(8,128)(2,1)S(1)}, u32[]{:S(2)}, u32[]{:S(2)}) %collective-permute-start.37) | collective-permute-done | bytes 204832 | tf_op jit(solution)/shard_map/ppermute | solution.py:326
  92.4 1.5 %collective-permute-start.32 = (bf16[320,256]{1,0:T(8,128)(2,1)S(1)}, bf16[320,256]{1,0:T(8,128)(2,1)S(1)}, u32[]{:S(2)}, u32[]{:S(2)}) collective-permute-start(bf16[320,256]{1,0:T(8,128)(2,1)S(1)} %add.7), channel_id=1, source_target_pairs={{0,2},{1,3},{2,0},{3,1},{4,6},{5,7},{6,4},{7,5},{8,10},{9,11},{10,... | collective-permute-start | bytes 491528 | tf_op jit(solution)/shard_map/ppermute | solution.py:366
  101.4 1.6 %collective-permute-start.44 = (bf16[80,1280]{1,0:T(8,128)(2,1)S(1)}, bf16[80,1280]{1,0:T(8,128)(2,1)S(1)}, u32[]{:S(2)}, u32[]{:S(2)}) collective-permute-start(bf16[80,1280]{1,0:T(8,128)(2,1)S(1)} %collective-permute-done.40.refs_11_), channel_id=1, source_target_pairs={{8,0},{16,8},{24,16},{28,24},{20,28},{12,20},{4,12},{0,4},{9,1},{1... | collective-permute-start | bytes 614408 | tf_op jit(solution)/shard_map/ppermute | solution.py:327
  105.0 1.9 %collective-permute-done.43.refs_14_ = bf16[80,1280]{1,0:T(8,128)(2,1)S(1)} collective-permute-done((bf16[80,1280]{1,0:T(8,128)(2,1)S(1)}, bf16[80,1280]{1,0:T(8,128)(2,1)S(1)}, u32[]{:S(2)}, u32[]{:S(2)}) %collective-permute-start.43) | collective-permute-done | bytes 204832 | tf_op jit(solution)/shard_map/ppermute | solution.py:326
  109.6 1.6 %collective-permute-done.45.near = bf16[2,320,256]{2,1,0:T(8,128)(2,1)S(1)} collective-permute-done((bf16[2,320,256]{2,1,0:T(8,128)(2,1)S(1)}, bf16[2,320,256]{2,1,0:T(8,128)(2,1)S(1)}, u32[]{:S(2)}, u32[]{:S(2)}) %collective-permute-start.45) | collective-permute-done | bytes 327712 | tf_op jit(solution)/shard_map/ppermute | solution.py:363
  111.2 1.6 %collective-permute-start.46 = (bf16[320,256]{1,0:T(8,128)(2,1)S(1)}, bf16[320,256]{1,0:T(8,128)(2,1)S(1)}, u32[]{:S(2)}, u32[]{:S(2)}) collective-permute-start(bf16[320,256]{1,0:T(8,128)(2,1)S(1)} %add.9), channel_id=1, source_target_pairs={{0,2},{1,3},{2,0},{3,1},{4,6},{5,7},{6,4},{7,5},{8,10},{9,11},{10,... | collective-permute-start | bytes 491528 | tf_op jit(solution)/shard_map/ppermute | solution.py:366
  113.3 4.2 %collective-permute-done.46.far = bf16[320,256]{1,0:T(8,128)(2,1)S(1)} collective-permute-done((bf16[320,256]{1,0:T(8,128)(2,1)S(1)}, bf16[320,256]{1,0:T(8,128)(2,1)S(1)}, u32[]{:S(2)}, u32[]{:S(2)}) %collective-permute-start.46) | collective-permute-done | bytes 163872 | tf_op jit(solution)/shard_map/ppermute | solution.py:366
  118.0 15.3 %all_to_all.5.arrived = bf16[8,160,128]{2,1,0:T(8,128)(2,1)S(1)} all-to-all(bf16[8,160,128]{2,1,0:T(8,128)(2,1)S(1)} %pack.1), channel_id=1, replica_groups=mesh['wide'=8,'narrow'=4] {'wide'}, dimensions={0} | all-to-all | bytes 655360 | tf_op jit(solution)/shard_map/all_to_all | solution.py:441
  (114 shorter events, 39.4 us)
Async XLA Ops:
  0.0 13.5 %collective-permute-start = (bf16[160,1280]{1,0:T(8,128)(2,1)}, bf16[160,1280]{1,0:T(8,128)(2,1)S(1)}, u32[]{:S(2)}, u32[]{:S(2)}) collective-permute-start(bf16[160,1280]{1,0:T(8,128)(2,1)} %refs_0_.9), channel_id=1, source_target_pairs={{0,8},{8,16},{16,24},{24,28},{28,20},{20,12},{12,4},{4,0},{1,9},{9... | collective-permute-start | bytes 1228808 | tf_op jit(solution)/shard_map/ppermute | solution.py:326
  3.0 12.6 %collective-permute-start.1 = (bf16[160,1280]{1,0:T(8,128)(2,1)}, bf16[160,1280]{1,0:T(8,128)(2,1)S(1)}, u32[]{:S(2)}, u32[]{:S(2)}) collective-permute-start(bf16[160,1280]{1,0:T(8,128)(2,1)} %refs_0_.9), channel_id=1, source_target_pairs={{8,0},{16,8},{24,16},{28,24},{20,28},{12,20},{4,12},{0,4},{9,1},{1... | collective-permute-start | bytes 1228808 | tf_op jit(solution)/shard_map/ppermute | solution.py:327
  3.0 19.2 %collective-permute-start.7 = (bf16[160,1280]{1,0:T(8,128)(2,1)}, bf16[160,1280]{1,0:T(8,128)(2,1)S(1)}, u32[]{:S(2)}, u32[]{:S(2)}) collective-permute-start(bf16[160,1280]{1,0:T(8,128)(2,1)} %bitcast.9), channel_id=1, source_target_pairs={{0,8},{8,16},{16,24},{24,28},{28,20},{20,12},{12,4},{4,0},{1,9},{9... | collective-permute-start | bytes 1228808 | tf_op jit(solution)/shard_map/ppermute | solution.py:326
  5.1 19.4 %collective-permute-start.4 = (bf16[160,1280]{1,0:T(8,128)(2,1)}, bf16[160,1280]{1,0:T(8,128)(2,1)S(1)}, u32[]{:S(2)}, u32[]{:S(2)}) collective-permute-start(bf16[160,1280]{1,0:T(8,128)(2,1)} %bitcast.10), channel_id=1, source_target_pairs={{8,0},{16,8},{24,16},{28,24},{20,28},{12,20},{4,12},{0,4},{9,1},{1... | collective-permute-start | bytes 1228808 | tf_op jit(solution)/shard_map/ppermute | solution.py:327
  13.5 17.6 %collective-permute-start.2 = (bf16[160,1280]{1,0:T(8,128)(2,1)S(1)}, bf16[160,1280]{1,0:T(8,128)(2,1)S(1)}, u32[]{:S(2)}, u32[]{:S(2)}) collective-permute-start(bf16[160,1280]{1,0:T(8,128)(2,1)S(1)} %collective-permute-done.refs_1_), channel_id=1, source_target_pairs={{0,8},{8,16},{16,24},{24,28},{28,20},{20,12},{12,4},{4,0},{1,9},{9... | collective-permute-start | bytes 1228808 | tf_op jit(solution)/shard_map/ppermute | solution.py:326
  15.6 18.7 %collective-permute-start.3 = (bf16[160,1280]{1,0:T(8,128)(2,1)S(1)}, bf16[160,1280]{1,0:T(8,128)(2,1)S(1)}, u32[]{:S(2)}, u32[]{:S(2)}) collective-permute-start(bf16[160,1280]{1,0:T(8,128)(2,1)S(1)} %collective-permute-done.1.refs_2_), channel_id=1, source_target_pairs={{8,0},{16,8},{24,16},{28,24},{20,28},{12,20},{4,12},{0,4},{9,1},{1... | collective-permute-start | bytes 1228808 | tf_op jit(solution)/shard_map/ppermute | solution.py:327
  15.6 18.6 %collective-permute-start.10 = (bf16[2,320,256]{2,1,0:T(8,128)(2,1)S(1)}, bf16[2,320,256]{2,1,0:T(8,128)(2,1)S(1)}, u32[]{:S(2)}, u32[]{:S(2)}) collective-permute-start(bf16[2,320,256]{2,1,0:T(8,128)(2,1)S(1)} %get-tuple-element.70.own.refs_0_), channel_id=1, source_target_pairs={{0,2},{1,3},{2,0},{3,1},{4,6},{5,7},{6,4},{7,5},{8,10},{9,11},{10,... | collective-permute-start | bytes 983048 | tf_op jit(solution)/shard_map/ppermute | solution.py:366
  22.2 14.1 %collective-permute-start.11 = (bf16[2,320,256]{2,1,0:T(8,128)(2,1)S(1)}, bf16[2,320,256]{2,1,0:T(8,128)(2,1)S(1)}, u32[]{:S(2)}, u32[]{:S(2)}) collective-permute-start(bf16[2,320,256]{2,1,0:T(8,128)(2,1)S(1)} %get-tuple-element.70.own.refs_0_), channel_id=1, source_target_pairs={{0,1},{1,0},{2,3},{3,2},{4,5},{5,4},{6,7},{7,6},{8,9},{9,8},{10,11... | collective-permute-start | bytes 983048 | tf_op jit(solution)/shard_map/ppermute | solution.py:363
  24.4 15.4 %collective-permute-start.9 = (bf16[160,1280]{1,0:T(8,128)(2,1)S(1)}, bf16[160,1280]{1,0:T(8,128)(2,1)S(1)}, u32[]{:S(2)}, u32[]{:S(2)}) collective-permute-start(bf16[160,1280]{1,0:T(8,128)(2,1)S(1)} %collective-permute-done.7.refs_6_), channel_id=1, source_target_pairs={{0,8},{8,16},{16,24},{24,28},{28,20},{20,12},{12,4},{4,0},{1,9},{9... | collective-permute-start | bytes 1228808 | tf_op jit(solution)/shard_map/ppermute | solution.py:326
  31.0 10.8 %collective-permute-start.8 = (bf16[160,1280]{1,0:T(8,128)(2,1)S(1)}, bf16[160,1280]{1,0:T(8,128)(2,1)S(1)}, u32[]{:S(2)}, u32[]{:S(2)}) collective-permute-start(bf16[160,1280]{1,0:T(8,128)(2,1)S(1)} %collective-permute-done.4.refs_7_), channel_id=1, source_target_pairs={{8,0},{16,8},{24,16},{28,24},{20,28},{12,20},{4,12},{0,4},{9,1},{1... | collective-permute-start | bytes 1228808 | tf_op jit(solution)/shard_map/ppermute | solution.py:327
  34.3 14.3 %collective-permute-start.5 = (bf16[160,1280]{1,0:T(8,128)(2,1)S(1)}, bf16[160,1280]{1,0:T(8,128)(2,1)S(1)}, u32[]{:S(2)}, u32[]{:S(2)}) collective-permute-start(bf16[160,1280]{1,0:T(8,128)(2,1)S(1)} %collective-permute-done.2.refs_3_), channel_id=1, source_target_pairs={{0,8},{8,16},{16,24},{24,28},{28,20},{20,12},{12,4},{4,0},{1,9},{9... | collective-permute-start | bytes 1228808 | tf_op jit(solution)/shard_map/ppermute | solution.py:326
  34.4 8.0 %collective-permute-start.15 = (bf16[2,320,256]{2,1,0:T(8,128)(2,1)S(1)}, bf16[2,320,256]{2,1,0:T(8,128)(2,1)S(1)}, u32[]{:S(2)}, u32[]{:S(2)}) collective-permute-start(bf16[2,320,256]{2,1,0:T(8,128)(2,1)S(1)} %get-tuple-element.76.own.refs_1_), channel_id=1, source_target_pairs={{0,2},{1,3},{2,0},{3,1},{4,6},{5,7},{6,4},{7,5},{8,10},{9,11},{10,... | collective-permute-start | bytes 983048 | tf_op jit(solution)/shard_map/ppermute | solution.py:366
  36.3 7.6 %collective-permute-start.12 = (bf16[2,320,256]{2,1,0:T(8,128)(2,1)S(1)}, bf16[2,320,256]{2,1,0:T(8,128)(2,1)S(1)}, u32[]{:S(2)}, u32[]{:S(2)}) collective-permute-start(bf16[2,320,256]{2,1,0:T(8,128)(2,1)S(1)} %collective-permute-done.10.over_x), channel_id=1, source_target_pairs={{0,1},{1,0},{2,3},{3,2},{4,5},{5,4},{6,7},{7,6},{8,9},{9,8},{10,11... | collective-permute-start | bytes 983048 | tf_op jit(solution)/shard_map/ppermute | solution.py:363
  39.8 12.5 %collective-permute-start.6 = (bf16[160,1280]{1,0:T(8,128)(2,1)S(1)}, bf16[160,1280]{1,0:T(8,128)(2,1)S(1)}, u32[]{:S(2)}, u32[]{:S(2)}) collective-permute-start(bf16[160,1280]{1,0:T(8,128)(2,1)S(1)} %collective-permute-done.3.refs_4_), channel_id=1, source_target_pairs={{8,0},{16,8},{24,16},{28,24},{20,28},{12,20},{4,12},{0,4},{9,1},{1... | collective-permute-start | bytes 1228808 | tf_op jit(solution)/shard_map/ppermute | solution.py:327
  41.9 15.5 %collective-permute-start.18 = (bf16[160,1280]{1,0:T(8,128)(2,1)S(1)}, bf16[160,1280]{1,0:T(8,128)(2,1)S(1)}, u32[]{:S(2)}, u32[]{:S(2)}) collective-permute-start(bf16[160,1280]{1,0:T(8,128)(2,1)S(1)} %collective-permute-done.9.refs_8_), channel_id=1, source_target_pairs={{0,8},{8,16},{16,24},{24,28},{28,20},{20,12},{12,4},{4,0},{1,9},{9... | collective-permute-start | bytes 1228808 | tf_op jit(solution)/shard_map/ppermute | solution.py:326
  42.3 18.7 %collective-permute-start.21 = (bf16[160,1280]{1,0:T(8,128)(2,1)S(1)}, bf16[160,1280]{1,0:T(8,128)(2,1)S(1)}, u32[]{:S(2)}, u32[]{:S(2)}) collective-permute-start(bf16[160,1280]{1,0:T(8,128)(2,1)S(1)} %collective-permute-done.8.refs_9_), channel_id=1, source_target_pairs={{8,0},{16,8},{24,16},{28,24},{20,28},{12,20},{4,12},{0,4},{9,1},{1... | collective-permute-start | bytes 1228808 | tf_op jit(solution)/shard_map/ppermute | solution.py:327
  43.9 15.6 %collective-permute-start.16 = (bf16[2,320,256]{2,1,0:T(8,128)(2,1)S(1)}, bf16[2,320,256]{2,1,0:T(8,128)(2,1)S(1)}, u32[]{:S(2)}, u32[]{:S(2)}) collective-permute-start(bf16[2,320,256]{2,1,0:T(8,128)(2,1)S(1)} %get-tuple-element.76.own.refs_1_), channel_id=1, source_target_pairs={{0,1},{1,0},{2,3},{3,2},{4,5},{5,4},{6,7},{7,6},{8,9},{9,8},{10,11... | collective-permute-start | bytes 983048 | tf_op jit(solution)/shard_map/ppermute | solution.py:363
  48.6 10.9 %collective-permute-start.17 = (bf16[2,320,256]{2,1,0:T(8,128)(2,1)S(1)}, bf16[2,320,256]{2,1,0:T(8,128)(2,1)S(1)}, u32[]{:S(2)}, u32[]{:S(2)}) collective-permute-start(bf16[2,320,256]{2,1,0:T(8,128)(2,1)S(1)} %collective-permute-done.15.over_x), channel_id=1, source_target_pairs={{0,1},{1,0},{2,3},{3,2},{4,5},{5,4},{6,7},{7,6},{8,9},{9,8},{10,11... | collective-permute-start | bytes 983048 | tf_op jit(solution)/shard_map/ppermute | solution.py:363
  52.3 10.7 %collective-permute-start.13 = (bf16[80,1280]{1,0:T(8,128)(2,1)S(1)}, bf16[80,1280]{1,0:T(8,128)(2,1)S(1)}, u32[]{:S(2)}, u32[]{:S(2)}) collective-permute-start(bf16[80,1280]{1,0:T(8,128)(2,1)S(1)} %slice.24), channel_id=1, source_target_pairs={{0,8},{8,16},{16,24},{24,28},{28,20},{20,12},{12,4},{4,0},{1,9},{9... | collective-permute-start | bytes 614408 | tf_op jit(solution)/shard_map/ppermute | solution.py:326
  57.4 7.7 %collective-permute-start.14 = (bf16[80,1280]{1,0:T(8,128)(2,1)S(1)}, bf16[80,1280]{1,0:T(8,128)(2,1)S(1)}, u32[]{:S(2)}, u32[]{:S(2)}) collective-permute-start(bf16[80,1280]{1,0:T(8,128)(2,1)S(1)} %slice.25), channel_id=1, source_target_pairs={{8,0},{16,8},{24,16},{28,24},{20,28},{12,20},{4,12},{0,4},{9,1},{1... | collective-permute-start | bytes 614408 | tf_op jit(solution)/shard_map/ppermute | solution.py:327
  60.9 8.5 %collective-permute-start.19 = (bf16[80,1280]{1,0:T(8,128)(2,1)S(1)}, bf16[80,1280]{1,0:T(8,128)(2,1)S(1)}, u32[]{:S(2)}, u32[]{:S(2)}) collective-permute-start(bf16[80,1280]{1,0:T(8,128)(2,1)S(1)} %slice.26), channel_id=1, source_target_pairs={{0,8},{8,16},{16,24},{24,28},{28,20},{20,12},{12,4},{4,0},{1,9},{9... | collective-permute-start | bytes 614408 | tf_op jit(solution)/shard_map/ppermute | solution.py:326
  61.0 8.5 %collective-permute-start.22 = (bf16[80,1280]{1,0:T(8,128)(2,1)S(1)}, bf16[80,1280]{1,0:T(8,128)(2,1)S(1)}, u32[]{:S(2)}, u32[]{:S(2)}) collective-permute-start(bf16[80,1280]{1,0:T(8,128)(2,1)S(1)} %slice.27), channel_id=1, source_target_pairs={{8,0},{16,8},{24,16},{28,24},{20,28},{12,20},{4,12},{0,4},{9,1},{1... | collective-permute-start | bytes 614408 | tf_op jit(solution)/shard_map/ppermute | solution.py:327
  63.1 11.8 %collective-permute-start.25 = (bf16[80,1280]{1,0:T(8,128)(2,1)S(1)}, bf16[80,1280]{1,0:T(8,128)(2,1)S(1)}, u32[]{:S(2)}, u32[]{:S(2)}) collective-permute-start(bf16[80,1280]{1,0:T(8,128)(2,1)S(1)} %get-tuple-element.89.refs_0_), channel_id=1, source_target_pairs={{0,8},{8,16},{16,24},{24,28},{28,20},{20,12},{12,4},{4,0},{1,9},{9... | collective-permute-start | bytes 614408 | tf_op jit(solution)/shard_map/ppermute | solution.py:326
  65.0 9.8 %collective-permute-start.26 = (bf16[80,1280]{1,0:T(8,128)(2,1)S(1)}, bf16[80,1280]{1,0:T(8,128)(2,1)S(1)}, u32[]{:S(2)}, u32[]{:S(2)}) collective-permute-start(bf16[80,1280]{1,0:T(8,128)(2,1)S(1)} %get-tuple-element.90.refs_1_), channel_id=1, source_target_pairs={{8,0},{16,8},{24,16},{28,24},{20,28},{12,20},{4,12},{0,4},{9,1},{1... | collective-permute-start | bytes 614408 | tf_op jit(solution)/shard_map/ppermute | solution.py:327
  69.4 8.3 %collective-permute-start.20 = (bf16[80,1280]{1,0:T(8,128)(2,1)S(1)}, bf16[80,1280]{1,0:T(8,128)(2,1)S(1)}, u32[]{:S(2)}, u32[]{:S(2)}) collective-permute-start(bf16[80,1280]{1,0:T(8,128)(2,1)S(1)} %get-tuple-element.90.refs_1_), channel_id=1, source_target_pairs={{0,8},{8,16},{16,24},{24,28},{28,20},{20,12},{12,4},{4,0},{1,9},{9... | collective-permute-start | bytes 614408 | tf_op jit(solution)/shard_map/ppermute | solution.py:326
  69.5 8.6 %collective-permute-start.23 = (bf16[80,1280]{1,0:T(8,128)(2,1)S(1)}, bf16[80,1280]{1,0:T(8,128)(2,1)S(1)}, u32[]{:S(2)}, u32[]{:S(2)}) collective-permute-start(bf16[80,1280]{1,0:T(8,128)(2,1)S(1)} %get-tuple-element.89.refs_0_), channel_id=1, source_target_pairs={{8,0},{16,8},{24,16},{28,24},{20,28},{12,20},{4,12},{0,4},{9,1},{1... | collective-permute-start | bytes 614408 | tf_op jit(solution)/shard_map/ppermute | solution.py:327
  79.4 7.4 %collective-permute-start.36 = (bf16[80,1280]{1,0:T(8,128)(2,1)S(1)}, bf16[80,1280]{1,0:T(8,128)(2,1)S(1)}, u32[]{:S(2)}, u32[]{:S(2)}) collective-permute-start(bf16[80,1280]{1,0:T(8,128)(2,1)S(1)} %collective-permute-done.26.refs_3_), channel_id=1, source_target_pairs={{8,0},{16,8},{24,16},{28,24},{20,28},{12,20},{4,12},{0,4},{9,1},{1... | collective-permute-start | bytes 614408 | tf_op jit(solution)/shard_map/ppermute | solution.py:327
  82.6 20.5 %collective-permute-start.24 = (bf16[320,1024]{1,0:T(8,128)(2,1)S(1)}, bf16[320,1024]{1,0:T(8,128)(2,1)S(1)}, u32[]{:S(2)}, u32[]{:S(2)}) collective-permute-start(bf16[320,1024]{1,0:T(8,128)(2,1)S(1)} %get-tuple-element.88), channel_id=1, source_target_pairs={{0,1},{1,0},{2,3},{3,2},{4,5},{5,4},{6,7},{7,6},{8,9},{9,8},{10,11... | collective-permute-start | bytes 1966088 | tf_op jit(solution)/shard_map/ppermute | solution.py:363
  82.7 7.5 %collective-permute-start.37 = (bf16[80,1280]{1,0:T(8,128)(2,1)S(1)}, bf16[80,1280]{1,0:T(8,128)(2,1)S(1)}, u32[]{:S(2)}, u32[]{:S(2)}) collective-permute-start(bf16[80,1280]{1,0:T(8,128)(2,1)S(1)} %collective-permute-done.20.refs_4_), channel_id=1, source_target_pairs={{0,8},{8,16},{16,24},{24,28},{28,20},{20,12},{12,4},{4,0},{1,9},{9... | collective-permute-start | bytes 614408 | tf_op jit(solution)/shard_map/ppermute | solution.py:326
  83.9 7.4 %collective-permute-start.38 = (bf16[80,1280]{1,0:T(8,128)(2,1)S(1)}, bf16[80,1280]{1,0:T(8,128)(2,1)S(1)}, u32[]{:S(2)}, u32[]{:S(2)}) collective-permute-start(bf16[80,1280]{1,0:T(8,128)(2,1)S(1)} %collective-permute-done.23.refs_5_), channel_id=1, source_target_pairs={{8,0},{16,8},{24,16},{28,24},{20,28},{12,20},{4,12},{0,4},{9,1},{1... | collective-permute-start | bytes 614408 | tf_op jit(solution)/shard_map/ppermute | solution.py:327
  86.8 7.9 %collective-permute-start.30 = (bf16[320,256]{1,0:T(8,128)(2,1)S(1)}, bf16[320,256]{1,0:T(8,128)(2,1)S(1)}, u32[]{:S(2)}, u32[]{:S(2)}) collective-permute-start(bf16[320,256]{1,0:T(8,128)(2,1)S(1)} %add.6), channel_id=1, source_target_pairs={{0,2},{1,3},{2,0},{3,1},{4,6},{5,7},{6,4},{7,5},{8,10},{9,11},{10,... | collective-permute-start | bytes 491528 | tf_op jit(solution)/shard_map/ppermute | solution.py:366
  96.8 7.9 %collective-permute-start.41 = (bf16[80,1280]{1,0:T(8,128)(2,1)S(1)}, bf16[80,1280]{1,0:T(8,128)(2,1)S(1)}, u32[]{:S(2)}, u32[]{:S(2)}) collective-permute-start(bf16[80,1280]{1,0:T(8,128)(2,1)S(1)} %collective-permute-done.37.refs_8_), channel_id=1, source_target_pairs={{0,8},{8,16},{16,24},{24,28},{28,20},{20,12},{12,4},{4,0},{1,9},{9... | collective-permute-start | bytes 614408 | tf_op jit(solution)/shard_map/ppermute | solution.py:326
  (24 other events, 169.9 us)
